TPU v7x, 32 devices: a whole 2x2x4 slice. The times are simulated.
32 devices in a mesh: ep: 16 (over z, y, x), tp: 2 (over core).
Axes of the slice: x: 2, y: 2, z: 4, core: 2. Of those that a mesh axis runs over, the one named last changes fastest.
Arguments:
- tokens: bfloat16 [256, 7168], P('ep', 'tp'), may hold values from -6 to 6
- expert_ids: int32 [256, 8], P('ep'), may hold values from 0 to 15, all different within a row; in each aligned block of 16 rows (0 to 15, 16 to 31, ...) at most 16 rows name the same one
- gate_weights: float32 [256, 8], P('ep'), may hold values from 0.1 to 1
- expert_gate_up: bfloat16 [16, 7168, 2, 1024], P('ep', None, None, 'tp'), may hold values from -0.0625 to 0.0625
- expert_down: bfloat16 [16, 7168, 1024], P('ep', None, 'tp'), may hold values from -0.1875 to 0.1875
- queries: bfloat16 [256, 64, 576], P('ep', 'tp'), may hold values from -8 to 8
- latent_cache: bfloat16 [768, 16, 576], P('ep'), may hold values from -8 to 8
- block_source: int32 [768], replicated, may hold values from 0 to 767, as said below
- block_request: int32 [768], P('ep'), may hold values from -1 to 15, as said below
- block_used: int32 [768], P('ep'), may hold values from 0 to 16, as said below
Outputs:
- moe_out: bfloat16 [256, 7168], P('ep', 'tp')
- attention_out: bfloat16 [256, 64, 512], P('ep', 'tp')
Inputs may be any that keep to these rules, and one draw needn't show every extreme that they name: `expert_ids`: each row names 8 different experts; among the rows of one index of ep no expert is named by more than 16 rows, a bound that some block reaches. `block_source`: A permutation. `block_request`: within one index of ep each row holds a run of 1 to 3 consecutive slots, rows in order from the first slot, unused slots (-1) after them; some index of ep holds 3 slots for every row, and some has unused slots. `block_used`: 16 in every used slot but a row's last one, which holds 2 to 16; 0 in unused slots.
All inputs are finite; a program needn't handle non-finite values.
Results may differ from a plain program's by a relative error of at most 0.015.
Values may be sent and summed in bfloat16 or wider, within the bound.
No kernel may reach another device: no remote copies, remote signals or barrier semaphores. Data moves between devices by JAX's collectives and lax.ppermute only.
A program may use at most 64 MiB of HBM per device.

v0:
```python
import jax
import jax.numpy as jnp
from jax import lax
from jax.sharding import PartitionSpec as P

KV = 512


score_scale = 192.0 ** (-0.5)


def move_blocks(flat_cache, block_source):
    spread = lax.all_to_all(flat_cache, "ep", split_axis=1, concat_axis=0, tiled=True)
    ordered = jnp.take(spread, block_source, axis=0)
    return lax.all_to_all(ordered, "ep", split_axis=0, concat_axis=1, tiled=True)


def body(
    tokens,
    expert_ids,
    gate_weights,
    expert_gate_up,
    expert_down,
    queries,
    latent_cache,
    block_source,
    block_request,
    block_used,
):
    row_count, top_count = expert_ids.shape
    ep_size = lax.axis_size("ep")
    capacity = min(row_count, max(2, 2 * row_count * top_count // ep_size))
    slot_count = ep_size * capacity
    expert_range = jnp.arange(ep_size, dtype=jnp.int32)
    flat_destination = expert_ids.reshape(-1)
    device_hot = (flat_destination[:, None] == expert_range[None, :]).astype(jnp.int32)
    position = jnp.sum((jnp.cumsum(device_hot, axis=0) - device_hot) * device_hot, axis=1)
    slot_of = flat_destination * capacity + position
    placed = slot_of[:, None] == jnp.arange(slot_count, dtype=jnp.int32)[None, :]
    row_place = jnp.any(placed.reshape(row_count, top_count, slot_count), axis=1).astype(
        jnp.bfloat16
    )
    weight_place = jnp.sum(
        jnp.where(placed, gate_weights.reshape(-1)[:, None], 0.0).reshape(
            row_count, top_count, slot_count
        ),
        axis=1,
    )
    contract_rows = (((0,), (0,)), ((), ()))
    full_rows = lax.all_gather(tokens, "tp", axis=1, tiled=True)
    outgoing = lax.dot_general(
        row_place, full_rows, contract_rows, preferred_element_type=jnp.float32
    ).astype(jnp.bfloat16)
    arrived = lax.all_to_all(
        outgoing.reshape(ep_size, capacity, -1), "ep", split_axis=0, concat_axis=0, tiled=True
    )
    slot_rows = arrived.reshape(slot_count, -1)
    gate_and_up = jnp.einsum(
        "sd,dgf->sgf", slot_rows, expert_gate_up[0], preferred_element_type=jnp.float32
    )
    hidden = (jax.nn.silu(gate_and_up[:, 0]) * gate_and_up[:, 1]).astype(jnp.bfloat16)
    partial_value = lax.dot_general(
        hidden, expert_down[0], (((1,), (1,)), ((), ())), preferred_element_type=jnp.float32
    )
    summed = lax.psum_scatter(
        partial_value.astype(jnp.bfloat16), "tp", scatter_dimension=1, tiled=True
    )
    returned = lax.all_to_all(
        summed.reshape(ep_size, capacity, -1), "ep", split_axis=0, concat_axis=0, tiled=True
    )
    returned_rows = returned.reshape(slot_count, -1).astype(jnp.float32)
    moe_out = jnp.dot(
        weight_place,
        returned_rows,
        precision=lax.Precision.HIGHEST,
        preferred_element_type=jnp.float32,
    ).astype(jnp.bfloat16)
    slot_total, block_size, latent = latent_cache.shape
    flat_cache = latent_cache.reshape(slot_total, block_size * latent)
    cache_now = move_blocks(flat_cache, block_source)
    key_rows = cache_now.reshape(slot_total * block_size, latent)
    owner_token = jnp.repeat(block_request, block_size)
    limit_token = jnp.repeat(block_used, block_size)
    within = jnp.tile(jnp.arange(block_size, dtype=jnp.int32), slot_total)
    visible = (owner_token[None, :] == jnp.arange(row_count, dtype=jnp.int32)[:, None]) & (
        within < limit_token
    )[None, :]
    scores = (
        jnp.einsum("rhc,tc->rht", queries, key_rows, preferred_element_type=jnp.float32)
        * score_scale
    )
    scores = jnp.where(visible[:, None, :], scores, -jnp.inf)
    row_max = jnp.max(scores, axis=2, keepdims=True)
    exponent_terms = jnp.exp(scores - row_max)
    weights = (exponent_terms / jnp.sum(exponent_terms, axis=2, keepdims=True)).astype(jnp.bfloat16)
    attended = jnp.einsum(
        "rht,tc->rhc", weights, key_rows[:, :KV], preferred_element_type=jnp.float32
    ).astype(jnp.bfloat16)
    return (moe_out, attended)


def solution(mesh):
    placed = (
        P("ep", "tp"),
        P("ep", None),
        P("ep", None),
        P("ep", None, None, "tp"),
        P("ep", None, "tp"),
        P("ep", "tp", None),
        P("ep", None, None),
        P(),
        P("ep"),
        P("ep"),
    )
    return jax.shard_map(
        body,
        mesh=mesh,
        in_specs=placed,
        out_specs=(P("ep", "tp"), P("ep", "tp", None)),
        check_vma=False,
    )
```

profile of v0, /device:TPU:0, one launch (start us, length us, event | category | flops | bytes accessed | tf_op | source)
XLA Modules:
  0.0 226.0 jit_solution(387374229851591327)
XLA Ops:
  7.2 0.8 copy.34
  8.2 0.2 reduce_window_sum.11
  8.4 0.2 select_reduce_fusion.1
  8.8 2.4 %all_gather.3 = bf16[16,7168]{1,0:T(8,128)(2,1)S(1)} all-gather(bf16[16,3584]{1,0:T(8,128)(2,1)} %param.10), channel_id=1, replica_groups=mesh['ep'=16,'tp'=2] {'tp'}, dimensions={1}, use_global_device_ids=true | all-gather | bytes 344064 | tf_op jit(solution)/shard_map/all_gather | solution.py:50
  11.2 1.1 convolution_convert_fusion.1
  12.3 91.1 %all_to_all.39 = bf16[16,16,7168]{2,1,0:T(8,128)(2,1)S(1)} all-to-all(bf16[16,16,7168]{2,1,0:T(8,128)(2,1)S(1)} %bitcast.36), channel_id=1, replica_groups=mesh['ep'=16,'tp'=2] {'ep'}, dimensions={0} | all-to-all | bytes 7340032 | tf_op jit(solution)/shard_map/all_to_all | solution.py:54
  103.4 7.9 %fusion.1 = f32[256,2,512]{2,0,1:T(8,128)S(1)} fusion(bf16[256,7168,1]{1,0,2:T(8,128)(2,1)S(1)} %bitcast.40, bf16[7168,2,512]{2,1,0:T(2,128)(2,1)} %bitcast.44), kind=kOutput, calls=%fused_computation.2 | convolution fusion | flops 3758096384 | bytes 19398656 | tf_op jit(solution)/shard_map/sd,dgf->sgf/dot_general | solution.py:58
  111.4 3.9 %convolution_convert_fusion = bf16[256,7168]{1,0:T(8,128)(2,1)} fusion(bf16[1,7168,512]{2,1,0:T(8,128)(2,1)S(1)} %bitcast.46, f32[256,2,512]{2,0,1:T(8,128)S(1)} %fusion.1), kind=kOutput, calls=%fused_computation.4 | convolution fusion | flops 1881669632 | bytes 12058624 | tf_op jit(solution)/shard_map/dot_general | solution.py:62
  115.4 1.2 copy-done.2
  116.5 1.2 copy.38
  117.7 3.9 %all-to-all-start.2 = ((bf16[48,16,576]{2,0,1:T(8,128)(2,1)}), bf16[48,16,576]{2,0,1:T(8,128)(2,1)S(1)}, u32[]{:S(2)}, u32[]{:S(2)}) async-start(bf16[48,16,576]{2,0,1:T(8,128)(2,1)} %copy.38), calls=%async_computation.3 | async-start | bytes 1966080 | tf_op jit(solution)/shard_map/all_to_all | solution.py:13
  121.8 22.3 %all-to-all-done.2 = bf16[48,16,576]{2,0,1:T(8,128)(2,1)S(1)} async-done(((bf16[48,16,576]{2,0,1:T(8,128)(2,1)}), bf16[48,16,576]{2,0,1:T(8,128)(2,1)S(1)}, u32[]{:S(2)}, u32[]{:S(2)}) %all-to-all-start.2) | async-done | bytes 884768 | tf_op jit(solution)/shard_map/all_to_all | solution.py:13
  144.1 2.8 %gather_fusion = bf16[768,576]{1,0:T(8,128)(2,1)S(1)} fusion(bf16[768,576]{1,0:T(8,128)(2,1)S(1)} %bitcast.35, s32[1024]{0:T(1024)S(1)} %pad_clamp_fusion), kind=kCustom, calls=%fused_computation | custom fusion | bytes 1772544 | tf_op jit(solution)/shard_map/jit(_take)/gather | solution.py:14
  146.9 0.2 broadcast_select_fusion
  147.1 29.2 %all_to_all.40 = bf16[16,48,576]{2,1,0:T(8,128)(2,1)S(1)} all-to-all(bf16[16,48,576]{2,1,0:T(8,128)(2,1)S(1)} %broadcast_select_fusion), channel_id=1, replica_groups=mesh['ep'=16,'tp'=2] {'ep'}, dimensions={0} | all-to-all | bytes 1769472 | tf_op jit(solution)/shard_map/all_to_all | solution.py:15
  176.3 3.9 %all-to-all-start.1 = ((bf16[16,16,3584]{2,1,0:T(8,128)(2,1)}), bf16[16,16,3584]{2,1,0:T(8,128)(2,1)S(1)}, u32[]{:S(2)}, u32[]{:S(2)}) async-start(bf16[16,16,3584]{2,1,0:T(8,128)(2,1)} %bitcast.41), calls=%async_computation.2 | async-start | bytes 3670016 | tf_op jit(solution)/shard_map/all_to_all | solution.py:68
  180.6 0.1 select_reduce_fusion
  180.8 0.2 copy.39
  181.0 0.8 bitcast_select_fusion
  181.9 1.2 copy-done.1
  183.1 0.4 fusion.14
  183.5 4.2 %convolution_convert_fusion.3 = bf16[16,32,512]{2,1,0:T(8,128)(2,1)} fusion(bf16[768,576]{1,0:T(8,128)(2,1)} %bitcast.43, f32[16,32]{1,0:T(8,128)S(1)} %fusion.14, f32[16,32,768]{2,1,0:T(8,128)} %copy-done.1), kind=kOutput, calls=%fused_computation.12 | convolution fusion | flops 404096256 | bytes 4458496 | tf_op jit(solution)/shard_map/rht,tc->rhc/dot_general | solution.py:96
  187.6 30.0 %all-to-all-done.1 = bf16[16,16,3584]{2,1,0:T(8,128)(2,1)S(1)} async-done(((bf16[16,16,3584]{2,1,0:T(8,128)(2,1)}), bf16[16,16,3584]{2,1,0:T(8,128)(2,1)S(1)}, u32[]{:S(2)}, u32[]{:S(2)}) %all-to-all-start.1) | async-done | bytes 1835040 | tf_op jit(solution)/shard_map/all_to_all | solution.py:68
  217.6 1.5 convolution_convert_fusion.2
  (37 shorter events, 1.1 us)
Async XLA Ops:
  7.2 173.8 %copy-start = (bf16[16,32,576]{2,1,0:T(8,128)(2,1)S(1)}, bf16[16,32,576]{2,1,0:T(8,128)(2,1)}, u32[]{:S(2)}) copy-start(bf16[16,32,576]{2,1,0:T(8,128)(2,1)} %param.15) | copy-start | bytes 1769476
  7.2 169.1 %reduce-scatter.2.cloned.1.call-start = ((), (), s32[]{:S(2)}) async-start(), calls=%async_computation.5 | async-start | bytes 5505024 | tf_op jit(solution)/shard_map/reduce_scatter | solution.py:65
  12.3 99.1 %slice-start = ((s8[7340032]{0:T(1024)(128)(4,1)}), s8[4194304]{0:T(1024)(128)(4,1)S(1)}, s32[]{:S(2)}) async-start(s8[7340032]{0:T(1024)(128)(4,1)} %bitcast.45), calls=%async_computation.6 | async-start | bytes 8388608
  103.4 8.0 %slice-start.1 = ((s8[7340032]{0:T(1024)(128)(4,1)}), s8[3145728]{0:T(1024)(128)(4,1)S(1)}, s32[]{:S(2)}) async-start(s8[7340032]{0:T(1024)(128)(4,1)} %bitcast.45), calls=%async_computation.7 | async-start | bytes 6291456
  115.3 1.2 copy-start.2
  116.5 5.1 %copy-start.4 = (s32[768]{0:T(1024)S(1)}, s32[768]{0:T(1024)}, u32[]{:S(2)}) copy-start(s32[768]{0:T(1024)} %param.17) | copy-start | bytes 9220
  117.7 26.4 %all-to-all-start.2 = ((bf16[48,16,576]{2,0,1:T(8,128)(2,1)}), bf16[48,16,576]{2,0,1:T(8,128)(2,1)S(1)}, u32[]{:S(2)}, u32[]{:S(2)}) async-start(bf16[48,16,576]{2,0,1:T(8,128)(2,1)} %copy.38), calls=%async_computation.3 | async-start | bytes 1966080 | tf_op jit(solution)/shard_map/all_to_all | solution.py:13
  176.3 3.9 %copy-start.5 = (f32[16,8]{0,1:T(8,128)S(1)}, f32[16,8]{0,1:T(8,128)}, u32[]{:S(2)}) copy-start(f32[16,8]{0,1:T(8,128)} %param.12) | copy-start | bytes 1540
  176.3 4.0 %copy-start.6 = (s32[48]{0:T(128)S(1)}, s32[48]{0:T(128)}, u32[]{:S(2)}) copy-start(s32[48]{0:T(128)} %param.18) | copy-start | bytes 580
  176.3 4.2 %copy-start.7 = (s32[48]{0:T(128)S(1)}, s32[48]{0:T(128)}, u32[]{:S(2)}) copy-start(s32[48]{0:T(128)} %param.19) | copy-start | bytes 580
  176.3 41.3 %all-to-all-start.1 = ((bf16[16,16,3584]{2,1,0:T(8,128)(2,1)}), bf16[16,16,3584]{2,1,0:T(8,128)(2,1)S(1)}, u32[]{:S(2)}, u32[]{:S(2)}) async-start(bf16[16,16,3584]{2,1,0:T(8,128)(2,1)} %bitcast.41), calls=%async_computation.2 | async-start | bytes 3670016 | tf_op jit(solution)/shard_map/all_to_all | solution.py:68
  181.0 0.9 copy-start.3
  181.9 1.2 copy-start.1
Sparse Core Ops, SparseCore 0:
  115.5 9.8 reduce-scatter.1
where the time goes:
time: 229 us; the launch traced here: 226 us
  blocking collectives  123 us (54%)
  waiting for transfers between devices  52.4 us (23%)
  matrix products  19.4 us (8%)
  between operations  14.2 us (6%)
  local copies, waits for them, and re-layouts  7.93 us (3%)
  starting transfers between devices  7.88 us (3%)
    all_to_all x1, blocking collectives, body(): lax.all_to_all(outgoing.reshape(ep_size, capacity, -1), 'ep', split_axis=...  91.1 us
    all_to_all x1, waiting for transfers between devices, body(): lax.all_to_all(summed.reshape(ep_size, capacity, -1), 'ep', split_axis=0,...  30 us
    all_to_all x1, blocking collectives, move_blocks(): lax.all_to_all(ordered, 'ep', split_axis=0, concat_axis=1, tiled=True)  29.2 us
    all_to_all x1, waiting for transfers between devices, move_blocks(): lax.all_to_all(flat_cache, 'ep', split_axis=1, concat_axis=0, tiled=True)  22.3 us
    dot_general x1, matrix products, body(): jnp.einsum('sd,dgf->sgf', slot_rows, expert_gate_up[0], preferred_element...  7.94 us
  transfers between devices with their start and end apart: 3, of which 2 were waited for; matrix products, arithmetic and copies ran while one was open for 5% of the time, Pallas kernels for 0%

commit v1 on v0

v1 whole, which is shorter than its diff:
```python
import jax
import jax.numpy as jnp
from jax import lax
from jax.sharding import PartitionSpec as P

KV = 512


score_scale = 192.0 ** (-0.5)


def move_blocks(latent_cache, block_source):
    ep_size = lax.axis_size("ep")
    tp_size = lax.axis_size("tp")
    slots, block_size, latent = latent_cache.shape
    share = slots // tp_size
    piece = block_size * latent // ep_size
    mine = lax.dynamic_slice_in_dim(latent_cache, lax.axis_index("tp") * share, share, axis=0)
    pieces = mine.reshape(share, ep_size, piece).transpose(1, 0, 2)
    spread = lax.all_to_all(pieces, "ep", split_axis=0, concat_axis=0, tiled=True)
    every = lax.all_gather(spread, "tp", axis=0, tiled=False)
    source_device = block_source // slots
    source_slot = block_source % slots
    row = (source_slot // share) * (ep_size * share) + source_device * share + source_slot % share
    row = lax.dynamic_slice_in_dim(
        row.reshape(ep_size, tp_size, share), lax.axis_index("tp"), 1, axis=1
    ).reshape(-1)
    ordered = jnp.take(every.reshape(-1, piece), row, axis=0, mode="clip")
    arrived = lax.all_to_all(
        ordered.reshape(ep_size, share, piece), "ep", split_axis=0, concat_axis=0, tiled=True
    )
    if piece != latent:
        arrived = arrived.transpose(1, 0, 2).reshape(share, block_size, latent).transpose(1, 0, 2)
    return lax.all_gather(arrived, "tp", axis=0, tiled=False)


def ep_bits():
    ep_size = lax.axis_size("ep")
    return [1 << place for place in reversed(range(ep_size.bit_length() - 1))]


def exchange(value, bit):
    ep_size = lax.axis_size("ep")
    return lax.ppermute(value, "ep", [(index, index ^ bit) for index in range(ep_size)])


def swap_tp(value):
    tp_size = lax.axis_size("tp")
    return [
        lax.ppermute(value, "tp", [(index, (index + step) % tp_size) for index in range(tp_size)])
        for step in range(1, tp_size)
    ]


def gather_blocks(block, order):
    bits = ep_bits()[::-1]
    value = block.reshape((1,) * len(bits) + block.shape)
    for bit in order:
        value = jnp.concatenate([value, exchange(value, bit)], axis=bits.index(bit))
    return value.reshape((-1,) + block.shape[1:])


def scatter_sum(partial, order):
    bits = ep_bits()[::-1]
    ep_size = lax.axis_size("ep")
    block = (partial.shape[0] // ep_size,) + partial.shape[1:]
    value = partial.reshape((2,) * len(bits) + block)
    for bit in reversed(order):
        axis = bits.index(bit)
        kept = lax.slice_in_dim(value, 0, 1, axis=axis)
        sent = lax.slice_in_dim(value, 1, 2, axis=axis)
        value = (kept.astype(jnp.float32) + exchange(sent, bit).astype(jnp.float32)).astype(
            jnp.bfloat16
        )
    return value.reshape(block)


def three_parts(value):
    parts = []
    for _ in range(3):
        part = lax.reduce_precision(value, 8, 7)
        parts.append(part.astype(jnp.bfloat16))
        value = value - part
    return parts


def body(
    tokens,
    expert_ids,
    gate_weights,
    expert_gate_up,
    expert_down,
    queries,
    latent_cache,
    block_source,
    block_request,
    block_used,
):
    row_count, top_count = expert_ids.shape
    ep_size = lax.axis_size("ep")
    tp_size = lax.axis_size("tp")
    tp_index = lax.axis_index("tp")
    bits = ep_bits()
    orders = (bits, bits[:-2] + [bits[-1], bits[-2]])
    width = tokens.shape[1]
    cut = width // 2
    expert_range = jnp.arange(ep_size, dtype=jnp.int32)
    dense_gate = jnp.sum(
        jnp.where(
            expert_ids[:, :, None] == expert_range[None, None, :], gate_weights[:, :, None], 0.0
        ),
        axis=1,
    )
    gate_parts = jnp.concatenate(three_parts(dense_gate), axis=1)
    pad = -gate_parts.shape[1] % 128
    sent_rows = (
        jnp.concatenate([tokens[:, :cut], jnp.pad(gate_parts, ((0, 0), (0, pad)))], axis=1),
        tokens[:, cut:],
    )
    gathered = [gather_blocks(rows, order) for rows, order in zip(sent_rows, orders)]
    all_gate = gathered[0][:, cut : cut + 3 * ep_size].astype(jnp.float32)
    mine = (jnp.arange(3 * ep_size, dtype=jnp.int32) % ep_size) == lax.axis_index("ep")
    my_gate = jnp.sum(jnp.where(mine[None, :], all_gate, 0.0), axis=1)
    halves = (gathered[0][:, :cut], gathered[1])
    gate_and_up = 0.0
    for part, half_rows in enumerate(halves):
        for step, rows in enumerate([half_rows] + swap_tp(half_rows)):
            start = ((tp_index + tp_size - step) % tp_size) * width + part * cut
            weight = lax.dynamic_slice_in_dim(expert_gate_up[0], start, cut, axis=0)
            gate_and_up = gate_and_up + jnp.einsum(
                "sd,dgf->sgf", rows, weight, preferred_element_type=jnp.float32
            )
    hidden = (
        jax.nn.silu(gate_and_up[:, 0]) * gate_and_up[:, 1] * my_gate[:, None]
    ).astype(jnp.bfloat16)

    def down(start):
        weight = lax.dynamic_slice_in_dim(expert_down[0], start, cut, axis=0)
        return lax.dot_general(
            hidden, weight, (((1,), (1,)), ((), ())), preferred_element_type=jnp.float32
        ).astype(jnp.bfloat16)

    moe_parts = []
    for part, order in enumerate(orders):
        total = down(tp_index * width + part * cut).astype(jnp.float32)
        for step in range(1, tp_size):
            target = (tp_index + step) % tp_size
            other = lax.ppermute(
                down(target * width + part * cut),
                "tp",
                [(index, (index + step) % tp_size) for index in range(tp_size)],
            )
            total = total + other.astype(jnp.float32)
        moe_parts.append(scatter_sum(total.astype(jnp.bfloat16), order))
    moe_out = jnp.concatenate(moe_parts, axis=1)

    slot_total, block_size, latent = latent_cache.shape
    half = slot_total // tp_size
    key_rows = move_blocks(latent_cache, block_source).reshape(slot_total * block_size, latent)

    def per_token(values):
        return jnp.broadcast_to(
            values.reshape(tp_size, 1, half), (tp_size, block_size, half)
        ).reshape(-1)

    owner_token = per_token(block_request)
    limit_token = per_token(block_used)
    within = jnp.broadcast_to(
        jnp.arange(block_size, dtype=jnp.int32)[None, :, None], (tp_size, block_size, half)
    ).reshape(-1)
    visible = (owner_token[None, :] == jnp.arange(row_count, dtype=jnp.int32)[:, None]) & (
        within < limit_token
    )[None, :]
    scores = (
        jnp.einsum("rhc,tc->rht", queries, key_rows, preferred_element_type=jnp.float32)
        * score_scale
    )
    scores = jnp.where(visible[:, None, :], scores, -jnp.inf)
    row_max = jnp.max(scores, axis=2, keepdims=True)
    exponent_terms = jnp.exp(scores - row_max)
    weights = (exponent_terms / jnp.sum(exponent_terms, axis=2, keepdims=True)).astype(jnp.bfloat16)
    attended = jnp.einsum(
        "rht,tc->rhc", weights, key_rows[:, :KV], preferred_element_type=jnp.float32
    ).astype(jnp.bfloat16)
    return (moe_out, attended)


def solution(mesh):
    placed = (
        P("ep", "tp"),
        P("ep", None),
        P("ep", None),
        P("ep", None, None, "tp"),
        P("ep", None, "tp"),
        P("ep", "tp", None),
        P("ep", None, None),
        P(),
        P("ep"),
        P("ep"),
    )
    return jax.shard_map(
        body,
        mesh=mesh,
        in_specs=placed,
        out_specs=(P("ep", "tp"), P("ep", "tp", None)),
        check_vma=False,
    )
```

time: 229 us -> 124 us (0.54)
  blocking collectives: 123 us -> 5.3 us
  starting transfers between devices: 7.88 us -> 38.9 us
  waiting for transfers between devices: 52.4 us -> 26.3 us
  local copies, waits for them, and re-layouts: 7.93 us -> 25.8 us
  between operations: 14.2 us -> 1.1 us
  other arithmetic: 1.44 us -> 5.27 us
    all_to_all x2 -> x0, blocking collectives: 120 us -> none  [the longest x1 91.1 us: body(): lax.all_to_all(outgoing.reshape(ep_size, capacity, -1), 'ep', split_axis=...]
    all_to_all x2, waiting for transfers between devices: 52.3 us -> 0.01 us  [the longest x1 0.01 us: move_blocks(): lax.all_to_all(pieces, 'ep', split_axis=0, concat_axis=0, tiled=True)]
    ppermute x0 -> x20, waiting for transfers between devices: none -> 26.3 us  [the longest x16 26.3 us: exchange(): lax.ppermute(value, 'ep', [(index, index ^ bit) for index in range(ep_siz...]
    ppermute x0 -> x20, starting transfers between devices: none -> 25.8 us  [the longest x16 24.3 us: exchange(): lax.ppermute(value, 'ep', [(index, index ^ bit) for index in range(ep_siz...]
    dynamic_slice x0 -> x3, local copies, waits for them, and re-layouts: none -> 15.3 us  [the longest x1 15.3 us: body(): weight = lax.dynamic_slice_in_dim(expert_gate_up[0], start, cut, axis=0)]
    all_to_all x2, starting transfers between devices: 7.84 us -> 13.1 us  [the longest x1 7.12 us: move_blocks(): lax.all_to_all(pieces, 'ep', split_axis=0, concat_axis=0, tiled=True)]
    dot_general x4 -> x8, matrix products: 14.5 us -> 17.6 us  [the longest x4 11.1 us: down(): lax.dot_general(hidden, weight, (((1,), (1,)), ((), ())), preferred_eleme...]
    concatenate x0 -> x10, other arithmetic: none -> 2.95 us  [the longest x8 2.22 us: gather_blocks(): value = jnp.concatenate([value, exchange(value, bit)], axis=bits.index(bit))]
  transfers between devices with their start and end apart: 3 -> 22, of which waited for: 2 -> 10; matrix products, arithmetic and copies ran while one was open for 5% -> 37% of each run, Pallas kernels for 0% -> 0%
where the time goes in v1:
time: 124 us; the launch traced here: 123 us
  starting transfers between devices  38.9 us (31%)
  waiting for transfers between devices  26.3 us (21%)
  local copies, waits for them, and re-layouts  25.8 us (21%)
  matrix products  20.4 us (16%)
  blocking collectives  5.3 us (4%)
  other arithmetic  5.27 us (4%)
    ppermute x16, waiting for transfers between devices, exchange(): lax.ppermute(value, 'ep', [(index, index ^ bit) for index in range(ep_siz...  26.3 us
    ppermute x16, starting transfers between devices, exchange(): lax.ppermute(value, 'ep', [(index, index ^ bit) for index in range(ep_siz...  24.3 us
    dynamic_slice x1, local copies, waits for them, and re-layouts, body(): weight = lax.dynamic_slice_in_dim(expert_gate_up[0], start, cut, axis=0)  15.3 us
    dot_general x4, matrix products, down(): lax.dot_general(hidden, weight, (((1,), (1,)), ((), ())), preferred_eleme...  11.1 us
    all_to_all x1, starting transfers between devices, move_blocks(): lax.all_to_all(pieces, 'ep', split_axis=0, concat_axis=0, tiled=True)  7.12 us
    dot_general x4, matrix products, body(): jnp.einsum('sd,dgf->sgf', rows, weight, preferred_element_type=jnp.float32)  6.52 us
    all_to_all x1, starting transfers between devices, move_blocks(): lax.all_to_all(ordered.reshape(ep_size, share, piece), 'ep', split_axis=0...  5.98 us
    unnamed x21, local copies, waits for them, and re-layouts  5.46 us
  transfers between devices with their start and end apart: 22, of which 10 were waited for; matrix products, arithmetic and copies ran while one was open for 37% of the time, Pallas kernels for 0%

profile of v1, /device:TPU:0, one launch (start us, length us, event | category | flops | bytes accessed | tf_op | source)
XLA Modules:
  0.0 123.1 jit_solution(839778044248355591)
XLA Ops:
  3.3 4.1 %collective-permute-start = (bf16[1,1,1,1,16,1920]{5,4,3,2,1,0:T(8,128)(2,1)S(1)}, bf16[1,1,1,1,16,1920]{5,4,3,2,1,0:T(8,128)(2,1)S(1)}, u32[]{:S(2)}, u32[]{:S(2)}) collective-permute-start(bf16[1,1,1,1,16,1920]{5,4,3,2,1,0:T(8,128)(2,1)S(1)} %maximum_bitcast_fusion), channel_id=1, source_target_pairs={{0,16},{2,18},{4,20},{6,22},{8,24},{10,26},{12,28},{14,30},{16,0},... | collective-permute-start | bytes 184328 | tf_op jit(solution)/shard_map/ppermute | solution.py:44
  8.4 7.1 %all-to-all-start = ((bf16[16,24,576]{2,1,0:T(8,128)(2,1)}), bf16[16,24,576]{2,1,0:T(8,128)(2,1)S(1)}, u32[]{:S(2)}, u32[]{:S(2)}) async-start(bf16[16,24,576]{2,1,0:T(8,128)(2,1)} %bitcast.85), calls=%async_computation | async-start | bytes 983040 | tf_op jit(solution)/shard_map/all_to_all | solution.py:20
  16.3 15.3 %constant_dynamic-slice_fusion.3 = (bf16[1,1792,2,512]{3,2,1,0:T(2,128)(2,1)}, bf16[1,1792,2,512]{3,2,1,0:T(2,128)(2,1)}, bf16[1,1792,2,512]{3,2,1,0:T(2,128)(2,1)}, bf16[1,1792,2,512]{3,2,1,0:T(2,128)(2,1)}) fusion(bf16[1,7168,2,512]{3,2,1,0:T(2,128)(2,1)} %param.13, s32[]{:T(128)S(6)} %select_n.89, s32[]{:T(128)S(6)} %select_n.87, s32[]{:T(128)S(6)} %select_n.91, ...), kind=kLoop, calls=%fused_computation.113 | loop fusion | bytes 29360144 | tf_op jit(solution)/shard_map/dynamic_slice | solution.py:129
  31.6 2.0 %collective-permute-start.6 = (bf16[1,1,1,2,16,1792]{5,4,3,2,1,0:T(8,128)(2,1)S(1)}, bf16[1,1,1,2,16,1792]{5,4,3,2,1,0:T(8,128)(2,1)S(1)}, u32[]{:S(2)}, u32[]{:S(2)}) collective-permute-start(bf16[1,1,1,2,16,1792]{5,4,3,2,1,0:T(8,128)(2,1)S(1)} %pad_maximum_fusion.7), channel_id=1, source_target_pairs={{0,8},{2,10},{4,12},{6,14},{8,0},{10,2},{12,4},{14,6},{16,24},{18,... | collective-permute-start | bytes 344072 | tf_op jit(solution)/shard_map/ppermute | solution.py:44
  33.8 3.5 %collective-permute-done.6 = bf16[1,1,1,2,16,1792]{5,4,3,2,1,0:T(8,128)(2,1)S(1)} collective-permute-done((bf16[1,1,1,2,16,1792]{5,4,3,2,1,0:T(8,128)(2,1)S(1)}, bf16[1,1,1,2,16,1792]{5,4,3,2,1,0:T(8,128)(2,1)S(1)}, u32[]{:S(2)}, u32[]{:S(2)}) %collective-permute-start.6) | collective-permute-done | bytes 114720 | tf_op jit(solution)/shard_map/ppermute | solution.py:44
  40.4 3.0 %collective-permute-done.7 = bf16[1,1,2,2,16,1792]{5,4,3,2,1,0:T(8,128)(2,1)S(1)} collective-permute-done((bf16[1,1,2,2,16,1792]{5,4,3,2,1,0:T(8,128)(2,1)S(1)}, bf16[1,1,2,2,16,1792]{5,4,3,2,1,0:T(8,128)(2,1)S(1)}, u32[]{:S(2)}, u32[]{:S(2)}) %collective-permute-start.7) | collective-permute-done | bytes 229408 | tf_op jit(solution)/shard_map/ppermute | solution.py:44
  48.3 2.5 %all-gather = bf16[32,24,576]{2,1,0:T(8,128)(2,1)S(1)} all-gather(bf16[16,24,576]{2,1,0:T(8,128)(2,1)S(1)} %all-to-all-done), channel_id=2, replica_groups=mesh['ep'=16,'tp'=2] {'tp'}, dimensions={0}, use_global_device_ids=true | all-gather | bytes 1327104 | tf_op jit(solution)/shard_map/all_gather | solution.py:21
  50.8 2.6 %gather_fusion = bf16[384,576]{1,0:T(8,128)(2,1)} fusion(bf16[768,576]{1,0:T(8,128)(2,1)S(1)} %bitcast.86, s32[1024]{0:T(1024)S(1)} %pad_clamp_fusion), kind=kCustom, calls=%fused_computation | custom fusion | bytes 886272 | tf_op jit(solution)/shard_map/jit(_take)/gather | solution.py:28
  53.4 6.0 %all-to-all-start.1 = ((bf16[16,24,576]{2,1,0:T(8,128)(2,1)}), bf16[16,24,576]{2,1,0:T(8,128)(2,1)S(1)}, u32[]{:S(2)}, u32[]{:S(2)}) async-start(bf16[16,24,576]{2,1,0:T(8,128)(2,1)} %bitcast.24), calls=%async_computation.1 | async-start | bytes 983040 | tf_op jit(solution)/shard_map/all_to_all | solution.py:29
  60.6 3.1 %fusion.3 = f32[256,2,512]{2,0,1:T(8,128)S(1)} fusion(bf16[256,1792,1]{1,0,2:T(8,128)(2,1)S(1)} %bitcast.96, bf16[1,1792,2,512]{3,2,1,0:T(2,128)(2,1)} %get-tuple-element.5), kind=kOutput, calls=%fused_computation.4 | convolution fusion | flops 939524096 | bytes 5636096 | tf_op jit(solution)/shard_map/sd,dgf->sgf/dot_general | solution.py:130
  71.2 3.2 %convolution_convert_fusion.2 = bf16[256,1792]{1,0:T(8,128)(2,1)} fusion(bf16[1,7168,512]{2,1,0:T(8,128)(2,1)} %param.14, s32[]{:T(128)S(6)} %select_n.89, bf16[256,1,512]{2,0,1:T(8,128)(2,1)S(1)} %fusion.43), kind=kOutput, calls=%fused_computation.16 | convolution fusion | flops 470220800 | bytes 3014660 | tf_op jit(solution)/shard_map/dot_general | solution.py:139
  74.9 2.8 %all-gather.1 = bf16[32,24,576]{2,1,0:T(8,128)(2,1)S(1)} all-gather(bf16[16,24,576]{2,1,0:T(8,128)(2,1)S(1)} %all-to-all-done.1), channel_id=3, replica_groups=mesh['ep'=16,'tp'=2] {'tp'}, dimensions={0}, use_global_device_ids=true | all-gather | bytes 1327104 | tf_op jit(solution)/shard_map/all_gather | solution.py:34
  78.9 3.1 %convolution_convert_fusion = bf16[256,1792]{1,0:T(8,128)(2,1)} fusion(bf16[1,7168,512]{2,1,0:T(8,128)(2,1)} %param.14, s32[]{:T(128)S(6)} %select_n.91, bf16[256,1,512]{2,0,1:T(8,128)(2,1)S(1)} %fusion.43), kind=kOutput, calls=%fused_computation.14 | convolution fusion | flops 470220800 | bytes 3014660 | tf_op jit(solution)/shard_map/dot_general | solution.py:139
  82.4 2.4 %add_convert_fusion.1 = bf16[256,1792]{1,0:T(8,128)(2,1)S(1)} fusion(bf16[256,1792]{1,0:T(8,128)(2,1)} %collective-permute-done.10, bf16[1,7168,512]{2,1,0:T(8,128)(2,1)} %param.14, s32[]{:T(128)S(6)} %select_n.94, bf16[256,1,512]{2,0,1:T(8,128)(2,1)S(1)} %fusion.43), kind=kOutput, calls=%fused_computation.27 | convolution fusion | flops 472055808 | bytes 3932164 | tf_op jit(solution)/shard_map/dot_general | solution.py:139
  85.6 1.9 %collective-permute-start.11 = (bf16[1,2,2,2,16,1792]{5,4,3,2,1,0:T(8,128)(2,1)}, bf16[1,2,2,2,16,1792]{5,4,3,2,1,0:T(8,128)(2,1)}, u32[]{:S(2)}, u32[]{:S(2)}) collective-permute-start(bf16[1,2,2,2,16,1792]{5,4,3,2,1,0:T(8,128)(2,1)} %bitcast.16), channel_id=1, source_target_pairs={{0,2},{2,0},{4,6},{6,4},{8,10},{10,8},{12,14},{14,12},{16,18},{18,... | collective-permute-start | bytes 1376264 | tf_op jit(solution)/shard_map/ppermute | solution.py:44
  87.6 1.9 %convolution_convert_fusion.4 = bf16[16,32,512]{2,1,0:T(8,128)(2,1)} fusion(bf16[768,576]{1,0:T(8,128)(2,1)S(1)} %bitcast.94, f32[16,32]{1,0:T(8,128)S(1)} %fusion.73, f32[16,32,768]{2,1,0:T(8,128)S(1)} %bitcast_select_fusion), kind=kOutput, calls=%fused_computation.37 | convolution fusion | flops 404096256 | bytes 4464640 | tf_op jit(solution)/shard_map/rht,tc->rhc/dot_general | solution.py:182
  89.5 2.4 %add_convert_fusion = bf16[256,1792]{1,0:T(8,128)(2,1)S(1)} fusion(bf16[256,1792]{1,0:T(8,128)(2,1)} %collective-permute-done.15, bf16[1,7168,512]{2,1,0:T(8,128)(2,1)} %param.14, s32[]{:T(128)S(6)} %select_n.95, bf16[256,1,512]{2,0,1:T(8,128)(2,1)S(1)} %fusion.43), kind=kOutput, calls=%fused_computation.24 | convolution fusion | flops 472055808 | bytes 3932164 | tf_op jit(solution)/shard_map/dot_general | solution.py:139
  93.5 5.2 %collective-permute-done.11 = bf16[1,2,2,2,16,1792]{5,4,3,2,1,0:T(8,128)(2,1)} collective-permute-done((bf16[1,2,2,2,16,1792]{5,4,3,2,1,0:T(8,128)(2,1)}, bf16[1,2,2,2,16,1792]{5,4,3,2,1,0:T(8,128)(2,1)}, u32[]{:S(2)}, u32[]{:S(2)}) %collective-permute-start.11) | collective-permute-done | bytes 458784 | tf_op jit(solution)/shard_map/ppermute | solution.py:44
  99.9 1.8 %collective-permute-start.12 = (bf16[1,1,2,2,16,1792]{5,4,3,2,1,0:T(8,128)(2,1)S(1)}, bf16[1,1,2,2,16,1792]{5,4,3,2,1,0:T(8,128)(2,1)S(1)}, u32[]{:S(2)}, u32[]{:S(2)}) collective-permute-start(bf16[1,1,2,2,16,1792]{5,4,3,2,1,0:T(8,128)(2,1)S(1)} %slice.106), channel_id=1, source_target_pairs={{0,4},{2,6},{4,0},{6,2},{8,12},{10,14},{12,8},{14,10},{16,20},{18,... | collective-permute-start | bytes 688136 | tf_op jit(solution)/shard_map/ppermute | solution.py:44
  101.7 3.8 %collective-permute-done.16 = bf16[2,1,2,2,16,1792]{5,4,3,2,1,0:T(8,128)(2,1)S(1)} collective-permute-done((bf16[2,1,2,2,16,1792]{5,4,3,2,1,0:T(8,128)(2,1)S(1)}, bf16[2,1,2,2,16,1792]{5,4,3,2,1,0:T(8,128)(2,1)S(1)}, u32[]{:S(2)}, u32[]{:S(2)}) %collective-permute-start.16) | collective-permute-done | bytes 458784 | tf_op jit(solution)/shard_map/ppermute | solution.py:44
  105.7 3.5 %collective-permute-done.12 = bf16[1,1,2,2,16,1792]{5,4,3,2,1,0:T(8,128)(2,1)S(1)} collective-permute-done((bf16[1,1,2,2,16,1792]{5,4,3,2,1,0:T(8,128)(2,1)S(1)}, bf16[1,1,2,2,16,1792]{5,4,3,2,1,0:T(8,128)(2,1)S(1)}, u32[]{:S(2)}, u32[]{:S(2)}) %collective-permute-start.12) | collective-permute-done | bytes 229408 | tf_op jit(solution)/shard_map/ppermute | solution.py:44
  114.8 2.4 %collective-permute-start.14 = (bf16[1,1,1,1,16,1792]{5,4,3,2,1,0:T(8,128)(2,1)S(1)}, bf16[1,1,1,1,16,1792]{5,4,3,2,1,0:T(8,128)(2,1)S(1)}, u32[]{:S(2)}, u32[]{:S(2)}) collective-permute-start(bf16[1,1,1,1,16,1792]{5,4,3,2,1,0:T(8,128)(2,1)S(1)} %slice.110), channel_id=1, source_target_pairs={{0,16},{2,18},{4,20},{6,22},{8,24},{10,26},{12,28},{14,30},{16,0},... | collective-permute-start | bytes 172040 | tf_op jit(solution)/shard_map/ppermute | solution.py:44
  117.3 1.8 %collective-permute-start.19 = (bf16[1,1,1,1,16,1792]{5,4,3,2,1,0:T(8,128)(2,1)S(1)}, bf16[1,1,1,1,16,1792]{5,4,3,2,1,0:T(8,128)(2,1)S(1)}, u32[]{:S(2)}, u32[]{:S(2)}) collective-permute-start(bf16[1,1,1,1,16,1792]{5,4,3,2,1,0:T(8,128)(2,1)S(1)} %slice.118), channel_id=1, source_target_pairs={{0,16},{2,18},{4,20},{6,22},{8,24},{10,26},{12,28},{14,30},{16,0},... | collective-permute-start | bytes 172040 | tf_op jit(solution)/shard_map/ppermute | solution.py:44
  119.9 2.5 %collective-permute-done.19 = bf16[1,1,1,1,16,1792]{5,4,3,2,1,0:T(8,128)(2,1)S(1)} collective-permute-done((bf16[1,1,1,1,16,1792]{5,4,3,2,1,0:T(8,128)(2,1)S(1)}, bf16[1,1,1,1,16,1792]{5,4,3,2,1,0:T(8,128)(2,1)S(1)}, u32[]{:S(2)}, u32[]{:S(2)}) %collective-permute-start.19) | collective-permute-done | bytes 57376 | tf_op jit(solution)/shard_map/ppermute | solution.py:44
  (103 shorter events, 34.0 us)
Async XLA Ops:
  0.7 15.4 %copy-start.8 = (s32[48]{0:T(128)S(1)}, s32[48]{0:T(128)}, u32[]{:S(2)}) copy-start(s32[48]{0:T(128)} %param.19) | copy-start | bytes 580
  3.3 30.2 %collective-permute-start = (bf16[1,1,1,1,16,1920]{5,4,3,2,1,0:T(8,128)(2,1)S(1)}, bf16[1,1,1,1,16,1920]{5,4,3,2,1,0:T(8,128)(2,1)S(1)}, u32[]{:S(2)}, u32[]{:S(2)}) collective-permute-start(bf16[1,1,1,1,16,1920]{5,4,3,2,1,0:T(8,128)(2,1)S(1)} %maximum_bitcast_fusion), channel_id=1, source_target_pairs={{0,16},{2,18},{4,20},{6,22},{8,24},{10,26},{12,28},{14,30},{16,0},... | collective-permute-start | bytes 184328 | tf_op jit(solution)/shard_map/ppermute | solution.py:44
  7.4 24.1 %collective-permute-start.5 = (bf16[1,1,1,1,16,1792]{5,4,3,2,1,0:T(8,128)(2,1)S(1)}, bf16[1,1,1,1,16,1792]{5,4,3,2,1,0:T(8,128)(2,1)S(1)}, u32[]{:S(2)}, u32[]{:S(2)}) collective-permute-start(bf16[1,1,1,1,16,1792]{5,4,3,2,1,0:T(8,128)(2,1)S(1)} %get-tuple-element.9), channel_id=1, source_target_pairs={{0,16},{2,18},{4,20},{6,22},{8,24},{10,26},{12,28},{14,30},{16,0},... | collective-permute-start | bytes 172040 | tf_op jit(solution)/shard_map/ppermute | solution.py:44
  8.4 39.8 %all-to-all-start = ((bf16[16,24,576]{2,1,0:T(8,128)(2,1)}), bf16[16,24,576]{2,1,0:T(8,128)(2,1)S(1)}, u32[]{:S(2)}, u32[]{:S(2)}) async-start(bf16[16,24,576]{2,1,0:T(8,128)(2,1)} %bitcast.85), calls=%async_computation | async-start | bytes 983040 | tf_op jit(solution)/shard_map/all_to_all | solution.py:20
  31.6 5.6 %collective-permute-start.6 = (bf16[1,1,1,2,16,1792]{5,4,3,2,1,0:T(8,128)(2,1)S(1)}, bf16[1,1,1,2,16,1792]{5,4,3,2,1,0:T(8,128)(2,1)S(1)}, u32[]{:S(2)}, u32[]{:S(2)}) collective-permute-start(bf16[1,1,1,2,16,1792]{5,4,3,2,1,0:T(8,128)(2,1)S(1)} %pad_maximum_fusion.7), channel_id=1, source_target_pairs={{0,8},{2,10},{4,12},{6,14},{8,0},{10,2},{12,4},{14,6},{16,24},{18,... | collective-permute-start | bytes 344072 | tf_op jit(solution)/shard_map/ppermute | solution.py:44
  33.6 5.2 %collective-permute-start.1 = (bf16[1,1,1,2,16,1920]{5,4,3,2,1,0:T(8,128)(2,1)S(1)}, bf16[1,1,1,2,16,1920]{5,4,3,2,1,0:T(8,128)(2,1)S(1)}, u32[]{:S(2)}, u32[]{:S(2)}) collective-permute-start(bf16[1,1,1,2,16,1920]{5,4,3,2,1,0:T(8,128)(2,1)S(1)} %pad_maximum_fusion.6), channel_id=1, source_target_pairs={{0,8},{2,10},{4,12},{6,14},{8,0},{10,2},{12,4},{14,6},{16,24},{18,... | collective-permute-start | bytes 368648 | tf_op jit(solution)/shard_map/ppermute | solution.py:44
  37.3 6.1 %collective-permute-start.7 = (bf16[1,1,2,2,16,1792]{5,4,3,2,1,0:T(8,128)(2,1)S(1)}, bf16[1,1,2,2,16,1792]{5,4,3,2,1,0:T(8,128)(2,1)S(1)}, u32[]{:S(2)}, u32[]{:S(2)}) collective-permute-start(bf16[1,1,2,2,16,1792]{5,4,3,2,1,0:T(8,128)(2,1)S(1)} %pad_maximum_fusion.5), channel_id=1, source_target_pairs={{0,2},{2,0},{4,6},{6,4},{8,10},{10,8},{12,14},{14,12},{16,18},{18,... | collective-permute-start | bytes 688136 | tf_op jit(solution)/shard_map/ppermute | solution.py:44
  38.8 8.5 %collective-permute-start.2 = (bf16[1,1,2,2,16,1920]{5,4,3,2,1,0:T(8,128)(2,1)S(1)}, bf16[1,1,2,2,16,1920]{5,4,3,2,1,0:T(8,128)(2,1)S(1)}, u32[]{:S(2)}, u32[]{:S(2)}) collective-permute-start(bf16[1,1,2,2,16,1920]{5,4,3,2,1,0:T(8,128)(2,1)S(1)} %pad_maximum_fusion.4), channel_id=1, source_target_pairs={{0,4},{2,6},{4,0},{6,2},{8,12},{10,14},{12,8},{14,10},{16,20},{18,... | collective-permute-start | bytes 737288 | tf_op jit(solution)/shard_map/ppermute | solution.py:44
  44.2 15.2 %collective-permute-start.8 = (bf16[2,1,2,2,16,1792]{5,4,3,2,1,0:T(8,128)(2,1)}, bf16[2,1,2,2,16,1792]{5,4,3,2,1,0:T(8,128)(2,1)}, u32[]{:S(2)}, u32[]{:S(2)}) collective-permute-start(bf16[2,1,2,2,16,1792]{5,4,3,2,1,0:T(8,128)(2,1)} %pad_maximum_fusion.3), channel_id=1, source_target_pairs={{0,4},{2,6},{4,0},{6,2},{8,12},{10,14},{12,8},{14,10},{16,20},{18,... | collective-permute-start | bytes 1376264 | tf_op jit(solution)/shard_map/ppermute | solution.py:44
  47.4 16.3 %collective-permute-start.3 = (bf16[1,2,2,2,16,1920]{5,4,3,2,1,0:T(8,128)(2,1)S(1)}, bf16[1,2,2,2,16,1920]{5,4,3,2,1,0:T(8,128)(2,1)S(1)}, u32[]{:S(2)}, u32[]{:S(2)}) collective-permute-start(bf16[1,2,2,2,16,1920]{5,4,3,2,1,0:T(8,128)(2,1)S(1)} %pad_maximum_fusion.2), channel_id=1, source_target_pairs={{0,2},{2,0},{4,6},{6,4},{8,10},{10,8},{12,14},{14,12},{16,18},{18,... | collective-permute-start | bytes 1474568 | tf_op jit(solution)/shard_map/ppermute | solution.py:44
  53.4 21.5 %all-to-all-start.1 = ((bf16[16,24,576]{2,1,0:T(8,128)(2,1)}), bf16[16,24,576]{2,1,0:T(8,128)(2,1)S(1)}, u32[]{:S(2)}, u32[]{:S(2)}) async-start(bf16[16,24,576]{2,1,0:T(8,128)(2,1)} %bitcast.24), calls=%async_computation.1 | async-start | bytes 983040 | tf_op jit(solution)/shard_map/all_to_all | solution.py:29
  60.5 6.4 %collective-permute-start.9 = (bf16[256,1792]{1,0:T(8,128)(2,1)S(1)}, bf16[256,1792]{1,0:T(8,128)(2,1)S(1)}, u32[]{:S(2)}, u32[]{:S(2)}) collective-permute-start(bf16[256,1792]{1,0:T(8,128)(2,1)S(1)} %bitcast.95), channel_id=1, source_target_pairs={{0,1},{1,0},{2,3},{3,2},{4,5},{5,4},{6,7},{7,6},{8,9},{9,8},{10,11... | collective-permute-start | bytes 2752520 | tf_op jit(solution)/shard_map/ppermute | solution.py:50
  64.0 5.0 %collective-permute-start.4 = (bf16[256,1792]{1,0:T(8,128)(2,1)S(1)}, bf16[256,1792]{1,0:T(8,128)(2,1)S(1)}, u32[]{:S(2)}, u32[]{:S(2)}) collective-permute-start(bf16[256,1792]{1,0:T(8,128)(2,1)S(1)} %slice.99), channel_id=1, source_target_pairs={{0,1},{1,0},{2,3},{3,2},{4,5},{5,4},{6,7},{7,6},{8,9},{9,8},{10,11... | collective-permute-start | bytes 2752520 | tf_op jit(solution)/shard_map/ppermute | solution.py:50
  74.4 8.0 %collective-permute-start.10 = (bf16[256,1792]{1,0:T(8,128)(2,1)}, bf16[256,1792]{1,0:T(8,128)(2,1)}, u32[]{:S(2)}, u32[]{:S(2)}) collective-permute-start(bf16[256,1792]{1,0:T(8,128)(2,1)} %convolution_convert_fusion.2), channel_id=1, source_target_pairs={{0,1},{1,0},{2,3},{3,2},{4,5},{5,4},{6,7},{7,6},{8,9},{9,8},{10,11... | collective-permute-start | bytes 2752520 | tf_op jit(solution)/shard_map/ppermute | solution.py:148
  82.0 7.5 %collective-permute-start.15 = (bf16[256,1792]{1,0:T(8,128)(2,1)}, bf16[256,1792]{1,0:T(8,128)(2,1)}, u32[]{:S(2)}, u32[]{:S(2)}) collective-permute-start(bf16[256,1792]{1,0:T(8,128)(2,1)} %convolution_convert_fusion), channel_id=1, source_target_pairs={{0,1},{1,0},{2,3},{3,2},{4,5},{5,4},{6,7},{7,6},{8,9},{9,8},{10,11... | collective-permute-start | bytes 2752520 | tf_op jit(solution)/shard_map/ppermute | solution.py:148
  85.6 13.1 %collective-permute-start.11 = (bf16[1,2,2,2,16,1792]{5,4,3,2,1,0:T(8,128)(2,1)}, bf16[1,2,2,2,16,1792]{5,4,3,2,1,0:T(8,128)(2,1)}, u32[]{:S(2)}, u32[]{:S(2)}) collective-permute-start(bf16[1,2,2,2,16,1792]{5,4,3,2,1,0:T(8,128)(2,1)} %bitcast.16), channel_id=1, source_target_pairs={{0,2},{2,0},{4,6},{6,4},{8,10},{10,8},{12,14},{14,12},{16,18},{18,... | collective-permute-start | bytes 1376264 | tf_op jit(solution)/shard_map/ppermute | solution.py:44
  92.0 13.5 %collective-permute-start.16 = (bf16[2,1,2,2,16,1792]{5,4,3,2,1,0:T(8,128)(2,1)S(1)}, bf16[2,1,2,2,16,1792]{5,4,3,2,1,0:T(8,128)(2,1)S(1)}, u32[]{:S(2)}, u32[]{:S(2)}) collective-permute-start(bf16[2,1,2,2,16,1792]{5,4,3,2,1,0:T(8,128)(2,1)S(1)} %slice.112), channel_id=1, source_target_pairs={{0,4},{2,6},{4,0},{6,2},{8,12},{10,14},{12,8},{14,10},{16,20},{18,... | collective-permute-start | bytes 1376264 | tf_op jit(solution)/shard_map/ppermute | solution.py:44
  99.9 9.4 %collective-permute-start.12 = (bf16[1,1,2,2,16,1792]{5,4,3,2,1,0:T(8,128)(2,1)S(1)}, bf16[1,1,2,2,16,1792]{5,4,3,2,1,0:T(8,128)(2,1)S(1)}, u32[]{:S(2)}, u32[]{:S(2)}) collective-permute-start(bf16[1,1,2,2,16,1792]{5,4,3,2,1,0:T(8,128)(2,1)S(1)} %slice.106), channel_id=1, source_target_pairs={{0,4},{2,6},{4,0},{6,2},{8,12},{10,14},{12,8},{14,10},{16,20},{18,... | collective-permute-start | bytes 688136 | tf_op jit(solution)/shard_map/ppermute | solution.py:44
  105.4 17.6 %copy-start.1 = (bf16[48,16,576]{2,1,0:T(8,128)(2,1)S(1)}, bf16[48,16,576]{2,1,0:T(8,128)(2,1)}, u32[]{:S(2)}) copy-start(bf16[48,16,576]{2,1,0:T(8,128)(2,1)} %param.16) | copy-start | bytes 2654212
  105.6 6.1 %collective-permute-start.17 = (bf16[1,1,2,2,16,1792]{5,4,3,2,1,0:T(8,128)(2,1)S(1)}, bf16[1,1,2,2,16,1792]{5,4,3,2,1,0:T(8,128)(2,1)S(1)}, u32[]{:S(2)}, u32[]{:S(2)}) collective-permute-start(bf16[1,1,2,2,16,1792]{5,4,3,2,1,0:T(8,128)(2,1)S(1)} %slice.114), channel_id=1, source_target_pairs={{0,2},{2,0},{4,6},{6,4},{8,10},{10,8},{12,14},{14,12},{16,18},{18,... | collective-permute-start | bytes 688136 | tf_op jit(solution)/shard_map/ppermute | solution.py:44
  109.3 5.4 %collective-permute-start.13 = (bf16[1,1,1,2,16,1792]{5,4,3,2,1,0:T(8,128)(2,1)S(1)}, bf16[1,1,1,2,16,1792]{5,4,3,2,1,0:T(8,128)(2,1)S(1)}, u32[]{:S(2)}, u32[]{:S(2)}) collective-permute-start(bf16[1,1,1,2,16,1792]{5,4,3,2,1,0:T(8,128)(2,1)S(1)} %slice.108), channel_id=1, source_target_pairs={{0,8},{2,10},{4,12},{6,14},{8,0},{10,2},{12,4},{14,6},{16,24},{18,... | collective-permute-start | bytes 344072 | tf_op jit(solution)/shard_map/ppermute | solution.py:44
  111.7 5.5 %collective-permute-start.18 = (bf16[1,1,1,2,16,1792]{5,4,3,2,1,0:T(8,128)(2,1)S(1)}, bf16[1,1,1,2,16,1792]{5,4,3,2,1,0:T(8,128)(2,1)S(1)}, u32[]{:S(2)}, u32[]{:S(2)}) collective-permute-start(bf16[1,1,1,2,16,1792]{5,4,3,2,1,0:T(8,128)(2,1)S(1)} %slice.116), channel_id=1, source_target_pairs={{0,8},{2,10},{4,12},{6,14},{8,0},{10,2},{12,4},{14,6},{16,24},{18,... | collective-permute-start | bytes 344072 | tf_op jit(solution)/shard_map/ppermute | solution.py:44
  114.8 5.1 %collective-permute-start.14 = (bf16[1,1,1,1,16,1792]{5,4,3,2,1,0:T(8,128)(2,1)S(1)}, bf16[1,1,1,1,16,1792]{5,4,3,2,1,0:T(8,128)(2,1)S(1)}, u32[]{:S(2)}, u32[]{:S(2)}) collective-permute-start(bf16[1,1,1,1,16,1792]{5,4,3,2,1,0:T(8,128)(2,1)S(1)} %slice.110), channel_id=1, source_target_pairs={{0,16},{2,18},{4,20},{6,22},{8,24},{10,26},{12,28},{14,30},{16,0},... | collective-permute-start | bytes 172040 | tf_op jit(solution)/shard_map/ppermute | solution.py:44
  117.3 5.1 %collective-permute-start.19 = (bf16[1,1,1,1,16,1792]{5,4,3,2,1,0:T(8,128)(2,1)S(1)}, bf16[1,1,1,1,16,1792]{5,4,3,2,1,0:T(8,128)(2,1)S(1)}, u32[]{:S(2)}, u32[]{:S(2)}) collective-permute-start(bf16[1,1,1,1,16,1792]{5,4,3,2,1,0:T(8,128)(2,1)S(1)} %slice.118), channel_id=1, source_target_pairs={{0,16},{2,18},{4,20},{6,22},{8,24},{10,26},{12,28},{14,30},{16,0},... | collective-permute-start | bytes 172040 | tf_op jit(solution)/shard_map/ppermute | solution.py:44
  (7 other events, 49.7 us)

commit v2 on v1

v2 whole, which is shorter than its diff:
```python
import functools

import jax
import jax.numpy as jnp
from jax import lax
from jax.experimental import pallas as pl
from jax.experimental.pallas import tpu as pltpu
from jax.sharding import PartitionSpec as P

KV = 512


score_scale = 192.0 ** (-0.5)

WHOLE = pl.BlockSpec(memory_space=pltpu.VMEM)


def kernel_call(kernel, out_shape, arguments, flops, in_specs=None, scratch_shapes=()):
    moved = sum(array.size * array.dtype.itemsize for array in arguments)
    out_leaves = jax.tree.leaves(out_shape)
    moved += sum(array.size * array.dtype.itemsize for array in out_leaves)
    return pl.pallas_call(
        kernel,
        out_shape=out_shape,
        in_specs=in_specs or [WHOLE] * len(arguments),
        out_specs=jax.tree.map(lambda _: WHOLE, out_shape),
        scratch_shapes=scratch_shapes,
        compiler_params=pltpu.CompilerParams(vmem_limit_bytes=40 << 20),
        cost_estimate=pl.CostEstimate(flops=flops, bytes_accessed=moved, transcendentals=0),
    )(*arguments)


def tie(values, others):
    return lax.optimization_barrier((values, others))[0]


def ep_bits():
    ep_size = lax.axis_size("ep")
    return [1 << place for place in reversed(range(ep_size.bit_length() - 1))]


def exchange(value, bit):
    ep_size = lax.axis_size("ep")
    return lax.ppermute(value, "ep", [(index, index ^ bit) for index in range(ep_size)])


def pass_tp(value, step):
    tp_size = lax.axis_size("tp")
    return lax.ppermute(
        value, "tp", [(index, (index + step) % tp_size) for index in range(tp_size)]
    )


def swap_tp(value):
    return [pass_tp(value, step) for step in range(1, lax.axis_size("tp"))]


def gather_blocks(block, order, last=None):
    bits = ep_bits()[::-1]
    value = block.reshape((1,) * len(bits) + block.shape)
    for bit in order[:-1]:
        value = jnp.concatenate([value, exchange(value, bit)], axis=bits.index(bit))
    arrived = exchange(value, order[-1])
    if last is not None:
        last(value)
    return value, arrived, bits.index(order[-1])


def join(halves, axis):
    whole = jnp.concatenate(halves, axis=axis)
    return whole.reshape((-1,) + whole.shape[-1:])


def sum_kernel(rows, count, picked, *refs):
    out = refs[count]
    for place, blocks in enumerate(picked):
        total = refs[0][blocks[0] * rows : (blocks[0] + 1) * rows].astype(jnp.float32)
        for ref, block in zip(refs[1:count], blocks[1:]):
            total = total + ref[block * rows : (block + 1) * rows].astype(jnp.float32)
        out[place * rows : (place + 1) * rows] = total.astype(out.dtype)


def add_up(terms, places, rows):
    arrays = [array for array, _ in terms]
    picked = [[held.index(place) for _, held in terms] for place in places]
    shape = jax.ShapeDtypeStruct((len(places) * rows, arrays[0].shape[1]), jnp.bfloat16)
    kernel = functools.partial(sum_kernel, rows, len(arrays), picked)
    return kernel_call(kernel, shape, arrays, flops=shape.size * len(arrays))


def scatter_sum(arrays, order, rows, first=None, last=None):
    bits = ep_bits()[::-1]
    number = len(bits)
    places = [
        sum(((spot >> (number - 1 - axis)) & 1) * bit for axis, bit in enumerate(bits))
        for spot in range(1 << number)
    ]
    terms = [(array, places) for array in arrays]
    for bit in reversed(order):
        sent_places = [place for place in places if place & bit]
        places = [place for place in places if not place & bit]
        sent = add_up(terms, sent_places, rows)
        if first is not None and bit == order[-1]:
            sent = first(sent)
        if last is not None and bit == order[0]:
            sent = last(sent)
        terms = terms + [(exchange(sent, bit), [place ^ bit for place in sent_places])]
    return add_up(terms, places, rows)


def three_parts(value):
    parts = []
    for _ in range(3):
        part = lax.reduce_precision(value, 8, 7)
        parts.append(part.astype(jnp.bfloat16))
        value = value - part
    return parts


def pick(choices, index):
    value = choices[0]
    for number, choice in enumerate(choices[1:], 1):
        value = jnp.where(index == number, choice, value)
    return value


def down_kernel(step, parts, tp_size, cut, hidden, weight, *refs):
    outs, held, arrived = refs[:parts], refs[parts], refs[parts + 1]
    target = lax.rem(lax.axis_index("tp") + step, tp_size)
    copies = []
    for part in range(parts):
        start = pl.multiple_of(target * (parts * cut) + part * cut, cut)
        copies.append(
            pltpu.make_async_copy(
                weight.at[pl.ds(start, cut)],
                held.at[pl.ds(part * cut, cut)],
                arrived.at[part],
            )
        )
    for copy in copies:
        copy.start()
    width = 256 if cut % 256 == 0 else 128
    chunk = min(256, hidden.shape[0])
    for part in range(parts):
        copies[part].wait()
        for column in range(0, cut, width):
            for row in range(0, hidden.shape[0], chunk):
                outs[part][row : row + chunk, column : column + width] = lax.dot_general(
                    hidden[row : row + chunk],
                    held[part * cut + column : part * cut + column + width],
                    (((1,), (1,)), ((), ())),
                    preferred_element_type=jnp.float32,
                ).astype(jnp.bfloat16)


def down(hidden, weight, step, parts):
    tp_size = lax.axis_size("tp")
    cut = weight.shape[0] // tp_size // parts
    shape = jax.ShapeDtypeStruct((hidden.shape[0], cut), jnp.bfloat16)
    return kernel_call(
        functools.partial(down_kernel, step, parts, tp_size, cut),
        [shape] * parts,
        [hidden, weight],
        flops=2 * hidden.size * cut * parts,
        in_specs=[WHOLE, pl.BlockSpec(memory_space=pl.ANY)],
        scratch_shapes=[
            pltpu.VMEM((parts * cut, weight.shape[1]), weight.dtype),
            pltpu.SemaphoreType.DMA((parts,)),
        ],
    )


def order_kernel(index, *refs):
    rows, out = refs[:-1], refs[-1]
    columns = lax.broadcasted_iota(jnp.int32, (out.shape[0], rows[0].shape[0]), 1)
    total = jnp.zeros(out.shape, jnp.float32)
    for step, ref in enumerate(rows):
        hot = (columns == index[:, step : step + 1]).astype(jnp.bfloat16)
        total = total + jnp.dot(hot, ref[...], preferred_element_type=jnp.float32)
    out[...] = total.astype(out.dtype)


def cache_out(latent_cache):
    ep_size = lax.axis_size("ep")
    slots, block_size, latent = latent_cache.shape
    share = slots // lax.axis_size("tp")
    mine = lax.dynamic_slice_in_dim(latent_cache, lax.axis_index("tp") * share, share, axis=0)
    return mine.reshape(share, ep_size, block_size * latent // ep_size).transpose(1, 0, 2)


def cache_turn(pieces, block_source, slots):
    ep_size = lax.axis_size("ep")
    tp_size = lax.axis_size("tp")
    tp_index = lax.axis_index("tp")
    share, piece = pieces.shape[1:]
    spread = lax.all_to_all(pieces, "ep", split_axis=0, concat_axis=0, tiled=True)
    wanted = lax.dynamic_slice_in_dim(
        block_source.reshape(ep_size, tp_size, share), tp_index, 1, axis=1
    ).reshape(-1)
    place = (wanted // slots) * share + wanted % share
    holder = (wanted % slots) // share
    from_step = (tp_index + tp_size - holder) % tp_size
    index = jnp.where(
        from_step[:, None] == jnp.arange(tp_size, dtype=jnp.int32)[None, :], place[:, None], -1
    )
    rows = [part.reshape(-1, piece) for part in [spread] + swap_tp(spread)]
    shape = jax.ShapeDtypeStruct(rows[0].shape, rows[0].dtype)
    ordered = kernel_call(
        order_kernel, shape, [index] + rows, flops=2 * tp_size * rows[0].size * rows[0].shape[0]
    )
    return ordered.reshape(ep_size, share, piece)


def cache_in(ordered, block_size, latent):
    share, piece = ordered.shape[1:]
    arrived = lax.all_to_all(ordered, "ep", split_axis=0, concat_axis=0, tiled=True)
    if piece != latent:
        arrived = arrived.transpose(1, 0, 2).reshape(share, block_size, latent).transpose(1, 0, 2)
    return arrived


def attention_kernel(heads, chunk, owner, queries, *refs):
    keys, out = refs[:-1], refs[-1]
    tokens = keys[0].shape[0]
    for start in range(0, queries.shape[0], chunk):
        row = (lax.broadcasted_iota(jnp.int32, (chunk, tokens), 0) + start) // heads
        scores = []
        for step, key in enumerate(keys):
            part = lax.dot_general(
                queries[start : start + chunk],
                key[...],
                (((1,), (1,)), ((), ())),
                preferred_element_type=jnp.float32,
            )
            scores.append(
                jnp.where(row == owner[step : step + 1, :], part * score_scale, -jnp.inf)
            )
        row_max = scores[0].max(axis=1, keepdims=True)
        for part in scores[1:]:
            row_max = jnp.maximum(row_max, part.max(axis=1, keepdims=True))
        terms = [jnp.exp(part - row_max) for part in scores]
        total = sum(term.sum(axis=1, keepdims=True) for term in terms)
        attended = jnp.zeros((chunk, KV), jnp.float32)
        for term, key in zip(terms, keys):
            attended = attended + jnp.dot(
                (term / total).astype(jnp.bfloat16),
                key[:, :KV],
                preferred_element_type=jnp.float32,
            )
        out[start : start + chunk] = attended.astype(out.dtype)


def attend(queries, keys, block_request, block_used):
    tp_size = lax.axis_size("tp")
    row_count, heads, latent = queries.shape
    block_size, share = keys[0].shape[:2]
    within = jnp.arange(block_size, dtype=jnp.int32)[:, None]
    owners = []
    for step in range(tp_size):
        first = ((lax.axis_index("tp") + tp_size - step) % tp_size) * share
        owner = lax.dynamic_slice_in_dim(block_request, first, share)[None, :]
        limit = lax.dynamic_slice_in_dim(block_used, first, share)[None, :]
        owners.append(jnp.where(within < limit, owner, -1).reshape(1, -1))
    keys = [part.reshape(-1, latent) for part in keys]
    rows = queries.reshape(-1, latent)
    shape = jax.ShapeDtypeStruct((rows.shape[0], KV), jnp.bfloat16)
    result = kernel_call(
        functools.partial(attention_kernel, heads, min(128, rows.shape[0])),
        shape,
        [jnp.concatenate(owners, axis=0), rows] + keys,
        flops=4 * rows.size * keys[0].shape[0] * tp_size,
    )
    return result.reshape(row_count, heads, KV)


def body(
    tokens,
    expert_ids,
    gate_weights,
    expert_gate_up,
    expert_down,
    queries,
    latent_cache,
    block_source,
    block_request,
    block_used,
):
    row_count, top_count = expert_ids.shape
    slot_total, block_size, latent = latent_cache.shape
    ep_size = lax.axis_size("ep")
    tp_size = lax.axis_size("tp")
    tp_index = lax.axis_index("tp")
    bits = ep_bits()
    orders = (bits, bits[:-2] + [bits[-1], bits[-2]])
    parts = len(orders)
    cut = tokens.shape[1] // parts
    held = {}

    sent_rows = [tokens[:, part * cut : (part + 1) * cut] for part in range(parts)]
    expert_ids, gate_weights = tie((expert_ids, gate_weights), sent_rows[0])
    expert_range = jnp.arange(ep_size, dtype=jnp.int32)
    dense_gate = jnp.sum(
        jnp.where(
            expert_ids[:, :, None] == expert_range[None, None, :], gate_weights[:, :, None], 0.0
        ),
        axis=1,
    )
    gate_parts = jnp.concatenate(three_parts(dense_gate), axis=1)
    pad = -gate_parts.shape[1] % 128
    sent_rows[-1] = jnp.concatenate(
        [sent_rows[-1], jnp.pad(gate_parts, ((0, 0), (0, pad)))], axis=1
    )

    def beside_last_gather(sent):
        pieces = tie(cache_out(latent_cache), sent)
        held["ordered"] = cache_turn(pieces, block_source, slot_total)

    hooks = [None] * (parts - 1) + [beside_last_gather]
    columns = [[None] * parts for _ in range(tp_size)]
    for part, (rows, order, hook) in enumerate(zip(sent_rows, orders, hooks)):
        early, late, axis = gather_blocks(rows, order, hook)
        steps = [(early, late)] + list(zip(swap_tp(early), swap_tp(late)))
        steps = [join(halves, axis) for halves in steps]
        if part == parts - 1:
            all_gate = steps[0][:, cut : cut + 3 * ep_size].astype(jnp.float32)
        for owner in range(tp_size):
            chosen = pick(steps, (tp_index + tp_size - owner) % tp_size)
            columns[owner][part] = chosen[:, :cut]
    mine = (jnp.arange(3 * ep_size, dtype=jnp.int32) % ep_size) == lax.axis_index("ep")
    my_gate = jnp.sum(jnp.where(mine[None, :], all_gate, 0.0), axis=1)
    gate_and_up = jnp.einsum(
        "sd,dgf->sgf",
        jnp.concatenate([column for group in columns for column in group], axis=1),
        expert_gate_up[0],
        preferred_element_type=jnp.float32,
    )
    hidden = (
        jax.nn.silu(gate_and_up[:, 0]) * gate_and_up[:, 1] * my_gate[:, None]
    ).astype(jnp.bfloat16)

    sums = [[] for _ in range(parts)]
    for step in range(1, tp_size):
        for part, other in enumerate(down(hidden, expert_down[0], step, parts)):
            sums[part].append(pass_tp(other, step))
    own = down(hidden, expert_down[0], 0, parts)

    def beside_first_sum(sent):
        sent, held["ordered"] = lax.optimization_barrier((sent, held["ordered"]))
        return sent

    def beside_last_sum(sent):
        keys = cache_in(held["ordered"], block_size, latent)
        sent, held["keys"] = lax.optimization_barrier((sent, keys))
        return sent

    moe_parts = []
    for part, order in enumerate(orders):
        final = part == parts - 1
        moe_parts.append(
            scatter_sum(
                [own[part]] + sums[part],
                order,
                row_count,
                beside_first_sum if final else None,
                beside_last_sum if final else None,
            )
        )
    moe_out = jnp.concatenate(moe_parts, axis=1)
    keys = [held["keys"]] + swap_tp(held["keys"])
    return (moe_out, attend(queries, keys, block_request, block_used))


def solution(mesh):
    placed = (
        P("ep", "tp"),
        P("ep", None),
        P("ep", None),
        P("ep", None, None, "tp"),
        P("ep", None, "tp"),
        P("ep", "tp", None),
        P("ep", None, None),
        P(),
        P("ep"),
        P("ep"),
    )
    return jax.shard_map(
        body,
        mesh=mesh,
        in_specs=placed,
        out_specs=(P("ep", "tp"), P("ep", "tp", None)),
        check_vma=False,
    )
```

time: 124 us -> 126 us (1.016)
  Pallas kernels: 0 us -> 23.3 us
  matrix products: 20.4 us -> 9.27 us
  starting transfers between devices: 38.9 us -> 46.9 us
  local copies, waits for them, and re-layouts: 25.8 us -> 19.4 us
  waiting for transfers between devices: 26.3 us -> 20.5 us
  blocking collectives: 5.3 us -> 0 us
    pallas_call x0 -> x14, Pallas kernels: none -> 23.3 us  [kernel_call(): pl.pallas_call(kernel, out_shape=out_shape, in_specs=in_specs or [WHOLE]...]
    dynamic_slice x3 -> x2, local copies, waits for them, and re-layouts: 15.3 us -> 0.12 us  [the longest x1 0.08 us: attend(): limit = lax.dynamic_slice_in_dim(block_used, first, share)[None, :]]
    dot_general x10 -> x1, matrix products: 20.4 us -> 9.27 us  [body(): jnp.einsum('sd,dgf->sgf', jnp.concatenate([column for group in columns fo...]
    unnamed x21 -> x42, local copies, waits for them, and re-layouts: 5.46 us -> 16.2 us
    ppermute x16, starting transfers between devices: 24.3 us -> 30.9 us  [exchange(): lax.ppermute(value, 'ep', [(index, index ^ bit) for index in range(ep_siz...]
    ppermute x16, waiting for transfers between devices: 26.3 us -> 20.1 us  [exchange(): lax.ppermute(value, 'ep', [(index, index ^ bit) for index in range(ep_siz...]
    all_gather x2 -> x0, blocking collectives: 5.3 us -> none  [the longest x1 2.8 us: move_blocks(): return lax.all_gather(arrived, 'tp', axis=0, tiled=False)]
    gather x1 -> x0, local copies, waits for them, and re-layouts: 2.63 us -> none  [move_blocks(): ordered = jnp.take(every.reshape(-1, piece), row, axis=0, mode='clip')]
  transfers between devices with their start and end apart: 22 -> 26, of which waited for: 10 -> 11; matrix products, arithmetic and copies ran while one was open for 37% -> 14% of each run, Pallas kernels for 0% -> 15%
where the time goes in v2:
time: 126 us; the launch traced here: 125 us
  starting transfers between devices  46.9 us (37%)
  Pallas kernels  23.3 us (18%)
  waiting for transfers between devices  20.5 us (16%)
  local copies, waits for them, and re-layouts  19.4 us (15%)
  matrix products  9.27 us (7%)
  other arithmetic  4.03 us (3%)
    ppermute x16, starting transfers between devices, exchange(): lax.ppermute(value, 'ep', [(index, index ^ bit) for index in range(ep_siz...  30.9 us
    pallas_call x14, Pallas kernels, kernel_call(): pl.pallas_call(kernel, out_shape=out_shape, in_specs=in_specs or [WHOLE]...  23.3 us
    ppermute x16, waiting for transfers between devices, exchange(): lax.ppermute(value, 'ep', [(index, index ^ bit) for index in range(ep_siz...  20.1 us
    unnamed x42, local copies, waits for them, and re-layouts  16.2 us
    dot_general x1, matrix products, body(): jnp.einsum('sd,dgf->sgf', jnp.concatenate([column for group in columns fo...  9.27 us
    all_to_all x1, starting transfers between devices, cache_in(): lax.all_to_all(ordered, 'ep', split_axis=0, concat_axis=0, tiled=True)  9.12 us
    all_to_all x1, starting transfers between devices, cache_turn(): lax.all_to_all(pieces, 'ep', split_axis=0, concat_axis=0, tiled=True)  5.75 us
  transfers between devices with their start and end apart: 26, of which 11 were waited for; matrix products, arithmetic and copies ran while one was open for 14% of the time, Pallas kernels for 15%

profile of v2, /device:TPU:0, one launch (start us, length us, event | category | flops | bytes accessed | tf_op | source)
XLA Modules:
  0.0 124.5 jit_solution(2388367195863332617)
XLA Ops:
  1.6 4.1 %collective-permute-start = (bf16[1,1,1,1,16,1792]{5,4,3,2,1,0:T(8,128)(2,1)S(1)}, bf16[1,1,1,1,16,1792]{5,4,3,2,1,0:T(8,128)(2,1)S(1)}, u32[]{:S(2)}, u32[]{:S(2)}) collective-permute-start(bf16[1,1,1,1,16,1792]{5,4,3,2,1,0:T(8,128)(2,1)S(1)} %get-tuple-element.31), channel_id=1, source_target_pairs={{0,16},{2,18},{4,20},{6,22},{8,24},{10,26},{12,28},{14,30},{16,0},... | collective-permute-start | bytes 172040 | tf_op jit(solution)/shard_map/ppermute | solution.py:44
  8.5 2.9 %collective-permute-start.1 = (bf16[1,1,1,2,16,1792]{5,4,3,2,1,0:T(8,128)(2,1)S(1)}, bf16[1,1,1,2,16,1792]{5,4,3,2,1,0:T(8,128)(2,1)S(1)}, u32[]{:S(2)}, u32[]{:S(2)}) collective-permute-start(bf16[1,1,1,2,16,1792]{5,4,3,2,1,0:T(8,128)(2,1)S(1)} %pad_maximum_fusion.8), channel_id=1, source_target_pairs={{0,8},{2,10},{4,12},{6,14},{8,0},{10,2},{12,4},{14,6},{16,24},{18,... | collective-permute-start | bytes 344072 | tf_op jit(solution)/shard_map/ppermute | solution.py:44
  12.9 1.9 %collective-permute-start.7 = (bf16[1,1,1,2,16,1920]{5,4,3,2,1,0:T(8,128)(2,1)S(1)}, bf16[1,1,1,2,16,1920]{5,4,3,2,1,0:T(8,128)(2,1)S(1)}, u32[]{:S(2)}, u32[]{:S(2)}) collective-permute-start(bf16[1,1,1,2,16,1920]{5,4,3,2,1,0:T(8,128)(2,1)S(1)} %pad_maximum_fusion.7), channel_id=1, source_target_pairs={{0,8},{2,10},{4,12},{6,14},{8,0},{10,2},{12,4},{14,6},{16,24},{18,... | collective-permute-start | bytes 368648 | tf_op jit(solution)/shard_map/ppermute | solution.py:44
  17.9 1.6 %collective-permute-start.8 = (bf16[1,1,2,2,16,1920]{5,4,3,2,1,0:T(8,128)(2,1)S(1)}, bf16[1,1,2,2,16,1920]{5,4,3,2,1,0:T(8,128)(2,1)S(1)}, u32[]{:S(2)}, u32[]{:S(2)}) collective-permute-start(bf16[1,1,2,2,16,1920]{5,4,3,2,1,0:T(8,128)(2,1)S(1)} %pad_maximum_fusion.5), channel_id=1, source_target_pairs={{0,2},{2,0},{4,6},{6,4},{8,10},{10,8},{12,14},{14,12},{16,18},{18,... | collective-permute-start | bytes 737288 | tf_op jit(solution)/shard_map/ppermute | solution.py:44
  23.2 3.6 %collective-permute-done.8 = bf16[1,1,2,2,16,1920]{5,4,3,2,1,0:T(8,128)(2,1)S(1)} collective-permute-done((bf16[1,1,2,2,16,1920]{5,4,3,2,1,0:T(8,128)(2,1)S(1)}, bf16[1,1,2,2,16,1920]{5,4,3,2,1,0:T(8,128)(2,1)S(1)}, u32[]{:S(2)}, u32[]{:S(2)}) %collective-permute-start.8) | collective-permute-done | bytes 245792 | tf_op jit(solution)/shard_map/ppermute | solution.py:44
  26.8 1.6 %collective-permute-start.10 = (bf16[2,1,2,2,16,1920]{5,4,3,2,1,0:T(8,128)(2,1)S(1)}, bf16[2,1,2,2,16,1920]{5,4,3,2,1,0:T(8,128)(2,1)S(1)}, u32[]{:S(2)}, u32[]{:S(2)}) collective-permute-start(bf16[2,1,2,2,16,1920]{5,4,3,2,1,0:T(8,128)(2,1)S(1)} %pad_maximum_fusion.3), channel_id=1, source_target_pairs={{0,4},{2,6},{4,0},{6,2},{8,12},{10,14},{12,8},{14,10},{16,20},{18,... | collective-permute-start | bytes 1474568 | tf_op jit(solution)/shard_map/ppermute | solution.py:44
  29.4 5.8 %all-to-all-start = ((bf16[16,24,576]{2,1,0:T(8,128)(2,1)}), bf16[16,24,576]{2,1,0:T(8,128)(2,1)}, u32[]{:S(2)}, u32[]{:S(2)}) async-start(bf16[16,24,576]{2,1,0:T(8,128)(2,1)} %bitcast.34), calls=%async_computation | async-start | bytes 983040 | tf_op jit(solution)/shard_map/all_to_all | solution.py:196
  39.1 9.3 %fusion = f32[256,2,512]{2,0,1:T(8,128)S(1)} fusion(bf16[7168,2,512]{2,1,0:T(2,128)(2,1)} %bitcast.48, bf16[256,1792]{1,0:T(8,128)(2,1)S(1)} %get-tuple-element.28, bf16[256,1792]{1,0:T(8,128)(2,1)S(1)} %bitcast.47, bf16[256,1792]{1,0:T(8,128)(2,1)S(1)} %get-tuple-element.27, bf16[256,1792]{1,0:T(8,128)(2,1)S(1)} %bitcast.46), kind=kOutput, calls=%fused_computation | convolution fusion | flops 3772776448 | bytes 19398656 | tf_op jit(solution)/shard_map/sd,dgf->sgf/dot_general | solution.py:331
  48.6 2.7 %shard_map.114 = (bf16[256,1792]{1,0:T(8,128)(2,1)}, bf16[256,1792]{1,0:T(8,128)(2,1)}) custom-call(bf16[256,512]{1,0:T(8,128)(2,1)S(1)} %fusion.10.hidden, bf16[7168,512]{1,0:T(8,128)(2,1)S(1)} %bitcast.37), custom_call_target="tpu_custom_call" | custom-call | flops 939524096 | bytes 9437184 | tf_op jit(solution)/shard_map/pallas_call | solution.py:22
  52.9 3.1 %copy-done.1 = bf16[1,7168,512]{2,1,0:T(8,128)(2,1)S(1)} copy-done((bf16[1,7168,512]{2,1,0:T(8,128)(2,1)S(1)}, bf16[1,7168,512]{2,1,0:T(8,128)(2,1)}, u32[]{:S(2)}) %copy-start.1) | copy-done | bytes 7340056
  56.0 1.8 %shard_map.113 = (bf16[256,1792]{1,0:T(8,128)(2,1)S(1)}, bf16[256,1792]{1,0:T(8,128)(2,1)S(1)}) custom-call(bf16[256,512]{1,0:T(8,128)(2,1)S(1)} %fusion.10.hidden, bf16[7168,512]{1,0:T(8,128)(2,1)S(1)} %bitcast.38), custom_call_target="tpu_custom_call" | custom-call | flops 939524096 | bytes 9437184 | tf_op jit(solution)/shard_map/pallas_call | solution.py:22
  57.8 2.3 %shard_map.121 = bf16[384,576]{1,0:T(8,128)(2,1)S(1)} custom-call(s32[384,2]{1,0:T(8,128)S(1)} %fusion.11.index, bf16[384,576]{1,0:T(8,128)(2,1)} %bitcast.12.refs_0_, bf16[384,576]{1,0:T(8,128)(2,1)S(1)} %bitcast.40), custom_call_target="tpu_custom_call" | custom-call | flops 339738624 | bytes 1330176 | tf_op jit(solution)/shard_map/pallas_call | solution.py:22
  61.0 1.7 %collective-permute-start.19 = (bf16[128,1792]{1,0:T(8,128)(2,1)}, bf16[128,1792]{1,0:T(8,128)(2,1)S(1)}, u32[]{:S(2)}, u32[]{:S(2)}) collective-permute-start(bf16[128,1792]{1,0:T(8,128)(2,1)} %shard_map.120), channel_id=1, source_target_pairs={{0,4},{2,6},{4,0},{6,2},{8,12},{10,14},{12,8},{14,10},{16,20},{18,... | collective-permute-start | bytes 1376264 | tf_op jit(solution)/shard_map/ppermute | solution.py:44
  65.1 9.1 %all-to-all-start.1 = ((bf16[16,24,576]{2,1,0:T(8,128)(2,1)}), bf16[16,24,576]{2,1,0:T(8,128)(2,1)}, u32[]{:S(2)}, u32[]{:S(2)}) async-start(bf16[16,24,576]{2,1,0:T(8,128)(2,1)} %bitcast.39), calls=%async_computation.1 | async-start | bytes 983040 | tf_op jit(solution)/shard_map/all_to_all | solution.py:216
  76.2 1.8 %collective-permute-start.20 = (bf16[64,1792]{1,0:T(8,128)(2,1)}, bf16[64,1792]{1,0:T(8,128)(2,1)S(1)}, u32[]{:S(2)}, u32[]{:S(2)}) collective-permute-start(bf16[64,1792]{1,0:T(8,128)(2,1)} %shard_map.122), channel_id=1, source_target_pairs={{0,2},{2,0},{4,6},{6,4},{8,10},{10,8},{12,14},{14,12},{16,18},{18,... | collective-permute-start | bytes 688136 | tf_op jit(solution)/shard_map/ppermute | solution.py:44
  79.2 1.8 %shard_map.116 = bf16[64,1792]{1,0:T(8,128)(2,1)} custom-call(bf16[256,1792]{1,0:T(8,128)(2,1)S(1)} %copy-done.8, bf16[256,1792]{1,0:T(8,128)(2,1)S(1)} %collective-permute-done.12.refs_1_, bf16[128,1792]{1,0:T(8,128)(2,1)} %collective-permute-done.13.refs_2_), custom_call_target="tpu_custom_call" | custom-call | flops 344064 | bytes 2523136 | tf_op jit(solution)/shard_map/pallas_call | solution.py:22
  82.6 4.0 %collective-permute-done.20.refs_3_ = bf16[64,1792]{1,0:T(8,128)(2,1)S(1)} collective-permute-done((bf16[64,1792]{1,0:T(8,128)(2,1)}, bf16[64,1792]{1,0:T(8,128)(2,1)S(1)}, u32[]{:S(2)}, u32[]{:S(2)}) %collective-permute-start.20) | collective-permute-done | bytes 229408 | tf_op jit(solution)/shard_map/ppermute | solution.py:44
  88.6 1.6 %collective-permute-start.21 = (bf16[32,1792]{1,0:T(8,128)(2,1)}, bf16[32,1792]{1,0:T(8,128)(2,1)}, u32[]{:S(2)}, u32[]{:S(2)}) collective-permute-start(bf16[32,1792]{1,0:T(8,128)(2,1)} %shard_map.123), channel_id=1, source_target_pairs={{0,8},{2,10},{4,12},{6,14},{8,0},{10,2},{12,4},{14,6},{16,24},{18,... | collective-permute-start | bytes 344072 | tf_op jit(solution)/shard_map/ppermute | solution.py:44
  91.3 1.8 %shard_map.117 = bf16[32,1792]{1,0:T(8,128)(2,1)} custom-call(bf16[256,1792]{1,0:T(8,128)(2,1)S(1)} %copy-done.9, bf16[256,1792]{1,0:T(8,128)(2,1)S(1)} %collective-permute-done.12.refs_1_, bf16[128,1792]{1,0:T(8,128)(2,1)} %collective-permute-done.13.refs_2_, bf16[64,1792]{1,0:T(8,128)(2,1)} %collective-permute-done.14.refs_3_), custom_call_target="tpu_custom_call" | custom-call | flops 229376 | bytes 2637824 | tf_op jit(solution)/shard_map/pallas_call | solution.py:22
  94.3 3.9 %collective-permute-done.15.refs_4_ = bf16[32,1792]{1,0:T(8,128)(2,1)} collective-permute-done((bf16[32,1792]{1,0:T(8,128)(2,1)}, bf16[32,1792]{1,0:T(8,128)(2,1)}, u32[]{:S(2)}, u32[]{:S(2)}) %collective-permute-start.15) | collective-permute-done | bytes 114720 | tf_op jit(solution)/shard_map/ppermute | solution.py:44
  99.4 1.8 %shard_map.118 = bf16[16,1792]{1,0:T(8,128)(2,1)} custom-call(bf16[256,1792]{1,0:T(8,128)(2,1)S(1)} %copy-done.10, bf16[256,1792]{1,0:T(8,128)(2,1)S(1)} %collective-permute-done.12.refs_1_, bf16[128,1792]{1,0:T(8,128)(2,1)} %collective-permute-done.13.refs_2_, bf16[64,1792]{1,0:T(8,128)(2,1)} %collective-permute-done.14.refs_3_, ...), custom_call_target="tpu_custom_call" | custom-call | flops 143360 | bytes 2695168 | tf_op jit(solution)/shard_map/pallas_call | solution.py:22
  101.2 6.5 %collective-permute-start.16 = (bf16[16,1792]{1,0:T(8,128)(2,1)}, bf16[16,1792]{1,0:T(8,128)(2,1)}, u32[]{:S(2)}, u32[]{:S(2)}) collective-permute-start(bf16[16,1792]{1,0:T(8,128)(2,1)} %shard_map.118), channel_id=1, source_target_pairs={{0,16},{2,18},{4,20},{6,22},{8,24},{10,26},{12,28},{14,30},{16,0},... | collective-permute-start | bytes 172040 | tf_op jit(solution)/shard_map/ppermute | solution.py:44
  112.9 2.9 %collective-permute-done.22.refs_5_ = bf16[16,1792]{1,0:T(8,128)(2,1)S(1)} collective-permute-done((bf16[16,1792]{1,0:T(8,128)(2,1)}, bf16[16,1792]{1,0:T(8,128)(2,1)S(1)}, u32[]{:S(2)}, u32[]{:S(2)}) %collective-permute-start.22) | collective-permute-done | bytes 57376 | tf_op jit(solution)/shard_map/ppermute | solution.py:44
  119.7 4.9 %shard_map.126 = bf16[512,512]{1,0:T(8,128)(2,1)} custom-call(s32[2,384]{1,0:T(2,128)S(1)} %pad_add_fusion.owner, bf16[512,576]{1,0:T(8,128)(2,1)S(1)} %bitcast.41, bf16[384,576]{1,0:T(8,128)(2,1)} %bitcast.16.refs_0_, bf16[384,576]{1,0:T(8,128)(2,1)S(1)} %bitcast.42), custom_call_target="tpu_custom_call" | custom-call | flops 905969664 | bytes 2001920 | tf_op jit(solution)/shard_map/pallas_call | solution.py:22
  (124 shorter events, 41.2 us)
Async XLA Ops:
  1.6 6.9 %collective-permute-start = (bf16[1,1,1,1,16,1792]{5,4,3,2,1,0:T(8,128)(2,1)S(1)}, bf16[1,1,1,1,16,1792]{5,4,3,2,1,0:T(8,128)(2,1)S(1)}, u32[]{:S(2)}, u32[]{:S(2)}) collective-permute-start(bf16[1,1,1,1,16,1792]{5,4,3,2,1,0:T(8,128)(2,1)S(1)} %get-tuple-element.31), channel_id=1, source_target_pairs={{0,16},{2,18},{4,20},{6,22},{8,24},{10,26},{12,28},{14,30},{16,0},... | collective-permute-start | bytes 172040 | tf_op jit(solution)/shard_map/ppermute | solution.py:44
  7.4 5.4 %collective-permute-start.6 = (bf16[1,1,1,1,16,1920]{5,4,3,2,1,0:T(8,128)(2,1)S(1)}, bf16[1,1,1,1,16,1920]{5,4,3,2,1,0:T(8,128)(2,1)S(1)}, u32[]{:S(2)}, u32[]{:S(2)}) collective-permute-start(bf16[1,1,1,1,16,1920]{5,4,3,2,1,0:T(8,128)(2,1)S(1)} %maximum_bitcast_fusion.2), channel_id=1, source_target_pairs={{0,16},{2,18},{4,20},{6,22},{8,24},{10,26},{12,28},{14,30},{16,0},... | collective-permute-start | bytes 184328 | tf_op jit(solution)/shard_map/ppermute | solution.py:44
  8.5 6.3 %collective-permute-start.1 = (bf16[1,1,1,2,16,1792]{5,4,3,2,1,0:T(8,128)(2,1)S(1)}, bf16[1,1,1,2,16,1792]{5,4,3,2,1,0:T(8,128)(2,1)S(1)}, u32[]{:S(2)}, u32[]{:S(2)}) collective-permute-start(bf16[1,1,1,2,16,1792]{5,4,3,2,1,0:T(8,128)(2,1)S(1)} %pad_maximum_fusion.8), channel_id=1, source_target_pairs={{0,8},{2,10},{4,12},{6,14},{8,0},{10,2},{12,4},{14,6},{16,24},{18,... | collective-permute-start | bytes 344072 | tf_op jit(solution)/shard_map/ppermute | solution.py:44
  12.9 4.9 %collective-permute-start.7 = (bf16[1,1,1,2,16,1920]{5,4,3,2,1,0:T(8,128)(2,1)S(1)}, bf16[1,1,1,2,16,1920]{5,4,3,2,1,0:T(8,128)(2,1)S(1)}, u32[]{:S(2)}, u32[]{:S(2)}) collective-permute-start(bf16[1,1,1,2,16,1920]{5,4,3,2,1,0:T(8,128)(2,1)S(1)} %pad_maximum_fusion.7), channel_id=1, source_target_pairs={{0,8},{2,10},{4,12},{6,14},{8,0},{10,2},{12,4},{14,6},{16,24},{18,... | collective-permute-start | bytes 368648 | tf_op jit(solution)/shard_map/ppermute | solution.py:44
  14.8 6.1 %collective-permute-start.2 = (bf16[1,1,2,2,16,1792]{5,4,3,2,1,0:T(8,128)(2,1)S(1)}, bf16[1,1,2,2,16,1792]{5,4,3,2,1,0:T(8,128)(2,1)S(1)}, u32[]{:S(2)}, u32[]{:S(2)}) collective-permute-start(bf16[1,1,2,2,16,1792]{5,4,3,2,1,0:T(8,128)(2,1)S(1)} %pad_maximum_fusion.6), channel_id=1, source_target_pairs={{0,4},{2,6},{4,0},{6,2},{8,12},{10,14},{12,8},{14,10},{16,20},{18,... | collective-permute-start | bytes 688136 | tf_op jit(solution)/shard_map/ppermute | solution.py:44
  17.9 8.9 %collective-permute-start.8 = (bf16[1,1,2,2,16,1920]{5,4,3,2,1,0:T(8,128)(2,1)S(1)}, bf16[1,1,2,2,16,1920]{5,4,3,2,1,0:T(8,128)(2,1)S(1)}, u32[]{:S(2)}, u32[]{:S(2)}) collective-permute-start(bf16[1,1,2,2,16,1920]{5,4,3,2,1,0:T(8,128)(2,1)S(1)} %pad_maximum_fusion.5), channel_id=1, source_target_pairs={{0,2},{2,0},{4,6},{6,4},{8,10},{10,8},{12,14},{14,12},{16,18},{18,... | collective-permute-start | bytes 737288 | tf_op jit(solution)/shard_map/ppermute | solution.py:44
  21.7 13.5 %collective-permute-start.4 = (bf16[1,2,2,2,16,1792]{5,4,3,2,1,0:T(8,128)(2,1)}, bf16[1,2,2,2,16,1792]{5,4,3,2,1,0:T(8,128)(2,1)}, u32[]{:S(2)}, u32[]{:S(2)}) collective-permute-start(bf16[1,2,2,2,16,1792]{5,4,3,2,1,0:T(8,128)(2,1)} %pad_maximum_fusion.4), channel_id=1, source_target_pairs={{0,2},{2,0},{4,6},{6,4},{8,10},{10,8},{12,14},{14,12},{16,18},{18,... | collective-permute-start | bytes 1376264 | tf_op jit(solution)/shard_map/ppermute | solution.py:44
  23.2 12.3 %collective-permute-start.3 = (bf16[1,2,2,2,16,1792]{5,4,3,2,1,0:T(8,128)(2,1)}, bf16[1,2,2,2,16,1792]{5,4,3,2,1,0:T(8,128)(2,1)}, u32[]{:S(2)}, u32[]{:S(2)}) collective-permute-start(bf16[1,2,2,2,16,1792]{5,4,3,2,1,0:T(8,128)(2,1)} %pad_maximum_fusion.4), channel_id=1, source_target_pairs={{0,1},{1,0},{2,3},{3,2},{4,5},{5,4},{6,7},{7,6},{8,9},{9,8},{10,11... | collective-permute-start | bytes 1376264 | tf_op jit(solution)/shard_map/ppermute | solution.py:49
  26.8 10.1 %collective-permute-start.10 = (bf16[2,1,2,2,16,1920]{5,4,3,2,1,0:T(8,128)(2,1)S(1)}, bf16[2,1,2,2,16,1920]{5,4,3,2,1,0:T(8,128)(2,1)S(1)}, u32[]{:S(2)}, u32[]{:S(2)}) collective-permute-start(bf16[2,1,2,2,16,1920]{5,4,3,2,1,0:T(8,128)(2,1)S(1)} %pad_maximum_fusion.3), channel_id=1, source_target_pairs={{0,4},{2,6},{4,0},{6,2},{8,12},{10,14},{12,8},{14,10},{16,20},{18,... | collective-permute-start | bytes 1474568 | tf_op jit(solution)/shard_map/ppermute | solution.py:44
  29.4 9.1 %collective-permute-start.9 = (bf16[2,1,2,2,16,1920]{5,4,3,2,1,0:T(8,128)(2,1)S(1)}, bf16[2,1,2,2,16,1920]{5,4,3,2,1,0:T(8,128)(2,1)S(1)}, u32[]{:S(2)}, u32[]{:S(2)}) collective-permute-start(bf16[2,1,2,2,16,1920]{5,4,3,2,1,0:T(8,128)(2,1)S(1)} %pad_maximum_fusion.3), channel_id=1, source_target_pairs={{0,1},{1,0},{2,3},{3,2},{4,5},{5,4},{6,7},{7,6},{8,9},{9,8},{10,11... | collective-permute-start | bytes 1474568 | tf_op jit(solution)/shard_map/ppermute | solution.py:49
  29.4 23.1 %all-to-all-start = ((bf16[16,24,576]{2,1,0:T(8,128)(2,1)}), bf16[16,24,576]{2,1,0:T(8,128)(2,1)}, u32[]{:S(2)}, u32[]{:S(2)}) async-start(bf16[16,24,576]{2,1,0:T(8,128)(2,1)} %bitcast.34), calls=%async_computation | async-start | bytes 983040 | tf_op jit(solution)/shard_map/all_to_all | solution.py:196
  51.3 8.8 %collective-permute-start.17 = (bf16[256,1792]{1,0:T(8,128)(2,1)}, bf16[256,1792]{1,0:T(8,128)(2,1)S(1)}, u32[]{:S(2)}, u32[]{:S(2)}) collective-permute-start(bf16[256,1792]{1,0:T(8,128)(2,1)} %get-tuple-element.18), channel_id=1, source_target_pairs={{0,1},{1,0},{2,3},{3,2},{4,5},{5,4},{6,7},{7,6},{8,9},{9,8},{10,11... | collective-permute-start | bytes 2752520 | tf_op jit(solution)/shard_map/ppermute | solution.py:49
  51.5 11.2 %collective-permute-start.12 = (bf16[256,1792]{1,0:T(8,128)(2,1)}, bf16[256,1792]{1,0:T(8,128)(2,1)S(1)}, u32[]{:S(2)}, u32[]{:S(2)}) collective-permute-start(bf16[256,1792]{1,0:T(8,128)(2,1)} %get-tuple-element.16), channel_id=1, source_target_pairs={{0,1},{1,0},{2,3},{3,2},{4,5},{5,4},{6,7},{7,6},{8,9},{9,8},{10,11... | collective-permute-start | bytes 2752520 | tf_op jit(solution)/shard_map/ppermute | solution.py:49
  52.5 5.3 %collective-permute-start.18 = (bf16[16,24,576]{2,1,0:T(8,128)(2,1)}, bf16[16,24,576]{2,1,0:T(8,128)(2,1)S(1)}, u32[]{:S(2)}, u32[]{:S(2)}) collective-permute-start(bf16[16,24,576]{2,1,0:T(8,128)(2,1)} %all-to-all-done), channel_id=1, source_target_pairs={{0,1},{1,0},{2,3},{3,2},{4,5},{5,4},{6,7},{7,6},{8,9},{9,8},{10,11... | collective-permute-start | bytes 1327112 | tf_op jit(solution)/shard_map/ppermute | solution.py:49
  61.0 13.2 %collective-permute-start.19 = (bf16[128,1792]{1,0:T(8,128)(2,1)}, bf16[128,1792]{1,0:T(8,128)(2,1)S(1)}, u32[]{:S(2)}, u32[]{:S(2)}) collective-permute-start(bf16[128,1792]{1,0:T(8,128)(2,1)} %shard_map.120), channel_id=1, source_target_pairs={{0,4},{2,6},{4,0},{6,2},{8,12},{10,14},{12,8},{14,10},{16,20},{18,... | collective-permute-start | bytes 1376264 | tf_op jit(solution)/shard_map/ppermute | solution.py:44
  63.6 14.4 %collective-permute-start.13 = (bf16[128,1792]{1,0:T(8,128)(2,1)}, bf16[128,1792]{1,0:T(8,128)(2,1)}, u32[]{:S(2)}, u32[]{:S(2)}) collective-permute-start(bf16[128,1792]{1,0:T(8,128)(2,1)} %shard_map.115), channel_id=1, source_target_pairs={{0,2},{2,0},{4,6},{6,4},{8,10},{10,8},{12,14},{14,12},{16,18},{18,... | collective-permute-start | bytes 1376264 | tf_op jit(solution)/shard_map/ppermute | solution.py:44
  65.1 45.4 %all-to-all-start.1 = ((bf16[16,24,576]{2,1,0:T(8,128)(2,1)}), bf16[16,24,576]{2,1,0:T(8,128)(2,1)}, u32[]{:S(2)}, u32[]{:S(2)}) async-start(bf16[16,24,576]{2,1,0:T(8,128)(2,1)} %bitcast.39), calls=%async_computation.1 | async-start | bytes 983040 | tf_op jit(solution)/shard_map/all_to_all | solution.py:216
  76.2 10.5 %collective-permute-start.20 = (bf16[64,1792]{1,0:T(8,128)(2,1)}, bf16[64,1792]{1,0:T(8,128)(2,1)S(1)}, u32[]{:S(2)}, u32[]{:S(2)}) collective-permute-start(bf16[64,1792]{1,0:T(8,128)(2,1)} %shard_map.122), channel_id=1, source_target_pairs={{0,2},{2,0},{4,6},{6,4},{8,10},{10,8},{12,14},{14,12},{16,18},{18,... | collective-permute-start | bytes 688136 | tf_op jit(solution)/shard_map/ppermute | solution.py:44
  81.0 9.2 %collective-permute-start.14 = (bf16[64,1792]{1,0:T(8,128)(2,1)}, bf16[64,1792]{1,0:T(8,128)(2,1)}, u32[]{:S(2)}, u32[]{:S(2)}) collective-permute-start(bf16[64,1792]{1,0:T(8,128)(2,1)} %shard_map.116), channel_id=1, source_target_pairs={{0,4},{2,6},{4,0},{6,2},{8,12},{10,14},{12,8},{14,10},{16,20},{18,... | collective-permute-start | bytes 688136 | tf_op jit(solution)/shard_map/ppermute | solution.py:44
  88.6 19.1 %collective-permute-start.21 = (bf16[32,1792]{1,0:T(8,128)(2,1)}, bf16[32,1792]{1,0:T(8,128)(2,1)}, u32[]{:S(2)}, u32[]{:S(2)}) collective-permute-start(bf16[32,1792]{1,0:T(8,128)(2,1)} %shard_map.123), channel_id=1, source_target_pairs={{0,8},{2,10},{4,12},{6,14},{8,0},{10,2},{12,4},{14,6},{16,24},{18,... | collective-permute-start | bytes 344072 | tf_op jit(solution)/shard_map/ppermute | solution.py:44
  93.1 5.1 %collective-permute-start.15 = (bf16[32,1792]{1,0:T(8,128)(2,1)}, bf16[32,1792]{1,0:T(8,128)(2,1)}, u32[]{:S(2)}, u32[]{:S(2)}) collective-permute-start(bf16[32,1792]{1,0:T(8,128)(2,1)} %shard_map.117), channel_id=1, source_target_pairs={{0,8},{2,10},{4,12},{6,14},{8,0},{10,2},{12,4},{14,6},{16,24},{18,... | collective-permute-start | bytes 344072 | tf_op jit(solution)/shard_map/ppermute | solution.py:44
  101.2 9.3 %collective-permute-start.16 = (bf16[16,1792]{1,0:T(8,128)(2,1)}, bf16[16,1792]{1,0:T(8,128)(2,1)}, u32[]{:S(2)}, u32[]{:S(2)}) collective-permute-start(bf16[16,1792]{1,0:T(8,128)(2,1)} %shard_map.118), channel_id=1, source_target_pairs={{0,16},{2,18},{4,20},{6,22},{8,24},{10,26},{12,28},{14,30},{16,0},... | collective-permute-start | bytes 172040 | tf_op jit(solution)/shard_map/ppermute | solution.py:44
  110.4 5.3 %collective-permute-start.22 = (bf16[16,1792]{1,0:T(8,128)(2,1)}, bf16[16,1792]{1,0:T(8,128)(2,1)S(1)}, u32[]{:S(2)}, u32[]{:S(2)}) collective-permute-start(bf16[16,1792]{1,0:T(8,128)(2,1)} %copy-done.13), channel_id=1, source_target_pairs={{0,16},{2,18},{4,20},{6,22},{8,24},{10,26},{12,28},{14,30},{16,0},... | collective-permute-start | bytes 172040 | tf_op jit(solution)/shard_map/ppermute | solution.py:44
  110.4 8.1 %collective-permute-start.23 = (bf16[16,24,576]{2,1,0:T(8,128)(2,1)}, bf16[16,24,576]{2,1,0:T(8,128)(2,1)S(1)}, u32[]{:S(2)}, u32[]{:S(2)}) collective-permute-start(bf16[16,24,576]{2,1,0:T(8,128)(2,1)} %all-to-all-done.1), channel_id=1, source_target_pairs={{0,1},{1,0},{2,3},{3,2},{4,5},{5,4},{6,7},{7,6},{8,9},{9,8},{10,11... | collective-permute-start | bytes 1327112 | tf_op jit(solution)/shard_map/ppermute | solution.py:49
  (22 other events, 131.3 us)

commit v3 on v2

--- a/solution.py
+++ b/solution.py
@@ -25,7 +25,7 @@
         in_specs=in_specs or [WHOLE] * len(arguments),
         out_specs=jax.tree.map(lambda _: WHOLE, out_shape),
         scratch_shapes=scratch_shapes,
-        compiler_params=pltpu.CompilerParams(vmem_limit_bytes=40 << 20),
+        compiler_params=pltpu.CompilerParams(vmem_limit_bytes=54 << 20),
         cost_estimate=pl.CostEstimate(flops=flops, bytes_accessed=moved, transcendentals=0),
     )(*arguments)
 
@@ -55,57 +55,46 @@
     return [pass_tp(value, step) for step in range(1, lax.axis_size("tp"))]
 
 
-def gather_blocks(block, order, last=None):
-    bits = ep_bits()[::-1]
-    value = block.reshape((1,) * len(bits) + block.shape)
+def gather_blocks(block, order):
+    value = block[None]
     for bit in order[:-1]:
-        value = jnp.concatenate([value, exchange(value, bit)], axis=bits.index(bit))
-    arrived = exchange(value, order[-1])
-    if last is not None:
-        last(value)
-    return value, arrived, bits.index(order[-1])
-
-
-def join(halves, axis):
-    whole = jnp.concatenate(halves, axis=axis)
-    return whole.reshape((-1,) + whole.shape[-1:])
-
-
-def sum_kernel(rows, count, picked, *refs):
-    out = refs[count]
-    for place, blocks in enumerate(picked):
-        total = refs[0][blocks[0] * rows : (blocks[0] + 1) * rows].astype(jnp.float32)
-        for ref, block in zip(refs[1:count], blocks[1:]):
-            total = total + ref[block * rows : (block + 1) * rows].astype(jnp.float32)
-        out[place * rows : (place + 1) * rows] = total.astype(out.dtype)
-
-
-def add_up(terms, places, rows):
-    arrays = [array for array, _ in terms]
-    picked = [[held.index(place) for _, held in terms] for place in places]
-    shape = jax.ShapeDtypeStruct((len(places) * rows, arrays[0].shape[1]), jnp.bfloat16)
-    kernel = functools.partial(sum_kernel, rows, len(arrays), picked)
-    return kernel_call(kernel, shape, arrays, flops=shape.size * len(arrays))
-
-
-def scatter_sum(arrays, order, rows, first=None, last=None):
-    bits = ep_bits()[::-1]
-    number = len(bits)
-    places = [
-        sum(((spot >> (number - 1 - axis)) & 1) * bit for axis, bit in enumerate(bits))
-        for spot in range(1 << number)
-    ]
-    terms = [(array, places) for array in arrays]
+        value = jnp.concatenate([value, exchange(value, bit)], axis=0)
+    return value, exchange(value, order[-1])
+
+
+def places_of(order):
+    places = [0]
+    for bit in order:
+        places = places + [place ^ bit for place in places]
+    return places
+
+
+def join(halves, order, wanted):
+    axes = len(order)
+    whole = jnp.stack(halves)
+    whole = whole.reshape((2,) * axes + whole.shape[2:])
+    moved = [axes - 1 - order.index(bit) for bit in reversed(wanted)]
+    whole = whole.transpose(moved + [axes, axes + 1])
+    return whole.reshape(-1, whole.shape[-1])
+
+
+def scatter_sum(terms, order, first=None, last=None):
     for bit in reversed(order):
-        sent_places = [place for place in places if place & bit]
-        places = [place for place in places if not place & bit]
-        sent = add_up(terms, sent_places, rows)
+        half = terms[0].shape[0] // 2
+        sent = add_up([term[half:] for term in terms])
         if first is not None and bit == order[-1]:
             sent = first(sent)
         if last is not None and bit == order[0]:
             sent = last(sent)
-        terms = terms + [(exchange(sent, bit), [place ^ bit for place in sent_places])]
-    return add_up(terms, places, rows)
+        terms = [term[:half] for term in terms] + [exchange(sent, bit)]
+    return add_up(terms)
+
+
+def add_up(terms):
+    total = terms[0].astype(jnp.float32)
+    for term in terms[1:]:
+        total = total + term.astype(jnp.float32)
+    return total.astype(jnp.bfloat16)
 
 
 def three_parts(value):
@@ -124,48 +113,53 @@
     return value
 
 
-def down_kernel(step, parts, tp_size, cut, hidden, weight, *refs):
+def down_kernel(step, spots, tp_size, cut, width, rows, hidden, weight, *refs):
+    parts = len(spots)
     outs, held, arrived = refs[:parts], refs[parts], refs[parts + 1]
-    target = lax.rem(lax.axis_index("tp") + step, tp_size)
+    first = lax.rem(lax.axis_index("tp") + step, tp_size) * (parts * cut)
     copies = []
-    for part in range(parts):
-        start = pl.multiple_of(target * (parts * cut) + part * cut, cut)
+    for run in range(parts * cut // width):
+        start = pl.multiple_of(first + run * width, width)
         copies.append(
             pltpu.make_async_copy(
-                weight.at[pl.ds(start, cut)],
-                held.at[pl.ds(part * cut, cut)],
-                arrived.at[part],
+                weight.at[pl.ds(start, width)], held.at[pl.ds(run * width, width)], arrived.at[run]
             )
         )
     for copy in copies:
         copy.start()
+    chunk = min(256, hidden.shape[0])
+    for run, copy in enumerate(copies):
+        copy.wait()
+        part, column = divmod(run * width, cut)
+        for row in range(0, hidden.shape[0], chunk):
+            result = lax.dot_general(
+                hidden[row : row + chunk],
+                held[run * width : (run + 1) * width],
+                (((1,), (1,)), ((), ())),
+                preferred_element_type=jnp.float32,
+            ).astype(jnp.bfloat16)
+            for block in range(chunk // rows):
+                spot = spots[part][row // rows + block] * rows
+                outs[part][spot : spot + rows, column : column + width] = result[
+                    block * rows : (block + 1) * rows
+                ]
+
+
+def down(hidden, weight, step, spots, rows):
+    parts = len(spots)
+    tp_size = lax.axis_size("tp")
+    cut = weight.shape[0] // tp_size // parts
     width = 256 if cut % 256 == 0 else 128
-    chunk = min(256, hidden.shape[0])
-    for part in range(parts):
-        copies[part].wait()
-        for column in range(0, cut, width):
-            for row in range(0, hidden.shape[0], chunk):
-                outs[part][row : row + chunk, column : column + width] = lax.dot_general(
-                    hidden[row : row + chunk],
-                    held[part * cut + column : part * cut + column + width],
-                    (((1,), (1,)), ((), ())),
-                    preferred_element_type=jnp.float32,
-                ).astype(jnp.bfloat16)
-
-
-def down(hidden, weight, step, parts):
-    tp_size = lax.axis_size("tp")
-    cut = weight.shape[0] // tp_size // parts
     shape = jax.ShapeDtypeStruct((hidden.shape[0], cut), jnp.bfloat16)
     return kernel_call(
-        functools.partial(down_kernel, step, parts, tp_size, cut),
+        functools.partial(down_kernel, step, spots, tp_size, cut, width, rows),
         [shape] * parts,
         [hidden, weight],
         flops=2 * hidden.size * cut * parts,
         in_specs=[WHOLE, pl.BlockSpec(memory_space=pl.ANY)],
         scratch_shapes=[
             pltpu.VMEM((parts * cut, weight.shape[1]), weight.dtype),
-            pltpu.SemaphoreType.DMA((parts,)),
+            pltpu.SemaphoreType.DMA((parts * cut // width,)),
         ],
     )
 
@@ -265,7 +259,7 @@
     rows = queries.reshape(-1, latent)
     shape = jax.ShapeDtypeStruct((rows.shape[0], KV), jnp.bfloat16)
     result = kernel_call(
-        functools.partial(attention_kernel, heads, min(128, rows.shape[0])),
+        functools.partial(attention_kernel, heads, min(256, rows.shape[0])),
         shape,
         [jnp.concatenate(owners, axis=0), rows] + keys,
         flops=4 * rows.size * keys[0].shape[0] * tp_size,
@@ -294,10 +288,10 @@
     orders = (bits, bits[:-2] + [bits[-1], bits[-2]])
     parts = len(orders)
     cut = tokens.shape[1] // parts
-    held = {}
 
     sent_rows = [tokens[:, part * cut : (part + 1) * cut] for part in range(parts)]
-    expert_ids, gate_weights = tie((expert_ids, gate_weights), sent_rows[0])
+    pieces = tie(cache_out(latent_cache), sent_rows[0])
+    ordered = cache_turn(pieces, block_source, slot_total)
     expert_range = jnp.arange(ep_size, dtype=jnp.int32)
     dense_gate = jnp.sum(
         jnp.where(
@@ -311,16 +305,14 @@
         [sent_rows[-1], jnp.pad(gate_parts, ((0, 0), (0, pad)))], axis=1
     )
 
-    def beside_last_gather(sent):
-        pieces = tie(cache_out(latent_cache), sent)
-        held["ordered"] = cache_turn(pieces, block_source, slot_total)
-
-    hooks = [None] * (parts - 1) + [beside_last_gather]
+    halves = [gather_blocks(rows, order) for rows, order in zip(sent_rows, orders)]
+    last_sent = halves[-1][0]
+    halves[-1] = (last_sent, tie(halves[-1][1], ordered))
     columns = [[None] * parts for _ in range(tp_size)]
-    for part, (rows, order, hook) in enumerate(zip(sent_rows, orders, hooks)):
-        early, late, axis = gather_blocks(rows, order, hook)
-        steps = [(early, late)] + list(zip(swap_tp(early), swap_tp(late)))
-        steps = [join(halves, axis) for halves in steps]
+    for part, ((early, late), order) in enumerate(zip(halves, orders)):
+        passed = tie(early, last_sent) if part < parts - 1 else early
+        steps = [(early, late)] + list(zip(swap_tp(passed), swap_tp(late)))
+        steps = [join(pair, order, orders[0]) for pair in steps]
         if part == parts - 1:
             all_gate = steps[0][:, cut : cut + 3 * ep_size].astype(jnp.float32)
         for owner in range(tp_size):
@@ -338,19 +330,24 @@
         jax.nn.silu(gate_and_up[:, 0]) * gate_and_up[:, 1] * my_gate[:, None]
     ).astype(jnp.bfloat16)
 
+    keys = cache_in(ordered, block_size, latent)
+    places = [places_of(order) for order in orders]
+    spots = [[held.index(place) for place in places[0]] for held in places]
     sums = [[] for _ in range(parts)]
     for step in range(1, tp_size):
-        for part, other in enumerate(down(hidden, expert_down[0], step, parts)):
+        for part, other in enumerate(down(hidden, expert_down[0], step, spots, row_count)):
             sums[part].append(pass_tp(other, step))
-    own = down(hidden, expert_down[0], 0, parts)
+    own = down(hidden, expert_down[0], 0, spots, row_count)
+
+    held = {}
 
     def beside_first_sum(sent):
-        sent, held["ordered"] = lax.optimization_barrier((sent, held["ordered"]))
+        sent, near = lax.optimization_barrier((sent, keys))
+        held["attended"] = attend(queries, [near] + swap_tp(near), block_request, block_used)
         return sent
 
     def beside_last_sum(sent):
-        keys = cache_in(held["ordered"], block_size, latent)
-        sent, held["keys"] = lax.optimization_barrier((sent, keys))
+        sent, held["attended"] = lax.optimization_barrier((sent, held["attended"]))
         return sent
 
     moe_parts = []
@@ -360,14 +357,11 @@
             scatter_sum(
                 [own[part]] + sums[part],
                 order,
-                row_count,
                 beside_first_sum if final else None,
                 beside_last_sum if final else None,
             )
         )
-    moe_out = jnp.concatenate(moe_parts, axis=1)
-    keys = [held["keys"]] + swap_tp(held["keys"])
-    return (moe_out, attend(queries, keys, block_request, block_used))
+    return (jnp.concatenate(moe_parts, axis=1), held["attended"])
 
 
 def solution(mesh):

time: 126 us -> 132 us (1.048)
  waiting for transfers between devices: 20.5 us -> 38.1 us
  local copies, waits for them, and re-layouts: 19.4 us -> 5.58 us
  other arithmetic: 4.03 us -> 17.6 us
  starting transfers between devices: 46.9 us -> 37.5 us
    unnamed x42 -> x15, local copies, waits for them, and re-layouts: 16.2 us -> 3.21 us
    ppermute x16, waiting for transfers between devices: 20.1 us -> 32.1 us  [exchange(): lax.ppermute(value, 'ep', [(index, index ^ bit) for index in range(ep_siz...]
    convert_element_type x0 -> x10, other arithmetic: none -> 11.6 us  [add_up(): return total.astype(jnp.bfloat16)]
    ppermute x16, starting transfers between devices: 30.9 us -> 23 us  [exchange(): lax.ppermute(value, 'ep', [(index, index ^ bit) for index in range(ep_siz...]
    all_to_all x1, waiting for transfers between devices: 0.01 us -> 5.33 us  [cache_in(): lax.all_to_all(ordered, 'ep', split_axis=0, concat_axis=0, tiled=True)]
    all_to_all x1, starting transfers between devices: 9.12 us -> 5.71 us  [cache_in(): lax.all_to_all(ordered, 'ep', split_axis=0, concat_axis=0, tiled=True)]
    optimization_barrier x2 -> x0, local copies, waits for them, and re-layouts: 1.51 us -> none  [tie(): return lax.optimization_barrier((values, others))[0]]
    all_to_all x1, starting transfers between devices: 5.75 us -> 7.16 us  [cache_turn(): lax.all_to_all(pieces, 'ep', split_axis=0, concat_axis=0, tiled=True)]
  transfers between devices with their start and end apart: 26 -> 26, of which waited for: 11 -> 15; matrix products, arithmetic and copies ran while one was open for 14% -> 13% of each run, Pallas kernels for 15% -> 11%
where the time goes in v3:
time: 132 us; the launch traced here: 131 us
  waiting for transfers between devices  38.1 us (29%)
  starting transfers between devices  37.5 us (28%)
  Pallas kernels  22 us (17%)
  other arithmetic  17.6 us (13%)
  matrix products  9.12 us (7%)
  local copies, waits for them, and re-layouts  5.58 us (4%)
    ppermute x16, waiting for transfers between devices, exchange(): lax.ppermute(value, 'ep', [(index, index ^ bit) for index in range(ep_siz...  32.1 us
    ppermute x16, starting transfers between devices, exchange(): lax.ppermute(value, 'ep', [(index, index ^ bit) for index in range(ep_siz...  23 us
    pallas_call x4, Pallas kernels, kernel_call(): pl.pallas_call(kernel, out_shape=out_shape, in_specs=in_specs or [WHOLE]...  22 us
    convert_element_type x10, other arithmetic, add_up(): return total.astype(jnp.bfloat16)  11.6 us
    dot_general x1, matrix products, body(): jnp.einsum('sd,dgf->sgf', jnp.concatenate([column for group in columns fo...  9.12 us
    all_to_all x1, starting transfers between devices, cache_turn(): lax.all_to_all(pieces, 'ep', split_axis=0, concat_axis=0, tiled=True)  7.16 us
    all_to_all x1, starting transfers between devices, cache_in(): lax.all_to_all(ordered, 'ep', split_axis=0, concat_axis=0, tiled=True)  5.71 us
    all_to_all x1, waiting for transfers between devices, cache_in(): lax.all_to_all(ordered, 'ep', split_axis=0, concat_axis=0, tiled=True)  5.33 us
  transfers between devices with their start and end apart: 26, of which 15 were waited for; matrix products, arithmetic and copies ran while one was open for 13% of the time, Pallas kernels for 11%

profile of v3, /device:TPU:0, one launch (start us, length us, event | category | flops | bytes accessed | tf_op | source)
XLA Modules:
  0.0 130.9 jit_solution(286468591358201825)
XLA Ops:
  1.6 4.1 %collective-permute-start = (bf16[1,16,1792]{2,1,0:T(8,128)(2,1)S(1)}, bf16[1,16,1792]{2,1,0:T(8,128)(2,1)S(1)}, u32[]{:S(2)}, u32[]{:S(2)}) collective-permute-start(bf16[1,16,1792]{2,1,0:T(8,128)(2,1)S(1)} %get-tuple-element.33), channel_id=1, source_target_pairs={{0,16},{2,18},{4,20},{6,22},{8,24},{10,26},{12,28},{14,30},{16,0},... | collective-permute-start | bytes 172040 | tf_op jit(solution)/shard_map/ppermute | solution.py:44
  8.4 7.2 %all-to-all-start = ((bf16[16,24,576]{2,1,0:T(8,128)(2,1)}), bf16[16,24,576]{2,1,0:T(8,128)(2,1)S(1)}, u32[]{:S(2)}, u32[]{:S(2)}) async-start(bf16[16,24,576]{2,1,0:T(8,128)(2,1)} %bitcast.55), calls=%async_computation | async-start | bytes 983040 | tf_op jit(solution)/shard_map/all_to_all | solution.py:190
  16.4 2.0 %collective-permute-start.1 = (bf16[2,16,1792]{2,1,0:T(8,128)(2,1)S(1)}, bf16[2,16,1792]{2,1,0:T(8,128)(2,1)S(1)}, u32[]{:S(2)}, u32[]{:S(2)}) collective-permute-start(bf16[2,16,1792]{2,1,0:T(8,128)(2,1)S(1)} %pad_maximum_fusion.9), channel_id=1, source_target_pairs={{0,8},{2,10},{4,12},{6,14},{8,0},{10,2},{12,4},{14,6},{16,24},{18,... | collective-permute-start | bytes 344072 | tf_op jit(solution)/shard_map/ppermute | solution.py:44
  18.6 10.4 %collective-permute-done.1 = bf16[2,16,1792]{2,1,0:T(8,128)(2,1)S(1)} collective-permute-done((bf16[2,16,1792]{2,1,0:T(8,128)(2,1)S(1)}, bf16[2,16,1792]{2,1,0:T(8,128)(2,1)S(1)}, u32[]{:S(2)}, u32[]{:S(2)}) %collective-permute-start.1) | collective-permute-done | bytes 114720 | tf_op jit(solution)/shard_map/ppermute | solution.py:44
  30.4 1.5 %collective-permute-start.5 = (bf16[4,16,1920]{2,1,0:T(8,128)(2,1)S(1)}, bf16[4,16,1920]{2,1,0:T(8,128)(2,1)S(1)}, u32[]{:S(2)}, u32[]{:S(2)}) collective-permute-start(bf16[4,16,1920]{2,1,0:T(8,128)(2,1)S(1)} %pad_maximum_fusion.6), channel_id=1, source_target_pairs={{0,2},{2,0},{4,6},{6,4},{8,10},{10,8},{12,14},{14,12},{16,18},{18,... | collective-permute-start | bytes 737288 | tf_op jit(solution)/shard_map/ppermute | solution.py:44
  32.5 2.6 %collective-permute-done.2 = bf16[4,16,1792]{2,1,0:T(8,128)(2,1)S(1)} collective-permute-done((bf16[4,16,1792]{2,1,0:T(8,128)(2,1)S(1)}, bf16[4,16,1792]{2,1,0:T(8,128)(2,1)S(1)}, u32[]{:S(2)}, u32[]{:S(2)}) %collective-permute-start.2) | collective-permute-done | bytes 229408 | tf_op jit(solution)/shard_map/ppermute | solution.py:44
  37.4 2.0 %collective-permute-done.5 = bf16[4,16,1920]{2,1,0:T(8,128)(2,1)S(1)} collective-permute-done((bf16[4,16,1920]{2,1,0:T(8,128)(2,1)S(1)}, bf16[4,16,1920]{2,1,0:T(8,128)(2,1)S(1)}, u32[]{:S(2)}, u32[]{:S(2)}) %collective-permute-start.5) | collective-permute-done | bytes 245792 | tf_op jit(solution)/shard_map/ppermute | solution.py:44
  42.3 4.7 %collective-permute-done.7 = bf16[8,16,1792]{2,1,0:T(8,128)(2,1)} collective-permute-done((bf16[8,16,1792]{2,1,0:T(8,128)(2,1)}, bf16[8,16,1792]{2,1,0:T(8,128)(2,1)}, u32[]{:S(2)}, u32[]{:S(2)}) %collective-permute-start.7) | collective-permute-done | bytes 458784 | tf_op jit(solution)/shard_map/ppermute | solution.py:44
  48.3 2.8 %shard_map.113 = bf16[384,576]{1,0:T(8,128)(2,1)} custom-call(s32[384,2]{1,0:T(8,128)} %fusion.11.index, bf16[384,576]{1,0:T(8,128)(2,1)} %bitcast.61, bf16[384,576]{1,0:T(8,128)(2,1)} %bitcast.65), custom_call_target="tpu_custom_call" | custom-call | flops 339738624 | bytes 1330176 | tf_op jit(solution)/shard_map/pallas_call | solution.py:22
  53.2 9.1 %fusion = f32[256,2,512]{2,0,1:T(8,128)S(1)} fusion(bf16[7168,2,512]{2,1,0:T(2,128)(2,1)} %bitcast.72, bf16[256,1792]{1,0:T(8,128)(2,1)S(1)} %get-tuple-element.28, bf16[256,1792]{1,0:T(8,128)(2,1)S(1)} %bitcast.64, bf16[256,1792]{1,0:T(8,128)(2,1)S(1)} %get-tuple-element.27, bf16[256,1792]{1,0:T(8,128)(2,1)S(1)} %bitcast.63), kind=kOutput, calls=%fused_computation | convolution fusion | flops 3772776448 | bytes 19398656 | tf_op jit(solution)/shard_map/sd,dgf->sgf/dot_general | solution.py:323
  63.3 7.4 %shard_map.115 = (bf16[256,1792]{1,0:T(8,128)(2,1)}, bf16[256,1792]{1,0:T(8,128)(2,1)}) custom-call(bf16[256,512]{1,0:T(8,128)(2,1)} %fusion.10.hidden, bf16[7168,512]{1,0:T(8,128)(2,1)} %bitcast.56), custom_call_target="tpu_custom_call" | custom-call | flops 939524096 | bytes 9437184 | tf_op jit(solution)/shard_map/pallas_call | solution.py:22
  71.3 5.7 %all-to-all-start.1 = ((bf16[16,24,576]{2,1,0:T(8,128)(2,1)}), bf16[16,24,576]{2,1,0:T(8,128)(2,1)S(1)}, u32[]{:S(2)}, u32[]{:S(2)}) async-start(bf16[16,24,576]{2,1,0:T(8,128)(2,1)} %bitcast.12), calls=%async_computation.1 | async-start | bytes 983040 | tf_op jit(solution)/shard_map/all_to_all | solution.py:210
  77.1 7.4 %shard_map.114 = (bf16[256,1792]{1,0:T(8,128)(2,1)}, bf16[256,1792]{1,0:T(8,128)(2,1)}) custom-call(bf16[256,512]{1,0:T(8,128)(2,1)} %fusion.10.hidden, bf16[7168,512]{1,0:T(8,128)(2,1)} %bitcast.57), custom_call_target="tpu_custom_call" | custom-call | flops 939524096 | bytes 9437184 | tf_op jit(solution)/shard_map/pallas_call | solution.py:22
  84.5 1.9 %add_convert_fusion = bf16[128,1792]{1,0:T(8,128)(2,1)} fusion(bf16[256,1792]{1,0:T(8,128)(2,1)S(1)} %collective-permute-done.18, bf16[256,1792]{1,0:T(8,128)(2,1)} %get-tuple-element.18), kind=kLoop, calls=%fused_computation.13 | loop fusion | flops 917504 | bytes 1376256 | tf_op jit(solution)/shard_map/convert_element_type | solution.py:97
  86.5 5.3 %all-to-all-done.1 = bf16[16,24,576]{2,1,0:T(8,128)(2,1)S(1)} async-done(((bf16[16,24,576]{2,1,0:T(8,128)(2,1)}), bf16[16,24,576]{2,1,0:T(8,128)(2,1)S(1)}, u32[]{:S(2)}, u32[]{:S(2)}) %all-to-all-start.1) | async-done | bytes 442400 | tf_op jit(solution)/shard_map/all_to_all | solution.py:210
  91.8 2.1 %add_convert_fusion.1 = bf16[128,1792]{1,0:T(8,128)(2,1)} fusion(bf16[256,1792]{1,0:T(8,128)(2,1)S(1)} %collective-permute-done.13, bf16[256,1792]{1,0:T(8,128)(2,1)} %get-tuple-element.16), kind=kLoop, calls=%fused_computation.14 | loop fusion | flops 917504 | bytes 1376256 | tf_op jit(solution)/shard_map/convert_element_type | solution.py:97
  96.4 4.3 %shard_map.116 = bf16[512,512]{1,0:T(8,128)(2,1)} custom-call(s32[2,384]{1,0:T(2,128)} %pad_add_fusion.owner, bf16[512,576]{1,0:T(8,128)(2,1)} %bitcast.73, bf16[384,576]{1,0:T(8,128)(2,1)} %bitcast.66, bf16[384,576]{1,0:T(8,128)(2,1)} %bitcast.33.refs_1_), custom_call_target="tpu_custom_call" | custom-call | flops 905969664 | bytes 2001920 | tf_op jit(solution)/shard_map/pallas_call | solution.py:22
  100.7 3.0 %collective-permute-done.14 = bf16[128,1792]{1,0:T(8,128)(2,1)} collective-permute-done((bf16[128,1792]{1,0:T(8,128)(2,1)}, bf16[128,1792]{1,0:T(8,128)(2,1)}, u32[]{:S(2)}, u32[]{:S(2)}) %collective-permute-start.14) | collective-permute-done | bytes 458784 | tf_op jit(solution)/shard_map/ppermute | solution.py:44
  104.9 2.0 %collective-permute-start.15 = (bf16[64,1792]{1,0:T(8,128)(2,1)S(1)}, bf16[64,1792]{1,0:T(8,128)(2,1)S(1)}, u32[]{:S(2)}, u32[]{:S(2)}) collective-permute-start(bf16[64,1792]{1,0:T(8,128)(2,1)S(1)} %add_convert_fusion.3), channel_id=1, source_target_pairs={{0,4},{2,6},{4,0},{6,2},{8,12},{10,14},{12,8},{14,10},{16,20},{18,... | collective-permute-start | bytes 688136 | tf_op jit(solution)/shard_map/ppermute | solution.py:44
  106.8 1.9 %collective-permute-done.19 = bf16[128,1792]{1,0:T(8,128)(2,1)S(1)} collective-permute-done((bf16[128,1792]{1,0:T(8,128)(2,1)}, bf16[128,1792]{1,0:T(8,128)(2,1)S(1)}, u32[]{:S(2)}, u32[]{:S(2)}) %collective-permute-start.19) | collective-permute-done | bytes 458784 | tf_op jit(solution)/shard_map/ppermute | solution.py:44
  111.3 2.0 %collective-permute-done.15 = bf16[64,1792]{1,0:T(8,128)(2,1)S(1)} collective-permute-done((bf16[64,1792]{1,0:T(8,128)(2,1)S(1)}, bf16[64,1792]{1,0:T(8,128)(2,1)S(1)}, u32[]{:S(2)}, u32[]{:S(2)}) %collective-permute-start.15) | collective-permute-done | bytes 229408 | tf_op jit(solution)/shard_map/ppermute | solution.py:44
  120.5 1.6 %collective-permute-start.17 = (bf16[16,1792]{1,0:T(8,128)(2,1)S(1)}, bf16[16,1792]{1,0:T(8,128)(2,1)S(1)}, u32[]{:S(2)}, u32[]{:S(2)}) collective-permute-start(bf16[16,1792]{1,0:T(8,128)(2,1)S(1)} %add_convert_fusion.9), channel_id=1, source_target_pairs={{0,16},{2,18},{4,20},{6,22},{8,24},{10,26},{12,28},{14,30},{16,0},... | collective-permute-start | bytes 172040 | tf_op jit(solution)/shard_map/ppermute | solution.py:44
  123.6 1.7 %collective-permute-start.23 = (bf16[16,1792]{1,0:T(8,128)(2,1)S(1)}, bf16[16,1792]{1,0:T(8,128)(2,1)S(1)}, u32[]{:S(2)}, u32[]{:S(2)}) collective-permute-start(bf16[16,1792]{1,0:T(8,128)(2,1)S(1)} %add_convert_fusion.7), channel_id=1, source_target_pairs={{0,16},{2,18},{4,20},{6,22},{8,24},{10,26},{12,28},{14,30},{16,0},... | collective-permute-start | bytes 172040 | tf_op jit(solution)/shard_map/ppermute | solution.py:44
  125.3 1.8 %collective-permute-done.17 = bf16[16,1792]{1,0:T(8,128)(2,1)S(1)} collective-permute-done((bf16[16,1792]{1,0:T(8,128)(2,1)S(1)}, bf16[16,1792]{1,0:T(8,128)(2,1)S(1)}, u32[]{:S(2)}, u32[]{:S(2)}) %collective-permute-start.17) | collective-permute-done | bytes 57376 | tf_op jit(solution)/shard_map/ppermute | solution.py:44
  (93 shorter events, 35.5 us)
Async XLA Ops:
  1.6 14.8 %collective-permute-start = (bf16[1,16,1792]{2,1,0:T(8,128)(2,1)S(1)}, bf16[1,16,1792]{2,1,0:T(8,128)(2,1)S(1)}, u32[]{:S(2)}, u32[]{:S(2)}) collective-permute-start(bf16[1,16,1792]{2,1,0:T(8,128)(2,1)S(1)} %get-tuple-element.33), channel_id=1, source_target_pairs={{0,16},{2,18},{4,20},{6,22},{8,24},{10,26},{12,28},{14,30},{16,0},... | collective-permute-start | bytes 172040 | tf_op jit(solution)/shard_map/ppermute | solution.py:44
  7.4 11.0 %collective-permute-start.3 = (bf16[1,16,1920]{2,1,0:T(8,128)(2,1)S(1)}, bf16[1,16,1920]{2,1,0:T(8,128)(2,1)S(1)}, u32[]{:S(2)}, u32[]{:S(2)}) collective-permute-start(bf16[1,16,1920]{2,1,0:T(8,128)(2,1)S(1)} %maximum_bitcast_fusion.2), channel_id=1, source_target_pairs={{0,16},{2,18},{4,20},{6,22},{8,24},{10,26},{12,28},{14,30},{16,0},... | collective-permute-start | bytes 184328 | tf_op jit(solution)/shard_map/ppermute | solution.py:44
  8.4 32.5 %all-to-all-start = ((bf16[16,24,576]{2,1,0:T(8,128)(2,1)}), bf16[16,24,576]{2,1,0:T(8,128)(2,1)S(1)}, u32[]{:S(2)}, u32[]{:S(2)}) async-start(bf16[16,24,576]{2,1,0:T(8,128)(2,1)} %bitcast.55), calls=%async_computation | async-start | bytes 983040 | tf_op jit(solution)/shard_map/all_to_all | solution.py:190
  16.4 12.5 %collective-permute-start.1 = (bf16[2,16,1792]{2,1,0:T(8,128)(2,1)S(1)}, bf16[2,16,1792]{2,1,0:T(8,128)(2,1)S(1)}, u32[]{:S(2)}, u32[]{:S(2)}) collective-permute-start(bf16[2,16,1792]{2,1,0:T(8,128)(2,1)S(1)} %pad_maximum_fusion.9), channel_id=1, source_target_pairs={{0,8},{2,10},{4,12},{6,14},{8,0},{10,2},{12,4},{14,6},{16,24},{18,... | collective-permute-start | bytes 344072 | tf_op jit(solution)/shard_map/ppermute | solution.py:44
  18.4 11.9 %collective-permute-start.4 = (bf16[2,16,1920]{2,1,0:T(8,128)(2,1)S(1)}, bf16[2,16,1920]{2,1,0:T(8,128)(2,1)S(1)}, u32[]{:S(2)}, u32[]{:S(2)}) collective-permute-start(bf16[2,16,1920]{2,1,0:T(8,128)(2,1)S(1)} %pad_maximum_fusion.8), channel_id=1, source_target_pairs={{0,8},{2,10},{4,12},{6,14},{8,0},{10,2},{12,4},{14,6},{16,24},{18,... | collective-permute-start | bytes 368648 | tf_op jit(solution)/shard_map/ppermute | solution.py:44
  29.0 6.1 %collective-permute-start.2 = (bf16[4,16,1792]{2,1,0:T(8,128)(2,1)S(1)}, bf16[4,16,1792]{2,1,0:T(8,128)(2,1)S(1)}, u32[]{:S(2)}, u32[]{:S(2)}) collective-permute-start(bf16[4,16,1792]{2,1,0:T(8,128)(2,1)S(1)} %pad_maximum_fusion.7), channel_id=1, source_target_pairs={{0,4},{2,6},{4,0},{6,2},{8,12},{10,14},{12,8},{14,10},{16,20},{18,... | collective-permute-start | bytes 688136 | tf_op jit(solution)/shard_map/ppermute | solution.py:44
  30.4 9.0 %collective-permute-start.5 = (bf16[4,16,1920]{2,1,0:T(8,128)(2,1)S(1)}, bf16[4,16,1920]{2,1,0:T(8,128)(2,1)S(1)}, u32[]{:S(2)}, u32[]{:S(2)}) collective-permute-start(bf16[4,16,1920]{2,1,0:T(8,128)(2,1)S(1)} %pad_maximum_fusion.6), channel_id=1, source_target_pairs={{0,2},{2,0},{4,6},{6,4},{8,10},{10,8},{12,14},{14,12},{16,18},{18,... | collective-permute-start | bytes 737288 | tf_op jit(solution)/shard_map/ppermute | solution.py:44
  35.9 11.1 %collective-permute-start.7 = (bf16[8,16,1792]{2,1,0:T(8,128)(2,1)}, bf16[8,16,1792]{2,1,0:T(8,128)(2,1)}, u32[]{:S(2)}, u32[]{:S(2)}) collective-permute-start(bf16[8,16,1792]{2,1,0:T(8,128)(2,1)} %get-tuple-element.13), channel_id=1, source_target_pairs={{0,2},{2,0},{4,6},{6,4},{8,10},{10,8},{12,14},{14,12},{16,18},{18,... | collective-permute-start | bytes 1376264 | tf_op jit(solution)/shard_map/ppermute | solution.py:44
  39.4 11.7 %collective-permute-start.10 = (bf16[8,16,1920]{2,1,0:T(8,128)(2,1)S(1)}, bf16[8,16,1920]{2,1,0:T(8,128)(2,1)S(1)}, u32[]{:S(2)}, u32[]{:S(2)}) collective-permute-start(bf16[8,16,1920]{2,1,0:T(8,128)(2,1)S(1)} %pad_maximum_fusion.4), channel_id=1, source_target_pairs={{0,4},{2,6},{4,0},{6,2},{8,12},{10,14},{12,8},{14,10},{16,20},{18,... | collective-permute-start | bytes 1474568 | tf_op jit(solution)/shard_map/ppermute | solution.py:44
  40.9 6.6 %collective-permute-start.11 = (bf16[16,24,576]{2,1,0:T(8,128)(2,1)S(1)}, bf16[16,24,576]{2,1,0:T(8,128)(2,1)S(1)}, u32[]{:S(2)}, u32[]{:S(2)}) collective-permute-start(bf16[16,24,576]{2,1,0:T(8,128)(2,1)S(1)} %all-to-all-done), channel_id=1, source_target_pairs={{0,1},{1,0},{2,3},{3,2},{4,5},{5,4},{6,7},{7,6},{8,9},{9,8},{10,11... | collective-permute-start | bytes 1327112 | tf_op jit(solution)/shard_map/ppermute | solution.py:49
  41.8 9.6 %collective-permute-start.6 = (bf16[8,16,1792]{2,1,0:T(8,128)(2,1)}, bf16[8,16,1792]{2,1,0:T(8,128)(2,1)S(1)}, u32[]{:S(2)}, u32[]{:S(2)}) collective-permute-start(bf16[8,16,1792]{2,1,0:T(8,128)(2,1)} %get-tuple-element.13), channel_id=1, source_target_pairs={{0,1},{1,0},{2,3},{3,2},{4,5},{5,4},{6,7},{7,6},{8,9},{9,8},{10,11... | collective-permute-start | bytes 1376264 | tf_op jit(solution)/shard_map/ppermute | solution.py:49
  47.0 4.5 %collective-permute-start.8 = (bf16[8,16,1792]{2,1,0:T(8,128)(2,1)}, bf16[8,16,1792]{2,1,0:T(8,128)(2,1)S(1)}, u32[]{:S(2)}, u32[]{:S(2)}) collective-permute-start(bf16[8,16,1792]{2,1,0:T(8,128)(2,1)} %collective-permute-done.7), channel_id=1, source_target_pairs={{0,1},{1,0},{2,3},{3,2},{4,5},{5,4},{6,7},{7,6},{8,9},{9,8},{10,11... | collective-permute-start | bytes 1376264 | tf_op jit(solution)/shard_map/ppermute | solution.py:49
  47.0 5.6 %collective-permute-start.9 = (bf16[8,16,1920]{2,1,0:T(8,128)(2,1)S(1)}, bf16[8,16,1920]{2,1,0:T(8,128)(2,1)S(1)}, u32[]{:S(2)}, u32[]{:S(2)}) collective-permute-start(bf16[8,16,1920]{2,1,0:T(8,128)(2,1)S(1)} %pad_maximum_fusion.4), channel_id=1, source_target_pairs={{0,1},{1,0},{2,3},{3,2},{4,5},{5,4},{6,7},{7,6},{8,9},{9,8},{10,11... | collective-permute-start | bytes 1474568 | tf_op jit(solution)/shard_map/ppermute | solution.py:49
  70.7 13.8 %collective-permute-start.18 = (bf16[256,1792]{1,0:T(8,128)(2,1)}, bf16[256,1792]{1,0:T(8,128)(2,1)S(1)}, u32[]{:S(2)}, u32[]{:S(2)}) collective-permute-start(bf16[256,1792]{1,0:T(8,128)(2,1)} %get-tuple-element.19), channel_id=1, source_target_pairs={{0,1},{1,0},{2,3},{3,2},{4,5},{5,4},{6,7},{7,6},{8,9},{9,8},{10,11... | collective-permute-start | bytes 2752520 | tf_op jit(solution)/shard_map/ppermute | solution.py:49
  70.9 20.9 %collective-permute-start.13 = (bf16[256,1792]{1,0:T(8,128)(2,1)}, bf16[256,1792]{1,0:T(8,128)(2,1)S(1)}, u32[]{:S(2)}, u32[]{:S(2)}) collective-permute-start(bf16[256,1792]{1,0:T(8,128)(2,1)} %get-tuple-element.17), channel_id=1, source_target_pairs={{0,1},{1,0},{2,3},{3,2},{4,5},{5,4},{6,7},{7,6},{8,9},{9,8},{10,11... | collective-permute-start | bytes 2752520 | tf_op jit(solution)/shard_map/ppermute | solution.py:49
  71.3 20.5 %all-to-all-start.1 = ((bf16[16,24,576]{2,1,0:T(8,128)(2,1)}), bf16[16,24,576]{2,1,0:T(8,128)(2,1)S(1)}, u32[]{:S(2)}, u32[]{:S(2)}) async-start(bf16[16,24,576]{2,1,0:T(8,128)(2,1)} %bitcast.12), calls=%async_computation.1 | async-start | bytes 983040 | tf_op jit(solution)/shard_map/all_to_all | solution.py:210
  93.9 9.9 %collective-permute-start.14 = (bf16[128,1792]{1,0:T(8,128)(2,1)}, bf16[128,1792]{1,0:T(8,128)(2,1)}, u32[]{:S(2)}, u32[]{:S(2)}) collective-permute-start(bf16[128,1792]{1,0:T(8,128)(2,1)} %add_convert_fusion.1), channel_id=1, source_target_pairs={{0,2},{2,0},{4,6},{6,4},{8,10},{10,8},{12,14},{14,12},{16,18},{18,... | collective-permute-start | bytes 1376264 | tf_op jit(solution)/shard_map/ppermute | solution.py:44
  95.2 13.5 %collective-permute-start.19 = (bf16[128,1792]{1,0:T(8,128)(2,1)}, bf16[128,1792]{1,0:T(8,128)(2,1)S(1)}, u32[]{:S(2)}, u32[]{:S(2)}) collective-permute-start(bf16[128,1792]{1,0:T(8,128)(2,1)} %add_convert_fusion), channel_id=1, source_target_pairs={{0,4},{2,6},{4,0},{6,2},{8,12},{10,14},{12,8},{14,10},{16,20},{18,... | collective-permute-start | bytes 1376264 | tf_op jit(solution)/shard_map/ppermute | solution.py:44
  104.9 8.4 %collective-permute-start.15 = (bf16[64,1792]{1,0:T(8,128)(2,1)S(1)}, bf16[64,1792]{1,0:T(8,128)(2,1)S(1)}, u32[]{:S(2)}, u32[]{:S(2)}) collective-permute-start(bf16[64,1792]{1,0:T(8,128)(2,1)S(1)} %add_convert_fusion.3), channel_id=1, source_target_pairs={{0,4},{2,6},{4,0},{6,2},{8,12},{10,14},{12,8},{14,10},{16,20},{18,... | collective-permute-start | bytes 688136 | tf_op jit(solution)/shard_map/ppermute | solution.py:44
  109.8 6.9 %collective-permute-start.20 = (bf16[64,1792]{1,0:T(8,128)(2,1)S(1)}, bf16[64,1792]{1,0:T(8,128)(2,1)S(1)}, u32[]{:S(2)}, u32[]{:S(2)}) collective-permute-start(bf16[64,1792]{1,0:T(8,128)(2,1)S(1)} %add_convert_fusion.2), channel_id=1, source_target_pairs={{0,2},{2,0},{4,6},{6,4},{8,10},{10,8},{12,14},{14,12},{16,18},{18,... | collective-permute-start | bytes 688136 | tf_op jit(solution)/shard_map/ppermute | solution.py:44
  114.3 5.3 %collective-permute-start.16 = (bf16[32,1792]{1,0:T(8,128)(2,1)S(1)}, bf16[32,1792]{1,0:T(8,128)(2,1)S(1)}, u32[]{:S(2)}, u32[]{:S(2)}) collective-permute-start(bf16[32,1792]{1,0:T(8,128)(2,1)S(1)} %add_convert_fusion.5), channel_id=1, source_target_pairs={{0,8},{2,10},{4,12},{6,14},{8,0},{10,2},{12,4},{14,6},{16,24},{18,... | collective-permute-start | bytes 344072 | tf_op jit(solution)/shard_map/ppermute | solution.py:44
  117.6 5.1 %collective-permute-start.21 = (bf16[32,1792]{1,0:T(8,128)(2,1)S(1)}, bf16[32,1792]{1,0:T(8,128)(2,1)S(1)}, u32[]{:S(2)}, u32[]{:S(2)}) collective-permute-start(bf16[32,1792]{1,0:T(8,128)(2,1)S(1)} %add_convert_fusion.4), channel_id=1, source_target_pairs={{0,8},{2,10},{4,12},{6,14},{8,0},{10,2},{12,4},{14,6},{16,24},{18,... | collective-permute-start | bytes 344072 | tf_op jit(solution)/shard_map/ppermute | solution.py:44
  120.5 6.6 %collective-permute-start.17 = (bf16[16,1792]{1,0:T(8,128)(2,1)S(1)}, bf16[16,1792]{1,0:T(8,128)(2,1)S(1)}, u32[]{:S(2)}, u32[]{:S(2)}) collective-permute-start(bf16[16,1792]{1,0:T(8,128)(2,1)S(1)} %add_convert_fusion.9), channel_id=1, source_target_pairs={{0,16},{2,18},{4,20},{6,22},{8,24},{10,26},{12,28},{14,30},{16,0},... | collective-permute-start | bytes 172040 | tf_op jit(solution)/shard_map/ppermute | solution.py:44
  123.6 5.8 %collective-permute-start.23 = (bf16[16,1792]{1,0:T(8,128)(2,1)S(1)}, bf16[16,1792]{1,0:T(8,128)(2,1)S(1)}, u32[]{:S(2)}, u32[]{:S(2)}) collective-permute-start(bf16[16,1792]{1,0:T(8,128)(2,1)S(1)} %add_convert_fusion.7), channel_id=1, source_target_pairs={{0,16},{2,18},{4,20},{6,22},{8,24},{10,26},{12,28},{14,30},{16,0},... | collective-permute-start | bytes 172040 | tf_op jit(solution)/shard_map/ppermute | solution.py:44
  (8 other events, 52.1 us)

commit v4 on v3

v4 whole, which is shorter than its diff:
```python
import functools

import jax
import jax.numpy as jnp
from jax import lax
from jax.experimental import pallas as pl
from jax.experimental.pallas import tpu as pltpu
from jax.sharding import PartitionSpec as P

KV = 512


score_scale = 192.0 ** (-0.5)

WHOLE = pl.BlockSpec(memory_space=pltpu.VMEM)


def kernel_call(kernel, out_shape, arguments, flops, spare, in_specs=None, scratch_shapes=()):
    held = sum(array.size * array.dtype.itemsize for array in jax.tree.leaves(out_shape))
    for array, spec in zip(arguments, in_specs or [WHOLE] * len(arguments)):
        held += array.size * array.dtype.itemsize if spec is WHOLE else 0
    moved = sum(array.size * array.dtype.itemsize for array in arguments)
    return pl.pallas_call(
        kernel,
        out_shape=out_shape,
        in_specs=in_specs or [WHOLE] * len(arguments),
        out_specs=jax.tree.map(lambda _: WHOLE, out_shape),
        scratch_shapes=scratch_shapes,
        compiler_params=pltpu.CompilerParams(vmem_limit_bytes=held + spare),
        cost_estimate=pl.CostEstimate(
            flops=flops, bytes_accessed=moved + held, transcendentals=0
        ),
    )(*arguments)


def tie(values, others):
    return lax.optimization_barrier((values, others))[0]


def ep_bits():
    ep_size = lax.axis_size("ep")
    return [1 << place for place in reversed(range(ep_size.bit_length() - 1))]


def exchange(value, bit):
    ep_size = lax.axis_size("ep")
    return lax.ppermute(value, "ep", [(index, index ^ bit) for index in range(ep_size)])


def pass_tp(value, step):
    tp_size = lax.axis_size("tp")
    return lax.ppermute(
        value, "tp", [(index, (index + step) % tp_size) for index in range(tp_size)]
    )


def swap_tp(value):
    return [pass_tp(value, step) for step in range(1, lax.axis_size("tp"))]


def gather_rows(rows, orders, ends):
    value = rows[None]
    for bit in orders[0][:-2]:
        value = jnp.concatenate([value, exchange(value, bit)], axis=0)
    halves = []
    for order, start, end in zip(orders, (0,) + ends, ends):
        part = value[:, :, start:end]
        part = jnp.concatenate([part, exchange(part, order[-2])], axis=0)
        halves.append((part, exchange(part, order[-1])))
    return halves


def places_of(order):
    places = [0]
    for bit in order:
        places = places + [place ^ bit for place in places]
    return places


def join_kernel(spots, ends, count, tp_size, *refs):
    out = refs[-1]
    parts = len(spots)
    rows = out.shape[0] // len(spots[0])
    width = out.shape[1] // tp_size
    index = lax.axis_index("tp")

    def place(tp_index):
        for step in range(tp_size):
            owner = (tp_index - step) % tp_size
            for part in range(parts):
                start, end = ((0,) + ends)[part], ends[part]
                for half in range(2):
                    ref = refs[(step * parts + part) * 2 + half]
                    blocks = ref.shape[0] // rows
                    for block in range(blocks):
                        spot = spots[part][half * blocks + block] * rows
                        out[spot : spot + rows, owner * width + start : owner * width + end] = ref[
                            block * rows : (block + 1) * rows, : end - start
                        ]

    for tp_index in range(tp_size):
        pl.when(index == tp_index)(functools.partial(place, tp_index))


def join_rows(by_step, spots, ends, rows):
    tp_size = len(by_step)
    arrays = [
        half.reshape(-1, half.shape[-1]) for parts in by_step for pair in parts for half in pair
    ]
    shape = jax.ShapeDtypeStruct((len(spots[0]) * rows, ends[-1] * tp_size), jnp.bfloat16)
    return kernel_call(
        functools.partial(join_kernel, spots, ends, len(arrays), tp_size),
        shape,
        arrays,
        flops=0,
        spare=4 << 20,
    )


def scatter_sums(totals, orders, hooks):
    steps = len(orders[0])
    for step in range(steps):
        if step == 2:
            totals = [jnp.concatenate(totals, axis=1)]
        half = totals[0].shape[0] // 2
        sents = [total[half:] for total in totals]
        if step in hooks:
            sents[-1] = hooks[step](sents[-1])
        totals = [
            add_up([total[:half], exchange(sent, order[steps - 1 - step])])
            for total, sent, order in zip(totals, sents, orders)
        ]
    return totals[0]


def add_up(terms):
    total = terms[0].astype(jnp.float32)
    for term in terms[1:]:
        total = total + term.astype(jnp.float32)
    return total.astype(jnp.bfloat16)


def three_parts(value):
    parts = []
    for _ in range(3):
        part = lax.reduce_precision(value, 8, 7)
        parts.append(part.astype(jnp.bfloat16))
        value = value - part
    return parts


def down_kernel(spots, tp_size, cut, width, rows, hidden, weight, *refs):
    parts = len(spots)
    outs, (held, turned, arrived) = refs[:-3], refs[-3:]
    copies = []
    for step in range(tp_size):
        target = lax.rem(lax.axis_index("tp") + step + 1, tp_size)
        for part in range(parts):
            run = step * parts + part
            start = pl.multiple_of((target * parts + part) * cut, cut)
            copies.append(
                pltpu.make_async_copy(
                    weight.at[pl.ds(start, cut)],
                    held.at[pl.ds(run * cut, cut)],
                    arrived.at[run],
                )
            )
    for copy in copies:
        copy.start()
    chunk = min(256, hidden.shape[0])
    for part in range(parts):
        for block, spot in enumerate(spots[part]):
            turned[part, spot * rows : (spot + 1) * rows] = hidden[
                block * rows : (block + 1) * rows
            ]
    for run, copy in enumerate(copies):
        copy.wait()
        for column in range(0, cut, width):
            for row in range(0, hidden.shape[0], chunk):
                outs[run][row : row + chunk, column : column + width] = lax.dot_general(
                    turned[run % parts, row : row + chunk],
                    held[run * cut + column : run * cut + column + width],
                    (((1,), (1,)), ((), ())),
                    preferred_element_type=jnp.float32,
                ).astype(jnp.bfloat16)


def down(hidden, weight, spots, rows):
    parts = len(spots)
    tp_size = lax.axis_size("tp")
    cut = weight.shape[0] // tp_size // parts
    width = 256 if cut % 256 == 0 else 128
    shape = jax.ShapeDtypeStruct((hidden.shape[0], cut), jnp.bfloat16)
    outs = kernel_call(
        functools.partial(down_kernel, spots, tp_size, cut, width, rows),
        [shape] * (parts * tp_size),
        [hidden, weight],
        flops=2 * hidden.size * weight.shape[0],
        spare=weight.size * 2 + (4 << 20),
        in_specs=[WHOLE, pl.BlockSpec(memory_space=pl.ANY)],
        scratch_shapes=[
            pltpu.VMEM(weight.shape, weight.dtype),
            pltpu.VMEM((parts,) + hidden.shape, hidden.dtype),
            pltpu.SemaphoreType.DMA((parts * tp_size,)),
        ],
    )
    return [outs[step * parts : (step + 1) * parts] for step in range(tp_size)]


def order_kernel(index, *refs):
    rows, out = refs[:-1], refs[-1]
    columns = lax.broadcasted_iota(jnp.int32, (out.shape[0], rows[0].shape[0]), 1)
    total = jnp.zeros(out.shape, jnp.float32)
    for step, ref in enumerate(rows):
        hot = (columns == index[:, step : step + 1]).astype(jnp.bfloat16)
        total = total + jnp.dot(hot, ref[...], preferred_element_type=jnp.float32)
    out[...] = total.astype(out.dtype)


def cache_out(latent_cache):
    ep_size = lax.axis_size("ep")
    slots, block_size, latent = latent_cache.shape
    share = slots // lax.axis_size("tp")
    mine = lax.dynamic_slice_in_dim(latent_cache, lax.axis_index("tp") * share, share, axis=0)
    return mine.reshape(share, ep_size, block_size * latent // ep_size).transpose(1, 0, 2)


def cache_turn(pieces, block_source, slots):
    ep_size = lax.axis_size("ep")
    tp_size = lax.axis_size("tp")
    tp_index = lax.axis_index("tp")
    share, piece = pieces.shape[1:]
    spread = lax.all_to_all(pieces, "ep", split_axis=0, concat_axis=0, tiled=True)
    wanted = lax.dynamic_slice_in_dim(
        block_source.reshape(ep_size, tp_size, share), tp_index, 1, axis=1
    ).reshape(-1)
    place = (wanted // slots) * share + wanted % share
    holder = (wanted % slots) // share
    from_step = (tp_index + tp_size - holder) % tp_size
    index = jnp.where(
        from_step[:, None] == jnp.arange(tp_size, dtype=jnp.int32)[None, :], place[:, None], -1
    )
    rows = [part.reshape(-1, piece) for part in [spread] + swap_tp(spread)]
    shape = jax.ShapeDtypeStruct(rows[0].shape, rows[0].dtype)
    ordered = kernel_call(
        order_kernel,
        shape,
        [index] + rows,
        flops=2 * tp_size * rows[0].size * rows[0].shape[0],
        spare=6 << 20,
    )
    return ordered.reshape(ep_size, share, piece)


def cache_in(ordered, block_size, latent):
    share, piece = ordered.shape[1:]
    arrived = lax.all_to_all(ordered, "ep", split_axis=0, concat_axis=0, tiled=True)
    if piece != latent:
        arrived = arrived.transpose(1, 0, 2).reshape(share, block_size, latent).transpose(1, 0, 2)
    return arrived


def attention_kernel(chunk, owner, request, queries, *refs):
    keys, out = refs[:-1], refs[-1]
    for start in range(0, queries.shape[0], chunk):
        row = request[start : start + chunk]
        scores = []
        for step, key in enumerate(keys):
            part = lax.dot_general(
                queries[start : start + chunk],
                key[...],
                (((1,), (1,)), ((), ())),
                preferred_element_type=jnp.float32,
            )
            scores.append(
                jnp.where(row == owner[step : step + 1, :], part * score_scale, -jnp.inf)
            )
        row_max = scores[0].max(axis=1, keepdims=True)
        for part in scores[1:]:
            row_max = jnp.maximum(row_max, part.max(axis=1, keepdims=True))
        terms = [jnp.exp(part - row_max) for part in scores]
        total = 1.0 / sum(term.sum(axis=1, keepdims=True) for term in terms)
        attended = jnp.zeros((chunk, KV), jnp.float32)
        for term, key in zip(terms, keys):
            attended = attended + jnp.dot(
                (term * total).astype(jnp.bfloat16),
                key[:, :KV],
                preferred_element_type=jnp.float32,
            )
        out[start : start + chunk] = attended.astype(out.dtype)


def attend(queries, keys, block_request, block_used):
    tp_size = lax.axis_size("tp")
    row_count, heads, latent = queries.shape
    block_size, share = keys[0].shape[:2]
    within = jnp.arange(block_size, dtype=jnp.int32)[:, None]
    owners = []
    for step in range(tp_size):
        first = ((lax.axis_index("tp") + tp_size - step) % tp_size) * share
        owner = lax.dynamic_slice_in_dim(block_request, first, share)[None, :]
        limit = lax.dynamic_slice_in_dim(block_used, first, share)[None, :]
        owners.append(jnp.where(within < limit, owner, -1).reshape(1, -1))
    keys = [part.reshape(-1, latent) for part in keys]
    rows = queries.reshape(-1, latent)
    request = jnp.repeat(jnp.arange(row_count, dtype=jnp.int32), heads)[:, None]
    shape = jax.ShapeDtypeStruct((rows.shape[0], KV), jnp.bfloat16)
    result = kernel_call(
        functools.partial(attention_kernel, min(256, rows.shape[0])),
        shape,
        [jnp.concatenate(owners, axis=0), request, rows] + keys,
        flops=4 * rows.size * keys[0].shape[0] * tp_size,
        spare=8 << 20,
    )
    return result.reshape(row_count, heads, KV)


def body(
    tokens,
    expert_ids,
    gate_weights,
    expert_gate_up,
    expert_down,
    queries,
    latent_cache,
    block_source,
    block_request,
    block_used,
):
    row_count, top_count = expert_ids.shape
    slot_total, block_size, latent = latent_cache.shape
    ep_size = lax.axis_size("ep")
    tp_size = lax.axis_size("tp")
    tp_index = lax.axis_index("tp")
    bits = ep_bits()
    orders = (bits, bits[:-2] + [bits[-1], bits[-2]])
    parts = len(orders)
    cut = tokens.shape[1] // parts

    expert_range = jnp.arange(ep_size, dtype=jnp.int32)
    dense_gate = jnp.sum(
        jnp.where(
            expert_ids[:, :, None] == expert_range[None, None, :], gate_weights[:, :, None], 0.0
        ),
        axis=1,
    )
    gate_parts = jnp.concatenate(three_parts(dense_gate), axis=1)
    pad = -gate_parts.shape[1] % 128
    sent_rows = jnp.concatenate([tokens, jnp.pad(gate_parts, ((0, 0), (0, pad)))], axis=1)
    ends = tuple(cut * part for part in range(1, parts)) + (sent_rows.shape[1],)

    halves = gather_rows(sent_rows, orders, ends)
    last_sent = halves[-1][0]
    pieces = tie(cache_out(latent_cache), last_sent)
    ordered = cache_turn(pieces, block_source, slot_total)
    places = [places_of(order) for order in orders]
    to_first = [[places[0].index(place) for place in own] for own in places]
    from_first = [[own.index(place) for place in places[0]] for own in places]

    passed = [tie(early, last_sent) for early, _ in halves[:-1]]
    passed.append(tie(last_sent, halves[0][1]))
    arrived = [
        [(pass_tp(early, step), pass_tp(late, step)) for early, (_, late) in zip(passed, halves)]
        for step in range(1, tp_size)
    ]
    all_rows = join_rows(
        [halves] + arrived, to_first, tuple(cut * part for part in range(1, parts + 1)), row_count
    )
    gate_halves = [half[..., cut : cut + 3 * ep_size] for half in halves[-1]]
    all_gate = jnp.concatenate(gate_halves, axis=0)
    all_gate = jnp.stack([all_gate[block] for block in from_first[-1]]).astype(jnp.float32)
    mine = (jnp.arange(3 * ep_size, dtype=jnp.int32) % ep_size) == lax.axis_index("ep")
    my_gate = jnp.sum(jnp.where(mine, all_gate, 0.0), axis=2).reshape(-1)
    gate_and_up = jnp.einsum(
        "sd,dgf->sgf", all_rows, expert_gate_up[0], preferred_element_type=jnp.float32
    )
    hidden = (
        jax.nn.silu(gate_and_up[:, 0]) * gate_and_up[:, 1] * my_gate[:, None]
    ).astype(jnp.bfloat16)

    hidden = tie(hidden, ordered)
    by_step = down(hidden, expert_down[0], from_first, row_count)
    ordered = tie(ordered, by_step)
    sums = list(by_step[-1])
    for part in range(parts):
        others = [pass_tp(by_step[step - 1][part], step) for step in range(1, tp_size)]
        sums[part] = add_up([sums[part]] + others)
    keys = cache_in(ordered, block_size, latent)

    held = {}

    def beside_second_sum(sent):
        sent, near = lax.optimization_barrier((sent, keys))
        held["attended"] = attend(queries, [near] + swap_tp(near), block_request, block_used)
        return sent

    def beside_last_sum(sent):
        sent, held["attended"] = lax.optimization_barrier((sent, held["attended"]))
        return sent

    hooks = {1: beside_second_sum, len(bits) - 1: beside_last_sum}
    return (scatter_sums(sums, orders, hooks), held["attended"])


def solution(mesh):
    placed = (
        P("ep", "tp"),
        P("ep", None),
        P("ep", None),
        P("ep", None, None, "tp"),
        P("ep", None, "tp"),
        P("ep", "tp", None),
        P("ep", None, None),
        P(),
        P("ep"),
        P("ep"),
    )
    return jax.shard_map(
        body,
        mesh=mesh,
        in_specs=placed,
        out_specs=(P("ep", "tp"), P("ep", "tp", None)),
        check_vma=False,
    )
```

time: 132 us -> 116 us (0.88)
  waiting for transfers between devices: 38.1 us -> 49.6 us
  Pallas kernels: 22 us -> 11.6 us
  other arithmetic: 17.6 us -> 7.45 us
  starting transfers between devices: 37.5 us -> 32.9 us
    pallas_call x4, Pallas kernels: 22 us -> 11.6 us  [kernel_call(): pl.pallas_call(kernel, out_shape=out_shape, in_specs=in_specs or [WHOLE]...]
    all_to_all x1, waiting for transfers between devices: 0.01 us -> 9.36 us  [cache_turn(): lax.all_to_all(pieces, 'ep', split_axis=0, concat_axis=0, tiled=True)]
    ppermute x16 -> x12, waiting for transfers between devices: 32.1 us -> 40.2 us  [exchange(): lax.ppermute(value, 'ep', [(index, index ^ bit) for index in range(ep_siz...]
    convert_element_type x10 -> x8, other arithmetic: 11.6 us -> 4.77 us  [add_up(): return total.astype(jnp.bfloat16)]
    all_to_all x1, waiting for transfers between devices: 5.33 us -> 0.01 us  [cache_in(): lax.all_to_all(ordered, 'ep', split_axis=0, concat_axis=0, tiled=True)]
    ppermute x16 -> x12, starting transfers between devices: 23 us -> 19.8 us  [exchange(): lax.ppermute(value, 'ep', [(index, index ^ bit) for index in range(ep_siz...]
    unnamed x15 -> x21, local copies, waits for them, and re-layouts: 3.21 us -> 2.52 us
  transfers between devices with their start and end apart: 26 -> 22, of which waited for: 15 -> 11; matrix products, arithmetic and copies ran while one was open for 13% -> 14% of each run, Pallas kernels for 11% -> 5%
where the time goes in v4:
time: 116 us; the launch traced here: 115 us
  waiting for transfers between devices  49.6 us (43%)
  starting transfers between devices  32.9 us (28%)
  Pallas kernels  11.6 us (10%)
  matrix products  7.95 us (7%)
  other arithmetic  7.45 us (6%)
  local copies, waits for them, and re-layouts  4.47 us (4%)
    ppermute x12, waiting for transfers between devices, exchange(): lax.ppermute(value, 'ep', [(index, index ^ bit) for index in range(ep_siz...  40.2 us
    ppermute x12, starting transfers between devices, exchange(): lax.ppermute(value, 'ep', [(index, index ^ bit) for index in range(ep_siz...  19.8 us
    pallas_call x4, Pallas kernels, kernel_call(): pl.pallas_call(kernel, out_shape=out_shape, in_specs=in_specs or [WHOLE]...  11.6 us
    all_to_all x1, waiting for transfers between devices, cache_turn(): lax.all_to_all(pieces, 'ep', split_axis=0, concat_axis=0, tiled=True)  9.36 us
    dot_general x1, matrix products, body(): jnp.einsum('sd,dgf->sgf', all_rows, expert_gate_up[0], preferred_element_...  7.95 us
    all_to_all x1, starting transfers between devices, cache_turn(): lax.all_to_all(pieces, 'ep', split_axis=0, concat_axis=0, tiled=True)  6.9 us
    convert_element_type x8, other arithmetic, add_up(): return total.astype(jnp.bfloat16)  4.77 us
    all_to_all x1, starting transfers between devices, cache_in(): lax.all_to_all(ordered, 'ep', split_axis=0, concat_axis=0, tiled=True)  4.41 us
  transfers between devices with their start and end apart: 22, of which 11 were waited for; matrix products, arithmetic and copies ran while one was open for 14% of the time, Pallas kernels for 5%

profile of v4, /device:TPU:0, one launch (start us, length us, event | category | flops | bytes accessed | tf_op | source)
XLA Modules:
  0.0 115.0 jit_solution(11377009429951664837)
XLA Ops:
  3.4 4.1 %collective-permute-start = (bf16[1,16,3712]{2,1,0:T(8,128)(2,1)S(1)}, bf16[1,16,3712]{2,1,0:T(8,128)(2,1)S(1)}, u32[]{:S(2)}, u32[]{:S(2)}) collective-permute-start(bf16[1,16,3712]{2,1,0:T(8,128)(2,1)S(1)} %maximum_bitcast_fusion), channel_id=1, source_target_pairs={{0,16},{2,18},{4,20},{6,22},{8,24},{10,26},{12,28},{14,30},{16,0},... | collective-permute-start | bytes 356360 | tf_op jit(solution)/shard_map/ppermute | solution.py:47
  7.5 5.8 %collective-permute-done = bf16[1,16,3712]{2,1,0:T(8,128)(2,1)S(1)} collective-permute-done((bf16[1,16,3712]{2,1,0:T(8,128)(2,1)S(1)}, bf16[1,16,3712]{2,1,0:T(8,128)(2,1)S(1)}, u32[]{:S(2)}, u32[]{:S(2)}) %collective-permute-start) | collective-permute-done | bytes 118816 | tf_op jit(solution)/shard_map/ppermute | solution.py:47
  14.1 6.2 %collective-permute-done.1 = bf16[2,16,3712]{2,1,0:T(8,128)(2,1)S(1)} collective-permute-done((bf16[2,16,3712]{2,1,0:T(8,128)(2,1)S(1)}, bf16[2,16,3712]{2,1,0:T(8,128)(2,1)S(1)}, u32[]{:S(2)}, u32[]{:S(2)}) %collective-permute-start.1) | collective-permute-done | bytes 237600 | tf_op jit(solution)/shard_map/ppermute | solution.py:47
  21.7 1.6 %collective-permute-start.2 = (bf16[4,16,1792]{2,1,0:T(8,128)(2,1)S(1)}, bf16[4,16,1792]{2,1,0:T(8,128)(2,1)S(1)}, u32[]{:S(2)}, u32[]{:S(2)}) collective-permute-start(bf16[4,16,1792]{2,1,0:T(8,128)(2,1)S(1)} %slice.117), channel_id=1, source_target_pairs={{0,4},{2,6},{4,0},{6,2},{8,12},{10,14},{12,8},{14,10},{16,20},{18,... | collective-permute-start | bytes 688136 | tf_op jit(solution)/shard_map/ppermute | solution.py:47
  23.3 3.4 %collective-permute-done.4 = bf16[4,16,1920]{2,1,0:T(8,128)(2,1)S(1)} collective-permute-done((bf16[4,16,1920]{2,1,0:T(8,128)(2,1)S(1)}, bf16[4,16,1920]{2,1,0:T(8,128)(2,1)S(1)}, u32[]{:S(2)}, u32[]{:S(2)}) %collective-permute-start.4) | collective-permute-done | bytes 245792 | tf_op jit(solution)/shard_map/ppermute | solution.py:47
  26.8 1.4 %collective-permute-start.5 = (bf16[8,16,1920]{2,1,0:T(8,128)(2,1)S(1)}, bf16[8,16,1920]{2,1,0:T(8,128)(2,1)S(1)}, u32[]{:S(2)}, u32[]{:S(2)}) collective-permute-start(bf16[8,16,1920]{2,1,0:T(8,128)(2,1)S(1)} %pad_maximum_fusion), channel_id=1, source_target_pairs={{0,4},{2,6},{4,0},{6,2},{8,12},{10,14},{12,8},{14,10},{16,20},{18,... | collective-permute-start | bytes 1474568 | tf_op jit(solution)/shard_map/ppermute | solution.py:47
  31.3 6.9 %all-to-all-start = ((bf16[16,24,576]{2,1,0:T(8,128)(2,1)}), bf16[16,24,576]{2,1,0:T(8,128)(2,1)S(1)}, u32[]{:S(2)}, u32[]{:S(2)}) async-start(bf16[16,24,576]{2,1,0:T(8,128)(2,1)} %bitcast.36), calls=%async_computation | async-start | bytes 983040 | tf_op jit(solution)/shard_map/all_to_all | solution.py:233
  41.2 9.4 %all-to-all-done = bf16[16,24,576]{2,1,0:T(8,128)(2,1)S(1)} async-done(((bf16[16,24,576]{2,1,0:T(8,128)(2,1)}), bf16[16,24,576]{2,1,0:T(8,128)(2,1)S(1)}, u32[]{:S(2)}, u32[]{:S(2)}) %all-to-all-start) | async-done | bytes 442400 | tf_op jit(solution)/shard_map/all_to_all | solution.py:233
  50.6 2.0 %shard_map.113 = bf16[256,7168]{1,0:T(8,128)(2,1)S(1)} custom-call(bf16[128,1792]{1,0:T(8,128)(2,1)S(1)} %bitcast.42, bf16[128,1792]{1,0:T(8,128)(2,1)} %bitcast.2.refs_1_, bf16[128,1920]{1,0:T(8,128)(2,1)S(1)} %bitcast.40, bf16[128,1920]{1,0:T(8,128)(2,1)S(1)} %bitcast.43, bf16[128,1792]{1,0:T(8,128)(2,1)} %bitcast.5.refs_4_, ...), custom_call_target="tpu_custom_call" | custom-call | bytes 11272192 | tf_op jit(solution)/shard_map/pallas_call | solution.py:23
  52.6 8.0 %fusion = f32[256,2,512]{2,0,1:T(8,128)S(1)} fusion(bf16[7168,2,512]{2,1,0:T(2,128)(2,1)} %bitcast.47, bf16[256,7168]{1,0:T(8,128)(2,1)S(1)} %shard_map.113), kind=kOutput, calls=%fused_computation | convolution fusion | flops 3758096384 | bytes 19398656 | tf_op jit(solution)/shard_map/sd,dgf->sgf/dot_general | solution.py:374
  60.8 1.6 %shard_map.114 = bf16[384,576]{1,0:T(8,128)(2,1)} custom-call(s32[384,2]{1,0:T(8,128)S(1)} %fusion.7.index, bf16[384,576]{1,0:T(8,128)(2,1)S(1)} %bitcast.41, bf16[384,576]{1,0:T(8,128)(2,1)S(1)} %bitcast.44), custom_call_target="tpu_custom_call" | custom-call | flops 339738624 | bytes 2217984 | tf_op jit(solution)/shard_map/pallas_call | solution.py:23
  62.4 4.1 %shard_map.115 = (bf16[256,1792]{1,0:T(8,128)(2,1)}, bf16[256,1792]{1,0:T(8,128)(2,1)}, bf16[256,1792]{1,0:T(8,128)(2,1)S(1)}, bf16[256,1792]{1,0:T(8,128)(2,1)S(1)}) custom-call(bf16[256,512]{1,0:T(8,128)(2,1)S(1)} %fusion.5.hidden, bf16[7168,512]{1,0:T(8,128)(2,1)S(1)} %bitcast.39), custom_call_target="tpu_custom_call" | custom-call | flops 1879048192 | bytes 11534336 | tf_op jit(solution)/shard_map/pallas_call | solution.py:23
  67.2 4.4 %all-to-all-start.1 = ((bf16[16,24,576]{2,1,0:T(8,128)(2,1)}), bf16[16,24,576]{2,1,0:T(8,128)(2,1)}, u32[]{:S(2)}, u32[]{:S(2)}) async-start(bf16[16,24,576]{2,1,0:T(8,128)(2,1)} %bitcast.16), calls=%async_computation.1 | async-start | bytes 983040 | tf_op jit(solution)/shard_map/all_to_all | solution.py:257
  71.6 1.4 %add_convert_fusion.1 = bf16[256,1792]{1,0:T(8,128)(2,1)S(1)} fusion(bf16[256,1792]{1,0:T(8,128)(2,1)} %collective-permute-done.11, bf16[256,1792]{1,0:T(8,128)(2,1)S(1)} %get-tuple-element.19), kind=kLoop, calls=%fused_computation.4 | loop fusion | flops 1835008 | bytes 2752512 | tf_op jit(solution)/shard_map/convert_element_type | solution.py:140
  73.0 1.6 %collective-permute-start.12 = (bf16[128,1792]{1,0:T(8,128)(2,1)S(1)}, bf16[128,1792]{1,0:T(8,128)(2,1)S(1)}, u32[]{:S(2)}, u32[]{:S(2)}) collective-permute-start(bf16[128,1792]{1,0:T(8,128)(2,1)S(1)} %slice.125), channel_id=1, source_target_pairs={{0,2},{2,0},{4,6},{6,4},{8,10},{10,8},{12,14},{14,12},{16,18},{18,... | collective-permute-start | bytes 1376264 | tf_op jit(solution)/shard_map/ppermute | solution.py:47
  74.7 1.4 %add_convert_fusion = bf16[256,1792]{1,0:T(8,128)(2,1)S(1)} fusion(bf16[256,1792]{1,0:T(8,128)(2,1)} %collective-permute-done.14, bf16[256,1792]{1,0:T(8,128)(2,1)S(1)} %get-tuple-element.21), kind=kLoop, calls=%fused_computation.3 | loop fusion | flops 1835008 | bytes 2752512 | tf_op jit(solution)/shard_map/convert_element_type | solution.py:140
  76.1 1.5 %collective-permute-start.15 = (bf16[128,1792]{1,0:T(8,128)(2,1)S(1)}, bf16[128,1792]{1,0:T(8,128)(2,1)S(1)}, u32[]{:S(2)}, u32[]{:S(2)}) collective-permute-start(bf16[128,1792]{1,0:T(8,128)(2,1)S(1)} %slice.129), channel_id=1, source_target_pairs={{0,4},{2,6},{4,0},{6,2},{8,12},{10,14},{12,8},{14,10},{16,20},{18,... | collective-permute-start | bytes 1376264 | tf_op jit(solution)/shard_map/ppermute | solution.py:47
  77.7 12.3 %collective-permute-done.12 = bf16[128,1792]{1,0:T(8,128)(2,1)S(1)} collective-permute-done((bf16[128,1792]{1,0:T(8,128)(2,1)S(1)}, bf16[128,1792]{1,0:T(8,128)(2,1)S(1)}, u32[]{:S(2)}, u32[]{:S(2)}) %collective-permute-start.12) | collective-permute-done | bytes 458784 | tf_op jit(solution)/shard_map/ppermute | solution.py:47
  91.6 1.5 %collective-permute-start.16 = (bf16[64,1792]{1,0:T(8,128)(2,1)S(1)}, bf16[64,1792]{1,0:T(8,128)(2,1)S(1)}, u32[]{:S(2)}, u32[]{:S(2)}) collective-permute-start(bf16[64,1792]{1,0:T(8,128)(2,1)S(1)} %slice.131), channel_id=1, source_target_pairs={{0,2},{2,0},{4,6},{6,4},{8,10},{10,8},{12,14},{14,12},{16,18},{18,... | collective-permute-start | bytes 688136 | tf_op jit(solution)/shard_map/ppermute | solution.py:47
  93.1 4.4 %collective-permute-done.13 = bf16[64,1792]{1,0:T(8,128)(2,1)} collective-permute-done((bf16[64,1792]{1,0:T(8,128)(2,1)S(1)}, bf16[64,1792]{1,0:T(8,128)(2,1)}, u32[]{:S(2)}, u32[]{:S(2)}) %collective-permute-start.13) | collective-permute-done | bytes 229408 | tf_op jit(solution)/shard_map/ppermute | solution.py:47
  99.8 1.6 %collective-permute-start.17 = (bf16[32,3584]{1,0:T(8,128)(2,1)S(1)}, bf16[32,3584]{1,0:T(8,128)(2,1)S(1)}, u32[]{:S(2)}, u32[]{:S(2)}) collective-permute-start(bf16[32,3584]{1,0:T(8,128)(2,1)S(1)} %pad_maximum_fusion.4), channel_id=1, source_target_pairs={{0,8},{2,10},{4,12},{6,14},{8,0},{10,2},{12,4},{14,6},{16,24},{18,... | collective-permute-start | bytes 688136 | tf_op jit(solution)/shard_map/ppermute | solution.py:47
  101.8 3.9 %shard_map.116 = bf16[512,512]{1,0:T(8,128)(2,1)} custom-call(s32[2,384]{1,0:T(2,128)S(1)} %pad_add_fusion.owner, s32[512,1]{1,0:T(8,128)S(1)} %broadcast_in_dim_reshape.5.request, bf16[512,576]{1,0:T(8,128)(2,1)S(1)} %bitcast.45, bf16[384,576]{1,0:T(8,128)(2,1)} %bitcast.19.refs_0_, bf16[384,576]{1,0:T(8,128)(2,1)S(1)} %bitcast.46), custom_call_target="tpu_custom_call" | custom-call | flops 905969664 | bytes 3483648 | tf_op jit(solution)/shard_map/pallas_call | solution.py:23
  107.1 2.5 %collective-permute-start.19 = (bf16[16,3584]{1,0:T(8,128)(2,1)S(1)}, bf16[16,3584]{1,0:T(8,128)(2,1)S(1)}, u32[]{:S(2)}, u32[]{:S(2)}) collective-permute-start(bf16[16,3584]{1,0:T(8,128)(2,1)S(1)} %slice.135), channel_id=1, source_target_pairs={{0,16},{2,18},{4,20},{6,22},{8,24},{10,26},{12,28},{14,30},{16,0},... | collective-permute-start | bytes 344072 | tf_op jit(solution)/shard_map/ppermute | solution.py:47
  109.5 4.8 %collective-permute-done.19 = bf16[16,3584]{1,0:T(8,128)(2,1)S(1)} collective-permute-done((bf16[16,3584]{1,0:T(8,128)(2,1)S(1)}, bf16[16,3584]{1,0:T(8,128)(2,1)S(1)}, u32[]{:S(2)}, u32[]{:S(2)}) %collective-permute-start.19) | collective-permute-done | bytes 114720 | tf_op jit(solution)/shard_map/ppermute | solution.py:47
  (95 shorter events, 18.5 us)
Async XLA Ops:
  0.6 29.8 %copy-start = (bf16[48,16,576]{2,1,0:T(8,128)(2,1)S(1)}, bf16[48,16,576]{2,1,0:T(8,128)(2,1)}, u32[]{:S(2)}) copy-start(bf16[48,16,576]{2,1,0:T(8,128)(2,1)} %param.16) | copy-start | bytes 2654212
  0.6 29.1 %copy-start.4 = (s32[768]{0:T(1024)S(1)}, s32[768]{0:T(1024)}, u32[]{:S(2)}) copy-start(s32[768]{0:T(1024)} %param.17) | copy-start | bytes 9220
  3.4 9.9 %collective-permute-start = (bf16[1,16,3712]{2,1,0:T(8,128)(2,1)S(1)}, bf16[1,16,3712]{2,1,0:T(8,128)(2,1)S(1)}, u32[]{:S(2)}, u32[]{:S(2)}) collective-permute-start(bf16[1,16,3712]{2,1,0:T(8,128)(2,1)S(1)} %maximum_bitcast_fusion), channel_id=1, source_target_pairs={{0,16},{2,18},{4,20},{6,22},{8,24},{10,26},{12,28},{14,30},{16,0},... | collective-permute-start | bytes 356360 | tf_op jit(solution)/shard_map/ppermute | solution.py:47
  13.3 7.0 %collective-permute-start.1 = (bf16[2,16,3712]{2,1,0:T(8,128)(2,1)S(1)}, bf16[2,16,3712]{2,1,0:T(8,128)(2,1)S(1)}, u32[]{:S(2)}, u32[]{:S(2)}) collective-permute-start(bf16[2,16,3712]{2,1,0:T(8,128)(2,1)S(1)} %pad_maximum_fusion.3), channel_id=1, source_target_pairs={{0,8},{2,10},{4,12},{6,14},{8,0},{10,2},{12,4},{14,6},{16,24},{18,... | collective-permute-start | bytes 712712 | tf_op jit(solution)/shard_map/ppermute | solution.py:47
  20.4 6.3 %collective-permute-start.4 = (bf16[4,16,1920]{2,1,0:T(8,128)(2,1)S(1)}, bf16[4,16,1920]{2,1,0:T(8,128)(2,1)S(1)}, u32[]{:S(2)}, u32[]{:S(2)}) collective-permute-start(bf16[4,16,1920]{2,1,0:T(8,128)(2,1)S(1)} %slice.118), channel_id=1, source_target_pairs={{0,2},{2,0},{4,6},{6,4},{8,10},{10,8},{12,14},{14,12},{16,18},{18,... | collective-permute-start | bytes 737288 | tf_op jit(solution)/shard_map/ppermute | solution.py:47
  21.7 7.3 %collective-permute-start.2 = (bf16[4,16,1792]{2,1,0:T(8,128)(2,1)S(1)}, bf16[4,16,1792]{2,1,0:T(8,128)(2,1)S(1)}, u32[]{:S(2)}, u32[]{:S(2)}) collective-permute-start(bf16[4,16,1792]{2,1,0:T(8,128)(2,1)S(1)} %slice.117), channel_id=1, source_target_pairs={{0,4},{2,6},{4,0},{6,2},{8,12},{10,14},{12,8},{14,10},{16,20},{18,... | collective-permute-start | bytes 688136 | tf_op jit(solution)/shard_map/ppermute | solution.py:47
  26.8 11.7 %collective-permute-start.5 = (bf16[8,16,1920]{2,1,0:T(8,128)(2,1)S(1)}, bf16[8,16,1920]{2,1,0:T(8,128)(2,1)S(1)}, u32[]{:S(2)}, u32[]{:S(2)}) collective-permute-start(bf16[8,16,1920]{2,1,0:T(8,128)(2,1)S(1)} %pad_maximum_fusion), channel_id=1, source_target_pairs={{0,4},{2,6},{4,0},{6,2},{8,12},{10,14},{12,8},{14,10},{16,20},{18,... | collective-permute-start | bytes 1474568 | tf_op jit(solution)/shard_map/ppermute | solution.py:47
  29.1 9.2 %collective-permute-start.3 = (bf16[8,16,1792]{2,1,0:T(8,128)(2,1)S(1)}, bf16[8,16,1792]{2,1,0:T(8,128)(2,1)}, u32[]{:S(2)}, u32[]{:S(2)}) collective-permute-start(bf16[8,16,1792]{2,1,0:T(8,128)(2,1)S(1)} %pad_maximum_fusion.2), channel_id=1, source_target_pairs={{0,2},{2,0},{4,6},{6,4},{8,10},{10,8},{12,14},{14,12},{16,18},{18,... | collective-permute-start | bytes 1376264 | tf_op jit(solution)/shard_map/ppermute | solution.py:47
  31.3 19.3 %all-to-all-start = ((bf16[16,24,576]{2,1,0:T(8,128)(2,1)}), bf16[16,24,576]{2,1,0:T(8,128)(2,1)S(1)}, u32[]{:S(2)}, u32[]{:S(2)}) async-start(bf16[16,24,576]{2,1,0:T(8,128)(2,1)} %bitcast.36), calls=%async_computation | async-start | bytes 983040 | tf_op jit(solution)/shard_map/all_to_all | solution.py:233
  38.3 12.3 %collective-permute-start.8 = (bf16[8,16,1920]{2,1,0:T(8,128)(2,1)S(1)}, bf16[8,16,1920]{2,1,0:T(8,128)(2,1)}, u32[]{:S(2)}, u32[]{:S(2)}) collective-permute-start(bf16[8,16,1920]{2,1,0:T(8,128)(2,1)S(1)} %pad_maximum_fusion), channel_id=1, source_target_pairs={{0,1},{1,0},{2,3},{3,2},{4,5},{5,4},{6,7},{7,6},{8,9},{9,8},{10,11... | collective-permute-start | bytes 1474568 | tf_op jit(solution)/shard_map/ppermute | solution.py:52
  38.4 12.2 %collective-permute-start.9 = (bf16[8,16,1920]{2,1,0:T(8,128)(2,1)S(1)}, bf16[8,16,1920]{2,1,0:T(8,128)(2,1)}, u32[]{:S(2)}, u32[]{:S(2)}) collective-permute-start(bf16[8,16,1920]{2,1,0:T(8,128)(2,1)S(1)} %collective-permute-done.5), channel_id=1, source_target_pairs={{0,1},{1,0},{2,3},{3,2},{4,5},{5,4},{6,7},{7,6},{8,9},{9,8},{10,11... | collective-permute-start | bytes 1474568 | tf_op jit(solution)/shard_map/ppermute | solution.py:52
  39.0 11.6 %collective-permute-start.6 = (bf16[8,16,1792]{2,1,0:T(8,128)(2,1)S(1)}, bf16[8,16,1792]{2,1,0:T(8,128)(2,1)}, u32[]{:S(2)}, u32[]{:S(2)}) collective-permute-start(bf16[8,16,1792]{2,1,0:T(8,128)(2,1)S(1)} %pad_maximum_fusion.2), channel_id=1, source_target_pairs={{0,1},{1,0},{2,3},{3,2},{4,5},{5,4},{6,7},{7,6},{8,9},{9,8},{10,11... | collective-permute-start | bytes 1376264 | tf_op jit(solution)/shard_map/ppermute | solution.py:52
  39.2 11.4 %collective-permute-start.7 = (bf16[8,16,1792]{2,1,0:T(8,128)(2,1)}, bf16[8,16,1792]{2,1,0:T(8,128)(2,1)}, u32[]{:S(2)}, u32[]{:S(2)}) collective-permute-start(bf16[8,16,1792]{2,1,0:T(8,128)(2,1)} %collective-permute-done.3), channel_id=1, source_target_pairs={{0,1},{1,0},{2,3},{3,2},{4,5},{5,4},{6,7},{7,6},{8,9},{9,8},{10,11... | collective-permute-start | bytes 1376264 | tf_op jit(solution)/shard_map/ppermute | solution.py:52
  50.6 10.2 %collective-permute-start.10 = (bf16[16,24,576]{2,1,0:T(8,128)(2,1)S(1)}, bf16[16,24,576]{2,1,0:T(8,128)(2,1)S(1)}, u32[]{:S(2)}, u32[]{:S(2)}) collective-permute-start(bf16[16,24,576]{2,1,0:T(8,128)(2,1)S(1)} %all-to-all-done), channel_id=1, source_target_pairs={{0,1},{1,0},{2,3},{3,2},{4,5},{5,4},{6,7},{7,6},{8,9},{9,8},{10,11... | collective-permute-start | bytes 1327112 | tf_op jit(solution)/shard_map/ppermute | solution.py:52
  66.5 5.1 %collective-permute-start.11 = (bf16[256,1792]{1,0:T(8,128)(2,1)}, bf16[256,1792]{1,0:T(8,128)(2,1)}, u32[]{:S(2)}, u32[]{:S(2)}) collective-permute-start(bf16[256,1792]{1,0:T(8,128)(2,1)} %get-tuple-element.20), channel_id=1, source_target_pairs={{0,1},{1,0},{2,3},{3,2},{4,5},{5,4},{6,7},{7,6},{8,9},{9,8},{10,11... | collective-permute-start | bytes 2752520 | tf_op jit(solution)/shard_map/ppermute | solution.py:52
  67.0 7.7 %collective-permute-start.14 = (bf16[256,1792]{1,0:T(8,128)(2,1)}, bf16[256,1792]{1,0:T(8,128)(2,1)}, u32[]{:S(2)}, u32[]{:S(2)}) collective-permute-start(bf16[256,1792]{1,0:T(8,128)(2,1)} %get-tuple-element.22), channel_id=1, source_target_pairs={{0,1},{1,0},{2,3},{3,2},{4,5},{5,4},{6,7},{7,6},{8,9},{9,8},{10,11... | collective-permute-start | bytes 2752520 | tf_op jit(solution)/shard_map/ppermute | solution.py:52
  67.2 24.4 %all-to-all-start.1 = ((bf16[16,24,576]{2,1,0:T(8,128)(2,1)}), bf16[16,24,576]{2,1,0:T(8,128)(2,1)}, u32[]{:S(2)}, u32[]{:S(2)}) async-start(bf16[16,24,576]{2,1,0:T(8,128)(2,1)} %bitcast.16), calls=%async_computation.1 | async-start | bytes 983040 | tf_op jit(solution)/shard_map/all_to_all | solution.py:257
  73.0 16.9 %collective-permute-start.12 = (bf16[128,1792]{1,0:T(8,128)(2,1)S(1)}, bf16[128,1792]{1,0:T(8,128)(2,1)S(1)}, u32[]{:S(2)}, u32[]{:S(2)}) collective-permute-start(bf16[128,1792]{1,0:T(8,128)(2,1)S(1)} %slice.125), channel_id=1, source_target_pairs={{0,2},{2,0},{4,6},{6,4},{8,10},{10,8},{12,14},{14,12},{16,18},{18,... | collective-permute-start | bytes 1376264 | tf_op jit(solution)/shard_map/ppermute | solution.py:47
  76.1 15.3 %collective-permute-start.15 = (bf16[128,1792]{1,0:T(8,128)(2,1)S(1)}, bf16[128,1792]{1,0:T(8,128)(2,1)S(1)}, u32[]{:S(2)}, u32[]{:S(2)}) collective-permute-start(bf16[128,1792]{1,0:T(8,128)(2,1)S(1)} %slice.129), channel_id=1, source_target_pairs={{0,4},{2,6},{4,0},{6,2},{8,12},{10,14},{12,8},{14,10},{16,20},{18,... | collective-permute-start | bytes 1376264 | tf_op jit(solution)/shard_map/ppermute | solution.py:47
  90.1 7.4 %collective-permute-start.13 = (bf16[64,1792]{1,0:T(8,128)(2,1)S(1)}, bf16[64,1792]{1,0:T(8,128)(2,1)}, u32[]{:S(2)}, u32[]{:S(2)}) collective-permute-start(bf16[64,1792]{1,0:T(8,128)(2,1)S(1)} %slice.127), channel_id=1, source_target_pairs={{0,4},{2,6},{4,0},{6,2},{8,12},{10,14},{12,8},{14,10},{16,20},{18,... | collective-permute-start | bytes 688136 | tf_op jit(solution)/shard_map/ppermute | solution.py:47
  91.6 10.2 %collective-permute-start.18 = (bf16[16,24,576]{2,1,0:T(8,128)(2,1)}, bf16[16,24,576]{2,1,0:T(8,128)(2,1)S(1)}, u32[]{:S(2)}, u32[]{:S(2)}) collective-permute-start(bf16[16,24,576]{2,1,0:T(8,128)(2,1)} %all-to-all-done.1), channel_id=1, source_target_pairs={{0,1},{1,0},{2,3},{3,2},{4,5},{5,4},{6,7},{7,6},{8,9},{9,8},{10,11... | collective-permute-start | bytes 1327112 | tf_op jit(solution)/shard_map/ppermute | solution.py:52
  91.6 8.0 %collective-permute-start.16 = (bf16[64,1792]{1,0:T(8,128)(2,1)S(1)}, bf16[64,1792]{1,0:T(8,128)(2,1)S(1)}, u32[]{:S(2)}, u32[]{:S(2)}) collective-permute-start(bf16[64,1792]{1,0:T(8,128)(2,1)S(1)} %slice.131), channel_id=1, source_target_pairs={{0,2},{2,0},{4,6},{6,4},{8,10},{10,8},{12,14},{14,12},{16,18},{18,... | collective-permute-start | bytes 688136 | tf_op jit(solution)/shard_map/ppermute | solution.py:47
  99.8 7.2 %collective-permute-start.17 = (bf16[32,3584]{1,0:T(8,128)(2,1)S(1)}, bf16[32,3584]{1,0:T(8,128)(2,1)S(1)}, u32[]{:S(2)}, u32[]{:S(2)}) collective-permute-start(bf16[32,3584]{1,0:T(8,128)(2,1)S(1)} %pad_maximum_fusion.4), channel_id=1, source_target_pairs={{0,8},{2,10},{4,12},{6,14},{8,0},{10,2},{12,4},{14,6},{16,24},{18,... | collective-permute-start | bytes 688136 | tf_op jit(solution)/shard_map/ppermute | solution.py:47
  107.1 7.2 %collective-permute-start.19 = (bf16[16,3584]{1,0:T(8,128)(2,1)S(1)}, bf16[16,3584]{1,0:T(8,128)(2,1)S(1)}, u32[]{:S(2)}, u32[]{:S(2)}) collective-permute-start(bf16[16,3584]{1,0:T(8,128)(2,1)S(1)} %slice.135), channel_id=1, source_target_pairs={{0,16},{2,18},{4,20},{6,22},{8,24},{10,26},{12,28},{14,30},{16,0},... | collective-permute-start | bytes 344072 | tf_op jit(solution)/shard_map/ppermute | solution.py:47
  (7 other events, 67.7 us)

commit v5 on v4

--- a/solution.py
+++ b/solution.py
@@ -58,16 +58,22 @@
     return [pass_tp(value, step) for step in range(1, lax.axis_size("tp"))]
 
 
-def gather_rows(rows, orders, ends):
-    value = rows[None]
-    for bit in orders[0][:-2]:
+def gather_rows(rows, others, orders, ends):
+    shared = orders[0][:-2]
+    values = [
+        jnp.concatenate([value[None], exchange(value[None], shared[0])], axis=0)
+        for value in (rows, others)
+    ]
+    value = jnp.concatenate(values, axis=2)
+    for bit in shared[1:]:
+        shared_sent = value
         value = jnp.concatenate([value, exchange(value, bit)], axis=0)
     halves = []
     for order, start, end in zip(orders, (0,) + ends, ends):
         part = value[:, :, start:end]
         part = jnp.concatenate([part, exchange(part, order[-2])], axis=0)
         halves.append((part, exchange(part, order[-1])))
-    return halves
+    return halves, shared_sent
 
 
 def places_of(order):
@@ -225,12 +231,13 @@
     return mine.reshape(share, ep_size, block_size * latent // ep_size).transpose(1, 0, 2)
 
 
-def cache_turn(pieces, block_source, slots):
+def cache_turn(pieces, block_source, slots, before):
     ep_size = lax.axis_size("ep")
     tp_size = lax.axis_size("tp")
     tp_index = lax.axis_index("tp")
     share, piece = pieces.shape[1:]
     spread = lax.all_to_all(pieces, "ep", split_axis=0, concat_axis=0, tiled=True)
+    spread = tie(spread, before)
     wanted = lax.dynamic_slice_in_dim(
         block_source.reshape(ep_size, tp_size, share), tp_index, 1, axis=1
     ).reshape(-1)
@@ -346,13 +353,13 @@
     )
     gate_parts = jnp.concatenate(three_parts(dense_gate), axis=1)
     pad = -gate_parts.shape[1] % 128
-    sent_rows = jnp.concatenate([tokens, jnp.pad(gate_parts, ((0, 0), (0, pad)))], axis=1)
-    ends = tuple(cut * part for part in range(1, parts)) + (sent_rows.shape[1],)
-
-    halves = gather_rows(sent_rows, orders, ends)
+    gates = jnp.pad(gate_parts, ((0, 0), (0, pad)))
+    ends = tuple(cut * part for part in range(1, parts)) + (tokens.shape[1] + gates.shape[1],)
+    halves, shared_sent = gather_rows(tokens, gates, orders, ends)
     last_sent = halves[-1][0]
-    pieces = tie(cache_out(latent_cache), last_sent)
-    ordered = cache_turn(pieces, block_source, slot_total)
+    pieces = tie(cache_out(latent_cache), shared_sent)
+    ordered = cache_turn(pieces, block_source, slot_total, last_sent)
+    keys = cache_in(ordered, block_size, latent)
     places = [places_of(order) for order in orders]
     to_first = [[places[0].index(place) for place in own] for own in places]
     from_first = [[own.index(place) for place in places[0]] for own in places]
@@ -378,27 +385,24 @@
         jax.nn.silu(gate_and_up[:, 0]) * gate_and_up[:, 1] * my_gate[:, None]
     ).astype(jnp.bfloat16)
 
-    hidden = tie(hidden, ordered)
     by_step = down(hidden, expert_down[0], from_first, row_count)
-    ordered = tie(ordered, by_step)
     sums = list(by_step[-1])
     for part in range(parts):
         others = [pass_tp(by_step[step - 1][part], step) for step in range(1, tp_size)]
         sums[part] = add_up([sums[part]] + others)
-    keys = cache_in(ordered, block_size, latent)
 
     held = {}
 
-    def beside_second_sum(sent):
+    def beside_first_sum(sent):
         sent, near = lax.optimization_barrier((sent, keys))
         held["attended"] = attend(queries, [near] + swap_tp(near), block_request, block_used)
         return sent
 
-    def beside_last_sum(sent):
+    def beside_second_sum(sent):
         sent, held["attended"] = lax.optimization_barrier((sent, held["attended"]))
         return sent
 
-    hooks = {1: beside_second_sum, len(bits) - 1: beside_last_sum}
+    hooks = {0: beside_first_sum, 1: beside_second_sum}
     return (scatter_sums(sums, orders, hooks), held["attended"])
 
 

time: 116 us -> 128 us (1.10)
  waiting for transfers between devices: 49.6 us -> 55.2 us
  local copies, waits for them, and re-layouts: 4.47 us -> 7.71 us
  starting transfers between devices: 32.9 us -> 35.4 us
  other arithmetic: 7.45 us -> 8.99 us
    all_to_all x1, waiting for transfers between devices: 9.36 us -> 0.01 us  [cache_turn(): lax.all_to_all(pieces, 'ep', split_axis=0, concat_axis=0, tiled=True)]
    all_to_all x1, waiting for transfers between devices: 0.01 us -> 8.31 us  [cache_in(): lax.all_to_all(ordered, 'ep', split_axis=0, concat_axis=0, tiled=True)]
    ppermute x12 -> x13, waiting for transfers between devices: 40.2 us -> 44.2 us  [exchange(): lax.ppermute(value, 'ep', [(index, index ^ bit) for index in range(ep_siz...]
    unnamed x21 -> x35, local copies, waits for them, and re-layouts: 2.52 us -> 5.71 us
    ppermute x8, waiting for transfers between devices: 0.02 us -> 2.78 us  [pass_tp(): lax.ppermute(value, 'tp', [(index, (index + step) % tp_size) for index in...]
    all_to_all x1, starting transfers between devices: 4.41 us -> 6.9 us  [cache_in(): lax.all_to_all(ordered, 'ep', split_axis=0, concat_axis=0, tiled=True)]
    all_to_all x1, starting transfers between devices: 6.9 us -> 9.21 us  [cache_turn(): lax.all_to_all(pieces, 'ep', split_axis=0, concat_axis=0, tiled=True)]
    ppermute x12 -> x13, starting transfers between devices: 19.8 us -> 18.1 us  [exchange(): lax.ppermute(value, 'ep', [(index, index ^ bit) for index in range(ep_siz...]
  transfers between devices with their start and end apart: 22 -> 23, of which waited for: 11 -> 13; matrix products, arithmetic and copies ran while one was open for 14% -> 15% of each run, Pallas kernels for 5% -> 9%
where the time goes in v5:
time: 128 us
  waiting for transfers between devices  55.2 us (43%)
  starting transfers between devices  35.4 us (28%)
  Pallas kernels  11.1 us (9%)
  other arithmetic  8.99 us (7%)
  matrix products  7.95 us (6%)
  local copies, waits for them, and re-layouts  7.71 us (6%)
    ppermute x13, waiting for transfers between devices, exchange(): lax.ppermute(value, 'ep', [(index, index ^ bit) for index in range(ep_siz...  44.2 us
    ppermute x13, starting transfers between devices, exchange(): lax.ppermute(value, 'ep', [(index, index ^ bit) for index in range(ep_siz...  18.1 us
    pallas_call x4, Pallas kernels, kernel_call(): pl.pallas_call(kernel, out_shape=out_shape, in_specs=in_specs or [WHOLE]...  11.1 us
    all_to_all x1, starting transfers between devices, cache_turn(): lax.all_to_all(pieces, 'ep', split_axis=0, concat_axis=0, tiled=True)  9.21 us
    all_to_all x1, waiting for transfers between devices, cache_in(): lax.all_to_all(ordered, 'ep', split_axis=0, concat_axis=0, tiled=True)  8.31 us
    dot_general x1, matrix products, body(): jnp.einsum('sd,dgf->sgf', all_rows, expert_gate_up[0], preferred_element_...  7.95 us
    all_to_all x1, starting transfers between devices, cache_in(): lax.all_to_all(ordered, 'ep', split_axis=0, concat_axis=0, tiled=True)  6.9 us
    unnamed x35, local copies, waits for them, and re-layouts  5.71 us
  transfers between devices with their start and end apart: 23, of which 13 were waited for; matrix products, arithmetic and copies ran while one was open for 15% of the time, Pallas kernels for 9%

profile of v5, /device:TPU:0, one launch (start us, length us, event | category | flops | bytes accessed | tf_op | source)
XLA Modules:
  0.0 127.5 jit_solution(6947685232921060361)
XLA Ops:
  0.6 4.1 %collective-permute-start = (bf16[1,16,3584]{2,1,0:T(8,128)(2,1)}, bf16[1,16,3584]{2,1,0:T(8,128)(2,1)S(1)}, u32[]{:S(2)}, u32[]{:S(2)}) collective-permute-start(bf16[1,16,3584]{2,1,0:T(8,128)(2,1)} %bitcast.50), channel_id=1, source_target_pairs={{0,16},{2,18},{4,20},{6,22},{8,24},{10,26},{12,28},{14,30},{16,0},... | collective-permute-start | bytes 344072 | tf_op jit(solution)/shard_map/ppermute | solution.py:47
  6.6 4.4 %collective-permute-done.1 = bf16[1,16,128]{2,1,0:T(8,128)(2,1)S(1)} collective-permute-done((bf16[1,16,128]{2,1,0:T(8,128)(2,1)S(1)}, bf16[1,16,128]{2,1,0:T(8,128)(2,1)S(1)}, u32[]{:S(2)}, u32[]{:S(2)}) %collective-permute-start.1) | collective-permute-done | bytes 4128 | tf_op jit(solution)/shard_map/ppermute | solution.py:47
  12.0 1.6 %collective-permute-start.2 = (bf16[2,16,3712]{2,1,0:T(8,128)(2,1)S(1)}, bf16[2,16,3712]{2,1,0:T(8,128)(2,1)S(1)}, u32[]{:S(2)}, u32[]{:S(2)}) collective-permute-start(bf16[2,16,3712]{2,1,0:T(8,128)(2,1)S(1)} %maximum_maximum_fusion), channel_id=1, source_target_pairs={{0,8},{2,10},{4,12},{6,14},{8,0},{10,2},{12,4},{14,6},{16,24},{18,... | collective-permute-start | bytes 712712 | tf_op jit(solution)/shard_map/ppermute | solution.py:47
  13.6 5.0 %collective-permute-done.2 = bf16[2,16,3712]{2,1,0:T(8,128)(2,1)S(1)} collective-permute-done((bf16[2,16,3712]{2,1,0:T(8,128)(2,1)S(1)}, bf16[2,16,3712]{2,1,0:T(8,128)(2,1)S(1)}, u32[]{:S(2)}, u32[]{:S(2)}) %collective-permute-start.2) | collective-permute-done | bytes 237600 | tf_op jit(solution)/shard_map/ppermute | solution.py:47
  21.7 1.6 %collective-permute-start.3 = (bf16[4,16,1792]{2,1,0:T(8,128)(2,1)S(1)}, bf16[4,16,1792]{2,1,0:T(8,128)(2,1)S(1)}, u32[]{:S(2)}, u32[]{:S(2)}) collective-permute-start(bf16[4,16,1792]{2,1,0:T(8,128)(2,1)S(1)} %slice.117), channel_id=1, source_target_pairs={{0,4},{2,6},{4,0},{6,2},{8,12},{10,14},{12,8},{14,10},{16,20},{18,... | collective-permute-start | bytes 688136 | tf_op jit(solution)/shard_map/ppermute | solution.py:47
  23.3 3.3 %collective-permute-done.5 = bf16[4,16,1920]{2,1,0:T(8,128)(2,1)S(1)} collective-permute-done((bf16[4,16,1920]{2,1,0:T(8,128)(2,1)S(1)}, bf16[4,16,1920]{2,1,0:T(8,128)(2,1)S(1)}, u32[]{:S(2)}, u32[]{:S(2)}) %collective-permute-start.5) | collective-permute-done | bytes 245792 | tf_op jit(solution)/shard_map/ppermute | solution.py:47
  27.3 1.4 %collective-permute-start.6 = (bf16[8,16,1920]{2,1,0:T(8,128)(2,1)S(1)}, bf16[8,16,1920]{2,1,0:T(8,128)(2,1)S(1)}, u32[]{:S(2)}, u32[]{:S(2)}) collective-permute-start(bf16[8,16,1920]{2,1,0:T(8,128)(2,1)S(1)} %pad_maximum_fusion), channel_id=1, source_target_pairs={{0,4},{2,6},{4,0},{6,2},{8,12},{10,14},{12,8},{14,10},{16,20},{18,... | collective-permute-start | bytes 1474568 | tf_op jit(solution)/shard_map/ppermute | solution.py:47
  28.8 1.6 %collective-permute-start.4 = (bf16[8,16,1792]{2,1,0:T(8,128)(2,1)S(1)}, bf16[8,16,1792]{2,1,0:T(8,128)(2,1)}, u32[]{:S(2)}, u32[]{:S(2)}) collective-permute-start(bf16[8,16,1792]{2,1,0:T(8,128)(2,1)S(1)} %pad_maximum_fusion.2), channel_id=1, source_target_pairs={{0,2},{2,0},{4,6},{6,4},{8,10},{10,8},{12,14},{14,12},{16,18},{18,... | collective-permute-start | bytes 1376264 | tf_op jit(solution)/shard_map/ppermute | solution.py:47
  30.4 7.4 %collective-permute-done.4 = bf16[8,16,1792]{2,1,0:T(8,128)(2,1)} collective-permute-done((bf16[8,16,1792]{2,1,0:T(8,128)(2,1)S(1)}, bf16[8,16,1792]{2,1,0:T(8,128)(2,1)}, u32[]{:S(2)}, u32[]{:S(2)}) %collective-permute-start.4) | collective-permute-done | bytes 458784 | tf_op jit(solution)/shard_map/ppermute | solution.py:47
  40.4 9.2 %all-to-all-start = ((bf16[16,24,576]{2,1,0:T(8,128)(2,1)}), bf16[16,24,576]{2,1,0:T(8,128)(2,1)S(1)}, u32[]{:S(2)}, u32[]{:S(2)}) async-start(bf16[16,24,576]{2,1,0:T(8,128)(2,1)} %bitcast.49), calls=%async_computation | async-start | bytes 983040 | tf_op jit(solution)/shard_map/all_to_all | solution.py:239
  50.6 1.8 %shard_map.113 = bf16[256,7168]{1,0:T(8,128)(2,1)S(1)} custom-call(bf16[128,1792]{1,0:T(8,128)(2,1)S(1)} %bitcast.43, bf16[128,1792]{1,0:T(8,128)(2,1)} %bitcast.3.refs_1_, bf16[128,1920]{1,0:T(8,128)(2,1)S(1)} %bitcast.41, bf16[128,1920]{1,0:T(8,128)(2,1)S(1)} %bitcast.44, bf16[128,1792]{1,0:T(8,128)(2,1)} %bitcast.6.refs_4_, ...), custom_call_target="tpu_custom_call" | custom-call | bytes 11272192 | tf_op jit(solution)/shard_map/pallas_call | solution.py:23
  52.4 7.9 %fusion = f32[256,2,512]{2,0,1:T(8,128)S(1)} fusion(bf16[7168,2,512]{2,1,0:T(2,128)(2,1)} %bitcast.54, bf16[256,7168]{1,0:T(8,128)(2,1)S(1)} %shard_map.113), kind=kOutput, calls=%fused_computation | convolution fusion | flops 3758096384 | bytes 19398656 | tf_op jit(solution)/shard_map/sd,dgf->sgf/dot_general | solution.py:381
  60.6 3.7 %shard_map.114 = (bf16[256,1792]{1,0:T(8,128)(2,1)}, bf16[256,1792]{1,0:T(8,128)(2,1)S(1)}, bf16[256,1792]{1,0:T(8,128)(2,1)S(1)}, bf16[256,1792]{1,0:T(8,128)(2,1)S(1)}) custom-call(bf16[256,512]{1,0:T(8,128)(2,1)S(1)} %fusion.5.hidden, bf16[7168,512]{1,0:T(8,128)(2,1)S(1)} %bitcast.40), custom_call_target="tpu_custom_call" | custom-call | flops 1879048192 | bytes 11534336 | tf_op jit(solution)/shard_map/pallas_call | solution.py:23
  66.9 2.4 %collective-permute-done.15 = bf16[16,24,576]{2,1,0:T(8,128)(2,1)} collective-permute-done((bf16[16,24,576]{2,1,0:T(8,128)(2,1)S(1)}, bf16[16,24,576]{2,1,0:T(8,128)(2,1)}, u32[]{:S(2)}, u32[]{:S(2)}) %collective-permute-start.15) | collective-permute-done | bytes 442400 | tf_op jit(solution)/shard_map/ppermute | solution.py:52
  69.3 2.6 %shard_map.115 = bf16[384,576]{1,0:T(8,128)(2,1)} custom-call(s32[384,2]{1,0:T(8,128)S(1)} %fusion.7.index, bf16[384,576]{1,0:T(8,128)(2,1)S(1)} %bitcast.42, bf16[384,576]{1,0:T(8,128)(2,1)} %bitcast.17.refs_1_), custom_call_target="tpu_custom_call" | custom-call | flops 339738624 | bytes 2217984 | tf_op jit(solution)/shard_map/pallas_call | solution.py:23
  71.9 6.9 %all-to-all-start.1 = ((bf16[16,24,576]{2,1,0:T(8,128)(2,1)}), bf16[16,24,576]{2,1,0:T(8,128)(2,1)S(1)}, u32[]{:S(2)}, u32[]{:S(2)}) async-start(bf16[16,24,576]{2,1,0:T(8,128)(2,1)} %bitcast.18), calls=%async_computation.1 | async-start | bytes 983040 | tf_op jit(solution)/shard_map/all_to_all | solution.py:264
  80.3 2.0 %collective-permute-start.12 = (bf16[128,1792]{1,0:T(8,128)(2,1)S(1)}, bf16[128,1792]{1,0:T(8,128)(2,1)}, u32[]{:S(2)}, u32[]{:S(2)}) collective-permute-start(bf16[128,1792]{1,0:T(8,128)(2,1)S(1)} %slice.125), channel_id=1, source_target_pairs={{0,2},{2,0},{4,6},{6,4},{8,10},{10,8},{12,14},{14,12},{16,18},{18,... | collective-permute-start | bytes 1376264 | tf_op jit(solution)/shard_map/ppermute | solution.py:47
  85.4 8.3 %all-to-all-done.1 = bf16[16,24,576]{2,1,0:T(8,128)(2,1)S(1)} async-done(((bf16[16,24,576]{2,1,0:T(8,128)(2,1)}), bf16[16,24,576]{2,1,0:T(8,128)(2,1)S(1)}, u32[]{:S(2)}, u32[]{:S(2)}) %all-to-all-start.1) | async-done | bytes 442400 | tf_op jit(solution)/shard_map/all_to_all | solution.py:264
  95.6 2.9 %shard_map.116 = bf16[512,512]{1,0:T(8,128)(2,1)} custom-call(s32[2,384]{1,0:T(2,128)S(1)} %pad_add_fusion.owner, s32[512,1]{1,0:T(8,128)S(1)} %broadcast_in_dim_reshape.5.request, bf16[512,576]{1,0:T(8,128)(2,1)S(1)} %bitcast.47, bf16[384,576]{1,0:T(8,128)(2,1)S(1)} %bitcast.46, bf16[384,576]{1,0:T(8,128)(2,1)S(1)} %bitcast.48), custom_call_target="tpu_custom_call" | custom-call | flops 905969664 | bytes 3483648 | tf_op jit(solution)/shard_map/pallas_call | solution.py:23
  100.6 7.2 %collective-permute-done.16 = bf16[128,1792]{1,0:T(8,128)(2,1)S(1)} collective-permute-done((bf16[128,1792]{1,0:T(8,128)(2,1)}, bf16[128,1792]{1,0:T(8,128)(2,1)S(1)}, u32[]{:S(2)}, u32[]{:S(2)}) %collective-permute-start.16) | collective-permute-done | bytes 458784 | tf_op jit(solution)/shard_map/ppermute | solution.py:47
  108.6 3.8 %collective-permute-done.13 = bf16[64,1792]{1,0:T(8,128)(2,1)S(1)} collective-permute-done((bf16[64,1792]{1,0:T(8,128)(2,1)S(1)}, bf16[64,1792]{1,0:T(8,128)(2,1)S(1)}, u32[]{:S(2)}, u32[]{:S(2)}) %collective-permute-start.13) | collective-permute-done | bytes 229408 | tf_op jit(solution)/shard_map/ppermute | solution.py:47
  112.4 2.5 %collective-permute-done.18 = bf16[64,1792]{1,0:T(8,128)(2,1)S(1)} collective-permute-done((bf16[64,1792]{1,0:T(8,128)(2,1)S(1)}, bf16[64,1792]{1,0:T(8,128)(2,1)S(1)}, u32[]{:S(2)}, u32[]{:S(2)}) %collective-permute-start.18) | collective-permute-done | bytes 229408 | tf_op jit(solution)/shard_map/ppermute | solution.py:47
  116.2 4.9 %collective-permute-done.19 = bf16[32,3584]{1,0:T(8,128)(2,1)S(1)} collective-permute-done((bf16[32,3584]{1,0:T(8,128)(2,1)S(1)}, bf16[32,3584]{1,0:T(8,128)(2,1)S(1)}, u32[]{:S(2)}, u32[]{:S(2)}) %collective-permute-start.19) | collective-permute-done | bytes 229408 | tf_op jit(solution)/shard_map/ppermute | solution.py:47
  121.7 5.2 %collective-permute-done.20 = bf16[16,3584]{1,0:T(8,128)(2,1)S(1)} collective-permute-done((bf16[16,3584]{1,0:T(8,128)(2,1)S(1)}, bf16[16,3584]{1,0:T(8,128)(2,1)S(1)}, u32[]{:S(2)}, u32[]{:S(2)}) %collective-permute-start.20) | collective-permute-done | bytes 114720 | tf_op jit(solution)/shard_map/ppermute | solution.py:47
  (111 shorter events, 24.7 us)
Async XLA Ops:
  0.6 10.4 %collective-permute-start = (bf16[1,16,3584]{2,1,0:T(8,128)(2,1)}, bf16[1,16,3584]{2,1,0:T(8,128)(2,1)S(1)}, u32[]{:S(2)}, u32[]{:S(2)}) collective-permute-start(bf16[1,16,3584]{2,1,0:T(8,128)(2,1)} %bitcast.50), channel_id=1, source_target_pairs={{0,16},{2,18},{4,20},{6,22},{8,24},{10,26},{12,28},{14,30},{16,0},... | collective-permute-start | bytes 344072 | tf_op jit(solution)/shard_map/ppermute | solution.py:47
  6.5 43.1 %copy-start.7 = (bf16[16,3584]{1,0:T(8,128)(2,1)S(1)}, bf16[16,3584]{1,0:T(8,128)(2,1)}, u32[]{:S(2)}) copy-start(bf16[16,3584]{1,0:T(8,128)(2,1)} %param.10) | copy-start | bytes 344068
  6.5 4.5 %collective-permute-start.1 = (bf16[1,16,128]{2,1,0:T(8,128)(2,1)S(1)}, bf16[1,16,128]{2,1,0:T(8,128)(2,1)S(1)}, u32[]{:S(2)}, u32[]{:S(2)}) collective-permute-start(bf16[1,16,128]{2,1,0:T(8,128)(2,1)S(1)} %fusion.21), channel_id=1, source_target_pairs={{0,16},{2,18},{4,20},{6,22},{8,24},{10,26},{12,28},{14,30},{16,0},... | collective-permute-start | bytes 12296 | tf_op jit(solution)/shard_map/ppermute | solution.py:47
  12.0 6.7 %collective-permute-start.2 = (bf16[2,16,3712]{2,1,0:T(8,128)(2,1)S(1)}, bf16[2,16,3712]{2,1,0:T(8,128)(2,1)S(1)}, u32[]{:S(2)}, u32[]{:S(2)}) collective-permute-start(bf16[2,16,3712]{2,1,0:T(8,128)(2,1)S(1)} %maximum_maximum_fusion), channel_id=1, source_target_pairs={{0,8},{2,10},{4,12},{6,14},{8,0},{10,2},{12,4},{14,6},{16,24},{18,... | collective-permute-start | bytes 712712 | tf_op jit(solution)/shard_map/ppermute | solution.py:47
  20.3 6.3 %collective-permute-start.5 = (bf16[4,16,1920]{2,1,0:T(8,128)(2,1)S(1)}, bf16[4,16,1920]{2,1,0:T(8,128)(2,1)S(1)}, u32[]{:S(2)}, u32[]{:S(2)}) collective-permute-start(bf16[4,16,1920]{2,1,0:T(8,128)(2,1)S(1)} %slice.118), channel_id=1, source_target_pairs={{0,2},{2,0},{4,6},{6,4},{8,10},{10,8},{12,14},{14,12},{16,18},{18,... | collective-permute-start | bytes 737288 | tf_op jit(solution)/shard_map/ppermute | solution.py:47
  21.7 7.0 %collective-permute-start.3 = (bf16[4,16,1792]{2,1,0:T(8,128)(2,1)S(1)}, bf16[4,16,1792]{2,1,0:T(8,128)(2,1)S(1)}, u32[]{:S(2)}, u32[]{:S(2)}) collective-permute-start(bf16[4,16,1792]{2,1,0:T(8,128)(2,1)S(1)} %slice.117), channel_id=1, source_target_pairs={{0,4},{2,6},{4,0},{6,2},{8,12},{10,14},{12,8},{14,10},{16,20},{18,... | collective-permute-start | bytes 688136 | tf_op jit(solution)/shard_map/ppermute | solution.py:47
  27.3 11.0 %collective-permute-start.6 = (bf16[8,16,1920]{2,1,0:T(8,128)(2,1)S(1)}, bf16[8,16,1920]{2,1,0:T(8,128)(2,1)S(1)}, u32[]{:S(2)}, u32[]{:S(2)}) collective-permute-start(bf16[8,16,1920]{2,1,0:T(8,128)(2,1)S(1)} %pad_maximum_fusion), channel_id=1, source_target_pairs={{0,4},{2,6},{4,0},{6,2},{8,12},{10,14},{12,8},{14,10},{16,20},{18,... | collective-permute-start | bytes 1474568 | tf_op jit(solution)/shard_map/ppermute | solution.py:47
  28.8 9.0 %collective-permute-start.4 = (bf16[8,16,1792]{2,1,0:T(8,128)(2,1)S(1)}, bf16[8,16,1792]{2,1,0:T(8,128)(2,1)}, u32[]{:S(2)}, u32[]{:S(2)}) collective-permute-start(bf16[8,16,1792]{2,1,0:T(8,128)(2,1)S(1)} %pad_maximum_fusion.2), channel_id=1, source_target_pairs={{0,2},{2,0},{4,6},{6,4},{8,10},{10,8},{12,14},{14,12},{16,18},{18,... | collective-permute-start | bytes 1376264 | tf_op jit(solution)/shard_map/ppermute | solution.py:47
  37.8 12.7 %collective-permute-start.9 = (bf16[8,16,1920]{2,1,0:T(8,128)(2,1)S(1)}, bf16[8,16,1920]{2,1,0:T(8,128)(2,1)S(1)}, u32[]{:S(2)}, u32[]{:S(2)}) collective-permute-start(bf16[8,16,1920]{2,1,0:T(8,128)(2,1)S(1)} %pad_maximum_fusion), channel_id=1, source_target_pairs={{0,1},{1,0},{2,3},{3,2},{4,5},{5,4},{6,7},{7,6},{8,9},{9,8},{10,11... | collective-permute-start | bytes 1474568 | tf_op jit(solution)/shard_map/ppermute | solution.py:52
  38.3 12.2 %collective-permute-start.10 = (bf16[8,16,1920]{2,1,0:T(8,128)(2,1)S(1)}, bf16[8,16,1920]{2,1,0:T(8,128)(2,1)}, u32[]{:S(2)}, u32[]{:S(2)}) collective-permute-start(bf16[8,16,1920]{2,1,0:T(8,128)(2,1)S(1)} %collective-permute-done.6), channel_id=1, source_target_pairs={{0,1},{1,0},{2,3},{3,2},{4,5},{5,4},{6,7},{7,6},{8,9},{9,8},{10,11... | collective-permute-start | bytes 1474568 | tf_op jit(solution)/shard_map/ppermute | solution.py:52
  39.3 11.2 %collective-permute-start.7 = (bf16[8,16,1792]{2,1,0:T(8,128)(2,1)S(1)}, bf16[8,16,1792]{2,1,0:T(8,128)(2,1)}, u32[]{:S(2)}, u32[]{:S(2)}) collective-permute-start(bf16[8,16,1792]{2,1,0:T(8,128)(2,1)S(1)} %pad_maximum_fusion.2), channel_id=1, source_target_pairs={{0,1},{1,0},{2,3},{3,2},{4,5},{5,4},{6,7},{7,6},{8,9},{9,8},{10,11... | collective-permute-start | bytes 1376264 | tf_op jit(solution)/shard_map/ppermute | solution.py:52
  39.8 10.8 %collective-permute-start.8 = (bf16[8,16,1792]{2,1,0:T(8,128)(2,1)}, bf16[8,16,1792]{2,1,0:T(8,128)(2,1)}, u32[]{:S(2)}, u32[]{:S(2)}) collective-permute-start(bf16[8,16,1792]{2,1,0:T(8,128)(2,1)} %collective-permute-done.4), channel_id=1, source_target_pairs={{0,1},{1,0},{2,3},{3,2},{4,5},{5,4},{6,7},{7,6},{8,9},{9,8},{10,11... | collective-permute-start | bytes 1376264 | tf_op jit(solution)/shard_map/ppermute | solution.py:52
  40.4 25.6 %all-to-all-start = ((bf16[16,24,576]{2,1,0:T(8,128)(2,1)}), bf16[16,24,576]{2,1,0:T(8,128)(2,1)S(1)}, u32[]{:S(2)}, u32[]{:S(2)}) async-start(bf16[16,24,576]{2,1,0:T(8,128)(2,1)} %bitcast.49), calls=%async_computation | async-start | bytes 983040 | tf_op jit(solution)/shard_map/all_to_all | solution.py:239
  65.3 13.5 %collective-permute-start.11 = (bf16[256,1792]{1,0:T(8,128)(2,1)}, bf16[256,1792]{1,0:T(8,128)(2,1)}, u32[]{:S(2)}, u32[]{:S(2)}) collective-permute-start(bf16[256,1792]{1,0:T(8,128)(2,1)} %get-tuple-element.17), channel_id=1, source_target_pairs={{0,1},{1,0},{2,3},{3,2},{4,5},{5,4},{6,7},{7,6},{8,9},{9,8},{10,11... | collective-permute-start | bytes 2752520 | tf_op jit(solution)/shard_map/ppermute | solution.py:52
  65.9 3.4 %collective-permute-start.15 = (bf16[16,24,576]{2,1,0:T(8,128)(2,1)S(1)}, bf16[16,24,576]{2,1,0:T(8,128)(2,1)}, u32[]{:S(2)}, u32[]{:S(2)}) collective-permute-start(bf16[16,24,576]{2,1,0:T(8,128)(2,1)S(1)} %all-to-all-done), channel_id=1, source_target_pairs={{0,1},{1,0},{2,3},{3,2},{4,5},{5,4},{6,7},{7,6},{8,9},{9,8},{10,11... | collective-permute-start | bytes 1327112 | tf_op jit(solution)/shard_map/ppermute | solution.py:52
  66.5 15.7 %collective-permute-start.14 = (bf16[256,1792]{1,0:T(8,128)(2,1)}, bf16[256,1792]{1,0:T(8,128)(2,1)}, u32[]{:S(2)}, u32[]{:S(2)}) collective-permute-start(bf16[256,1792]{1,0:T(8,128)(2,1)} %copy-done.1), channel_id=1, source_target_pairs={{0,1},{1,0},{2,3},{3,2},{4,5},{5,4},{6,7},{7,6},{8,9},{9,8},{10,11... | collective-permute-start | bytes 2752520 | tf_op jit(solution)/shard_map/ppermute | solution.py:52
  71.9 21.8 %all-to-all-start.1 = ((bf16[16,24,576]{2,1,0:T(8,128)(2,1)}), bf16[16,24,576]{2,1,0:T(8,128)(2,1)S(1)}, u32[]{:S(2)}, u32[]{:S(2)}) async-start(bf16[16,24,576]{2,1,0:T(8,128)(2,1)} %bitcast.18), calls=%async_computation.1 | async-start | bytes 983040 | tf_op jit(solution)/shard_map/all_to_all | solution.py:264
  80.3 18.2 %collective-permute-start.12 = (bf16[128,1792]{1,0:T(8,128)(2,1)S(1)}, bf16[128,1792]{1,0:T(8,128)(2,1)}, u32[]{:S(2)}, u32[]{:S(2)}) collective-permute-start(bf16[128,1792]{1,0:T(8,128)(2,1)S(1)} %slice.125), channel_id=1, source_target_pairs={{0,2},{2,0},{4,6},{6,4},{8,10},{10,8},{12,14},{14,12},{16,18},{18,... | collective-permute-start | bytes 1376264 | tf_op jit(solution)/shard_map/ppermute | solution.py:47
  93.7 1.9 %collective-permute-start.17 = (bf16[16,24,576]{2,1,0:T(8,128)(2,1)S(1)}, bf16[16,24,576]{2,1,0:T(8,128)(2,1)S(1)}, u32[]{:S(2)}, u32[]{:S(2)}) collective-permute-start(bf16[16,24,576]{2,1,0:T(8,128)(2,1)S(1)} %all-to-all-done.1), channel_id=1, source_target_pairs={{0,1},{1,0},{2,3},{3,2},{4,5},{5,4},{6,7},{7,6},{8,9},{9,8},{10,11... | collective-permute-start | bytes 1327112 | tf_op jit(solution)/shard_map/ppermute | solution.py:52
  94.2 13.6 %collective-permute-start.16 = (bf16[128,1792]{1,0:T(8,128)(2,1)}, bf16[128,1792]{1,0:T(8,128)(2,1)S(1)}, u32[]{:S(2)}, u32[]{:S(2)}) collective-permute-start(bf16[128,1792]{1,0:T(8,128)(2,1)} %slice.129), channel_id=1, source_target_pairs={{0,4},{2,6},{4,0},{6,2},{8,12},{10,14},{12,8},{14,10},{16,20},{18,... | collective-permute-start | bytes 1376264 | tf_op jit(solution)/shard_map/ppermute | solution.py:47
  99.6 12.7 %collective-permute-start.13 = (bf16[64,1792]{1,0:T(8,128)(2,1)S(1)}, bf16[64,1792]{1,0:T(8,128)(2,1)S(1)}, u32[]{:S(2)}, u32[]{:S(2)}) collective-permute-start(bf16[64,1792]{1,0:T(8,128)(2,1)S(1)} %slice.127), channel_id=1, source_target_pairs={{0,4},{2,6},{4,0},{6,2},{8,12},{10,14},{12,8},{14,10},{16,20},{18,... | collective-permute-start | bytes 688136 | tf_op jit(solution)/shard_map/ppermute | solution.py:47
  107.9 6.9 %collective-permute-start.18 = (bf16[64,1792]{1,0:T(8,128)(2,1)S(1)}, bf16[64,1792]{1,0:T(8,128)(2,1)S(1)}, u32[]{:S(2)}, u32[]{:S(2)}) collective-permute-start(bf16[64,1792]{1,0:T(8,128)(2,1)S(1)} %slice.131), channel_id=1, source_target_pairs={{0,2},{2,0},{4,6},{6,4},{8,10},{10,8},{12,14},{14,12},{16,18},{18,... | collective-permute-start | bytes 688136 | tf_op jit(solution)/shard_map/ppermute | solution.py:47
  114.9 6.1 %collective-permute-start.19 = (bf16[32,3584]{1,0:T(8,128)(2,1)S(1)}, bf16[32,3584]{1,0:T(8,128)(2,1)S(1)}, u32[]{:S(2)}, u32[]{:S(2)}) collective-permute-start(bf16[32,3584]{1,0:T(8,128)(2,1)S(1)} %pad_maximum_fusion.3), channel_id=1, source_target_pairs={{0,8},{2,10},{4,12},{6,14},{8,0},{10,2},{12,4},{14,6},{16,24},{18,... | collective-permute-start | bytes 688136 | tf_op jit(solution)/shard_map/ppermute | solution.py:47
  121.1 5.8 %collective-permute-start.20 = (bf16[16,3584]{1,0:T(8,128)(2,1)S(1)}, bf16[16,3584]{1,0:T(8,128)(2,1)S(1)}, u32[]{:S(2)}, u32[]{:S(2)}) collective-permute-start(bf16[16,3584]{1,0:T(8,128)(2,1)S(1)} %slice.135), channel_id=1, source_target_pairs={{0,16},{2,18},{4,20},{6,22},{8,24},{10,26},{12,28},{14,30},{16,0},... | collective-permute-start | bytes 344072 | tf_op jit(solution)/shard_map/ppermute | solution.py:47
  (16 other events, 162.3 us)

commit v6 on v5

--- a/solution.py
+++ b/solution.py
@@ -66,14 +66,13 @@
     ]
     value = jnp.concatenate(values, axis=2)
     for bit in shared[1:]:
-        shared_sent = value
         value = jnp.concatenate([value, exchange(value, bit)], axis=0)
     halves = []
     for order, start, end in zip(orders, (0,) + ends, ends):
         part = value[:, :, start:end]
         part = jnp.concatenate([part, exchange(part, order[-2])], axis=0)
         halves.append((part, exchange(part, order[-1])))
-    return halves, shared_sent
+    return halves
 
 
 def places_of(order):
@@ -355,11 +354,9 @@
     pad = -gate_parts.shape[1] % 128
     gates = jnp.pad(gate_parts, ((0, 0), (0, pad)))
     ends = tuple(cut * part for part in range(1, parts)) + (tokens.shape[1] + gates.shape[1],)
-    halves, shared_sent = gather_rows(tokens, gates, orders, ends)
+    halves = gather_rows(tokens, gates, orders, ends)
     last_sent = halves[-1][0]
-    pieces = tie(cache_out(latent_cache), shared_sent)
-    ordered = cache_turn(pieces, block_source, slot_total, last_sent)
-    keys = cache_in(ordered, block_size, latent)
+    pieces = tie(cache_out(latent_cache), last_sent)
     places = [places_of(order) for order in orders]
     to_first = [[places[0].index(place) for place in own] for own in places]
     from_first = [[own.index(place) for place in places[0]] for own in places]
@@ -373,6 +370,7 @@
     all_rows = join_rows(
         [halves] + arrived, to_first, tuple(cut * part for part in range(1, parts + 1)), row_count
     )
+    ordered = cache_turn(pieces, block_source, slot_total, all_rows)
     gate_halves = [half[..., cut : cut + 3 * ep_size] for half in halves[-1]]
     all_gate = jnp.concatenate(gate_halves, axis=0)
     all_gate = jnp.stack([all_gate[block] for block in from_first[-1]]).astype(jnp.float32)
@@ -385,6 +383,7 @@
         jax.nn.silu(gate_and_up[:, 0]) * gate_and_up[:, 1] * my_gate[:, None]
     ).astype(jnp.bfloat16)
 
+    hidden = tie(hidden, ordered)
     by_step = down(hidden, expert_down[0], from_first, row_count)
     sums = list(by_step[-1])
     for part in range(parts):
@@ -394,15 +393,19 @@
     held = {}
 
     def beside_first_sum(sent):
-        sent, near = lax.optimization_barrier((sent, keys))
+        held["keys"] = cache_in(tie(ordered, sent), block_size, latent)
+        return sent
+
+    def beside_third_sum(sent):
+        sent, near = lax.optimization_barrier((sent, held["keys"]))
         held["attended"] = attend(queries, [near] + swap_tp(near), block_request, block_used)
         return sent
 
-    def beside_second_sum(sent):
+    def beside_last_sum(sent):
         sent, held["attended"] = lax.optimization_barrier((sent, held["attended"]))
         return sent
 
-    hooks = {0: beside_first_sum, 1: beside_second_sum}
+    hooks = {0: beside_first_sum, 2: beside_third_sum, len(bits) - 1: beside_last_sum}
     return (scatter_sums(sums, orders, hooks), held["attended"])
 
 

time: 128 us -> 120 us (0.938)
  waiting for transfers between devices: 55.2 us -> 41.5 us
  local copies, waits for them, and re-layouts: 7.71 us -> 10.7 us
  starting transfers between devices: 35.4 us -> 37.9 us
    ppermute x13, waiting for transfers between devices: 44.2 us -> 32.9 us  [exchange(): lax.ppermute(value, 'ep', [(index, index ^ bit) for index in range(ep_siz...]
    all_to_all x1, waiting for transfers between devices: 8.31 us -> 0.01 us  [cache_in(): lax.all_to_all(ordered, 'ep', split_axis=0, concat_axis=0, tiled=True)]
    all_to_all x1, waiting for transfers between devices: 0.01 us -> 4.38 us  [cache_turn(): lax.all_to_all(pieces, 'ep', split_axis=0, concat_axis=0, tiled=True)]
    ppermute x13, starting transfers between devices: 18.1 us -> 22.2 us  [exchange(): lax.ppermute(value, 'ep', [(index, index ^ bit) for index in range(ep_siz...]
    unnamed x35 -> x25, local copies, waits for them, and re-layouts: 5.71 us -> 8.68 us
    all_to_all x1, starting transfers between devices: 9.21 us -> 6.77 us  [cache_turn(): lax.all_to_all(pieces, 'ep', split_axis=0, concat_axis=0, tiled=True)]
    ppermute x8, waiting for transfers between devices: 2.78 us -> 4.21 us  [pass_tp(): lax.ppermute(value, 'tp', [(index, (index + step) % tp_size) for index in...]
  transfers between devices with their start and end apart: 23 -> 23, of which waited for: 13 -> 13; matrix products, arithmetic and copies ran while one was open for 15% -> 17% of each run, Pallas kernels for 9% -> 2%
where the time goes in v6:
time: 120 us; the launch traced here: 119 us
  waiting for transfers between devices  41.5 us (35%)
  starting transfers between devices  37.9 us (32%)
  local copies, waits for them, and re-layouts  10.7 us (9%)
  Pallas kernels  10.4 us (9%)
  other arithmetic  9.54 us (8%)
  matrix products  8.37 us (7%)
    ppermute x13, waiting for transfers between devices, exchange(): lax.ppermute(value, 'ep', [(index, index ^ bit) for index in range(ep_siz...  32.9 us
    ppermute x13, starting transfers between devices, exchange(): lax.ppermute(value, 'ep', [(index, index ^ bit) for index in range(ep_siz...  22.2 us
    pallas_call x4, Pallas kernels, kernel_call(): pl.pallas_call(kernel, out_shape=out_shape, in_specs=in_specs or [WHOLE]...  10.4 us
    unnamed x25, local copies, waits for them, and re-layouts  8.68 us
    dot_general x1, matrix products, body(): jnp.einsum('sd,dgf->sgf', all_rows, expert_gate_up[0], preferred_element_...  8.37 us
    all_to_all x1, starting transfers between devices, cache_in(): lax.all_to_all(ordered, 'ep', split_axis=0, concat_axis=0, tiled=True)  7.09 us
    all_to_all x1, starting transfers between devices, cache_turn(): lax.all_to_all(pieces, 'ep', split_axis=0, concat_axis=0, tiled=True)  6.77 us
    convert_element_type x8, other arithmetic, add_up(): return total.astype(jnp.bfloat16)  6.01 us
  transfers between devices with their start and end apart: 23, of which 13 were waited for; matrix products, arithmetic and copies ran while one was open for 17% of the time, Pallas kernels for 2%

profile of v6, /device:TPU:0, one launch (start us, length us, event | category | flops | bytes accessed | tf_op | source)
XLA Modules:
  0.0 119.4 jit_solution(6492116643226711894)
XLA Ops:
  0.7 4.1 %collective-permute-start = (bf16[1,16,3584]{2,1,0:T(8,128)(2,1)}, bf16[1,16,3584]{2,1,0:T(8,128)(2,1)S(1)}, u32[]{:S(2)}, u32[]{:S(2)}) collective-permute-start(bf16[1,16,3584]{2,1,0:T(8,128)(2,1)} %bitcast.47), channel_id=1, source_target_pairs={{0,16},{2,18},{4,20},{6,22},{8,24},{10,26},{12,28},{14,30},{16,0},... | collective-permute-start | bytes 344072 | tf_op jit(solution)/shard_map/ppermute | solution.py:47
  6.6 4.4 %collective-permute-done.1 = bf16[1,16,128]{2,1,0:T(8,128)(2,1)S(1)} collective-permute-done((bf16[1,16,128]{2,1,0:T(8,128)(2,1)S(1)}, bf16[1,16,128]{2,1,0:T(8,128)(2,1)S(1)}, u32[]{:S(2)}, u32[]{:S(2)}) %collective-permute-start.1) | collective-permute-done | bytes 4128 | tf_op jit(solution)/shard_map/ppermute | solution.py:47
  11.9 1.6 %collective-permute-start.2 = (bf16[2,16,3712]{2,1,0:T(8,128)(2,1)S(1)}, bf16[2,16,3712]{2,1,0:T(8,128)(2,1)S(1)}, u32[]{:S(2)}, u32[]{:S(2)}) collective-permute-start(bf16[2,16,3712]{2,1,0:T(8,128)(2,1)S(1)} %maximum_maximum_fusion), channel_id=1, source_target_pairs={{0,8},{2,10},{4,12},{6,14},{8,0},{10,2},{12,4},{14,6},{16,24},{18,... | collective-permute-start | bytes 712712 | tf_op jit(solution)/shard_map/ppermute | solution.py:47
  13.6 5.1 %collective-permute-done.2 = bf16[2,16,3712]{2,1,0:T(8,128)(2,1)S(1)} collective-permute-done((bf16[2,16,3712]{2,1,0:T(8,128)(2,1)S(1)}, bf16[2,16,3712]{2,1,0:T(8,128)(2,1)S(1)}, u32[]{:S(2)}, u32[]{:S(2)}) %collective-permute-start.2) | collective-permute-done | bytes 237600 | tf_op jit(solution)/shard_map/ppermute | solution.py:47
  21.7 1.6 %collective-permute-start.3 = (bf16[4,16,1792]{2,1,0:T(8,128)(2,1)S(1)}, bf16[4,16,1792]{2,1,0:T(8,128)(2,1)S(1)}, u32[]{:S(2)}, u32[]{:S(2)}) collective-permute-start(bf16[4,16,1792]{2,1,0:T(8,128)(2,1)S(1)} %slice.117), channel_id=1, source_target_pairs={{0,4},{2,6},{4,0},{6,2},{8,12},{10,14},{12,8},{14,10},{16,20},{18,... | collective-permute-start | bytes 688136 | tf_op jit(solution)/shard_map/ppermute | solution.py:47
  23.3 3.3 %collective-permute-done.5 = bf16[4,16,1920]{2,1,0:T(8,128)(2,1)S(1)} collective-permute-done((bf16[4,16,1920]{2,1,0:T(8,128)(2,1)S(1)}, bf16[4,16,1920]{2,1,0:T(8,128)(2,1)S(1)}, u32[]{:S(2)}, u32[]{:S(2)}) %collective-permute-start.5) | collective-permute-done | bytes 245792 | tf_op jit(solution)/shard_map/ppermute | solution.py:47
  31.9 6.8 %all-to-all-start = ((bf16[16,24,576]{2,1,0:T(8,128)(2,1)}), bf16[16,24,576]{2,1,0:T(8,128)(2,1)S(1)}, u32[]{:S(2)}, u32[]{:S(2)}) async-start(bf16[16,24,576]{2,1,0:T(8,128)(2,1)} %bitcast.37), calls=%async_computation | async-start | bytes 983040 | tf_op jit(solution)/shard_map/all_to_all | solution.py:238
  41.0 1.8 %collective-permute-done.7 = bf16[8,16,1792]{2,1,0:T(8,128)(2,1)} collective-permute-done((bf16[8,16,1792]{2,1,0:T(8,128)(2,1)S(1)}, bf16[8,16,1792]{2,1,0:T(8,128)(2,1)}, u32[]{:S(2)}, u32[]{:S(2)}) %collective-permute-start.7) | collective-permute-done | bytes 458784 | tf_op jit(solution)/shard_map/ppermute | solution.py:52
  43.0 1.8 %shard_map.113 = bf16[256,7168]{1,0:T(8,128)(2,1)S(1)} custom-call(bf16[128,1792]{1,0:T(8,128)(2,1)S(1)} %bitcast.41, bf16[128,1792]{1,0:T(8,128)(2,1)} %bitcast.3.refs_1_, bf16[128,1920]{1,0:T(8,128)(2,1)S(1)} %bitcast.39, bf16[128,1920]{1,0:T(8,128)(2,1)S(1)} %bitcast.42, bf16[128,1792]{1,0:T(8,128)(2,1)} %bitcast.6.refs_4_, ...), custom_call_target="tpu_custom_call" | custom-call | bytes 11272192 | tf_op jit(solution)/shard_map/pallas_call | solution.py:23
  44.8 1.8 %copy-done.2 = bf16[256,7168]{1,0:T(8,128)(2,1)} copy-done((bf16[256,7168]{1,0:T(8,128)(2,1)}, bf16[256,7168]{1,0:T(8,128)(2,1)S(1)}, u32[]{:S(2)}) %copy-start.2) | copy-done | bytes 3670040
  46.6 4.4 %all-to-all-done = bf16[16,24,576]{2,1,0:T(8,128)(2,1)S(1)} async-done(((bf16[16,24,576]{2,1,0:T(8,128)(2,1)}), bf16[16,24,576]{2,1,0:T(8,128)(2,1)S(1)}, u32[]{:S(2)}, u32[]{:S(2)}) %all-to-all-start) | async-done | bytes 442400 | tf_op jit(solution)/shard_map/all_to_all | solution.py:238
  51.0 8.4 %fusion = f32[256,2,512]{2,0,1:T(8,128)S(1)} fusion(bf16[7168,2,512]{2,1,0:T(2,128)(2,1)} %bitcast.51, bf16[256,7168]{1,0:T(8,128)(2,1)} %copy-done.2), kind=kOutput, calls=%fused_computation | convolution fusion | flops 3758096384 | bytes 19398656 | tf_op jit(solution)/shard_map/sd,dgf->sgf/dot_general | solution.py:379
  61.2 3.1 %copy-done.1 = bf16[1,7168,512]{2,1,0:T(8,128)(2,1)S(1)} copy-done((bf16[1,7168,512]{2,1,0:T(8,128)(2,1)S(1)}, bf16[1,7168,512]{2,1,0:T(8,128)(2,1)}, u32[]{:S(2)}) %copy-start.1) | copy-done | bytes 7340056
  64.2 4.0 %shard_map.115 = (bf16[256,1792]{1,0:T(8,128)(2,1)}, bf16[256,1792]{1,0:T(8,128)(2,1)}, bf16[256,1792]{1,0:T(8,128)(2,1)S(1)}, bf16[256,1792]{1,0:T(8,128)(2,1)S(1)}) custom-call(bf16[256,512]{1,0:T(8,128)(2,1)S(1)} %fusion.5.hidden, bf16[7168,512]{1,0:T(8,128)(2,1)S(1)} %bitcast.38), custom_call_target="tpu_custom_call" | custom-call | flops 1879048192 | bytes 11534336 | tf_op jit(solution)/shard_map/pallas_call | solution.py:23
  69.1 2.2 %collective-permute-done.12 = bf16[256,1792]{1,0:T(8,128)(2,1)} collective-permute-done((bf16[256,1792]{1,0:T(8,128)(2,1)}, bf16[256,1792]{1,0:T(8,128)(2,1)}, u32[]{:S(2)}, u32[]{:S(2)}) %collective-permute-start.12) | collective-permute-done | bytes 917536 | tf_op jit(solution)/shard_map/ppermute | solution.py:52
  76.5 7.1 %all-to-all-start.1 = ((bf16[16,24,576]{2,1,0:T(8,128)(2,1)}), bf16[16,24,576]{2,1,0:T(8,128)(2,1)S(1)}, u32[]{:S(2)}, u32[]{:S(2)}) async-start(bf16[16,24,576]{2,1,0:T(8,128)(2,1)} %bitcast.17), calls=%async_computation.1 | async-start | bytes 983040 | tf_op jit(solution)/shard_map/all_to_all | solution.py:263
  83.6 2.1 %collective-permute-done.13 = bf16[128,1792]{1,0:T(8,128)(2,1)} collective-permute-done((bf16[128,1792]{1,0:T(8,128)(2,1)S(1)}, bf16[128,1792]{1,0:T(8,128)(2,1)}, u32[]{:S(2)}, u32[]{:S(2)}) %collective-permute-start.13) | collective-permute-done | bytes 458784 | tf_op jit(solution)/shard_map/ppermute | solution.py:47
  88.0 4.3 %collective-permute-done.16 = bf16[128,1792]{1,0:T(8,128)(2,1)} collective-permute-done((bf16[128,1792]{1,0:T(8,128)(2,1)}, bf16[128,1792]{1,0:T(8,128)(2,1)}, u32[]{:S(2)}, u32[]{:S(2)}) %collective-permute-start.16) | collective-permute-done | bytes 458784 | tf_op jit(solution)/shard_map/ppermute | solution.py:47
  93.4 1.6 %collective-permute-start.17 = (bf16[64,1792]{1,0:T(8,128)(2,1)S(1)}, bf16[64,1792]{1,0:T(8,128)(2,1)S(1)}, u32[]{:S(2)}, u32[]{:S(2)}) collective-permute-start(bf16[64,1792]{1,0:T(8,128)(2,1)S(1)} %slice.131), channel_id=1, source_target_pairs={{0,2},{2,0},{4,6},{6,4},{8,10},{10,8},{12,14},{14,12},{16,18},{18,... | collective-permute-start | bytes 688136 | tf_op jit(solution)/shard_map/ppermute | solution.py:47
  95.1 3.5 %collective-permute-done.14 = bf16[64,1792]{1,0:T(8,128)(2,1)S(1)} collective-permute-done((bf16[64,1792]{1,0:T(8,128)(2,1)S(1)}, bf16[64,1792]{1,0:T(8,128)(2,1)S(1)}, u32[]{:S(2)}, u32[]{:S(2)}) %collective-permute-start.14) | collective-permute-done | bytes 229408 | tf_op jit(solution)/shard_map/ppermute | solution.py:47
  101.7 4.7 %collective-permute-done.18 = bf16[32,3584]{1,0:T(8,128)(2,1)S(1)} collective-permute-done((bf16[32,3584]{1,0:T(8,128)(2,1)S(1)}, bf16[32,3584]{1,0:T(8,128)(2,1)S(1)}, u32[]{:S(2)}, u32[]{:S(2)}) %collective-permute-start.18) | collective-permute-done | bytes 229408 | tf_op jit(solution)/shard_map/ppermute | solution.py:47
  106.4 3.0 %shard_map.116 = bf16[512,512]{1,0:T(8,128)(2,1)} custom-call(s32[2,384]{1,0:T(2,128)S(1)} %pad_add_fusion.owner, s32[512,1]{1,0:T(8,128)S(1)} %broadcast_in_dim_reshape.5.request, bf16[512,576]{1,0:T(8,128)(2,1)S(1)} %bitcast.45, bf16[384,576]{1,0:T(8,128)(2,1)S(1)} %bitcast.43, bf16[384,576]{1,0:T(8,128)(2,1)S(1)} %bitcast.46), custom_call_target="tpu_custom_call" | custom-call | flops 905969664 | bytes 3483648 | tf_op jit(solution)/shard_map/pallas_call | solution.py:23
  109.4 5.4 %collective-permute-start.20 = (bf16[16,3584]{1,0:T(8,128)(2,1)S(1)}, bf16[16,3584]{1,0:T(8,128)(2,1)S(1)}, u32[]{:S(2)}, u32[]{:S(2)}) collective-permute-start(bf16[16,3584]{1,0:T(8,128)(2,1)S(1)} %slice.135), channel_id=1, source_target_pairs={{0,16},{2,18},{4,20},{6,22},{8,24},{10,26},{12,28},{14,30},{16,0},... | collective-permute-start | bytes 344072 | tf_op jit(solution)/shard_map/ppermute | solution.py:47
  114.8 4.0 %collective-permute-done.20 = bf16[16,3584]{1,0:T(8,128)(2,1)S(1)} collective-permute-done((bf16[16,3584]{1,0:T(8,128)(2,1)S(1)}, bf16[16,3584]{1,0:T(8,128)(2,1)S(1)}, u32[]{:S(2)}, u32[]{:S(2)}) %collective-permute-start.20) | collective-permute-done | bytes 114720 | tf_op jit(solution)/shard_map/ppermute | solution.py:47
  (100 shorter events, 28.5 us)
Async XLA Ops:
  0.6 30.6 %copy-start.8 = (s32[768]{0:T(1024)S(1)}, s32[768]{0:T(1024)}, u32[]{:S(2)}) copy-start(s32[768]{0:T(1024)} %param.17) | copy-start | bytes 9220
  0.7 10.3 %collective-permute-start = (bf16[1,16,3584]{2,1,0:T(8,128)(2,1)}, bf16[1,16,3584]{2,1,0:T(8,128)(2,1)S(1)}, u32[]{:S(2)}, u32[]{:S(2)}) collective-permute-start(bf16[1,16,3584]{2,1,0:T(8,128)(2,1)} %bitcast.47), channel_id=1, source_target_pairs={{0,16},{2,18},{4,20},{6,22},{8,24},{10,26},{12,28},{14,30},{16,0},... | collective-permute-start | bytes 344072 | tf_op jit(solution)/shard_map/ppermute | solution.py:47
  6.5 4.5 %collective-permute-start.1 = (bf16[1,16,128]{2,1,0:T(8,128)(2,1)S(1)}, bf16[1,16,128]{2,1,0:T(8,128)(2,1)S(1)}, u32[]{:S(2)}, u32[]{:S(2)}) collective-permute-start(bf16[1,16,128]{2,1,0:T(8,128)(2,1)S(1)} %fusion.21), channel_id=1, source_target_pairs={{0,16},{2,18},{4,20},{6,22},{8,24},{10,26},{12,28},{14,30},{16,0},... | collective-permute-start | bytes 12296 | tf_op jit(solution)/shard_map/ppermute | solution.py:47
  11.9 6.7 %collective-permute-start.2 = (bf16[2,16,3712]{2,1,0:T(8,128)(2,1)S(1)}, bf16[2,16,3712]{2,1,0:T(8,128)(2,1)S(1)}, u32[]{:S(2)}, u32[]{:S(2)}) collective-permute-start(bf16[2,16,3712]{2,1,0:T(8,128)(2,1)S(1)} %maximum_maximum_fusion), channel_id=1, source_target_pairs={{0,8},{2,10},{4,12},{6,14},{8,0},{10,2},{12,4},{14,6},{16,24},{18,... | collective-permute-start | bytes 712712 | tf_op jit(solution)/shard_map/ppermute | solution.py:47
  20.3 6.3 %collective-permute-start.5 = (bf16[4,16,1920]{2,1,0:T(8,128)(2,1)S(1)}, bf16[4,16,1920]{2,1,0:T(8,128)(2,1)S(1)}, u32[]{:S(2)}, u32[]{:S(2)}) collective-permute-start(bf16[4,16,1920]{2,1,0:T(8,128)(2,1)S(1)} %slice.118), channel_id=1, source_target_pairs={{0,2},{2,0},{4,6},{6,4},{8,10},{10,8},{12,14},{14,12},{16,18},{18,... | collective-permute-start | bytes 737288 | tf_op jit(solution)/shard_map/ppermute | solution.py:47
  21.7 7.0 %collective-permute-start.3 = (bf16[4,16,1792]{2,1,0:T(8,128)(2,1)S(1)}, bf16[4,16,1792]{2,1,0:T(8,128)(2,1)S(1)}, u32[]{:S(2)}, u32[]{:S(2)}) collective-permute-start(bf16[4,16,1792]{2,1,0:T(8,128)(2,1)S(1)} %slice.117), channel_id=1, source_target_pairs={{0,4},{2,6},{4,0},{6,2},{8,12},{10,14},{12,8},{14,10},{16,20},{18,... | collective-permute-start | bytes 688136 | tf_op jit(solution)/shard_map/ppermute | solution.py:47
  27.3 11.5 %collective-permute-start.6 = (bf16[8,16,1920]{2,1,0:T(8,128)(2,1)S(1)}, bf16[8,16,1920]{2,1,0:T(8,128)(2,1)S(1)}, u32[]{:S(2)}, u32[]{:S(2)}) collective-permute-start(bf16[8,16,1920]{2,1,0:T(8,128)(2,1)S(1)} %pad_maximum_fusion), channel_id=1, source_target_pairs={{0,4},{2,6},{4,0},{6,2},{8,12},{10,14},{12,8},{14,10},{16,20},{18,... | collective-permute-start | bytes 1474568 | tf_op jit(solution)/shard_map/ppermute | solution.py:47
  28.8 9.9 %collective-permute-start.4 = (bf16[8,16,1792]{2,1,0:T(8,128)(2,1)S(1)}, bf16[8,16,1792]{2,1,0:T(8,128)(2,1)}, u32[]{:S(2)}, u32[]{:S(2)}) collective-permute-start(bf16[8,16,1792]{2,1,0:T(8,128)(2,1)S(1)} %pad_maximum_fusion.2), channel_id=1, source_target_pairs={{0,2},{2,0},{4,6},{6,4},{8,10},{10,8},{12,14},{14,12},{16,18},{18,... | collective-permute-start | bytes 1376264 | tf_op jit(solution)/shard_map/ppermute | solution.py:47
  31.9 19.1 %all-to-all-start = ((bf16[16,24,576]{2,1,0:T(8,128)(2,1)}), bf16[16,24,576]{2,1,0:T(8,128)(2,1)S(1)}, u32[]{:S(2)}, u32[]{:S(2)}) async-start(bf16[16,24,576]{2,1,0:T(8,128)(2,1)} %bitcast.37), calls=%async_computation | async-start | bytes 983040 | tf_op jit(solution)/shard_map/all_to_all | solution.py:238
  38.7 4.3 %collective-permute-start.9 = (bf16[8,16,1920]{2,1,0:T(8,128)(2,1)S(1)}, bf16[8,16,1920]{2,1,0:T(8,128)(2,1)}, u32[]{:S(2)}, u32[]{:S(2)}) collective-permute-start(bf16[8,16,1920]{2,1,0:T(8,128)(2,1)S(1)} %pad_maximum_fusion), channel_id=1, source_target_pairs={{0,1},{1,0},{2,3},{3,2},{4,5},{5,4},{6,7},{7,6},{8,9},{9,8},{10,11... | collective-permute-start | bytes 1474568 | tf_op jit(solution)/shard_map/ppermute | solution.py:52
  38.8 4.2 %collective-permute-start.10 = (bf16[8,16,1920]{2,1,0:T(8,128)(2,1)S(1)}, bf16[8,16,1920]{2,1,0:T(8,128)(2,1)}, u32[]{:S(2)}, u32[]{:S(2)}) collective-permute-start(bf16[8,16,1920]{2,1,0:T(8,128)(2,1)S(1)} %collective-permute-done.6), channel_id=1, source_target_pairs={{0,1},{1,0},{2,3},{3,2},{4,5},{5,4},{6,7},{7,6},{8,9},{9,8},{10,11... | collective-permute-start | bytes 1474568 | tf_op jit(solution)/shard_map/ppermute | solution.py:52
  39.4 3.3 %collective-permute-start.7 = (bf16[8,16,1792]{2,1,0:T(8,128)(2,1)S(1)}, bf16[8,16,1792]{2,1,0:T(8,128)(2,1)}, u32[]{:S(2)}, u32[]{:S(2)}) collective-permute-start(bf16[8,16,1792]{2,1,0:T(8,128)(2,1)S(1)} %pad_maximum_fusion.2), channel_id=1, source_target_pairs={{0,1},{1,0},{2,3},{3,2},{4,5},{5,4},{6,7},{7,6},{8,9},{9,8},{10,11... | collective-permute-start | bytes 1376264 | tf_op jit(solution)/shard_map/ppermute | solution.py:52
  39.6 3.4 %collective-permute-start.8 = (bf16[8,16,1792]{2,1,0:T(8,128)(2,1)}, bf16[8,16,1792]{2,1,0:T(8,128)(2,1)}, u32[]{:S(2)}, u32[]{:S(2)}) collective-permute-start(bf16[8,16,1792]{2,1,0:T(8,128)(2,1)} %collective-permute-done.4), channel_id=1, source_target_pairs={{0,1},{1,0},{2,3},{3,2},{4,5},{5,4},{6,7},{7,6},{8,9},{9,8},{10,11... | collective-permute-start | bytes 1376264 | tf_op jit(solution)/shard_map/ppermute | solution.py:52
  51.0 8.6 %collective-permute-start.11 = (bf16[16,24,576]{2,1,0:T(8,128)(2,1)S(1)}, bf16[16,24,576]{2,1,0:T(8,128)(2,1)S(1)}, u32[]{:S(2)}, u32[]{:S(2)}) collective-permute-start(bf16[16,24,576]{2,1,0:T(8,128)(2,1)S(1)} %all-to-all-done), channel_id=1, source_target_pairs={{0,1},{1,0},{2,3},{3,2},{4,5},{5,4},{6,7},{7,6},{8,9},{9,8},{10,11... | collective-permute-start | bytes 1327112 | tf_op jit(solution)/shard_map/ppermute | solution.py:52
  68.3 3.0 %collective-permute-start.12 = (bf16[256,1792]{1,0:T(8,128)(2,1)}, bf16[256,1792]{1,0:T(8,128)(2,1)}, u32[]{:S(2)}, u32[]{:S(2)}) collective-permute-start(bf16[256,1792]{1,0:T(8,128)(2,1)} %get-tuple-element.22), channel_id=1, source_target_pairs={{0,1},{1,0},{2,3},{3,2},{4,5},{5,4},{6,7},{7,6},{8,9},{9,8},{10,11... | collective-permute-start | bytes 2752520 | tf_op jit(solution)/shard_map/ppermute | solution.py:52
  68.9 4.5 %collective-permute-start.15 = (bf16[256,1792]{1,0:T(8,128)(2,1)}, bf16[256,1792]{1,0:T(8,128)(2,1)}, u32[]{:S(2)}, u32[]{:S(2)}) collective-permute-start(bf16[256,1792]{1,0:T(8,128)(2,1)} %get-tuple-element.24), channel_id=1, source_target_pairs={{0,1},{1,0},{2,3},{3,2},{4,5},{5,4},{6,7},{7,6},{8,9},{9,8},{10,11... | collective-permute-start | bytes 2752520 | tf_op jit(solution)/shard_map/ppermute | solution.py:52
  72.8 13.0 %collective-permute-start.13 = (bf16[128,1792]{1,0:T(8,128)(2,1)S(1)}, bf16[128,1792]{1,0:T(8,128)(2,1)}, u32[]{:S(2)}, u32[]{:S(2)}) collective-permute-start(bf16[128,1792]{1,0:T(8,128)(2,1)S(1)} %slice.125), channel_id=1, source_target_pairs={{0,2},{2,0},{4,6},{6,4},{8,10},{10,8},{12,14},{14,12},{16,18},{18,... | collective-permute-start | bytes 1376264 | tf_op jit(solution)/shard_map/ppermute | solution.py:47
  75.6 16.7 %collective-permute-start.16 = (bf16[128,1792]{1,0:T(8,128)(2,1)}, bf16[128,1792]{1,0:T(8,128)(2,1)}, u32[]{:S(2)}, u32[]{:S(2)}) collective-permute-start(bf16[128,1792]{1,0:T(8,128)(2,1)} %slice.129), channel_id=1, source_target_pairs={{0,4},{2,6},{4,0},{6,2},{8,12},{10,14},{12,8},{14,10},{16,20},{18,... | collective-permute-start | bytes 1376264 | tf_op jit(solution)/shard_map/ppermute | solution.py:47
  76.5 23.7 %all-to-all-start.1 = ((bf16[16,24,576]{2,1,0:T(8,128)(2,1)}), bf16[16,24,576]{2,1,0:T(8,128)(2,1)S(1)}, u32[]{:S(2)}, u32[]{:S(2)}) async-start(bf16[16,24,576]{2,1,0:T(8,128)(2,1)} %bitcast.17), calls=%async_computation.1 | async-start | bytes 983040 | tf_op jit(solution)/shard_map/all_to_all | solution.py:263
  87.0 11.5 %collective-permute-start.14 = (bf16[64,1792]{1,0:T(8,128)(2,1)S(1)}, bf16[64,1792]{1,0:T(8,128)(2,1)S(1)}, u32[]{:S(2)}, u32[]{:S(2)}) collective-permute-start(bf16[64,1792]{1,0:T(8,128)(2,1)S(1)} %slice.127), channel_id=1, source_target_pairs={{0,4},{2,6},{4,0},{6,2},{8,12},{10,14},{12,8},{14,10},{16,20},{18,... | collective-permute-start | bytes 688136 | tf_op jit(solution)/shard_map/ppermute | solution.py:47
  93.4 6.7 %collective-permute-start.17 = (bf16[64,1792]{1,0:T(8,128)(2,1)S(1)}, bf16[64,1792]{1,0:T(8,128)(2,1)S(1)}, u32[]{:S(2)}, u32[]{:S(2)}) collective-permute-start(bf16[64,1792]{1,0:T(8,128)(2,1)S(1)} %slice.131), channel_id=1, source_target_pairs={{0,2},{2,0},{4,6},{6,4},{8,10},{10,8},{12,14},{14,12},{16,18},{18,... | collective-permute-start | bytes 688136 | tf_op jit(solution)/shard_map/ppermute | solution.py:47
  100.2 6.1 %collective-permute-start.18 = (bf16[32,3584]{1,0:T(8,128)(2,1)S(1)}, bf16[32,3584]{1,0:T(8,128)(2,1)S(1)}, u32[]{:S(2)}, u32[]{:S(2)}) collective-permute-start(bf16[32,3584]{1,0:T(8,128)(2,1)S(1)} %pad_maximum_fusion.3), channel_id=1, source_target_pairs={{0,8},{2,10},{4,12},{6,14},{8,0},{10,2},{12,4},{14,6},{16,24},{18,... | collective-permute-start | bytes 688136 | tf_op jit(solution)/shard_map/ppermute | solution.py:47
  101.6 4.8 %collective-permute-start.19 = (bf16[16,24,576]{2,1,0:T(8,128)(2,1)S(1)}, bf16[16,24,576]{2,1,0:T(8,128)(2,1)S(1)}, u32[]{:S(2)}, u32[]{:S(2)}) collective-permute-start(bf16[16,24,576]{2,1,0:T(8,128)(2,1)S(1)} %all-to-all-done.1), channel_id=1, source_target_pairs={{0,1},{1,0},{2,3},{3,2},{4,5},{5,4},{6,7},{7,6},{8,9},{9,8},{10,11... | collective-permute-start | bytes 1327112 | tf_op jit(solution)/shard_map/ppermute | solution.py:52
  109.4 9.4 %collective-permute-start.20 = (bf16[16,3584]{1,0:T(8,128)(2,1)S(1)}, bf16[16,3584]{1,0:T(8,128)(2,1)S(1)}, u32[]{:S(2)}, u32[]{:S(2)}) collective-permute-start(bf16[16,3584]{1,0:T(8,128)(2,1)S(1)} %slice.135), channel_id=1, source_target_pairs={{0,16},{2,18},{4,20},{6,22},{8,24},{10,26},{12,28},{14,30},{16,0},... | collective-permute-start | bytes 344072 | tf_op jit(solution)/shard_map/ppermute | solution.py:47
  (11 other events, 111.2 us)

commit v7 on v6

--- a/solution.py
+++ b/solution.py
@@ -122,20 +122,22 @@
     )
 
 
-def scatter_sums(totals, orders, hooks):
+def scatter_sums(parts, orders, hooks):
     steps = len(orders[0])
     for step in range(steps):
+        half = parts[0][0].shape[0] // 2
+        sents = [add_up([term[half:] for term in terms]) for terms in parts]
+        kepts = [add_up([term[:half] for term in terms]) for terms in parts]
         if step == 2:
-            totals = [jnp.concatenate(totals, axis=1)]
-        half = totals[0].shape[0] // 2
-        sents = [total[half:] for total in totals]
+            sents = [jnp.concatenate(sents, axis=1)]
+            kepts = [jnp.concatenate(kepts, axis=1)]
         if step in hooks:
             sents[-1] = hooks[step](sents[-1])
-        totals = [
-            add_up([total[:half], exchange(sent, order[steps - 1 - step])])
-            for total, sent, order in zip(totals, sents, orders)
+        parts = [
+            [kept, exchange(sent, order[steps - 1 - step])]
+            for kept, sent, order in zip(kepts, sents, orders)
         ]
-    return totals[0]
+    return add_up(parts[0])
 
 
 def add_up(terms):
@@ -370,7 +372,6 @@
     all_rows = join_rows(
         [halves] + arrived, to_first, tuple(cut * part for part in range(1, parts + 1)), row_count
     )
-    ordered = cache_turn(pieces, block_source, slot_total, all_rows)
     gate_halves = [half[..., cut : cut + 3 * ep_size] for half in halves[-1]]
     all_gate = jnp.concatenate(gate_halves, axis=0)
     all_gate = jnp.stack([all_gate[block] for block in from_first[-1]]).astype(jnp.float32)
@@ -383,12 +384,13 @@
         jax.nn.silu(gate_and_up[:, 0]) * gate_and_up[:, 1] * my_gate[:, None]
     ).astype(jnp.bfloat16)
 
-    hidden = tie(hidden, ordered)
-    by_step = down(hidden, expert_down[0], from_first, row_count)
-    sums = list(by_step[-1])
+    ordered = cache_turn(pieces, block_source, slot_total, hidden)
+    down_weight = pltpu.with_memory_space_constraint(expert_down[0], pltpu.HBM)
+    by_step = down(hidden, down_weight, from_first, row_count)
+    sums = [[own] for own in by_step[-1]]
     for part in range(parts):
-        others = [pass_tp(by_step[step - 1][part], step) for step in range(1, tp_size)]
-        sums[part] = add_up([sums[part]] + others)
+        for step in range(1, tp_size):
+            sums[part].append(pass_tp(by_step[step - 1][part], step))
 
     held = {}
 

time: 120 us -> 119 us (level)
  waiting for transfers between devices: 41.5 us -> 47.4 us
  starting transfers between devices: 37.9 us -> 33.9 us
  local copies, waits for them, and re-layouts: 10.7 us -> 7.09 us
    ppermute x13, waiting for transfers between devices: 32.9 us -> 46 us  [exchange(): lax.ppermute(value, 'ep', [(index, index ^ bit) for index in range(ep_siz...]
    all_to_all x1, waiting for transfers between devices: 4.38 us -> 0.01 us  [cache_turn(): lax.all_to_all(pieces, 'ep', split_axis=0, concat_axis=0, tiled=True)]
    unnamed x25 -> x21, local copies, waits for them, and re-layouts: 8.68 us -> 5.24 us
    ppermute x8, waiting for transfers between devices: 4.21 us -> 1.48 us  [pass_tp(): lax.ppermute(value, 'tp', [(index, (index + step) % tp_size) for index in...]
    ppermute x13, starting transfers between devices: 22.2 us -> 19.5 us  [exchange(): lax.ppermute(value, 'ep', [(index, index ^ bit) for index in range(ep_siz...]
    all_to_all x1, starting transfers between devices: 7.09 us -> 4.64 us  [cache_in(): lax.all_to_all(ordered, 'ep', split_axis=0, concat_axis=0, tiled=True)]
    all_to_all x1, starting transfers between devices: 6.77 us -> 8.19 us  [cache_turn(): lax.all_to_all(pieces, 'ep', split_axis=0, concat_axis=0, tiled=True)]
  transfers between devices with their start and end apart: 23 -> 23, of which waited for: 13 -> 13; matrix products, arithmetic and copies ran while one was open for 17% -> 16% of each run, Pallas kernels for 2% -> 7%
where the time goes in v7:
time: 119 us; the launch traced here: 118 us
  waiting for transfers between devices  47.4 us (40%)
  starting transfers between devices  33.9 us (28%)
  Pallas kernels  10.9 us (9%)
  other arithmetic  10.1 us (8%)
  matrix products  7.79 us (7%)
  local copies, waits for them, and re-layouts  7.09 us (6%)
    ppermute x13, waiting for transfers between devices, exchange(): lax.ppermute(value, 'ep', [(index, index ^ bit) for index in range(ep_siz...  46 us
    ppermute x13, starting transfers between devices, exchange(): lax.ppermute(value, 'ep', [(index, index ^ bit) for index in range(ep_siz...  19.5 us
    pallas_call x4, Pallas kernels, kernel_call(): pl.pallas_call(kernel, out_shape=out_shape, in_specs=in_specs or [WHOLE]...  10.9 us
    all_to_all x1, starting transfers between devices, cache_turn(): lax.all_to_all(pieces, 'ep', split_axis=0, concat_axis=0, tiled=True)  8.19 us
    dot_general x1, matrix products, body(): jnp.einsum('sd,dgf->sgf', all_rows, expert_gate_up[0], preferred_element_...  7.79 us
    convert_element_type x8, other arithmetic, add_up(): return total.astype(jnp.bfloat16)  6.49 us
    unnamed x21, local copies, waits for them, and re-layouts  5.24 us
    all_to_all x1, starting transfers between devices, cache_in(): lax.all_to_all(ordered, 'ep', split_axis=0, concat_axis=0, tiled=True)  4.64 us
  transfers between devices with their start and end apart: 23, of which 13 were waited for; matrix products, arithmetic and copies ran while one was open for 16% of the time, Pallas kernels for 7%

profile of v7, /device:TPU:0, one launch (start us, length us, event | category | flops | bytes accessed | tf_op | source)
XLA Modules:
  0.0 118.2 jit_solution(6769361187048662261)
XLA Ops:
  0.6 4.1 %collective-permute-start = (bf16[1,16,3584]{2,1,0:T(8,128)(2,1)}, bf16[1,16,3584]{2,1,0:T(8,128)(2,1)S(1)}, u32[]{:S(2)}, u32[]{:S(2)}) collective-permute-start(bf16[1,16,3584]{2,1,0:T(8,128)(2,1)} %bitcast.49), channel_id=1, source_target_pairs={{0,16},{2,18},{4,20},{6,22},{8,24},{10,26},{12,28},{14,30},{16,0},... | collective-permute-start | bytes 344072 | tf_op jit(solution)/shard_map/ppermute | solution.py:47
  6.6 4.4 %collective-permute-done.1 = bf16[1,16,128]{2,1,0:T(8,128)(2,1)S(1)} collective-permute-done((bf16[1,16,128]{2,1,0:T(8,128)(2,1)S(1)}, bf16[1,16,128]{2,1,0:T(8,128)(2,1)S(1)}, u32[]{:S(2)}, u32[]{:S(2)}) %collective-permute-start.1) | collective-permute-done | bytes 4128 | tf_op jit(solution)/shard_map/ppermute | solution.py:47
  11.9 1.6 %collective-permute-start.2 = (bf16[2,16,3712]{2,1,0:T(8,128)(2,1)S(1)}, bf16[2,16,3712]{2,1,0:T(8,128)(2,1)S(1)}, u32[]{:S(2)}, u32[]{:S(2)}) collective-permute-start(bf16[2,16,3712]{2,1,0:T(8,128)(2,1)S(1)} %maximum_maximum_fusion), channel_id=1, source_target_pairs={{0,8},{2,10},{4,12},{6,14},{8,0},{10,2},{12,4},{14,6},{16,24},{18,... | collective-permute-start | bytes 712712 | tf_op jit(solution)/shard_map/ppermute | solution.py:47
  13.5 5.1 %collective-permute-done.2 = bf16[2,16,3712]{2,1,0:T(8,128)(2,1)S(1)} collective-permute-done((bf16[2,16,3712]{2,1,0:T(8,128)(2,1)S(1)}, bf16[2,16,3712]{2,1,0:T(8,128)(2,1)S(1)}, u32[]{:S(2)}, u32[]{:S(2)}) %collective-permute-start.2) | collective-permute-done | bytes 237600 | tf_op jit(solution)/shard_map/ppermute | solution.py:47
  21.1 1.6 %collective-permute-start.3 = (bf16[4,16,1792]{2,1,0:T(8,128)(2,1)S(1)}, bf16[4,16,1792]{2,1,0:T(8,128)(2,1)S(1)}, u32[]{:S(2)}, u32[]{:S(2)}) collective-permute-start(bf16[4,16,1792]{2,1,0:T(8,128)(2,1)S(1)} %slice.181), channel_id=1, source_target_pairs={{0,4},{2,6},{4,0},{6,2},{8,12},{10,14},{12,8},{14,10},{16,20},{18,... | collective-permute-start | bytes 688136 | tf_op jit(solution)/shard_map/ppermute | solution.py:47
  22.6 3.3 %collective-permute-done.5 = bf16[4,16,1920]{2,1,0:T(8,128)(2,1)S(1)} collective-permute-done((bf16[4,16,1920]{2,1,0:T(8,128)(2,1)S(1)}, bf16[4,16,1920]{2,1,0:T(8,128)(2,1)S(1)}, u32[]{:S(2)}, u32[]{:S(2)}) %collective-permute-start.5) | collective-permute-done | bytes 245792 | tf_op jit(solution)/shard_map/ppermute | solution.py:47
  29.2 8.3 %collective-permute-done.4 = bf16[8,16,1792]{2,1,0:T(8,128)(2,1)} collective-permute-done((bf16[8,16,1792]{2,1,0:T(8,128)(2,1)S(1)}, bf16[8,16,1792]{2,1,0:T(8,128)(2,1)}, u32[]{:S(2)}, u32[]{:S(2)}) %collective-permute-start.4) | collective-permute-done | bytes 458784 | tf_op jit(solution)/shard_map/ppermute | solution.py:47
  39.4 8.2 %all-to-all-start = ((bf16[16,24,576]{2,1,0:T(8,128)(2,1)}), bf16[16,24,576]{2,1,0:T(8,128)(2,1)S(1)}, u32[]{:S(2)}, u32[]{:S(2)}) async-start(bf16[16,24,576]{2,1,0:T(8,128)(2,1)} %bitcast.48), calls=%async_computation | async-start | bytes 983040 | tf_op jit(solution)/shard_map/all_to_all | solution.py:240
  49.3 1.7 %shard_map.113 = bf16[256,7168]{1,0:T(8,128)(2,1)S(1)} custom-call(bf16[128,1792]{1,0:T(8,128)(2,1)S(1)} %bitcast.40, bf16[128,1792]{1,0:T(8,128)(2,1)} %bitcast.3.refs_1_, bf16[128,1920]{1,0:T(8,128)(2,1)S(1)} %bitcast.38, bf16[128,1920]{1,0:T(8,128)(2,1)S(1)} %bitcast.41, bf16[128,1792]{1,0:T(8,128)(2,1)} %bitcast.6.refs_4_, ...), custom_call_target="tpu_custom_call" | custom-call | bytes 11272192 | tf_op jit(solution)/shard_map/pallas_call | solution.py:23
  51.0 7.8 %fusion = f32[256,2,512]{2,0,1:T(8,128)S(1)} fusion(bf16[7168,2,512]{2,1,0:T(2,128)(2,1)} %bitcast.53, bf16[256,7168]{1,0:T(8,128)(2,1)S(1)} %shard_map.113), kind=kOutput, calls=%fused_computation | convolution fusion | flops 3758096384 | bytes 19398656 | tf_op jit(solution)/shard_map/sd,dgf->sgf/dot_general | solution.py:380
  59.0 4.7 %shard_map.114 = (bf16[256,1792]{1,0:T(8,128)(2,1)}, bf16[256,1792]{1,0:T(8,128)(2,1)S(1)}, bf16[256,1792]{1,0:T(8,128)(2,1)S(1)}, bf16[256,1792]{1,0:T(8,128)(2,1)S(1)}) custom-call(bf16[256,512]{1,0:T(8,128)(2,1)S(1)} %fusion.5.hidden, bf16[7168,512]{1,0:T(8,128)(2,1)} %bitcast.47), custom_call_target="tpu_custom_call" | custom-call | flops 1879048192 | bytes 11534336 | tf_op jit(solution)/shard_map/pallas_call | solution.py:23
  67.9 1.6 %shard_map.115 = bf16[384,576]{1,0:T(8,128)(2,1)} custom-call(s32[384,2]{1,0:T(8,128)S(1)} %fusion.6.index, bf16[384,576]{1,0:T(8,128)(2,1)S(1)} %bitcast.39, bf16[384,576]{1,0:T(8,128)(2,1)S(1)} %bitcast.44), custom_call_target="tpu_custom_call" | custom-call | flops 339738624 | bytes 2217984 | tf_op jit(solution)/shard_map/pallas_call | solution.py:23
  69.5 2.3 %add_convert_fusion.3 = (bf16[128,1792]{1,0:T(8,128)(2,1)}, bf16[128,1792]{1,0:T(8,128)(2,1)}) fusion(bf16[256,1792]{1,0:T(8,128)(2,1)} %collective-permute-done.11, bf16[256,1792]{1,0:T(8,128)(2,1)S(1)} %get-tuple-element.17), kind=kLoop, calls=%fused_computation.6 | loop fusion | flops 1835008 | bytes 2752512 | tf_op jit(solution)/shard_map/convert_element_type | solution.py:147
  71.8 1.9 %collective-permute-start.12 = (bf16[128,1792]{1,0:T(8,128)(2,1)}, bf16[128,1792]{1,0:T(8,128)(2,1)S(1)}, u32[]{:S(2)}, u32[]{:S(2)}) collective-permute-start(bf16[128,1792]{1,0:T(8,128)(2,1)} %get-tuple-element.32), channel_id=1, source_target_pairs={{0,2},{2,0},{4,6},{6,4},{8,10},{10,8},{12,14},{14,12},{16,18},{18,... | collective-permute-start | bytes 1376264 | tf_op jit(solution)/shard_map/ppermute | solution.py:47
  76.2 4.6 %all-to-all-start.1 = ((bf16[16,24,576]{2,1,0:T(8,128)(2,1)}), bf16[16,24,576]{2,1,0:T(8,128)(2,1)S(1)}, u32[]{:S(2)}, u32[]{:S(2)}) async-start(bf16[16,24,576]{2,1,0:T(8,128)(2,1)} %bitcast.18), calls=%async_computation.1 | async-start | bytes 983040 | tf_op jit(solution)/shard_map/all_to_all | solution.py:265
  80.8 5.0 %collective-permute-done.12 = bf16[128,1792]{1,0:T(8,128)(2,1)S(1)} collective-permute-done((bf16[128,1792]{1,0:T(8,128)(2,1)}, bf16[128,1792]{1,0:T(8,128)(2,1)S(1)}, u32[]{:S(2)}, u32[]{:S(2)}) %collective-permute-start.12) | collective-permute-done | bytes 458784 | tf_op jit(solution)/shard_map/ppermute | solution.py:47
  87.0 2.0 %collective-permute-start.13 = (bf16[64,1792]{1,0:T(8,128)(2,1)S(1)}, bf16[64,1792]{1,0:T(8,128)(2,1)S(1)}, u32[]{:S(2)}, u32[]{:S(2)}) collective-permute-start(bf16[64,1792]{1,0:T(8,128)(2,1)S(1)} %get-tuple-element.36), channel_id=1, source_target_pairs={{0,4},{2,6},{4,0},{6,2},{8,12},{10,14},{12,8},{14,10},{16,20},{18,... | collective-permute-start | bytes 688136 | tf_op jit(solution)/shard_map/ppermute | solution.py:47
  89.0 3.3 %collective-permute-done.15 = bf16[128,1792]{1,0:T(8,128)(2,1)S(1)} collective-permute-done((bf16[128,1792]{1,0:T(8,128)(2,1)}, bf16[128,1792]{1,0:T(8,128)(2,1)S(1)}, u32[]{:S(2)}, u32[]{:S(2)}) %collective-permute-start.15) | collective-permute-done | bytes 458784 | tf_op jit(solution)/shard_map/ppermute | solution.py:47
  94.3 3.1 %collective-permute-done.13 = bf16[64,1792]{1,0:T(8,128)(2,1)S(1)} collective-permute-done((bf16[64,1792]{1,0:T(8,128)(2,1)S(1)}, bf16[64,1792]{1,0:T(8,128)(2,1)S(1)}, u32[]{:S(2)}, u32[]{:S(2)}) %collective-permute-start.13) | collective-permute-done | bytes 229408 | tf_op jit(solution)/shard_map/ppermute | solution.py:47
  97.5 2.9 %collective-permute-done.16 = bf16[64,1792]{1,0:T(8,128)(2,1)S(1)} collective-permute-done((bf16[64,1792]{1,0:T(8,128)(2,1)S(1)}, bf16[64,1792]{1,0:T(8,128)(2,1)S(1)}, u32[]{:S(2)}, u32[]{:S(2)}) %collective-permute-start.16) | collective-permute-done | bytes 229408 | tf_op jit(solution)/shard_map/ppermute | solution.py:47
  102.2 4.3 %collective-permute-done.18 = bf16[32,3584]{1,0:T(8,128)(2,1)S(1)} collective-permute-done((bf16[32,3584]{1,0:T(8,128)(2,1)S(1)}, bf16[32,3584]{1,0:T(8,128)(2,1)S(1)}, u32[]{:S(2)}, u32[]{:S(2)}) %collective-permute-start.18) | collective-permute-done | bytes 229408 | tf_op jit(solution)/shard_map/ppermute | solution.py:47
  107.6 2.9 %shard_map.116 = bf16[512,512]{1,0:T(8,128)(2,1)} custom-call(s32[2,384]{1,0:T(2,128)S(1)} %pad_add_fusion.owner, s32[512,1]{1,0:T(8,128)S(1)} %broadcast_in_dim_reshape.5.request, bf16[512,576]{1,0:T(8,128)(2,1)S(1)} %bitcast.45, bf16[384,576]{1,0:T(8,128)(2,1)S(1)} %bitcast.43, bf16[384,576]{1,0:T(8,128)(2,1)S(1)} %bitcast.46), custom_call_target="tpu_custom_call" | custom-call | flops 905969664 | bytes 3483648 | tf_op jit(solution)/shard_map/pallas_call | solution.py:23
  110.6 2.1 %collective-permute-start.20 = (bf16[16,3584]{1,0:T(8,128)(2,1)S(1)}, bf16[16,3584]{1,0:T(8,128)(2,1)S(1)}, u32[]{:S(2)}, u32[]{:S(2)}) collective-permute-start(bf16[16,3584]{1,0:T(8,128)(2,1)S(1)} %add_convert_fusion.9), channel_id=1, source_target_pairs={{0,16},{2,18},{4,20},{6,22},{8,24},{10,26},{12,28},{14,30},{16,0},... | collective-permute-start | bytes 344072 | tf_op jit(solution)/shard_map/ppermute | solution.py:47
  112.7 4.8 %collective-permute-done.20 = bf16[16,3584]{1,0:T(8,128)(2,1)S(1)} collective-permute-done((bf16[16,3584]{1,0:T(8,128)(2,1)S(1)}, bf16[16,3584]{1,0:T(8,128)(2,1)S(1)}, u32[]{:S(2)}, u32[]{:S(2)}) %collective-permute-start.20) | collective-permute-done | bytes 114720 | tf_op jit(solution)/shard_map/ppermute | solution.py:47
  (90 shorter events, 25.6 us)
Async XLA Ops:
  0.6 37.4 %copy-start = (bf16[48,16,576]{2,1,0:T(8,128)(2,1)S(1)}, bf16[48,16,576]{2,1,0:T(8,128)(2,1)}, u32[]{:S(2)}) copy-start(bf16[48,16,576]{2,1,0:T(8,128)(2,1)} %param.16) | copy-start | bytes 2654212
  0.6 10.3 %collective-permute-start = (bf16[1,16,3584]{2,1,0:T(8,128)(2,1)}, bf16[1,16,3584]{2,1,0:T(8,128)(2,1)S(1)}, u32[]{:S(2)}, u32[]{:S(2)}) collective-permute-start(bf16[1,16,3584]{2,1,0:T(8,128)(2,1)} %bitcast.49), channel_id=1, source_target_pairs={{0,16},{2,18},{4,20},{6,22},{8,24},{10,26},{12,28},{14,30},{16,0},... | collective-permute-start | bytes 344072 | tf_op jit(solution)/shard_map/ppermute | solution.py:47
  6.5 4.5 %collective-permute-start.1 = (bf16[1,16,128]{2,1,0:T(8,128)(2,1)S(1)}, bf16[1,16,128]{2,1,0:T(8,128)(2,1)S(1)}, u32[]{:S(2)}, u32[]{:S(2)}) collective-permute-start(bf16[1,16,128]{2,1,0:T(8,128)(2,1)S(1)} %fusion.21), channel_id=1, source_target_pairs={{0,16},{2,18},{4,20},{6,22},{8,24},{10,26},{12,28},{14,30},{16,0},... | collective-permute-start | bytes 12296 | tf_op jit(solution)/shard_map/ppermute | solution.py:47
  11.9 6.7 %collective-permute-start.2 = (bf16[2,16,3712]{2,1,0:T(8,128)(2,1)S(1)}, bf16[2,16,3712]{2,1,0:T(8,128)(2,1)S(1)}, u32[]{:S(2)}, u32[]{:S(2)}) collective-permute-start(bf16[2,16,3712]{2,1,0:T(8,128)(2,1)S(1)} %maximum_maximum_fusion), channel_id=1, source_target_pairs={{0,8},{2,10},{4,12},{6,14},{8,0},{10,2},{12,4},{14,6},{16,24},{18,... | collective-permute-start | bytes 712712 | tf_op jit(solution)/shard_map/ppermute | solution.py:47
  19.7 6.3 %collective-permute-start.5 = (bf16[4,16,1920]{2,1,0:T(8,128)(2,1)S(1)}, bf16[4,16,1920]{2,1,0:T(8,128)(2,1)S(1)}, u32[]{:S(2)}, u32[]{:S(2)}) collective-permute-start(bf16[4,16,1920]{2,1,0:T(8,128)(2,1)S(1)} %slice.182), channel_id=1, source_target_pairs={{0,2},{2,0},{4,6},{6,4},{8,10},{10,8},{12,14},{14,12},{16,18},{18,... | collective-permute-start | bytes 737288 | tf_op jit(solution)/shard_map/ppermute | solution.py:47
  21.1 7.7 %collective-permute-start.3 = (bf16[4,16,1792]{2,1,0:T(8,128)(2,1)S(1)}, bf16[4,16,1792]{2,1,0:T(8,128)(2,1)S(1)}, u32[]{:S(2)}, u32[]{:S(2)}) collective-permute-start(bf16[4,16,1792]{2,1,0:T(8,128)(2,1)S(1)} %slice.181), channel_id=1, source_target_pairs={{0,4},{2,6},{4,0},{6,2},{8,12},{10,14},{12,8},{14,10},{16,20},{18,... | collective-permute-start | bytes 688136 | tf_op jit(solution)/shard_map/ppermute | solution.py:47
  26.0 11.7 %collective-permute-start.6 = (bf16[8,16,1920]{2,1,0:T(8,128)(2,1)S(1)}, bf16[8,16,1920]{2,1,0:T(8,128)(2,1)S(1)}, u32[]{:S(2)}, u32[]{:S(2)}) collective-permute-start(bf16[8,16,1920]{2,1,0:T(8,128)(2,1)S(1)} %pad_maximum_fusion), channel_id=1, source_target_pairs={{0,4},{2,6},{4,0},{6,2},{8,12},{10,14},{12,8},{14,10},{16,20},{18,... | collective-permute-start | bytes 1474568 | tf_op jit(solution)/shard_map/ppermute | solution.py:47
  28.8 8.6 %collective-permute-start.4 = (bf16[8,16,1792]{2,1,0:T(8,128)(2,1)S(1)}, bf16[8,16,1792]{2,1,0:T(8,128)(2,1)}, u32[]{:S(2)}, u32[]{:S(2)}) collective-permute-start(bf16[8,16,1792]{2,1,0:T(8,128)(2,1)S(1)} %pad_maximum_fusion.2), channel_id=1, source_target_pairs={{0,2},{2,0},{4,6},{6,4},{8,10},{10,8},{12,14},{14,12},{16,18},{18,... | collective-permute-start | bytes 1376264 | tf_op jit(solution)/shard_map/ppermute | solution.py:47
  37.5 11.8 %collective-permute-start.9 = (bf16[8,16,1920]{2,1,0:T(8,128)(2,1)S(1)}, bf16[8,16,1920]{2,1,0:T(8,128)(2,1)S(1)}, u32[]{:S(2)}, u32[]{:S(2)}) collective-permute-start(bf16[8,16,1920]{2,1,0:T(8,128)(2,1)S(1)} %pad_maximum_fusion), channel_id=1, source_target_pairs={{0,1},{1,0},{2,3},{3,2},{4,5},{5,4},{6,7},{7,6},{8,9},{9,8},{10,11... | collective-permute-start | bytes 1474568 | tf_op jit(solution)/shard_map/ppermute | solution.py:52
  37.7 11.6 %collective-permute-start.10 = (bf16[8,16,1920]{2,1,0:T(8,128)(2,1)S(1)}, bf16[8,16,1920]{2,1,0:T(8,128)(2,1)}, u32[]{:S(2)}, u32[]{:S(2)}) collective-permute-start(bf16[8,16,1920]{2,1,0:T(8,128)(2,1)S(1)} %collective-permute-done.6), channel_id=1, source_target_pairs={{0,1},{1,0},{2,3},{3,2},{4,5},{5,4},{6,7},{7,6},{8,9},{9,8},{10,11... | collective-permute-start | bytes 1474568 | tf_op jit(solution)/shard_map/ppermute | solution.py:52
  38.9 10.3 %collective-permute-start.7 = (bf16[8,16,1792]{2,1,0:T(8,128)(2,1)S(1)}, bf16[8,16,1792]{2,1,0:T(8,128)(2,1)}, u32[]{:S(2)}, u32[]{:S(2)}) collective-permute-start(bf16[8,16,1792]{2,1,0:T(8,128)(2,1)S(1)} %pad_maximum_fusion.2), channel_id=1, source_target_pairs={{0,1},{1,0},{2,3},{3,2},{4,5},{5,4},{6,7},{7,6},{8,9},{9,8},{10,11... | collective-permute-start | bytes 1376264 | tf_op jit(solution)/shard_map/ppermute | solution.py:52
  39.1 10.2 %collective-permute-start.8 = (bf16[8,16,1792]{2,1,0:T(8,128)(2,1)}, bf16[8,16,1792]{2,1,0:T(8,128)(2,1)}, u32[]{:S(2)}, u32[]{:S(2)}) collective-permute-start(bf16[8,16,1792]{2,1,0:T(8,128)(2,1)} %collective-permute-done.4), channel_id=1, source_target_pairs={{0,1},{1,0},{2,3},{3,2},{4,5},{5,4},{6,7},{7,6},{8,9},{9,8},{10,11... | collective-permute-start | bytes 1376264 | tf_op jit(solution)/shard_map/ppermute | solution.py:52
  39.4 26.1 %all-to-all-start = ((bf16[16,24,576]{2,1,0:T(8,128)(2,1)}), bf16[16,24,576]{2,1,0:T(8,128)(2,1)S(1)}, u32[]{:S(2)}, u32[]{:S(2)}) async-start(bf16[16,24,576]{2,1,0:T(8,128)(2,1)} %bitcast.48), calls=%async_computation | async-start | bytes 983040 | tf_op jit(solution)/shard_map/all_to_all | solution.py:240
  64.7 4.7 %collective-permute-start.11 = (bf16[256,1792]{1,0:T(8,128)(2,1)}, bf16[256,1792]{1,0:T(8,128)(2,1)}, u32[]{:S(2)}, u32[]{:S(2)}) collective-permute-start(bf16[256,1792]{1,0:T(8,128)(2,1)} %get-tuple-element.18), channel_id=1, source_target_pairs={{0,1},{1,0},{2,3},{3,2},{4,5},{5,4},{6,7},{7,6},{8,9},{9,8},{10,11... | collective-permute-start | bytes 2752520 | tf_op jit(solution)/shard_map/ppermute | solution.py:52
  65.6 2.3 %collective-permute-start.17 = (bf16[16,24,576]{2,1,0:T(8,128)(2,1)S(1)}, bf16[16,24,576]{2,1,0:T(8,128)(2,1)S(1)}, u32[]{:S(2)}, u32[]{:S(2)}) collective-permute-start(bf16[16,24,576]{2,1,0:T(8,128)(2,1)S(1)} %all-to-all-done), channel_id=1, source_target_pairs={{0,1},{1,0},{2,3},{3,2},{4,5},{5,4},{6,7},{7,6},{8,9},{9,8},{10,11... | collective-permute-start | bytes 1327112 | tf_op jit(solution)/shard_map/ppermute | solution.py:52
  66.1 7.5 %collective-permute-start.14 = (bf16[256,1792]{1,0:T(8,128)(2,1)}, bf16[256,1792]{1,0:T(8,128)(2,1)S(1)}, u32[]{:S(2)}, u32[]{:S(2)}) collective-permute-start(bf16[256,1792]{1,0:T(8,128)(2,1)} %copy-done.1), channel_id=1, source_target_pairs={{0,1},{1,0},{2,3},{3,2},{4,5},{5,4},{6,7},{7,6},{8,9},{9,8},{10,11... | collective-permute-start | bytes 2752520 | tf_op jit(solution)/shard_map/ppermute | solution.py:52
  71.8 14.1 %collective-permute-start.12 = (bf16[128,1792]{1,0:T(8,128)(2,1)}, bf16[128,1792]{1,0:T(8,128)(2,1)S(1)}, u32[]{:S(2)}, u32[]{:S(2)}) collective-permute-start(bf16[128,1792]{1,0:T(8,128)(2,1)} %get-tuple-element.32), channel_id=1, source_target_pairs={{0,2},{2,0},{4,6},{6,4},{8,10},{10,8},{12,14},{14,12},{16,18},{18,... | collective-permute-start | bytes 1376264 | tf_op jit(solution)/shard_map/ppermute | solution.py:47
  74.7 17.6 %collective-permute-start.15 = (bf16[128,1792]{1,0:T(8,128)(2,1)}, bf16[128,1792]{1,0:T(8,128)(2,1)S(1)}, u32[]{:S(2)}, u32[]{:S(2)}) collective-permute-start(bf16[128,1792]{1,0:T(8,128)(2,1)} %get-tuple-element.34), channel_id=1, source_target_pairs={{0,4},{2,6},{4,0},{6,2},{8,12},{10,14},{12,8},{14,10},{16,20},{18,... | collective-permute-start | bytes 1376264 | tf_op jit(solution)/shard_map/ppermute | solution.py:47
  76.2 24.2 %all-to-all-start.1 = ((bf16[16,24,576]{2,1,0:T(8,128)(2,1)}), bf16[16,24,576]{2,1,0:T(8,128)(2,1)S(1)}, u32[]{:S(2)}, u32[]{:S(2)}) async-start(bf16[16,24,576]{2,1,0:T(8,128)(2,1)} %bitcast.18), calls=%async_computation.1 | async-start | bytes 983040 | tf_op jit(solution)/shard_map/all_to_all | solution.py:265
  87.0 10.4 %collective-permute-start.13 = (bf16[64,1792]{1,0:T(8,128)(2,1)S(1)}, bf16[64,1792]{1,0:T(8,128)(2,1)S(1)}, u32[]{:S(2)}, u32[]{:S(2)}) collective-permute-start(bf16[64,1792]{1,0:T(8,128)(2,1)S(1)} %get-tuple-element.36), channel_id=1, source_target_pairs={{0,4},{2,6},{4,0},{6,2},{8,12},{10,14},{12,8},{14,10},{16,20},{18,... | collective-permute-start | bytes 688136 | tf_op jit(solution)/shard_map/ppermute | solution.py:47
  94.2 6.1 %collective-permute-start.16 = (bf16[64,1792]{1,0:T(8,128)(2,1)S(1)}, bf16[64,1792]{1,0:T(8,128)(2,1)S(1)}, u32[]{:S(2)}, u32[]{:S(2)}) collective-permute-start(bf16[64,1792]{1,0:T(8,128)(2,1)S(1)} %get-tuple-element.38), channel_id=1, source_target_pairs={{0,2},{2,0},{4,6},{6,4},{8,10},{10,8},{12,14},{14,12},{16,18},{18,... | collective-permute-start | bytes 688136 | tf_op jit(solution)/shard_map/ppermute | solution.py:47
  100.4 6.1 %collective-permute-start.18 = (bf16[32,3584]{1,0:T(8,128)(2,1)S(1)}, bf16[32,3584]{1,0:T(8,128)(2,1)S(1)}, u32[]{:S(2)}, u32[]{:S(2)}) collective-permute-start(bf16[32,3584]{1,0:T(8,128)(2,1)S(1)} %pad_maximum_fusion.3), channel_id=1, source_target_pairs={{0,8},{2,10},{4,12},{6,14},{8,0},{10,2},{12,4},{14,6},{16,24},{18,... | collective-permute-start | bytes 688136 | tf_op jit(solution)/shard_map/ppermute | solution.py:47
  102.1 4.4 %collective-permute-start.19 = (bf16[16,24,576]{2,1,0:T(8,128)(2,1)S(1)}, bf16[16,24,576]{2,1,0:T(8,128)(2,1)S(1)}, u32[]{:S(2)}, u32[]{:S(2)}) collective-permute-start(bf16[16,24,576]{2,1,0:T(8,128)(2,1)S(1)} %all-to-all-done.1), channel_id=1, source_target_pairs={{0,1},{1,0},{2,3},{3,2},{4,5},{5,4},{6,7},{7,6},{8,9},{9,8},{10,11... | collective-permute-start | bytes 1327112 | tf_op jit(solution)/shard_map/ppermute | solution.py:52
  110.6 6.9 %collective-permute-start.20 = (bf16[16,3584]{1,0:T(8,128)(2,1)S(1)}, bf16[16,3584]{1,0:T(8,128)(2,1)S(1)}, u32[]{:S(2)}, u32[]{:S(2)}) collective-permute-start(bf16[16,3584]{1,0:T(8,128)(2,1)S(1)} %add_convert_fusion.9), channel_id=1, source_target_pairs={{0,16},{2,18},{4,20},{6,22},{8,24},{10,26},{12,28},{14,30},{16,0},... | collective-permute-start | bytes 344072 | tf_op jit(solution)/shard_map/ppermute | solution.py:47
  (8 other events, 58.7 us)

commit v8 on v7

--- a/solution.py
+++ b/solution.py
@@ -58,7 +58,7 @@
     return [pass_tp(value, step) for step in range(1, lax.axis_size("tp"))]
 
 
-def gather_rows(rows, others, orders, ends):
+def gather_rows(rows, others, orders, ends, beside, ahead):
     shared = orders[0][:-2]
     values = [
         jnp.concatenate([value[None], exchange(value[None], shared[0])], axis=0)
@@ -66,11 +66,15 @@
     ]
     value = jnp.concatenate(values, axis=2)
     for bit in shared[1:]:
+        if bit == shared[-1]:
+            beside(value)
         value = jnp.concatenate([value, exchange(value, bit)], axis=0)
     halves = []
     for order, start, end in zip(orders, (0,) + ends, ends):
         part = value[:, :, start:end]
         part = jnp.concatenate([part, exchange(part, order[-2])], axis=0)
+        if end == ends[-1]:
+            part = ahead(part)
         halves.append((part, exchange(part, order[-1])))
     return halves
 
@@ -232,13 +236,11 @@
     return mine.reshape(share, ep_size, block_size * latent // ep_size).transpose(1, 0, 2)
 
 
-def cache_turn(pieces, block_source, slots, before):
+def cache_turn(spread, block_source, slots):
     ep_size = lax.axis_size("ep")
     tp_size = lax.axis_size("tp")
     tp_index = lax.axis_index("tp")
-    share, piece = pieces.shape[1:]
-    spread = lax.all_to_all(pieces, "ep", split_axis=0, concat_axis=0, tiled=True)
-    spread = tie(spread, before)
+    share, piece = spread.shape[1:]
     wanted = lax.dynamic_slice_in_dim(
         block_source.reshape(ep_size, tp_size, share), tp_index, 1, axis=1
     ).reshape(-1)
@@ -356,9 +358,21 @@
     pad = -gate_parts.shape[1] % 128
     gates = jnp.pad(gate_parts, ((0, 0), (0, pad)))
     ends = tuple(cut * part for part in range(1, parts)) + (tokens.shape[1] + gates.shape[1],)
-    halves = gather_rows(tokens, gates, orders, ends)
-    last_sent = halves[-1][0]
-    pieces = tie(cache_out(latent_cache), last_sent)
+    held = {}
+
+    def beside_shared(sent):
+        pieces = tie(cache_out(latent_cache), sent)
+        held["spread"] = lax.all_to_all(pieces, "ep", split_axis=0, concat_axis=0, tiled=True)
+
+    def ahead_of_last(sent):
+        sent, held["spread"] = lax.optimization_barrier((sent, held["spread"]))
+        return sent
+
+    halves = gather_rows(tokens, gates, orders, ends, beside_shared, ahead_of_last)
+    last_sent, last_late = halves[-1]
+    ordered = cache_turn(held["spread"], block_source, slot_total)
+    last_late, ordered = lax.optimization_barrier((last_late, ordered))
+    halves[-1] = (last_sent, last_late)
     places = [places_of(order) for order in orders]
     to_first = [[places[0].index(place) for place in own] for own in places]
     from_first = [[own.index(place) for place in places[0]] for own in places]
@@ -384,7 +398,6 @@
         jax.nn.silu(gate_and_up[:, 0]) * gate_and_up[:, 1] * my_gate[:, None]
     ).astype(jnp.bfloat16)
 
-    ordered = cache_turn(pieces, block_source, slot_total, hidden)
     down_weight = pltpu.with_memory_space_constraint(expert_down[0], pltpu.HBM)
     by_step = down(hidden, down_weight, from_first, row_count)
     sums = [[own] for own in by_step[-1]]
@@ -392,19 +405,18 @@
         for step in range(1, tp_size):
             sums[part].append(pass_tp(by_step[step - 1][part], step))
 
-    held = {}
-
     def beside_first_sum(sent):
         held["keys"] = cache_in(tie(ordered, sent), block_size, latent)
         return sent
 
     def beside_third_sum(sent):
-        sent, near = lax.optimization_barrier((sent, held["keys"]))
-        held["attended"] = attend(queries, [near] + swap_tp(near), block_request, block_used)
+        near = tie(held["keys"], sent)
+        held["keys"] = [near] + swap_tp(near)
         return sent
 
     def beside_last_sum(sent):
-        sent, held["attended"] = lax.optimization_barrier((sent, held["attended"]))
+        keys = tie(held["keys"], sent)
+        held["attended"] = attend(queries, keys, block_request, block_used)
         return sent
 
     hooks = {0: beside_first_sum, 2: beside_third_sum, len(bits) - 1: beside_last_sum}

time: 119 us -> 117 us (0.983)
  waiting for transfers between devices: 47.4 us -> 50.4 us
  local copies, waits for them, and re-layouts: 7.09 us -> 4.18 us
  other arithmetic: 10.1 us -> 7.43 us
    ppermute x13, waiting for transfers between devices: 46 us -> 33.9 us  [exchange(): lax.ppermute(value, 'ep', [(index, index ^ bit) for index in range(ep_siz...]
    all_to_all x1, waiting for transfers between devices: 0.01 us -> 11.7 us  [cache_in(): lax.all_to_all(ordered, 'ep', split_axis=0, concat_axis=0, tiled=True)]
    ppermute x8, waiting for transfers between devices: 1.48 us -> 4.37 us  [pass_tp(): lax.ppermute(value, 'tp', [(index, (index + step) % tp_size) for index in...]
    unnamed x21 -> x11, local copies, waits for them, and re-layouts: 5.24 us -> 2.41 us
    all_to_all x1, starting transfers between devices: 8.19 us -> 5.54 us  [beside_shared(): lax.all_to_all(pieces, 'ep', split_axis=0, concat_axis=0, tiled=True)]
    convert_element_type x8, other arithmetic: 6.49 us -> 3.86 us  [add_up(): return total.astype(jnp.bfloat16)]
    all_to_all x1, starting transfers between devices: 4.64 us -> 6.13 us  [cache_in(): lax.all_to_all(ordered, 'ep', split_axis=0, concat_axis=0, tiled=True)]
    ppermute x13, starting transfers between devices: 19.5 us -> 20.9 us  [exchange(): lax.ppermute(value, 'ep', [(index, index ^ bit) for index in range(ep_siz...]
  transfers between devices with their start and end apart: 23 -> 23, of which waited for: 13 -> 15; matrix products, arithmetic and copies ran while one was open for 16% -> 9% of each run, Pallas kernels for 7% -> 1%
where the time goes in v8:
time: 117 us; the launch traced here: 116 us
  waiting for transfers between devices  50.4 us (43%)
  starting transfers between devices  34.3 us (29%)
  Pallas kernels  11.1 us (9%)
  matrix products  7.8 us (7%)
  other arithmetic  7.43 us (6%)
  local copies, waits for them, and re-layouts  4.18 us (4%)
    ppermute x13, waiting for transfers between devices, exchange(): lax.ppermute(value, 'ep', [(index, index ^ bit) for index in range(ep_siz...  33.9 us
    ppermute x13, starting transfers between devices, exchange(): lax.ppermute(value, 'ep', [(index, index ^ bit) for index in range(ep_siz...  20.9 us
    all_to_all x1, waiting for transfers between devices, cache_in(): lax.all_to_all(ordered, 'ep', split_axis=0, concat_axis=0, tiled=True)  11.7 us
    pallas_call x4, Pallas kernels, kernel_call(): pl.pallas_call(kernel, out_shape=out_shape, in_specs=in_specs or [WHOLE]...  11.1 us
    dot_general x1, matrix products, body(): jnp.einsum('sd,dgf->sgf', all_rows, expert_gate_up[0], preferred_element_...  7.8 us
    all_to_all x1, starting transfers between devices, cache_in(): lax.all_to_all(ordered, 'ep', split_axis=0, concat_axis=0, tiled=True)  6.13 us
    all_to_all x1, starting transfers between devices, beside_shared(): lax.all_to_all(pieces, 'ep', split_axis=0, concat_axis=0, tiled=True)  5.54 us
    ppermute x8, waiting for transfers between devices, pass_tp(): lax.ppermute(value, 'tp', [(index, (index + step) % tp_size) for index in...  4.37 us
  transfers between devices with their start and end apart: 23, of which 15 were waited for; matrix products, arithmetic and copies ran while one was open for 9% of the time, Pallas kernels for 1%

profile of v8, /device:TPU:0, one launch (start us, length us, event | category | flops | bytes accessed | tf_op | source)
XLA Modules:
  0.0 116.1 jit_solution(15102176149344564111)
XLA Ops:
  0.6 4.1 %collective-permute-start = (bf16[1,16,3584]{2,1,0:T(8,128)(2,1)}, bf16[1,16,3584]{2,1,0:T(8,128)(2,1)S(1)}, u32[]{:S(2)}, u32[]{:S(2)}) collective-permute-start(bf16[1,16,3584]{2,1,0:T(8,128)(2,1)} %bitcast.49), channel_id=1, source_target_pairs={{0,16},{2,18},{4,20},{6,22},{8,24},{10,26},{12,28},{14,30},{16,0},... | collective-permute-start | bytes 344072 | tf_op jit(solution)/shard_map/ppermute | solution.py:47
  6.6 4.4 %collective-permute-done.1 = bf16[1,16,128]{2,1,0:T(8,128)(2,1)S(1)} collective-permute-done((bf16[1,16,128]{2,1,0:T(8,128)(2,1)S(1)}, bf16[1,16,128]{2,1,0:T(8,128)(2,1)S(1)}, u32[]{:S(2)}, u32[]{:S(2)}) %collective-permute-start.1) | collective-permute-done | bytes 4128 | tf_op jit(solution)/shard_map/ppermute | solution.py:47
  11.9 1.6 %collective-permute-start.2 = (bf16[2,16,3712]{2,1,0:T(8,128)(2,1)S(1)}, bf16[2,16,3712]{2,1,0:T(8,128)(2,1)S(1)}, u32[]{:S(2)}, u32[]{:S(2)}) collective-permute-start(bf16[2,16,3712]{2,1,0:T(8,128)(2,1)S(1)} %maximum_maximum_fusion), channel_id=1, source_target_pairs={{0,8},{2,10},{4,12},{6,14},{8,0},{10,2},{12,4},{14,6},{16,24},{18,... | collective-permute-start | bytes 712712 | tf_op jit(solution)/shard_map/ppermute | solution.py:47
  14.5 5.5 %all-to-all-start = ((bf16[16,24,576]{2,1,0:T(8,128)(2,1)}), bf16[16,24,576]{2,1,0:T(8,128)(2,1)S(1)}, u32[]{:S(2)}, u32[]{:S(2)}) async-start(bf16[16,24,576]{2,1,0:T(8,128)(2,1)} %bitcast.37), calls=%async_computation | async-start | bytes 983040 | tf_op jit(solution)/shard_map/all_to_all | solution.py:365
  20.9 2.0 %collective-permute-start.3 = (bf16[4,16,1792]{2,1,0:T(8,128)(2,1)S(1)}, bf16[4,16,1792]{2,1,0:T(8,128)(2,1)S(1)}, u32[]{:S(2)}, u32[]{:S(2)}) collective-permute-start(bf16[4,16,1792]{2,1,0:T(8,128)(2,1)S(1)} %pad_maximum_fusion.5), channel_id=1, source_target_pairs={{0,4},{2,6},{4,0},{6,2},{8,12},{10,14},{12,8},{14,10},{16,20},{18,... | collective-permute-start | bytes 688136 | tf_op jit(solution)/shard_map/ppermute | solution.py:47
  23.7 1.5 %collective-permute-start.5 = (bf16[4,16,1920]{2,1,0:T(8,128)(2,1)S(1)}, bf16[4,16,1920]{2,1,0:T(8,128)(2,1)S(1)}, u32[]{:S(2)}, u32[]{:S(2)}) collective-permute-start(bf16[4,16,1920]{2,1,0:T(8,128)(2,1)S(1)} %pad_maximum_fusion.2), channel_id=1, source_target_pairs={{0,2},{2,0},{4,6},{6,4},{8,10},{10,8},{12,14},{14,12},{16,18},{18,... | collective-permute-start | bytes 737288 | tf_op jit(solution)/shard_map/ppermute | solution.py:47
  26.0 6.2 %collective-permute-done.3 = bf16[4,16,1792]{2,1,0:T(8,128)(2,1)S(1)} collective-permute-done((bf16[4,16,1792]{2,1,0:T(8,128)(2,1)S(1)}, bf16[4,16,1792]{2,1,0:T(8,128)(2,1)S(1)}, u32[]{:S(2)}, u32[]{:S(2)}) %collective-permute-start.3) | collective-permute-done | bytes 229408 | tf_op jit(solution)/shard_map/ppermute | solution.py:47
  36.8 7.6 %collective-permute-done.4 = bf16[8,16,1792]{2,1,0:T(8,128)(2,1)} collective-permute-done((bf16[8,16,1792]{2,1,0:T(8,128)(2,1)S(1)}, bf16[8,16,1792]{2,1,0:T(8,128)(2,1)}, u32[]{:S(2)}, u32[]{:S(2)}) %collective-permute-start.4) | collective-permute-done | bytes 458784 | tf_op jit(solution)/shard_map/ppermute | solution.py:47
  44.9 1.6 %shard_map.113 = bf16[384,576]{1,0:T(8,128)(2,1)} custom-call(s32[384,2]{1,0:T(8,128)S(1)} %fusion.7.index, bf16[384,576]{1,0:T(8,128)(2,1)S(1)} %bitcast.39, bf16[384,576]{1,0:T(8,128)(2,1)S(1)} %bitcast.45), custom_call_target="tpu_custom_call" | custom-call | flops 339738624 | bytes 2217984 | tf_op jit(solution)/shard_map/pallas_call | solution.py:23
  48.4 1.5 %shard_map.114 = bf16[256,7168]{1,0:T(8,128)(2,1)S(1)} custom-call(bf16[128,1792]{1,0:T(8,128)(2,1)S(1)} %bitcast.40, bf16[128,1792]{1,0:T(8,128)(2,1)} %bitcast.3.refs_1_, bf16[128,1920]{1,0:T(8,128)(2,1)S(1)} %bitcast.38, bf16[128,1920]{1,0:T(8,128)(2,1)S(1)} %bitcast.41, bf16[128,1792]{1,0:T(8,128)(2,1)} %bitcast.10.refs_4_, ...), custom_call_target="tpu_custom_call" | custom-call | bytes 11272192 | tf_op jit(solution)/shard_map/pallas_call | solution.py:23
  49.9 7.8 %fusion = f32[256,2,512]{2,0,1:T(8,128)S(1)} fusion(bf16[7168,2,512]{2,1,0:T(2,128)(2,1)} %bitcast.53, bf16[256,7168]{1,0:T(8,128)(2,1)S(1)} %shard_map.114), kind=kOutput, calls=%fused_computation | convolution fusion | flops 3758096384 | bytes 19398656 | tf_op jit(solution)/shard_map/sd,dgf->sgf/dot_general | solution.py:394
  57.9 5.1 %shard_map.115 = (bf16[256,1792]{1,0:T(8,128)(2,1)}, bf16[256,1792]{1,0:T(8,128)(2,1)}, bf16[256,1792]{1,0:T(8,128)(2,1)S(1)}, bf16[256,1792]{1,0:T(8,128)(2,1)S(1)}) custom-call(bf16[256,512]{1,0:T(8,128)(2,1)S(1)} %fusion.5.hidden, bf16[7168,512]{1,0:T(8,128)(2,1)} %bitcast.48), custom_call_target="tpu_custom_call" | custom-call | flops 1879048192 | bytes 11534336 | tf_op jit(solution)/shard_map/pallas_call | solution.py:23
  63.6 2.3 %collective-permute-done.15 = bf16[256,1792]{1,0:T(8,128)(2,1)} collective-permute-done((bf16[256,1792]{1,0:T(8,128)(2,1)}, bf16[256,1792]{1,0:T(8,128)(2,1)}, u32[]{:S(2)}, u32[]{:S(2)}) %collective-permute-start.15) | collective-permute-done | bytes 917536 | tf_op jit(solution)/shard_map/ppermute | solution.py:52
  65.9 1.4 %add_convert_fusion.1 = (bf16[128,1792]{1,0:T(8,128)(2,1)S(1)}, bf16[128,1792]{1,0:T(8,128)(2,1)S(1)}) fusion(bf16[256,1792]{1,0:T(8,128)(2,1)} %collective-permute-done.15, bf16[256,1792]{1,0:T(8,128)(2,1)S(1)} %get-tuple-element.25), kind=kLoop, calls=%fused_computation.4 | loop fusion | flops 1835008 | bytes 2752512 | tf_op jit(solution)/shard_map/convert_element_type | solution.py:151
  68.2 1.4 %add_convert_fusion.3 = (bf16[128,1792]{1,0:T(8,128)(2,1)S(1)}, bf16[128,1792]{1,0:T(8,128)(2,1)S(1)}) fusion(bf16[256,1792]{1,0:T(8,128)(2,1)} %collective-permute-done.12, bf16[256,1792]{1,0:T(8,128)(2,1)S(1)} %get-tuple-element.23), kind=kLoop, calls=%fused_computation.6 | loop fusion | flops 1835008 | bytes 2752512 | tf_op jit(solution)/shard_map/convert_element_type | solution.py:151
  69.6 1.6 %collective-permute-start.13 = (bf16[128,1792]{1,0:T(8,128)(2,1)S(1)}, bf16[128,1792]{1,0:T(8,128)(2,1)S(1)}, u32[]{:S(2)}, u32[]{:S(2)}) collective-permute-start(bf16[128,1792]{1,0:T(8,128)(2,1)S(1)} %get-tuple-element.36), channel_id=1, source_target_pairs={{0,2},{2,0},{4,6},{6,4},{8,10},{10,8},{12,14},{14,12},{16,18},{18,... | collective-permute-start | bytes 1376264 | tf_op jit(solution)/shard_map/ppermute | solution.py:47
  71.2 8.7 %collective-permute-done.16 = bf16[128,1792]{1,0:T(8,128)(2,1)S(1)} collective-permute-done((bf16[128,1792]{1,0:T(8,128)(2,1)S(1)}, bf16[128,1792]{1,0:T(8,128)(2,1)S(1)}, u32[]{:S(2)}, u32[]{:S(2)}) %collective-permute-start.16) | collective-permute-done | bytes 458784 | tf_op jit(solution)/shard_map/ppermute | solution.py:47
  82.1 1.5 %collective-permute-start.14 = (bf16[64,1792]{1,0:T(8,128)(2,1)S(1)}, bf16[64,1792]{1,0:T(8,128)(2,1)S(1)}, u32[]{:S(2)}, u32[]{:S(2)}) collective-permute-start(bf16[64,1792]{1,0:T(8,128)(2,1)S(1)} %get-tuple-element.40), channel_id=1, source_target_pairs={{0,4},{2,6},{4,0},{6,2},{8,12},{10,14},{12,8},{14,10},{16,20},{18,... | collective-permute-start | bytes 688136 | tf_op jit(solution)/shard_map/ppermute | solution.py:47
  83.6 3.4 %collective-permute-done.17 = bf16[64,1792]{1,0:T(8,128)(2,1)S(1)} collective-permute-done((bf16[64,1792]{1,0:T(8,128)(2,1)S(1)}, bf16[64,1792]{1,0:T(8,128)(2,1)S(1)}, u32[]{:S(2)}, u32[]{:S(2)}) %collective-permute-start.17) | collective-permute-done | bytes 229408 | tf_op jit(solution)/shard_map/ppermute | solution.py:47
  87.0 1.6 %collective-permute-done.14 = bf16[64,1792]{1,0:T(8,128)(2,1)S(1)} collective-permute-done((bf16[64,1792]{1,0:T(8,128)(2,1)S(1)}, bf16[64,1792]{1,0:T(8,128)(2,1)S(1)}, u32[]{:S(2)}, u32[]{:S(2)}) %collective-permute-start.14) | collective-permute-done | bytes 229408 | tf_op jit(solution)/shard_map/ppermute | solution.py:47
  90.0 6.1 %all-to-all-start.1 = ((bf16[16,24,576]{2,1,0:T(8,128)(2,1)}), bf16[16,24,576]{2,1,0:T(8,128)(2,1)S(1)}, u32[]{:S(2)}, u32[]{:S(2)}) async-start(bf16[16,24,576]{2,1,0:T(8,128)(2,1)} %bitcast.8), calls=%async_computation.1 | async-start | bytes 983040 | tf_op jit(solution)/shard_map/all_to_all | solution.py:267
  96.2 2.9 %collective-permute-start.19 = (bf16[16,3584]{1,0:T(8,128)(2,1)S(1)}, bf16[16,3584]{1,0:T(8,128)(2,1)S(1)}, u32[]{:S(2)}, u32[]{:S(2)}) collective-permute-start(bf16[16,3584]{1,0:T(8,128)(2,1)S(1)} %add_convert_fusion.9), channel_id=1, source_target_pairs={{0,16},{2,18},{4,20},{6,22},{8,24},{10,26},{12,28},{14,30},{16,0},... | collective-permute-start | bytes 344072 | tf_op jit(solution)/shard_map/ppermute | solution.py:47
  99.6 11.7 %all-to-all-done.1 = bf16[16,24,576]{2,1,0:T(8,128)(2,1)S(1)} async-done(((bf16[16,24,576]{2,1,0:T(8,128)(2,1)}), bf16[16,24,576]{2,1,0:T(8,128)(2,1)S(1)}, u32[]{:S(2)}, u32[]{:S(2)}) %all-to-all-start.1) | async-done | bytes 442400 | tf_op jit(solution)/shard_map/all_to_all | solution.py:267
  113.2 3.0 %shard_map.116 = bf16[512,512]{1,0:T(8,128)(2,1)} custom-call(s32[2,384]{1,0:T(2,128)S(1)} %pad_add_fusion.owner, s32[512,1]{1,0:T(8,128)S(1)} %broadcast_in_dim_reshape.5.request, bf16[512,576]{1,0:T(8,128)(2,1)S(1)} %bitcast.46, bf16[384,576]{1,0:T(8,128)(2,1)S(1)} %bitcast.44, bf16[384,576]{1,0:T(8,128)(2,1)S(1)} %bitcast.47), custom_call_target="tpu_custom_call" | custom-call | flops 905969664 | bytes 3483648 | tf_op jit(solution)/shard_map/pallas_call | solution.py:23
  (79 shorter events, 20.6 us)
Async XLA Ops:
  0.6 10.3 %collective-permute-start = (bf16[1,16,3584]{2,1,0:T(8,128)(2,1)}, bf16[1,16,3584]{2,1,0:T(8,128)(2,1)S(1)}, u32[]{:S(2)}, u32[]{:S(2)}) collective-permute-start(bf16[1,16,3584]{2,1,0:T(8,128)(2,1)} %bitcast.49), channel_id=1, source_target_pairs={{0,16},{2,18},{4,20},{6,22},{8,24},{10,26},{12,28},{14,30},{16,0},... | collective-permute-start | bytes 344072 | tf_op jit(solution)/shard_map/ppermute | solution.py:47
  6.5 4.5 %collective-permute-start.1 = (bf16[1,16,128]{2,1,0:T(8,128)(2,1)S(1)}, bf16[1,16,128]{2,1,0:T(8,128)(2,1)S(1)}, u32[]{:S(2)}, u32[]{:S(2)}) collective-permute-start(bf16[1,16,128]{2,1,0:T(8,128)(2,1)S(1)} %fusion.18), channel_id=1, source_target_pairs={{0,16},{2,18},{4,20},{6,22},{8,24},{10,26},{12,28},{14,30},{16,0},... | collective-permute-start | bytes 12296 | tf_op jit(solution)/shard_map/ppermute | solution.py:47
  11.9 8.1 %collective-permute-start.2 = (bf16[2,16,3712]{2,1,0:T(8,128)(2,1)S(1)}, bf16[2,16,3712]{2,1,0:T(8,128)(2,1)S(1)}, u32[]{:S(2)}, u32[]{:S(2)}) collective-permute-start(bf16[2,16,3712]{2,1,0:T(8,128)(2,1)S(1)} %maximum_maximum_fusion), channel_id=1, source_target_pairs={{0,8},{2,10},{4,12},{6,14},{8,0},{10,2},{12,4},{14,6},{16,24},{18,... | collective-permute-start | bytes 712712 | tf_op jit(solution)/shard_map/ppermute | solution.py:47
  14.5 19.9 %all-to-all-start = ((bf16[16,24,576]{2,1,0:T(8,128)(2,1)}), bf16[16,24,576]{2,1,0:T(8,128)(2,1)S(1)}, u32[]{:S(2)}, u32[]{:S(2)}) async-start(bf16[16,24,576]{2,1,0:T(8,128)(2,1)} %bitcast.37), calls=%async_computation | async-start | bytes 983040 | tf_op jit(solution)/shard_map/all_to_all | solution.py:365
  20.9 11.3 %collective-permute-start.3 = (bf16[4,16,1792]{2,1,0:T(8,128)(2,1)S(1)}, bf16[4,16,1792]{2,1,0:T(8,128)(2,1)S(1)}, u32[]{:S(2)}, u32[]{:S(2)}) collective-permute-start(bf16[4,16,1792]{2,1,0:T(8,128)(2,1)S(1)} %pad_maximum_fusion.5), channel_id=1, source_target_pairs={{0,4},{2,6},{4,0},{6,2},{8,12},{10,14},{12,8},{14,10},{16,20},{18,... | collective-permute-start | bytes 688136 | tf_op jit(solution)/shard_map/ppermute | solution.py:47
  23.7 10.3 %collective-permute-start.5 = (bf16[4,16,1920]{2,1,0:T(8,128)(2,1)S(1)}, bf16[4,16,1920]{2,1,0:T(8,128)(2,1)S(1)}, u32[]{:S(2)}, u32[]{:S(2)}) collective-permute-start(bf16[4,16,1920]{2,1,0:T(8,128)(2,1)S(1)} %pad_maximum_fusion.2), channel_id=1, source_target_pairs={{0,2},{2,0},{4,6},{6,4},{8,10},{10,8},{12,14},{14,12},{16,18},{18,... | collective-permute-start | bytes 737288 | tf_op jit(solution)/shard_map/ppermute | solution.py:47
  32.2 12.2 %collective-permute-start.4 = (bf16[8,16,1792]{2,1,0:T(8,128)(2,1)S(1)}, bf16[8,16,1792]{2,1,0:T(8,128)(2,1)}, u32[]{:S(2)}, u32[]{:S(2)}) collective-permute-start(bf16[8,16,1792]{2,1,0:T(8,128)(2,1)S(1)} %pad_maximum_fusion.1), channel_id=1, source_target_pairs={{0,2},{2,0},{4,6},{6,4},{8,10},{10,8},{12,14},{14,12},{16,18},{18,... | collective-permute-start | bytes 1376264 | tf_op jit(solution)/shard_map/ppermute | solution.py:47
  34.4 12.1 %collective-permute-start.6 = (bf16[8,16,1920]{2,1,0:T(8,128)(2,1)S(1)}, bf16[8,16,1920]{2,1,0:T(8,128)(2,1)S(1)}, u32[]{:S(2)}, u32[]{:S(2)}) collective-permute-start(bf16[8,16,1920]{2,1,0:T(8,128)(2,1)S(1)} %pad_maximum_fusion), channel_id=1, source_target_pairs={{0,4},{2,6},{4,0},{6,2},{8,12},{10,14},{12,8},{14,10},{16,20},{18,... | collective-permute-start | bytes 1474568 | tf_op jit(solution)/shard_map/ppermute | solution.py:47
  35.9 9.0 %collective-permute-start.7 = (bf16[16,24,576]{2,1,0:T(8,128)(2,1)S(1)}, bf16[16,24,576]{2,1,0:T(8,128)(2,1)S(1)}, u32[]{:S(2)}, u32[]{:S(2)}) collective-permute-start(bf16[16,24,576]{2,1,0:T(8,128)(2,1)S(1)} %all-to-all-done), channel_id=1, source_target_pairs={{0,1},{1,0},{2,3},{3,2},{4,5},{5,4},{6,7},{7,6},{8,9},{9,8},{10,11... | collective-permute-start | bytes 1327112 | tf_op jit(solution)/shard_map/ppermute | solution.py:52
  36.2 10.5 %collective-permute-start.8 = (bf16[8,16,1792]{2,1,0:T(8,128)(2,1)S(1)}, bf16[8,16,1792]{2,1,0:T(8,128)(2,1)}, u32[]{:S(2)}, u32[]{:S(2)}) collective-permute-start(bf16[8,16,1792]{2,1,0:T(8,128)(2,1)S(1)} %pad_maximum_fusion.1), channel_id=1, source_target_pairs={{0,1},{1,0},{2,3},{3,2},{4,5},{5,4},{6,7},{7,6},{8,9},{9,8},{10,11... | collective-permute-start | bytes 1376264 | tf_op jit(solution)/shard_map/ppermute | solution.py:52
  44.4 2.9 %collective-permute-start.10 = (bf16[8,16,1920]{2,1,0:T(8,128)(2,1)S(1)}, bf16[8,16,1920]{2,1,0:T(8,128)(2,1)S(1)}, u32[]{:S(2)}, u32[]{:S(2)}) collective-permute-start(bf16[8,16,1920]{2,1,0:T(8,128)(2,1)S(1)} %pad_maximum_fusion), channel_id=1, source_target_pairs={{0,1},{1,0},{2,3},{3,2},{4,5},{5,4},{6,7},{7,6},{8,9},{9,8},{10,11... | collective-permute-start | bytes 1474568 | tf_op jit(solution)/shard_map/ppermute | solution.py:52
  44.4 2.8 %collective-permute-start.9 = (bf16[8,16,1792]{2,1,0:T(8,128)(2,1)}, bf16[8,16,1792]{2,1,0:T(8,128)(2,1)}, u32[]{:S(2)}, u32[]{:S(2)}) collective-permute-start(bf16[8,16,1792]{2,1,0:T(8,128)(2,1)} %collective-permute-done.4), channel_id=1, source_target_pairs={{0,1},{1,0},{2,3},{3,2},{4,5},{5,4},{6,7},{7,6},{8,9},{9,8},{10,11... | collective-permute-start | bytes 1376264 | tf_op jit(solution)/shard_map/ppermute | solution.py:52
  46.5 1.9 %collective-permute-start.11 = (bf16[8,16,1920]{2,1,0:T(8,128)(2,1)S(1)}, bf16[8,16,1920]{2,1,0:T(8,128)(2,1)S(1)}, u32[]{:S(2)}, u32[]{:S(2)}) collective-permute-start(bf16[8,16,1920]{2,1,0:T(8,128)(2,1)S(1)} %collective-permute-done.6), channel_id=1, source_target_pairs={{0,1},{1,0},{2,3},{3,2},{4,5},{5,4},{6,7},{7,6},{8,9},{9,8},{10,11... | collective-permute-start | bytes 1474568 | tf_op jit(solution)/shard_map/ppermute | solution.py:52
  57.7 55.4 %copy-start.1 = (bf16[16,32,576]{2,1,0:T(8,128)(2,1)S(1)}, bf16[16,32,576]{2,1,0:T(8,128)(2,1)}, u32[]{:S(2)}) copy-start(bf16[16,32,576]{2,1,0:T(8,128)(2,1)} %param.15) | copy-start | bytes 1769476
  63.0 2.9 %collective-permute-start.15 = (bf16[256,1792]{1,0:T(8,128)(2,1)}, bf16[256,1792]{1,0:T(8,128)(2,1)}, u32[]{:S(2)}, u32[]{:S(2)}) collective-permute-start(bf16[256,1792]{1,0:T(8,128)(2,1)} %get-tuple-element.26), channel_id=1, source_target_pairs={{0,1},{1,0},{2,3},{3,2},{4,5},{5,4},{6,7},{7,6},{8,9},{9,8},{10,11... | collective-permute-start | bytes 2752520 | tf_op jit(solution)/shard_map/ppermute | solution.py:52
  63.2 5.0 %collective-permute-start.12 = (bf16[256,1792]{1,0:T(8,128)(2,1)}, bf16[256,1792]{1,0:T(8,128)(2,1)}, u32[]{:S(2)}, u32[]{:S(2)}) collective-permute-start(bf16[256,1792]{1,0:T(8,128)(2,1)} %get-tuple-element.24), channel_id=1, source_target_pairs={{0,1},{1,0},{2,3},{3,2},{4,5},{5,4},{6,7},{7,6},{8,9},{9,8},{10,11... | collective-permute-start | bytes 2752520 | tf_op jit(solution)/shard_map/ppermute | solution.py:52
  67.3 12.6 %collective-permute-start.16 = (bf16[128,1792]{1,0:T(8,128)(2,1)S(1)}, bf16[128,1792]{1,0:T(8,128)(2,1)S(1)}, u32[]{:S(2)}, u32[]{:S(2)}) collective-permute-start(bf16[128,1792]{1,0:T(8,128)(2,1)S(1)} %get-tuple-element.38), channel_id=1, source_target_pairs={{0,4},{2,6},{4,0},{6,2},{8,12},{10,14},{12,8},{14,10},{16,20},{18,... | collective-permute-start | bytes 1376264 | tf_op jit(solution)/shard_map/ppermute | solution.py:47
  69.6 12.3 %collective-permute-start.13 = (bf16[128,1792]{1,0:T(8,128)(2,1)S(1)}, bf16[128,1792]{1,0:T(8,128)(2,1)S(1)}, u32[]{:S(2)}, u32[]{:S(2)}) collective-permute-start(bf16[128,1792]{1,0:T(8,128)(2,1)S(1)} %get-tuple-element.36), channel_id=1, source_target_pairs={{0,2},{2,0},{4,6},{6,4},{8,10},{10,8},{12,14},{14,12},{16,18},{18,... | collective-permute-start | bytes 1376264 | tf_op jit(solution)/shard_map/ppermute | solution.py:47
  80.0 6.9 %collective-permute-start.17 = (bf16[64,1792]{1,0:T(8,128)(2,1)S(1)}, bf16[64,1792]{1,0:T(8,128)(2,1)S(1)}, u32[]{:S(2)}, u32[]{:S(2)}) collective-permute-start(bf16[64,1792]{1,0:T(8,128)(2,1)S(1)} %get-tuple-element.42), channel_id=1, source_target_pairs={{0,2},{2,0},{4,6},{6,4},{8,10},{10,8},{12,14},{14,12},{16,18},{18,... | collective-permute-start | bytes 688136 | tf_op jit(solution)/shard_map/ppermute | solution.py:47
  82.1 6.6 %collective-permute-start.14 = (bf16[64,1792]{1,0:T(8,128)(2,1)S(1)}, bf16[64,1792]{1,0:T(8,128)(2,1)S(1)}, u32[]{:S(2)}, u32[]{:S(2)}) collective-permute-start(bf16[64,1792]{1,0:T(8,128)(2,1)S(1)} %get-tuple-element.40), channel_id=1, source_target_pairs={{0,4},{2,6},{4,0},{6,2},{8,12},{10,14},{12,8},{14,10},{16,20},{18,... | collective-permute-start | bytes 688136 | tf_op jit(solution)/shard_map/ppermute | solution.py:47
  88.7 7.5 %collective-permute-start.18 = (bf16[32,3584]{1,0:T(8,128)(2,1)S(1)}, bf16[32,3584]{1,0:T(8,128)(2,1)S(1)}, u32[]{:S(2)}, u32[]{:S(2)}) collective-permute-start(bf16[32,3584]{1,0:T(8,128)(2,1)S(1)} %pad_maximum_fusion.6), channel_id=1, source_target_pairs={{0,8},{2,10},{4,12},{6,14},{8,0},{10,2},{12,4},{14,6},{16,24},{18,... | collective-permute-start | bytes 688136 | tf_op jit(solution)/shard_map/ppermute | solution.py:47
  90.0 21.3 %all-to-all-start.1 = ((bf16[16,24,576]{2,1,0:T(8,128)(2,1)}), bf16[16,24,576]{2,1,0:T(8,128)(2,1)S(1)}, u32[]{:S(2)}, u32[]{:S(2)}) async-start(bf16[16,24,576]{2,1,0:T(8,128)(2,1)} %bitcast.8), calls=%async_computation.1 | async-start | bytes 983040 | tf_op jit(solution)/shard_map/all_to_all | solution.py:267
  96.2 15.8 %collective-permute-start.19 = (bf16[16,3584]{1,0:T(8,128)(2,1)S(1)}, bf16[16,3584]{1,0:T(8,128)(2,1)S(1)}, u32[]{:S(2)}, u32[]{:S(2)}) collective-permute-start(bf16[16,3584]{1,0:T(8,128)(2,1)S(1)} %add_convert_fusion.9), channel_id=1, source_target_pairs={{0,16},{2,18},{4,20},{6,22},{8,24},{10,26},{12,28},{14,30},{16,0},... | collective-permute-start | bytes 344072 | tf_op jit(solution)/shard_map/ppermute | solution.py:47
  111.3 1.9 %collective-permute-start.20 = (bf16[16,24,576]{2,1,0:T(8,128)(2,1)S(1)}, bf16[16,24,576]{2,1,0:T(8,128)(2,1)S(1)}, u32[]{:S(2)}, u32[]{:S(2)}) collective-permute-start(bf16[16,24,576]{2,1,0:T(8,128)(2,1)S(1)} %all-to-all-done.1), channel_id=1, source_target_pairs={{0,1},{1,0},{2,3},{3,2},{4,5},{5,4},{6,7},{7,6},{8,9},{9,8},{10,11... | collective-permute-start | bytes 1327112 | tf_op jit(solution)/shard_map/ppermute | solution.py:52
  (3 other events, 77.4 us)

commit v9 on v8

--- a/solution.py
+++ b/solution.py
@@ -200,14 +200,14 @@
     parts = len(spots)
     tp_size = lax.axis_size("tp")
     cut = weight.shape[0] // tp_size // parts
-    width = 256 if cut % 256 == 0 else 128
+    width = cut
     shape = jax.ShapeDtypeStruct((hidden.shape[0], cut), jnp.bfloat16)
     outs = kernel_call(
         functools.partial(down_kernel, spots, tp_size, cut, width, rows),
         [shape] * (parts * tp_size),
         [hidden, weight],
         flops=2 * hidden.size * weight.shape[0],
-        spare=weight.size * 2 + (4 << 20),
+        spare=weight.size * 2 + (8 << 20),
         in_specs=[WHOLE, pl.BlockSpec(memory_space=pl.ANY)],
         scratch_shapes=[
             pltpu.VMEM(weight.shape, weight.dtype),
@@ -369,10 +369,10 @@
         return sent
 
     halves = gather_rows(tokens, gates, orders, ends, beside_shared, ahead_of_last)
-    last_sent, last_late = halves[-1]
+    last_sent = halves[-1][0]
     ordered = cache_turn(held["spread"], block_source, slot_total)
-    last_late, ordered = lax.optimization_barrier((last_late, ordered))
-    halves[-1] = (last_sent, last_late)
+    first_late, ordered = lax.optimization_barrier((halves[0][1], ordered))
+    halves[0] = (halves[0][0], first_late)
     places = [places_of(order) for order in orders]
     to_first = [[places[0].index(place) for place in own] for own in places]
     from_first = [[own.index(place) for place in places[0]] for own in places]
@@ -410,7 +410,7 @@
         return sent
 
     def beside_third_sum(sent):
-        near = tie(held["keys"], sent)
+        sent, near = lax.optimization_barrier((sent, held["keys"]))
         held["keys"] = [near] + swap_tp(near)
         return sent
 

time: 117 us -> 113 us (0.966); the launches traced: 116 us -> 111 us
  waiting for transfers between devices: 50.4 us -> 42.5 us
  other arithmetic: 7.43 us -> 11.2 us
  starting transfers between devices: 34.3 us -> 32.9 us
    all_to_all x1, waiting for transfers between devices: 11.7 us -> 0.01 us  [cache_in(): lax.all_to_all(ordered, 'ep', split_axis=0, concat_axis=0, tiled=True)]
    convert_element_type x8, other arithmetic: 3.86 us -> 7.67 us  [add_up(): return total.astype(jnp.bfloat16)]
    all_to_all x1, waiting for transfers between devices: 0.39 us -> 2.26 us  [beside_shared(): lax.all_to_all(pieces, 'ep', split_axis=0, concat_axis=0, tiled=True)]
    ppermute x8, waiting for transfers between devices: 4.37 us -> 5.88 us  [pass_tp(): lax.ppermute(value, 'tp', [(index, (index + step) % tp_size) for index in...]
    ppermute x13, starting transfers between devices: 20.9 us -> 19.5 us  [exchange(): lax.ppermute(value, 'ep', [(index, index ^ bit) for index in range(ep_siz...]
  transfers between devices with their start and end apart: 23 -> 23, of which waited for: 15 -> 14; matrix products, arithmetic and copies ran while one was open for 9% -> 13% of each run, Pallas kernels for 1% -> 1%
where the time goes in v9:
time: 113 us; the launch traced here: 111 us
  waiting for transfers between devices  42.5 us (38%)
  starting transfers between devices  32.9 us (29%)
  other arithmetic  11.2 us (10%)
  Pallas kernels  11.1 us (10%)
  matrix products  7.78 us (7%)
  local copies, waits for them, and re-layouts  4.19 us (4%)
    ppermute x13, waiting for transfers between devices, exchange(): lax.ppermute(value, 'ep', [(index, index ^ bit) for index in range(ep_siz...  34.3 us
    ppermute x13, starting transfers between devices, exchange(): lax.ppermute(value, 'ep', [(index, index ^ bit) for index in range(ep_siz...  19.5 us
    pallas_call x4, Pallas kernels, kernel_call(): pl.pallas_call(kernel, out_shape=out_shape, in_specs=in_specs or [WHOLE]...  11.1 us
    dot_general x1, matrix products, body(): jnp.einsum('sd,dgf->sgf', all_rows, expert_gate_up[0], preferred_element_...  7.78 us
    convert_element_type x8, other arithmetic, add_up(): return total.astype(jnp.bfloat16)  7.67 us
    all_to_all x1, starting transfers between devices, cache_in(): lax.all_to_all(ordered, 'ep', split_axis=0, concat_axis=0, tiled=True)  6.09 us
    ppermute x8, waiting for transfers between devices, pass_tp(): lax.ppermute(value, 'tp', [(index, (index + step) % tp_size) for index in...  5.88 us
    all_to_all x1, starting transfers between devices, beside_shared(): lax.all_to_all(pieces, 'ep', split_axis=0, concat_axis=0, tiled=True)  5.54 us
  transfers between devices with their start and end apart: 23, of which 14 were waited for; matrix products, arithmetic and copies ran while one was open for 13% of the time, Pallas kernels for 1%

profile of v9, /device:TPU:0, one launch (start us, length us, event | category | flops | bytes accessed | tf_op | source)
XLA Modules:
  0.0 110.6 jit_solution(1571088101844343385)
XLA Ops:
  0.6 4.1 %collective-permute-start = (bf16[1,16,3584]{2,1,0:T(8,128)(2,1)}, bf16[1,16,3584]{2,1,0:T(8,128)(2,1)S(1)}, u32[]{:S(2)}, u32[]{:S(2)}) collective-permute-start(bf16[1,16,3584]{2,1,0:T(8,128)(2,1)} %bitcast.49), channel_id=1, source_target_pairs={{0,16},{2,18},{4,20},{6,22},{8,24},{10,26},{12,28},{14,30},{16,0},... | collective-permute-start | bytes 344072 | tf_op jit(solution)/shard_map/ppermute | solution.py:47
  6.6 4.4 %collective-permute-done.1 = bf16[1,16,128]{2,1,0:T(8,128)(2,1)S(1)} collective-permute-done((bf16[1,16,128]{2,1,0:T(8,128)(2,1)S(1)}, bf16[1,16,128]{2,1,0:T(8,128)(2,1)S(1)}, u32[]{:S(2)}, u32[]{:S(2)}) %collective-permute-start.1) | collective-permute-done | bytes 4128 | tf_op jit(solution)/shard_map/ppermute | solution.py:47
  11.9 1.6 %collective-permute-start.2 = (bf16[2,16,3712]{2,1,0:T(8,128)(2,1)S(1)}, bf16[2,16,3712]{2,1,0:T(8,128)(2,1)S(1)}, u32[]{:S(2)}, u32[]{:S(2)}) collective-permute-start(bf16[2,16,3712]{2,1,0:T(8,128)(2,1)S(1)} %maximum_maximum_fusion), channel_id=1, source_target_pairs={{0,8},{2,10},{4,12},{6,14},{8,0},{10,2},{12,4},{14,6},{16,24},{18,... | collective-permute-start | bytes 712712 | tf_op jit(solution)/shard_map/ppermute | solution.py:47
  14.5 5.5 %all-to-all-start = ((bf16[16,24,576]{2,1,0:T(8,128)(2,1)}), bf16[16,24,576]{2,1,0:T(8,128)(2,1)S(1)}, u32[]{:S(2)}, u32[]{:S(2)}) async-start(bf16[16,24,576]{2,1,0:T(8,128)(2,1)} %bitcast.37), calls=%async_computation | async-start | bytes 983040 | tf_op jit(solution)/shard_map/all_to_all | solution.py:365
  20.9 2.0 %collective-permute-start.5 = (bf16[4,16,1920]{2,1,0:T(8,128)(2,1)S(1)}, bf16[4,16,1920]{2,1,0:T(8,128)(2,1)S(1)}, u32[]{:S(2)}, u32[]{:S(2)}) collective-permute-start(bf16[4,16,1920]{2,1,0:T(8,128)(2,1)S(1)} %pad_maximum_fusion.2), channel_id=1, source_target_pairs={{0,2},{2,0},{4,6},{6,4},{8,10},{10,8},{12,14},{14,12},{16,18},{18,... | collective-permute-start | bytes 737288 | tf_op jit(solution)/shard_map/ppermute | solution.py:47
  26.6 5.7 %collective-permute-done.5 = bf16[4,16,1920]{2,1,0:T(8,128)(2,1)S(1)} collective-permute-done((bf16[4,16,1920]{2,1,0:T(8,128)(2,1)S(1)}, bf16[4,16,1920]{2,1,0:T(8,128)(2,1)S(1)}, u32[]{:S(2)}, u32[]{:S(2)}) %collective-permute-start.5) | collective-permute-done | bytes 245792 | tf_op jit(solution)/shard_map/ppermute | solution.py:47
  32.3 2.3 %all-to-all-done = bf16[16,24,576]{2,1,0:T(8,128)(2,1)S(1)} async-done(((bf16[16,24,576]{2,1,0:T(8,128)(2,1)}), bf16[16,24,576]{2,1,0:T(8,128)(2,1)S(1)}, u32[]{:S(2)}, u32[]{:S(2)}) %all-to-all-start) | async-done | bytes 442400 | tf_op jit(solution)/shard_map/all_to_all | solution.py:365
  37.9 1.6 %shard_map.113 = bf16[384,576]{1,0:T(8,128)(2,1)} custom-call(s32[384,2]{1,0:T(8,128)S(1)} %fusion.7.index, bf16[384,576]{1,0:T(8,128)(2,1)S(1)} %bitcast.39, bf16[384,576]{1,0:T(8,128)(2,1)S(1)} %bitcast.45), custom_call_target="tpu_custom_call" | custom-call | flops 339738624 | bytes 2217984 | tf_op jit(solution)/shard_map/pallas_call | solution.py:23
  39.4 5.9 %collective-permute-done.4 = bf16[8,16,1792]{2,1,0:T(8,128)(2,1)} collective-permute-done((bf16[8,16,1792]{2,1,0:T(8,128)(2,1)S(1)}, bf16[8,16,1792]{2,1,0:T(8,128)(2,1)}, u32[]{:S(2)}, u32[]{:S(2)}) %collective-permute-start.4) | collective-permute-done | bytes 458784 | tf_op jit(solution)/shard_map/ppermute | solution.py:47
  46.1 2.0 %collective-permute-done.9 = bf16[8,16,1792]{2,1,0:T(8,128)(2,1)} collective-permute-done((bf16[8,16,1792]{2,1,0:T(8,128)(2,1)}, bf16[8,16,1792]{2,1,0:T(8,128)(2,1)}, u32[]{:S(2)}, u32[]{:S(2)}) %collective-permute-start.9) | collective-permute-done | bytes 458784 | tf_op jit(solution)/shard_map/ppermute | solution.py:52
  50.1 7.8 %fusion = f32[256,2,512]{2,0,1:T(8,128)S(1)} fusion(bf16[7168,2,512]{2,1,0:T(2,128)(2,1)} %bitcast.53, bf16[256,7168]{1,0:T(8,128)(2,1)S(1)} %shard_map.114), kind=kOutput, calls=%fused_computation | convolution fusion | flops 3758096384 | bytes 19398656 | tf_op jit(solution)/shard_map/sd,dgf->sgf/dot_general | solution.py:394
  58.1 5.0 %shard_map.115 = (bf16[256,1792]{1,0:T(8,128)(2,1)}, bf16[256,1792]{1,0:T(8,128)(2,1)}, bf16[256,1792]{1,0:T(8,128)(2,1)S(1)}, bf16[256,1792]{1,0:T(8,128)(2,1)S(1)}) custom-call(bf16[256,512]{1,0:T(8,128)(2,1)S(1)} %fusion.5.hidden, bf16[7168,512]{1,0:T(8,128)(2,1)} %bitcast.48), custom_call_target="tpu_custom_call" | custom-call | flops 1879048192 | bytes 11534336 | tf_op jit(solution)/shard_map/pallas_call | solution.py:23
  63.7 2.3 %collective-permute-done.15 = bf16[256,1792]{1,0:T(8,128)(2,1)} collective-permute-done((bf16[256,1792]{1,0:T(8,128)(2,1)}, bf16[256,1792]{1,0:T(8,128)(2,1)}, u32[]{:S(2)}, u32[]{:S(2)}) %collective-permute-start.15) | collective-permute-done | bytes 917536 | tf_op jit(solution)/shard_map/ppermute | solution.py:52
  66.0 2.3 %add_convert_fusion.1 = (bf16[128,1792]{1,0:T(8,128)(2,1)}, bf16[128,1792]{1,0:T(8,128)(2,1)}) fusion(bf16[256,1792]{1,0:T(8,128)(2,1)} %collective-permute-done.15, bf16[256,1792]{1,0:T(8,128)(2,1)S(1)} %get-tuple-element.26), kind=kLoop, calls=%fused_computation.4 | loop fusion | flops 1835008 | bytes 2752512 | tf_op jit(solution)/shard_map/convert_element_type | solution.py:151
  69.1 2.2 %add_convert_fusion.3 = (bf16[128,1792]{1,0:T(8,128)(2,1)S(1)}, bf16[128,1792]{1,0:T(8,128)(2,1)}) fusion(bf16[256,1792]{1,0:T(8,128)(2,1)} %collective-permute-done.12, bf16[256,1792]{1,0:T(8,128)(2,1)S(1)} %get-tuple-element.24), kind=kLoop, calls=%fused_computation.6 | loop fusion | flops 1835008 | bytes 2752512 | tf_op jit(solution)/shard_map/convert_element_type | solution.py:151
  72.2 6.1 %all-to-all-start.1 = ((bf16[16,24,576]{2,1,0:T(8,128)(2,1)}), bf16[16,24,576]{2,1,0:T(8,128)(2,1)S(1)}, u32[]{:S(2)}, u32[]{:S(2)}) async-start(bf16[16,24,576]{2,1,0:T(8,128)(2,1)} %bitcast.6), calls=%async_computation.1 | async-start | bytes 983040 | tf_op jit(solution)/shard_map/all_to_all | solution.py:267
  78.3 3.5 %collective-permute-done.16 = bf16[128,1792]{1,0:T(8,128)(2,1)S(1)} collective-permute-done((bf16[128,1792]{1,0:T(8,128)(2,1)}, bf16[128,1792]{1,0:T(8,128)(2,1)S(1)}, u32[]{:S(2)}, u32[]{:S(2)}) %collective-permute-start.16) | collective-permute-done | bytes 458784 | tf_op jit(solution)/shard_map/ppermute | solution.py:47
  84.0 3.0 %collective-permute-done.13 = bf16[128,1792]{1,0:T(8,128)(2,1)} collective-permute-done((bf16[128,1792]{1,0:T(8,128)(2,1)}, bf16[128,1792]{1,0:T(8,128)(2,1)}, u32[]{:S(2)}, u32[]{:S(2)}) %collective-permute-start.13) | collective-permute-done | bytes 458784 | tf_op jit(solution)/shard_map/ppermute | solution.py:47
  89.6 4.4 %collective-permute-done.17 = bf16[64,1792]{1,0:T(8,128)(2,1)S(1)} collective-permute-done((bf16[64,1792]{1,0:T(8,128)(2,1)S(1)}, bf16[64,1792]{1,0:T(8,128)(2,1)S(1)}, u32[]{:S(2)}, u32[]{:S(2)}) %collective-permute-start.17) | collective-permute-done | bytes 229408 | tf_op jit(solution)/shard_map/ppermute | solution.py:47
  94.7 1.8 %collective-permute-start.18 = (bf16[32,3584]{1,0:T(8,128)(2,1)S(1)}, bf16[32,3584]{1,0:T(8,128)(2,1)S(1)}, u32[]{:S(2)}, u32[]{:S(2)}) collective-permute-start(bf16[32,3584]{1,0:T(8,128)(2,1)S(1)} %pad_maximum_fusion.6), channel_id=1, source_target_pairs={{0,8},{2,10},{4,12},{6,14},{8,0},{10,2},{12,4},{14,6},{16,24},{18,... | collective-permute-start | bytes 688136 | tf_op jit(solution)/shard_map/ppermute | solution.py:47
  96.5 4.6 %collective-permute-done.18 = bf16[32,3584]{1,0:T(8,128)(2,1)S(1)} collective-permute-done((bf16[32,3584]{1,0:T(8,128)(2,1)S(1)}, bf16[32,3584]{1,0:T(8,128)(2,1)S(1)}, u32[]{:S(2)}, u32[]{:S(2)}) %collective-permute-start.18) | collective-permute-done | bytes 229408 | tf_op jit(solution)/shard_map/ppermute | solution.py:47
  101.1 2.8 %collective-permute-start.19 = (bf16[16,3584]{1,0:T(8,128)(2,1)S(1)}, bf16[16,3584]{1,0:T(8,128)(2,1)S(1)}, u32[]{:S(2)}, u32[]{:S(2)}) collective-permute-start(bf16[16,3584]{1,0:T(8,128)(2,1)S(1)} %add_convert_fusion.9), channel_id=1, source_target_pairs={{0,16},{2,18},{4,20},{6,22},{8,24},{10,26},{12,28},{14,30},{16,0},... | collective-permute-start | bytes 344072 | tf_op jit(solution)/shard_map/ppermute | solution.py:47
  104.5 2.4 %collective-permute-done.19 = bf16[16,3584]{1,0:T(8,128)(2,1)S(1)} collective-permute-done((bf16[16,3584]{1,0:T(8,128)(2,1)S(1)}, bf16[16,3584]{1,0:T(8,128)(2,1)S(1)}, u32[]{:S(2)}, u32[]{:S(2)}) %collective-permute-start.19) | collective-permute-done | bytes 114720 | tf_op jit(solution)/shard_map/ppermute | solution.py:47
  107.6 3.0 %shard_map.116 = bf16[512,512]{1,0:T(8,128)(2,1)} custom-call(s32[2,384]{1,0:T(2,128)S(1)} %pad_add_fusion.owner, s32[512,1]{1,0:T(8,128)S(1)} %broadcast_in_dim_reshape.5.request, bf16[512,576]{1,0:T(8,128)(2,1)S(1)} %bitcast.46, bf16[384,576]{1,0:T(8,128)(2,1)S(1)} %bitcast.44, bf16[384,576]{1,0:T(8,128)(2,1)S(1)} %bitcast.47), custom_call_target="tpu_custom_call" | custom-call | flops 905969664 | bytes 3483648 | tf_op jit(solution)/shard_map/pallas_call | solution.py:23
  (79 shorter events, 23.4 us)
Async XLA Ops:
  0.6 10.3 %collective-permute-start = (bf16[1,16,3584]{2,1,0:T(8,128)(2,1)}, bf16[1,16,3584]{2,1,0:T(8,128)(2,1)S(1)}, u32[]{:S(2)}, u32[]{:S(2)}) collective-permute-start(bf16[1,16,3584]{2,1,0:T(8,128)(2,1)} %bitcast.49), channel_id=1, source_target_pairs={{0,16},{2,18},{4,20},{6,22},{8,24},{10,26},{12,28},{14,30},{16,0},... | collective-permute-start | bytes 344072 | tf_op jit(solution)/shard_map/ppermute | solution.py:47
  6.5 4.5 %collective-permute-start.1 = (bf16[1,16,128]{2,1,0:T(8,128)(2,1)S(1)}, bf16[1,16,128]{2,1,0:T(8,128)(2,1)S(1)}, u32[]{:S(2)}, u32[]{:S(2)}) collective-permute-start(bf16[1,16,128]{2,1,0:T(8,128)(2,1)S(1)} %fusion.18), channel_id=1, source_target_pairs={{0,16},{2,18},{4,20},{6,22},{8,24},{10,26},{12,28},{14,30},{16,0},... | collective-permute-start | bytes 12296 | tf_op jit(solution)/shard_map/ppermute | solution.py:47
  11.9 8.1 %collective-permute-start.2 = (bf16[2,16,3712]{2,1,0:T(8,128)(2,1)S(1)}, bf16[2,16,3712]{2,1,0:T(8,128)(2,1)S(1)}, u32[]{:S(2)}, u32[]{:S(2)}) collective-permute-start(bf16[2,16,3712]{2,1,0:T(8,128)(2,1)S(1)} %maximum_maximum_fusion), channel_id=1, source_target_pairs={{0,8},{2,10},{4,12},{6,14},{8,0},{10,2},{12,4},{14,6},{16,24},{18,... | collective-permute-start | bytes 712712 | tf_op jit(solution)/shard_map/ppermute | solution.py:47
  14.5 20.1 %all-to-all-start = ((bf16[16,24,576]{2,1,0:T(8,128)(2,1)}), bf16[16,24,576]{2,1,0:T(8,128)(2,1)S(1)}, u32[]{:S(2)}, u32[]{:S(2)}) async-start(bf16[16,24,576]{2,1,0:T(8,128)(2,1)} %bitcast.37), calls=%async_computation | async-start | bytes 983040 | tf_op jit(solution)/shard_map/all_to_all | solution.py:365
  20.9 11.3 %collective-permute-start.5 = (bf16[4,16,1920]{2,1,0:T(8,128)(2,1)S(1)}, bf16[4,16,1920]{2,1,0:T(8,128)(2,1)S(1)}, u32[]{:S(2)}, u32[]{:S(2)}) collective-permute-start(bf16[4,16,1920]{2,1,0:T(8,128)(2,1)S(1)} %pad_maximum_fusion.2), channel_id=1, source_target_pairs={{0,2},{2,0},{4,6},{6,4},{8,10},{10,8},{12,14},{14,12},{16,18},{18,... | collective-permute-start | bytes 737288 | tf_op jit(solution)/shard_map/ppermute | solution.py:47
  25.0 10.3 %collective-permute-start.3 = (bf16[4,16,1792]{2,1,0:T(8,128)(2,1)S(1)}, bf16[4,16,1792]{2,1,0:T(8,128)(2,1)S(1)}, u32[]{:S(2)}, u32[]{:S(2)}) collective-permute-start(bf16[4,16,1792]{2,1,0:T(8,128)(2,1)S(1)} %pad_maximum_fusion.5), channel_id=1, source_target_pairs={{0,4},{2,6},{4,0},{6,2},{8,12},{10,14},{12,8},{14,10},{16,20},{18,... | collective-permute-start | bytes 688136 | tf_op jit(solution)/shard_map/ppermute | solution.py:47
  34.5 11.3 %collective-permute-start.7 = (bf16[8,16,1920]{2,1,0:T(8,128)(2,1)S(1)}, bf16[8,16,1920]{2,1,0:T(8,128)(2,1)S(1)}, u32[]{:S(2)}, u32[]{:S(2)}) collective-permute-start(bf16[8,16,1920]{2,1,0:T(8,128)(2,1)S(1)} %pad_maximum_fusion), channel_id=1, source_target_pairs={{0,4},{2,6},{4,0},{6,2},{8,12},{10,14},{12,8},{14,10},{16,20},{18,... | collective-permute-start | bytes 1474568 | tf_op jit(solution)/shard_map/ppermute | solution.py:47
  35.4 10.0 %collective-permute-start.4 = (bf16[8,16,1792]{2,1,0:T(8,128)(2,1)S(1)}, bf16[8,16,1792]{2,1,0:T(8,128)(2,1)}, u32[]{:S(2)}, u32[]{:S(2)}) collective-permute-start(bf16[8,16,1792]{2,1,0:T(8,128)(2,1)S(1)} %pad_maximum_fusion.1), channel_id=1, source_target_pairs={{0,2},{2,0},{4,6},{6,4},{8,10},{10,8},{12,14},{14,12},{16,18},{18,... | collective-permute-start | bytes 1376264 | tf_op jit(solution)/shard_map/ppermute | solution.py:47
  36.0 1.9 %collective-permute-start.6 = (bf16[16,24,576]{2,1,0:T(8,128)(2,1)S(1)}, bf16[16,24,576]{2,1,0:T(8,128)(2,1)S(1)}, u32[]{:S(2)}, u32[]{:S(2)}) collective-permute-start(bf16[16,24,576]{2,1,0:T(8,128)(2,1)S(1)} %all-to-all-done), channel_id=1, source_target_pairs={{0,1},{1,0},{2,3},{3,2},{4,5},{5,4},{6,7},{7,6},{8,9},{9,8},{10,11... | collective-permute-start | bytes 1327112 | tf_op jit(solution)/shard_map/ppermute | solution.py:52
  36.2 9.9 %collective-permute-start.8 = (bf16[8,16,1792]{2,1,0:T(8,128)(2,1)S(1)}, bf16[8,16,1792]{2,1,0:T(8,128)(2,1)}, u32[]{:S(2)}, u32[]{:S(2)}) collective-permute-start(bf16[8,16,1792]{2,1,0:T(8,128)(2,1)S(1)} %pad_maximum_fusion.1), channel_id=1, source_target_pairs={{0,1},{1,0},{2,3},{3,2},{4,5},{5,4},{6,7},{7,6},{8,9},{9,8},{10,11... | collective-permute-start | bytes 1376264 | tf_op jit(solution)/shard_map/ppermute | solution.py:52
  45.3 2.8 %collective-permute-start.9 = (bf16[8,16,1792]{2,1,0:T(8,128)(2,1)}, bf16[8,16,1792]{2,1,0:T(8,128)(2,1)}, u32[]{:S(2)}, u32[]{:S(2)}) collective-permute-start(bf16[8,16,1792]{2,1,0:T(8,128)(2,1)} %collective-permute-done.4), channel_id=1, source_target_pairs={{0,1},{1,0},{2,3},{3,2},{4,5},{5,4},{6,7},{7,6},{8,9},{9,8},{10,11... | collective-permute-start | bytes 1376264 | tf_op jit(solution)/shard_map/ppermute | solution.py:52
  45.3 2.8 %collective-permute-start.10 = (bf16[8,16,1920]{2,1,0:T(8,128)(2,1)S(1)}, bf16[8,16,1920]{2,1,0:T(8,128)(2,1)S(1)}, u32[]{:S(2)}, u32[]{:S(2)}) collective-permute-start(bf16[8,16,1920]{2,1,0:T(8,128)(2,1)S(1)} %pad_maximum_fusion), channel_id=1, source_target_pairs={{0,1},{1,0},{2,3},{3,2},{4,5},{5,4},{6,7},{7,6},{8,9},{9,8},{10,11... | collective-permute-start | bytes 1474568 | tf_op jit(solution)/shard_map/ppermute | solution.py:52
  45.9 2.7 %collective-permute-start.11 = (bf16[8,16,1920]{2,1,0:T(8,128)(2,1)S(1)}, bf16[8,16,1920]{2,1,0:T(8,128)(2,1)S(1)}, u32[]{:S(2)}, u32[]{:S(2)}) collective-permute-start(bf16[8,16,1920]{2,1,0:T(8,128)(2,1)S(1)} %collective-permute-done.7), channel_id=1, source_target_pairs={{0,1},{1,0},{2,3},{3,2},{4,5},{5,4},{6,7},{7,6},{8,9},{9,8},{10,11... | collective-permute-start | bytes 1474568 | tf_op jit(solution)/shard_map/ppermute | solution.py:52
  57.9 49.7 %copy-start.1 = (bf16[16,32,576]{2,1,0:T(8,128)(2,1)S(1)}, bf16[16,32,576]{2,1,0:T(8,128)(2,1)}, u32[]{:S(2)}) copy-start(bf16[16,32,576]{2,1,0:T(8,128)(2,1)} %param.15) | copy-start | bytes 1769476
  63.2 2.9 %collective-permute-start.15 = (bf16[256,1792]{1,0:T(8,128)(2,1)}, bf16[256,1792]{1,0:T(8,128)(2,1)}, u32[]{:S(2)}, u32[]{:S(2)}) collective-permute-start(bf16[256,1792]{1,0:T(8,128)(2,1)} %get-tuple-element.27), channel_id=1, source_target_pairs={{0,1},{1,0},{2,3},{3,2},{4,5},{5,4},{6,7},{7,6},{8,9},{9,8},{10,11... | collective-permute-start | bytes 2752520 | tf_op jit(solution)/shard_map/ppermute | solution.py:52
  63.4 5.8 %collective-permute-start.12 = (bf16[256,1792]{1,0:T(8,128)(2,1)}, bf16[256,1792]{1,0:T(8,128)(2,1)}, u32[]{:S(2)}, u32[]{:S(2)}) collective-permute-start(bf16[256,1792]{1,0:T(8,128)(2,1)} %get-tuple-element.25), channel_id=1, source_target_pairs={{0,1},{1,0},{2,3},{3,2},{4,5},{5,4},{6,7},{7,6},{8,9},{9,8},{10,11... | collective-permute-start | bytes 2752520 | tf_op jit(solution)/shard_map/ppermute | solution.py:52
  68.4 13.4 %collective-permute-start.16 = (bf16[128,1792]{1,0:T(8,128)(2,1)}, bf16[128,1792]{1,0:T(8,128)(2,1)S(1)}, u32[]{:S(2)}, u32[]{:S(2)}) collective-permute-start(bf16[128,1792]{1,0:T(8,128)(2,1)} %get-tuple-element.40), channel_id=1, source_target_pairs={{0,4},{2,6},{4,0},{6,2},{8,12},{10,14},{12,8},{14,10},{16,20},{18,... | collective-permute-start | bytes 1376264 | tf_op jit(solution)/shard_map/ppermute | solution.py:47
  71.3 15.7 %collective-permute-start.13 = (bf16[128,1792]{1,0:T(8,128)(2,1)}, bf16[128,1792]{1,0:T(8,128)(2,1)}, u32[]{:S(2)}, u32[]{:S(2)}) collective-permute-start(bf16[128,1792]{1,0:T(8,128)(2,1)} %get-tuple-element.38), channel_id=1, source_target_pairs={{0,2},{2,0},{4,6},{6,4},{8,10},{10,8},{12,14},{14,12},{16,18},{18,... | collective-permute-start | bytes 1376264 | tf_op jit(solution)/shard_map/ppermute | solution.py:47
  72.2 22.4 %all-to-all-start.1 = ((bf16[16,24,576]{2,1,0:T(8,128)(2,1)}), bf16[16,24,576]{2,1,0:T(8,128)(2,1)S(1)}, u32[]{:S(2)}, u32[]{:S(2)}) async-start(bf16[16,24,576]{2,1,0:T(8,128)(2,1)} %bitcast.6), calls=%async_computation.1 | async-start | bytes 983040 | tf_op jit(solution)/shard_map/all_to_all | solution.py:267
  83.0 11.0 %collective-permute-start.17 = (bf16[64,1792]{1,0:T(8,128)(2,1)S(1)}, bf16[64,1792]{1,0:T(8,128)(2,1)S(1)}, u32[]{:S(2)}, u32[]{:S(2)}) collective-permute-start(bf16[64,1792]{1,0:T(8,128)(2,1)S(1)} %get-tuple-element.44), channel_id=1, source_target_pairs={{0,2},{2,0},{4,6},{6,4},{8,10},{10,8},{12,14},{14,12},{16,18},{18,... | collective-permute-start | bytes 688136 | tf_op jit(solution)/shard_map/ppermute | solution.py:47
  88.2 6.4 %collective-permute-start.14 = (bf16[64,1792]{1,0:T(8,128)(2,1)S(1)}, bf16[64,1792]{1,0:T(8,128)(2,1)S(1)}, u32[]{:S(2)}, u32[]{:S(2)}) collective-permute-start(bf16[64,1792]{1,0:T(8,128)(2,1)S(1)} %get-tuple-element.42), channel_id=1, source_target_pairs={{0,4},{2,6},{4,0},{6,2},{8,12},{10,14},{12,8},{14,10},{16,20},{18,... | collective-permute-start | bytes 688136 | tf_op jit(solution)/shard_map/ppermute | solution.py:47
  94.7 6.5 %collective-permute-start.18 = (bf16[32,3584]{1,0:T(8,128)(2,1)S(1)}, bf16[32,3584]{1,0:T(8,128)(2,1)S(1)}, u32[]{:S(2)}, u32[]{:S(2)}) collective-permute-start(bf16[32,3584]{1,0:T(8,128)(2,1)S(1)} %pad_maximum_fusion.6), channel_id=1, source_target_pairs={{0,8},{2,10},{4,12},{6,14},{8,0},{10,2},{12,4},{14,6},{16,24},{18,... | collective-permute-start | bytes 688136 | tf_op jit(solution)/shard_map/ppermute | solution.py:47
  101.1 5.8 %collective-permute-start.19 = (bf16[16,3584]{1,0:T(8,128)(2,1)S(1)}, bf16[16,3584]{1,0:T(8,128)(2,1)S(1)}, u32[]{:S(2)}, u32[]{:S(2)}) collective-permute-start(bf16[16,3584]{1,0:T(8,128)(2,1)S(1)} %add_convert_fusion.9), channel_id=1, source_target_pairs={{0,16},{2,18},{4,20},{6,22},{8,24},{10,26},{12,28},{14,30},{16,0},... | collective-permute-start | bytes 344072 | tf_op jit(solution)/shard_map/ppermute | solution.py:47
  104.5 3.1 %collective-permute-start.20 = (bf16[16,24,576]{2,1,0:T(8,128)(2,1)S(1)}, bf16[16,24,576]{2,1,0:T(8,128)(2,1)S(1)}, u32[]{:S(2)}, u32[]{:S(2)}) collective-permute-start(bf16[16,24,576]{2,1,0:T(8,128)(2,1)S(1)} %all-to-all-done.1), channel_id=1, source_target_pairs={{0,1},{1,0},{2,3},{3,2},{4,5},{5,4},{6,7},{7,6},{8,9},{9,8},{10,11... | collective-permute-start | bytes 1327112 | tf_op jit(solution)/shard_map/ppermute | solution.py:52
  (3 other events, 90.0 us)

commit v10 on v9

--- a/solution.py
+++ b/solution.py
@@ -131,16 +131,19 @@
     for step in range(steps):
         half = parts[0][0].shape[0] // 2
         sents = [add_up([term[half:] for term in terms]) for terms in parts]
-        kepts = [add_up([term[:half] for term in terms]) for terms in parts]
+        kepts = [[term[:half] for term in terms] for terms in parts]
+        if step > 0:
+            kepts = [[add_up(terms)] for terms in kepts]
         if step == 2:
             sents = [jnp.concatenate(sents, axis=1)]
-            kepts = [jnp.concatenate(kepts, axis=1)]
+            kepts = [[jnp.concatenate([kept for kept, in kepts], axis=1)]]
         if step in hooks:
             sents[-1] = hooks[step](sents[-1])
         parts = [
-            [kept, exchange(sent, order[steps - 1 - step])]
+            kept + [exchange(sent, order[steps - 1 - step])]
             for kept, sent, order in zip(kepts, sents, orders)
         ]
+    parts[0][-1] = hooks[-1](parts[0][-1])
     return add_up(parts[0])
 
 
@@ -270,10 +273,14 @@
     return arrived
 
 
-def attention_kernel(chunk, owner, request, queries, *refs):
+def attention_kernel(heads, chunk, owner, queries, *refs):
     keys, out = refs[:-1], refs[-1]
     for start in range(0, queries.shape[0], chunk):
-        row = request[start : start + chunk]
+        row = lax.broadcasted_iota(jnp.int32, (chunk, keys[0].shape[0]), 0) + start
+        if heads & (heads - 1):
+            row = row // heads
+        else:
+            row = row >> (heads.bit_length() - 1)
         scores = []
         for step, key in enumerate(keys):
             part = lax.dot_general(
@@ -313,12 +320,11 @@
         owners.append(jnp.where(within < limit, owner, -1).reshape(1, -1))
     keys = [part.reshape(-1, latent) for part in keys]
     rows = queries.reshape(-1, latent)
-    request = jnp.repeat(jnp.arange(row_count, dtype=jnp.int32), heads)[:, None]
     shape = jax.ShapeDtypeStruct((rows.shape[0], KV), jnp.bfloat16)
     result = kernel_call(
-        functools.partial(attention_kernel, min(256, rows.shape[0])),
+        functools.partial(attention_kernel, heads, min(256, rows.shape[0])),
         shape,
-        [jnp.concatenate(owners, axis=0), request, rows] + keys,
+        [jnp.concatenate(owners, axis=0), rows] + keys,
         flops=4 * rows.size * keys[0].shape[0] * tp_size,
         spare=8 << 20,
     )
@@ -370,7 +376,7 @@
 
     halves = gather_rows(tokens, gates, orders, ends, beside_shared, ahead_of_last)
     last_sent = halves[-1][0]
-    ordered = cache_turn(held["spread"], block_source, slot_total)
+    ordered = cache_turn(held["spread"], tie(block_source, last_sent), slot_total)
     first_late, ordered = lax.optimization_barrier((halves[0][1], ordered))
     halves[0] = (halves[0][0], first_late)
     places = [places_of(order) for order in orders]
@@ -415,11 +421,20 @@
         return sent
 
     def beside_last_sum(sent):
-        keys = tie(held["keys"], sent)
+        sent, keys = lax.optimization_barrier((sent, held["keys"]))
         held["attended"] = attend(queries, keys, block_request, block_used)
         return sent
 
-    hooks = {0: beside_first_sum, 2: beside_third_sum, len(bits) - 1: beside_last_sum}
+    def ahead_of_end(arrived):
+        arrived, held["attended"] = lax.optimization_barrier((arrived, held["attended"]))
+        return arrived
+
+    hooks = {
+        0: beside_first_sum,
+        2: beside_third_sum,
+        len(bits) - 1: beside_last_sum,
+        -1: ahead_of_end,
+    }
     return (scatter_sums(sums, orders, hooks), held["attended"])
 
 

time: 113 us -> 109 us (0.965); the launches traced: 111 us -> 108 us
  starting transfers between devices: 32.9 us -> 30.4 us
    ppermute x13, starting transfers between devices: 19.5 us -> 17 us  [exchange(): lax.ppermute(value, 'ep', [(index, index ^ bit) for index in range(ep_siz...]
    all_to_all x1, waiting for transfers between devices: 2.26 us -> 0.39 us  [beside_shared(): lax.all_to_all(pieces, 'ep', split_axis=0, concat_axis=0, tiled=True)]
    ppermute x13, waiting for transfers between devices: 34.3 us -> 36 us  [exchange(): lax.ppermute(value, 'ep', [(index, index ^ bit) for index in range(ep_siz...]
  transfers between devices with their start and end apart: 23 -> 23, of which waited for: 14 -> 16; matrix products, arithmetic and copies ran while one was open for 13% -> 12% of each run, Pallas kernels for 1% -> 4%
where the time goes in v10:
time: 109 us; the launch traced here: 108 us
  waiting for transfers between devices  41.5 us (38%)
  starting transfers between devices  30.4 us (28%)
  other arithmetic  11.1 us (10%)
  Pallas kernels  11.1 us (10%)
  matrix products  7.79 us (7%)
  local copies, waits for them, and re-layouts  5 us (5%)
    ppermute x13, waiting for transfers between devices, exchange(): lax.ppermute(value, 'ep', [(index, index ^ bit) for index in range(ep_siz...  36 us
    ppermute x13, starting transfers between devices, exchange(): lax.ppermute(value, 'ep', [(index, index ^ bit) for index in range(ep_siz...  17 us
    pallas_call x4, Pallas kernels, kernel_call(): pl.pallas_call(kernel, out_shape=out_shape, in_specs=in_specs or [WHOLE]...  11.1 us
    dot_general x1, matrix products, body(): jnp.einsum('sd,dgf->sgf', all_rows, expert_gate_up[0], preferred_element_...  7.79 us
    convert_element_type x8, other arithmetic, add_up(): return total.astype(jnp.bfloat16)  7.52 us
    all_to_all x1, starting transfers between devices, cache_in(): lax.all_to_all(ordered, 'ep', split_axis=0, concat_axis=0, tiled=True)  6.09 us
    all_to_all x1, starting transfers between devices, beside_shared(): lax.all_to_all(pieces, 'ep', split_axis=0, concat_axis=0, tiled=True)  5.54 us
    ppermute x8, waiting for transfers between devices, pass_tp(): lax.ppermute(value, 'tp', [(index, (index + step) % tp_size) for index in...  5.02 us
  transfers between devices with their start and end apart: 23, of which 16 were waited for; matrix products, arithmetic and copies ran while one was open for 12% of the time, Pallas kernels for 4%

profile of v10, /device:TPU:0, one launch (start us, length us, event | category | flops | bytes accessed | tf_op | source)
XLA Modules:
  0.0 107.8 jit_solution(16921208463802519819)
XLA Ops:
  0.6 4.1 %collective-permute-start = (bf16[1,16,3584]{2,1,0:T(8,128)(2,1)}, bf16[1,16,3584]{2,1,0:T(8,128)(2,1)S(1)}, u32[]{:S(2)}, u32[]{:S(2)}) collective-permute-start(bf16[1,16,3584]{2,1,0:T(8,128)(2,1)} %bitcast.49), channel_id=1, source_target_pairs={{0,16},{2,18},{4,20},{6,22},{8,24},{10,26},{12,28},{14,30},{16,0},... | collective-permute-start | bytes 344072 | tf_op jit(solution)/shard_map/ppermute | solution.py:47
  6.6 4.4 %collective-permute-done.1 = bf16[1,16,128]{2,1,0:T(8,128)(2,1)S(1)} collective-permute-done((bf16[1,16,128]{2,1,0:T(8,128)(2,1)S(1)}, bf16[1,16,128]{2,1,0:T(8,128)(2,1)S(1)}, u32[]{:S(2)}, u32[]{:S(2)}) %collective-permute-start.1) | collective-permute-done | bytes 4128 | tf_op jit(solution)/shard_map/ppermute | solution.py:47
  11.9 1.6 %collective-permute-start.2 = (bf16[2,16,3712]{2,1,0:T(8,128)(2,1)S(1)}, bf16[2,16,3712]{2,1,0:T(8,128)(2,1)S(1)}, u32[]{:S(2)}, u32[]{:S(2)}) collective-permute-start(bf16[2,16,3712]{2,1,0:T(8,128)(2,1)S(1)} %maximum_maximum_fusion), channel_id=1, source_target_pairs={{0,8},{2,10},{4,12},{6,14},{8,0},{10,2},{12,4},{14,6},{16,24},{18,... | collective-permute-start | bytes 712712 | tf_op jit(solution)/shard_map/ppermute | solution.py:47
  14.5 5.5 %all-to-all-start = ((bf16[16,24,576]{2,1,0:T(8,128)(2,1)}), bf16[16,24,576]{2,1,0:T(8,128)(2,1)S(1)}, u32[]{:S(2)}, u32[]{:S(2)}) async-start(bf16[16,24,576]{2,1,0:T(8,128)(2,1)} %bitcast.37), calls=%async_computation | async-start | bytes 983040 | tf_op jit(solution)/shard_map/all_to_all | solution.py:371
  20.9 2.0 %collective-permute-start.3 = (bf16[4,16,1792]{2,1,0:T(8,128)(2,1)S(1)}, bf16[4,16,1792]{2,1,0:T(8,128)(2,1)S(1)}, u32[]{:S(2)}, u32[]{:S(2)}) collective-permute-start(bf16[4,16,1792]{2,1,0:T(8,128)(2,1)S(1)} %pad_maximum_fusion.5), channel_id=1, source_target_pairs={{0,4},{2,6},{4,0},{6,2},{8,12},{10,14},{12,8},{14,10},{16,20},{18,... | collective-permute-start | bytes 688136 | tf_op jit(solution)/shard_map/ppermute | solution.py:47
  23.7 1.5 %collective-permute-start.5 = (bf16[4,16,1920]{2,1,0:T(8,128)(2,1)S(1)}, bf16[4,16,1920]{2,1,0:T(8,128)(2,1)S(1)}, u32[]{:S(2)}, u32[]{:S(2)}) collective-permute-start(bf16[4,16,1920]{2,1,0:T(8,128)(2,1)S(1)} %pad_maximum_fusion.2), channel_id=1, source_target_pairs={{0,2},{2,0},{4,6},{6,4},{8,10},{10,8},{12,14},{14,12},{16,18},{18,... | collective-permute-start | bytes 737288 | tf_op jit(solution)/shard_map/ppermute | solution.py:47
  25.2 6.9 %collective-permute-done.3 = bf16[4,16,1792]{2,1,0:T(8,128)(2,1)S(1)} collective-permute-done((bf16[4,16,1792]{2,1,0:T(8,128)(2,1)S(1)}, bf16[4,16,1792]{2,1,0:T(8,128)(2,1)S(1)}, u32[]{:S(2)}, u32[]{:S(2)}) %collective-permute-start.3) | collective-permute-done | bytes 229408 | tf_op jit(solution)/shard_map/ppermute | solution.py:47
  38.7 1.6 %shard_map.113 = bf16[384,576]{1,0:T(8,128)(2,1)} custom-call(s32[384,2]{1,0:T(8,128)S(1)} %fusion.7.index, bf16[384,576]{1,0:T(8,128)(2,1)S(1)} %bitcast.39, bf16[384,576]{1,0:T(8,128)(2,1)S(1)} %bitcast.45), custom_call_target="tpu_custom_call" | custom-call | flops 339738624 | bytes 2217984 | tf_op jit(solution)/shard_map/pallas_call | solution.py:23
  40.2 4.2 %collective-permute-done.4 = bf16[8,16,1792]{2,1,0:T(8,128)(2,1)} collective-permute-done((bf16[8,16,1792]{2,1,0:T(8,128)(2,1)S(1)}, bf16[8,16,1792]{2,1,0:T(8,128)(2,1)}, u32[]{:S(2)}, u32[]{:S(2)}) %collective-permute-start.4) | collective-permute-done | bytes 458784 | tf_op jit(solution)/shard_map/ppermute | solution.py:47
  47.8 1.5 %shard_map.114 = bf16[256,7168]{1,0:T(8,128)(2,1)S(1)} custom-call(bf16[128,1792]{1,0:T(8,128)(2,1)S(1)} %bitcast.40, bf16[128,1792]{1,0:T(8,128)(2,1)} %bitcast.7.refs_1_, bf16[128,1920]{1,0:T(8,128)(2,1)S(1)} %bitcast.38, bf16[128,1920]{1,0:T(8,128)(2,1)S(1)} %bitcast.41, bf16[128,1792]{1,0:T(8,128)(2,1)} %bitcast.10.refs_4_, ...), custom_call_target="tpu_custom_call" | custom-call | bytes 11272192 | tf_op jit(solution)/shard_map/pallas_call | solution.py:23
  49.4 7.8 %fusion = f32[256,2,512]{2,0,1:T(8,128)S(1)} fusion(bf16[7168,2,512]{2,1,0:T(2,128)(2,1)} %bitcast.53, bf16[256,7168]{1,0:T(8,128)(2,1)S(1)} %shard_map.114), kind=kOutput, calls=%fused_computation | convolution fusion | flops 3758096384 | bytes 19398656 | tf_op jit(solution)/shard_map/sd,dgf->sgf/dot_general | solution.py:400
  57.4 5.0 %shard_map.115 = (bf16[256,1792]{1,0:T(8,128)(2,1)}, bf16[256,1792]{1,0:T(8,128)(2,1)}, bf16[256,1792]{1,0:T(8,128)(2,1)S(1)}, bf16[256,1792]{1,0:T(8,128)(2,1)S(1)}) custom-call(bf16[256,512]{1,0:T(8,128)(2,1)S(1)} %fusion.5.hidden, bf16[7168,512]{1,0:T(8,128)(2,1)} %bitcast.48), custom_call_target="tpu_custom_call" | custom-call | flops 1879048192 | bytes 11534336 | tf_op jit(solution)/shard_map/pallas_call | solution.py:23
  63.1 2.2 %collective-permute-done.15 = bf16[256,1792]{1,0:T(8,128)(2,1)} collective-permute-done((bf16[256,1792]{1,0:T(8,128)(2,1)}, bf16[256,1792]{1,0:T(8,128)(2,1)}, u32[]{:S(2)}, u32[]{:S(2)}) %collective-permute-start.15) | collective-permute-done | bytes 917536 | tf_op jit(solution)/shard_map/ppermute | solution.py:52
  65.3 1.9 %add_convert_fusion = bf16[128,1792]{1,0:T(8,128)(2,1)} fusion(bf16[256,1792]{1,0:T(8,128)(2,1)} %collective-permute-done.15, bf16[256,1792]{1,0:T(8,128)(2,1)S(1)} %get-tuple-element.31), kind=kLoop, calls=%fused_computation.3 | loop fusion | flops 917504 | bytes 1376256 | tf_op jit(solution)/shard_map/convert_element_type | solution.py:154
  68.5 1.9 %add_convert_fusion.1 = bf16[128,1792]{1,0:T(8,128)(2,1)} fusion(bf16[256,1792]{1,0:T(8,128)(2,1)} %collective-permute-done.12, bf16[256,1792]{1,0:T(8,128)(2,1)S(1)} %get-tuple-element.29), kind=kLoop, calls=%fused_computation.4 | loop fusion | flops 917504 | bytes 1376256 | tf_op jit(solution)/shard_map/convert_element_type | solution.py:154
  71.3 6.1 %all-to-all-start.1 = ((bf16[16,24,576]{2,1,0:T(8,128)(2,1)}), bf16[16,24,576]{2,1,0:T(8,128)(2,1)S(1)}, u32[]{:S(2)}, u32[]{:S(2)}) async-start(bf16[16,24,576]{2,1,0:T(8,128)(2,1)} %bitcast.6), calls=%async_computation.1 | async-start | bytes 983040 | tf_op jit(solution)/shard_map/all_to_all | solution.py:270
  77.4 3.0 %collective-permute-done.16 = bf16[128,1792]{1,0:T(8,128)(2,1)} collective-permute-done((bf16[128,1792]{1,0:T(8,128)(2,1)}, bf16[128,1792]{1,0:T(8,128)(2,1)}, u32[]{:S(2)}, u32[]{:S(2)}) %collective-permute-start.16) | collective-permute-done | bytes 458784 | tf_op jit(solution)/shard_map/ppermute | solution.py:47
  80.4 1.4 %add_convert_fusion.3 = (bf16[64,1792]{1,0:T(8,128)(2,1)S(1)}, bf16[64,1792]{1,0:T(8,128)(2,1)S(1)}) fusion(bf16[128,1792]{1,0:T(8,128)(2,1)} %collective-permute-done.16, bf16[256,1792]{1,0:T(8,128)(2,1)} %collective-permute-done.15, bf16[256,1792]{1,0:T(8,128)(2,1)S(1)} %get-tuple-element.31), kind=kLoop, calls=%fused_computation.14 | loop fusion | flops 1376256 | bytes 1835008 | tf_op jit(solution)/shard_map/convert_element_type | solution.py:154
  82.5 3.6 %collective-permute-done.13 = bf16[128,1792]{1,0:T(8,128)(2,1)} collective-permute-done((bf16[128,1792]{1,0:T(8,128)(2,1)}, bf16[128,1792]{1,0:T(8,128)(2,1)}, u32[]{:S(2)}, u32[]{:S(2)}) %collective-permute-start.13) | collective-permute-done | bytes 458784 | tf_op jit(solution)/shard_map/ppermute | solution.py:47
  86.1 1.4 %add_convert_fusion.5 = (bf16[64,1792]{1,0:T(8,128)(2,1)S(1)}, bf16[64,1792]{1,0:T(8,128)(2,1)S(1)}) fusion(bf16[128,1792]{1,0:T(8,128)(2,1)} %collective-permute-done.13, bf16[256,1792]{1,0:T(8,128)(2,1)} %collective-permute-done.12, bf16[256,1792]{1,0:T(8,128)(2,1)S(1)} %get-tuple-element.29), kind=kLoop, calls=%fused_computation.16 | loop fusion | flops 1376256 | bytes 1835008 | tf_op jit(solution)/shard_map/convert_element_type | solution.py:154
  87.6 5.4 %collective-permute-done.17 = bf16[64,1792]{1,0:T(8,128)(2,1)S(1)} collective-permute-done((bf16[64,1792]{1,0:T(8,128)(2,1)S(1)}, bf16[64,1792]{1,0:T(8,128)(2,1)S(1)}, u32[]{:S(2)}, u32[]{:S(2)}) %collective-permute-start.17) | collective-permute-done | bytes 229408 | tf_op jit(solution)/shard_map/ppermute | solution.py:47
  94.8 5.3 %collective-permute-done.18 = bf16[32,3584]{1,0:T(8,128)(2,1)S(1)} collective-permute-done((bf16[32,3584]{1,0:T(8,128)(2,1)S(1)}, bf16[32,3584]{1,0:T(8,128)(2,1)S(1)}, u32[]{:S(2)}, u32[]{:S(2)}) %collective-permute-start.18) | collective-permute-done | bytes 229408 | tf_op jit(solution)/shard_map/ppermute | solution.py:47
  100.1 2.0 %collective-permute-start.20 = (bf16[16,3584]{1,0:T(8,128)(2,1)S(1)}, bf16[16,3584]{1,0:T(8,128)(2,1)S(1)}, u32[]{:S(2)}, u32[]{:S(2)}) collective-permute-start(bf16[16,3584]{1,0:T(8,128)(2,1)S(1)} %add_convert_fusion.7), channel_id=1, source_target_pairs={{0,16},{2,18},{4,20},{6,22},{8,24},{10,26},{12,28},{14,30},{16,0},... | collective-permute-start | bytes 344072 | tf_op jit(solution)/shard_map/ppermute | solution.py:47
  103.2 3.0 %shard_map.116 = bf16[512,512]{1,0:T(8,128)(2,1)} custom-call(s32[2,384]{1,0:T(2,128)S(1)} %pad_add_fusion.owner, bf16[512,576]{1,0:T(8,128)(2,1)S(1)} %bitcast.46, bf16[384,576]{1,0:T(8,128)(2,1)S(1)} %bitcast.44, bf16[384,576]{1,0:T(8,128)(2,1)S(1)} %bitcast.47), custom_call_target="tpu_custom_call" | custom-call | flops 905969664 | bytes 3479552 | tf_op jit(solution)/shard_map/pallas_call | solution.py:23
  (77 shorter events, 23.3 us)
Async XLA Ops:
  0.6 10.3 %collective-permute-start = (bf16[1,16,3584]{2,1,0:T(8,128)(2,1)}, bf16[1,16,3584]{2,1,0:T(8,128)(2,1)S(1)}, u32[]{:S(2)}, u32[]{:S(2)}) collective-permute-start(bf16[1,16,3584]{2,1,0:T(8,128)(2,1)} %bitcast.49), channel_id=1, source_target_pairs={{0,16},{2,18},{4,20},{6,22},{8,24},{10,26},{12,28},{14,30},{16,0},... | collective-permute-start | bytes 344072 | tf_op jit(solution)/shard_map/ppermute | solution.py:47
  6.5 4.5 %collective-permute-start.1 = (bf16[1,16,128]{2,1,0:T(8,128)(2,1)S(1)}, bf16[1,16,128]{2,1,0:T(8,128)(2,1)S(1)}, u32[]{:S(2)}, u32[]{:S(2)}) collective-permute-start(bf16[1,16,128]{2,1,0:T(8,128)(2,1)S(1)} %fusion.18), channel_id=1, source_target_pairs={{0,16},{2,18},{4,20},{6,22},{8,24},{10,26},{12,28},{14,30},{16,0},... | collective-permute-start | bytes 12296 | tf_op jit(solution)/shard_map/ppermute | solution.py:47
  11.9 8.1 %collective-permute-start.2 = (bf16[2,16,3712]{2,1,0:T(8,128)(2,1)S(1)}, bf16[2,16,3712]{2,1,0:T(8,128)(2,1)S(1)}, u32[]{:S(2)}, u32[]{:S(2)}) collective-permute-start(bf16[2,16,3712]{2,1,0:T(8,128)(2,1)S(1)} %maximum_maximum_fusion), channel_id=1, source_target_pairs={{0,8},{2,10},{4,12},{6,14},{8,0},{10,2},{12,4},{14,6},{16,24},{18,... | collective-permute-start | bytes 712712 | tf_op jit(solution)/shard_map/ppermute | solution.py:47
  14.5 19.9 %all-to-all-start = ((bf16[16,24,576]{2,1,0:T(8,128)(2,1)}), bf16[16,24,576]{2,1,0:T(8,128)(2,1)S(1)}, u32[]{:S(2)}, u32[]{:S(2)}) async-start(bf16[16,24,576]{2,1,0:T(8,128)(2,1)} %bitcast.37), calls=%async_computation | async-start | bytes 983040 | tf_op jit(solution)/shard_map/all_to_all | solution.py:371
  20.9 11.3 %collective-permute-start.3 = (bf16[4,16,1792]{2,1,0:T(8,128)(2,1)S(1)}, bf16[4,16,1792]{2,1,0:T(8,128)(2,1)S(1)}, u32[]{:S(2)}, u32[]{:S(2)}) collective-permute-start(bf16[4,16,1792]{2,1,0:T(8,128)(2,1)S(1)} %pad_maximum_fusion.5), channel_id=1, source_target_pairs={{0,4},{2,6},{4,0},{6,2},{8,12},{10,14},{12,8},{14,10},{16,20},{18,... | collective-permute-start | bytes 688136 | tf_op jit(solution)/shard_map/ppermute | solution.py:47
  23.7 10.3 %collective-permute-start.5 = (bf16[4,16,1920]{2,1,0:T(8,128)(2,1)S(1)}, bf16[4,16,1920]{2,1,0:T(8,128)(2,1)S(1)}, u32[]{:S(2)}, u32[]{:S(2)}) collective-permute-start(bf16[4,16,1920]{2,1,0:T(8,128)(2,1)S(1)} %pad_maximum_fusion.2), channel_id=1, source_target_pairs={{0,2},{2,0},{4,6},{6,4},{8,10},{10,8},{12,14},{14,12},{16,18},{18,... | collective-permute-start | bytes 737288 | tf_op jit(solution)/shard_map/ppermute | solution.py:47
  32.2 12.2 %collective-permute-start.4 = (bf16[8,16,1792]{2,1,0:T(8,128)(2,1)S(1)}, bf16[8,16,1792]{2,1,0:T(8,128)(2,1)}, u32[]{:S(2)}, u32[]{:S(2)}) collective-permute-start(bf16[8,16,1792]{2,1,0:T(8,128)(2,1)S(1)} %pad_maximum_fusion.1), channel_id=1, source_target_pairs={{0,2},{2,0},{4,6},{6,4},{8,10},{10,8},{12,14},{14,12},{16,18},{18,... | collective-permute-start | bytes 1376264 | tf_op jit(solution)/shard_map/ppermute | solution.py:47
  34.4 11.6 %collective-permute-start.7 = (bf16[8,16,1920]{2,1,0:T(8,128)(2,1)S(1)}, bf16[8,16,1920]{2,1,0:T(8,128)(2,1)S(1)}, u32[]{:S(2)}, u32[]{:S(2)}) collective-permute-start(bf16[8,16,1920]{2,1,0:T(8,128)(2,1)S(1)} %pad_maximum_fusion), channel_id=1, source_target_pairs={{0,4},{2,6},{4,0},{6,2},{8,12},{10,14},{12,8},{14,10},{16,20},{18,... | collective-permute-start | bytes 1474568 | tf_op jit(solution)/shard_map/ppermute | solution.py:47
  36.7 1.9 %collective-permute-start.6 = (bf16[16,24,576]{2,1,0:T(8,128)(2,1)S(1)}, bf16[16,24,576]{2,1,0:T(8,128)(2,1)S(1)}, u32[]{:S(2)}, u32[]{:S(2)}) collective-permute-start(bf16[16,24,576]{2,1,0:T(8,128)(2,1)S(1)} %all-to-all-done), channel_id=1, source_target_pairs={{0,1},{1,0},{2,3},{3,2},{4,5},{5,4},{6,7},{7,6},{8,9},{9,8},{10,11... | collective-permute-start | bytes 1327112 | tf_op jit(solution)/shard_map/ppermute | solution.py:52
  36.8 9.4 %collective-permute-start.8 = (bf16[8,16,1792]{2,1,0:T(8,128)(2,1)S(1)}, bf16[8,16,1792]{2,1,0:T(8,128)(2,1)}, u32[]{:S(2)}, u32[]{:S(2)}) collective-permute-start(bf16[8,16,1792]{2,1,0:T(8,128)(2,1)S(1)} %pad_maximum_fusion.1), channel_id=1, source_target_pairs={{0,1},{1,0},{2,3},{3,2},{4,5},{5,4},{6,7},{7,6},{8,9},{9,8},{10,11... | collective-permute-start | bytes 1376264 | tf_op jit(solution)/shard_map/ppermute | solution.py:52
  44.4 2.8 %collective-permute-start.9 = (bf16[8,16,1792]{2,1,0:T(8,128)(2,1)}, bf16[8,16,1792]{2,1,0:T(8,128)(2,1)}, u32[]{:S(2)}, u32[]{:S(2)}) collective-permute-start(bf16[8,16,1792]{2,1,0:T(8,128)(2,1)} %collective-permute-done.4), channel_id=1, source_target_pairs={{0,1},{1,0},{2,3},{3,2},{4,5},{5,4},{6,7},{7,6},{8,9},{9,8},{10,11... | collective-permute-start | bytes 1376264 | tf_op jit(solution)/shard_map/ppermute | solution.py:52
  44.4 2.8 %collective-permute-start.10 = (bf16[8,16,1920]{2,1,0:T(8,128)(2,1)S(1)}, bf16[8,16,1920]{2,1,0:T(8,128)(2,1)S(1)}, u32[]{:S(2)}, u32[]{:S(2)}) collective-permute-start(bf16[8,16,1920]{2,1,0:T(8,128)(2,1)S(1)} %pad_maximum_fusion), channel_id=1, source_target_pairs={{0,1},{1,0},{2,3},{3,2},{4,5},{5,4},{6,7},{7,6},{8,9},{9,8},{10,11... | collective-permute-start | bytes 1474568 | tf_op jit(solution)/shard_map/ppermute | solution.py:52
  46.0 1.9 %collective-permute-start.11 = (bf16[8,16,1920]{2,1,0:T(8,128)(2,1)S(1)}, bf16[8,16,1920]{2,1,0:T(8,128)(2,1)S(1)}, u32[]{:S(2)}, u32[]{:S(2)}) collective-permute-start(bf16[8,16,1920]{2,1,0:T(8,128)(2,1)S(1)} %collective-permute-done.7), channel_id=1, source_target_pairs={{0,1},{1,0},{2,3},{3,2},{4,5},{5,4},{6,7},{7,6},{8,9},{9,8},{10,11... | collective-permute-start | bytes 1474568 | tf_op jit(solution)/shard_map/ppermute | solution.py:52
  49.4 13.6 %copy-start.2 = (s32[48]{0:T(128)S(1)}, s32[48]{0:T(128)}, u32[]{:S(2)}) copy-start(s32[48]{0:T(128)} %param.19) | copy-start | bytes 580
  62.4 2.9 %collective-permute-start.15 = (bf16[256,1792]{1,0:T(8,128)(2,1)}, bf16[256,1792]{1,0:T(8,128)(2,1)}, u32[]{:S(2)}, u32[]{:S(2)}) collective-permute-start(bf16[256,1792]{1,0:T(8,128)(2,1)} %get-tuple-element.32), channel_id=1, source_target_pairs={{0,1},{1,0},{2,3},{3,2},{4,5},{5,4},{6,7},{7,6},{8,9},{9,8},{10,11... | collective-permute-start | bytes 2752520 | tf_op jit(solution)/shard_map/ppermute | solution.py:52
  62.6 5.8 %collective-permute-start.12 = (bf16[256,1792]{1,0:T(8,128)(2,1)}, bf16[256,1792]{1,0:T(8,128)(2,1)}, u32[]{:S(2)}, u32[]{:S(2)}) collective-permute-start(bf16[256,1792]{1,0:T(8,128)(2,1)} %get-tuple-element.30), channel_id=1, source_target_pairs={{0,1},{1,0},{2,3},{3,2},{4,5},{5,4},{6,7},{7,6},{8,9},{9,8},{10,11... | collective-permute-start | bytes 2752520 | tf_op jit(solution)/shard_map/ppermute | solution.py:52
  67.2 13.2 %collective-permute-start.16 = (bf16[128,1792]{1,0:T(8,128)(2,1)}, bf16[128,1792]{1,0:T(8,128)(2,1)}, u32[]{:S(2)}, u32[]{:S(2)}) collective-permute-start(bf16[128,1792]{1,0:T(8,128)(2,1)} %add_convert_fusion), channel_id=1, source_target_pairs={{0,4},{2,6},{4,0},{6,2},{8,12},{10,14},{12,8},{14,10},{16,20},{18,... | collective-permute-start | bytes 1376264 | tf_op jit(solution)/shard_map/ppermute | solution.py:47
  70.4 15.7 %collective-permute-start.13 = (bf16[128,1792]{1,0:T(8,128)(2,1)}, bf16[128,1792]{1,0:T(8,128)(2,1)}, u32[]{:S(2)}, u32[]{:S(2)}) collective-permute-start(bf16[128,1792]{1,0:T(8,128)(2,1)} %add_convert_fusion.1), channel_id=1, source_target_pairs={{0,2},{2,0},{4,6},{6,4},{8,10},{10,8},{12,14},{14,12},{16,18},{18,... | collective-permute-start | bytes 1376264 | tf_op jit(solution)/shard_map/ppermute | solution.py:47
  71.3 22.7 %all-to-all-start.1 = ((bf16[16,24,576]{2,1,0:T(8,128)(2,1)}), bf16[16,24,576]{2,1,0:T(8,128)(2,1)S(1)}, u32[]{:S(2)}, u32[]{:S(2)}) async-start(bf16[16,24,576]{2,1,0:T(8,128)(2,1)} %bitcast.6), calls=%async_computation.1 | async-start | bytes 983040 | tf_op jit(solution)/shard_map/all_to_all | solution.py:270
  81.8 11.2 %collective-permute-start.17 = (bf16[64,1792]{1,0:T(8,128)(2,1)S(1)}, bf16[64,1792]{1,0:T(8,128)(2,1)S(1)}, u32[]{:S(2)}, u32[]{:S(2)}) collective-permute-start(bf16[64,1792]{1,0:T(8,128)(2,1)S(1)} %get-tuple-element.48), channel_id=1, source_target_pairs={{0,2},{2,0},{4,6},{6,4},{8,10},{10,8},{12,14},{14,12},{16,18},{18,... | collective-permute-start | bytes 688136 | tf_op jit(solution)/shard_map/ppermute | solution.py:47
  87.5 6.3 %collective-permute-start.14 = (bf16[64,1792]{1,0:T(8,128)(2,1)S(1)}, bf16[64,1792]{1,0:T(8,128)(2,1)S(1)}, u32[]{:S(2)}, u32[]{:S(2)}) collective-permute-start(bf16[64,1792]{1,0:T(8,128)(2,1)S(1)} %get-tuple-element.46), channel_id=1, source_target_pairs={{0,4},{2,6},{4,0},{6,2},{8,12},{10,14},{12,8},{14,10},{16,20},{18,... | collective-permute-start | bytes 688136 | tf_op jit(solution)/shard_map/ppermute | solution.py:47
  94.0 6.1 %collective-permute-start.18 = (bf16[32,3584]{1,0:T(8,128)(2,1)S(1)}, bf16[32,3584]{1,0:T(8,128)(2,1)S(1)}, u32[]{:S(2)}, u32[]{:S(2)}) collective-permute-start(bf16[32,3584]{1,0:T(8,128)(2,1)S(1)} %pad_maximum_fusion.6), channel_id=1, source_target_pairs={{0,8},{2,10},{4,12},{6,14},{8,0},{10,2},{12,4},{14,6},{16,24},{18,... | collective-permute-start | bytes 688136 | tf_op jit(solution)/shard_map/ppermute | solution.py:47
  94.7 5.4 %collective-permute-start.19 = (bf16[16,24,576]{2,1,0:T(8,128)(2,1)S(1)}, bf16[16,24,576]{2,1,0:T(8,128)(2,1)S(1)}, u32[]{:S(2)}, u32[]{:S(2)}) collective-permute-start(bf16[16,24,576]{2,1,0:T(8,128)(2,1)S(1)} %all-to-all-done.1), channel_id=1, source_target_pairs={{0,1},{1,0},{2,3},{3,2},{4,5},{5,4},{6,7},{7,6},{8,9},{9,8},{10,11... | collective-permute-start | bytes 1327112 | tf_op jit(solution)/shard_map/ppermute | solution.py:52
  100.1 7.0 %collective-permute-start.20 = (bf16[16,3584]{1,0:T(8,128)(2,1)S(1)}, bf16[16,3584]{1,0:T(8,128)(2,1)S(1)}, u32[]{:S(2)}, u32[]{:S(2)}) collective-permute-start(bf16[16,3584]{1,0:T(8,128)(2,1)S(1)} %add_convert_fusion.7), channel_id=1, source_target_pairs={{0,16},{2,18},{4,20},{6,22},{8,24},{10,26},{12,28},{14,30},{16,0},... | collective-permute-start | bytes 344072 | tf_op jit(solution)/shard_map/ppermute | solution.py:47
  (3 other events, 27.6 us)

commit v11 on v10

--- a/solution.py
+++ b/solution.py
@@ -126,25 +126,27 @@
     )
 
 
-def scatter_sums(parts, orders, hooks):
+def scatter_sums(sums, orders, hooks):
     steps = len(orders[0])
+    kepts, sents = zip(*sums)
+    kepts, sents = list(kepts), list(sents)
     for step in range(steps):
-        half = parts[0][0].shape[0] // 2
-        sents = [add_up([term[half:] for term in terms]) for terms in parts]
-        kepts = [[term[:half] for term in terms] for terms in parts]
-        if step > 0:
-            kepts = [[add_up(terms)] for terms in kepts]
-        if step == 2:
-            sents = [jnp.concatenate(sents, axis=1)]
-            kepts = [[jnp.concatenate([kept for kept, in kepts], axis=1)]]
         if step in hooks:
             sents[-1] = hooks[step](sents[-1])
-        parts = [
-            kept + [exchange(sent, order[steps - 1 - step])]
+        terms = [
+            [kept, exchange(sent, order[steps - 1 - step])]
             for kept, sent, order in zip(kepts, sents, orders)
         ]
-    parts[0][-1] = hooks[-1](parts[0][-1])
-    return add_up(parts[0])
+        if step == steps - 1:
+            break
+        half = kepts[0].shape[0] // 2
+        sents = [add_up([term[half:] for term in pair]) for pair in terms]
+        kepts = [add_up([term[:half] for term in pair]) for pair in terms]
+        if step == 1:
+            sents = [jnp.concatenate(sents, axis=1)]
+            kepts = [jnp.concatenate(kepts, axis=1)]
+    kept, arrived = terms[0]
+    return add_up([kept, hooks[-1](arrived)])
 
 
 def add_up(terms):
@@ -163,62 +165,111 @@
     return parts
 
 
-def down_kernel(spots, tp_size, cut, width, rows, hidden, weight, *refs):
+def turn_rows(hidden, turned, spots, rows):
+    for block, spot in enumerate(spots):
+        turned[spot * rows : (spot + 1) * rows] = hidden[block * rows : (block + 1) * rows]
+
+
+def down_product(turned, weight, row, chunk, column, width):
+    return lax.dot_general(
+        turned[row : row + chunk],
+        weight[column : column + width],
+        (((1,), (1,)), ((), ())),
+        preferred_element_type=jnp.float32,
+    )
+
+
+def others_kernel(step, spots, tp_size, cut, rows, hidden, weight, *refs):
     parts = len(spots)
-    outs, (held, turned, arrived) = refs[:-3], refs[-3:]
+    outs, (held, turned, arrived) = refs[:parts], refs[parts:]
+    target = lax.rem(lax.axis_index("tp") + step, tp_size)
     copies = []
-    for step in range(tp_size):
-        target = lax.rem(lax.axis_index("tp") + step + 1, tp_size)
-        for part in range(parts):
-            run = step * parts + part
-            start = pl.multiple_of((target * parts + part) * cut, cut)
-            copies.append(
-                pltpu.make_async_copy(
-                    weight.at[pl.ds(start, cut)],
-                    held.at[pl.ds(run * cut, cut)],
-                    arrived.at[run],
-                )
+    for part in range(parts):
+        start = pl.multiple_of((target * parts + part) * cut, cut)
+        copies.append(
+            pltpu.make_async_copy(
+                weight.at[pl.ds(start, cut)], held.at[part], arrived.at[part]
             )
+        )
     for copy in copies:
         copy.start()
     chunk = min(256, hidden.shape[0])
-    for part in range(parts):
-        for block, spot in enumerate(spots[part]):
-            turned[part, spot * rows : (spot + 1) * rows] = hidden[
-                block * rows : (block + 1) * rows
-            ]
-    for run, copy in enumerate(copies):
+    for part, copy in enumerate(copies):
+        turn_rows(hidden, turned.at[part], spots[part], rows)
         copy.wait()
-        for column in range(0, cut, width):
-            for row in range(0, hidden.shape[0], chunk):
-                outs[run][row : row + chunk, column : column + width] = lax.dot_general(
-                    turned[run % parts, row : row + chunk],
-                    held[run * cut + column : run * cut + column + width],
-                    (((1,), (1,)), ((), ())),
-                    preferred_element_type=jnp.float32,
-                ).astype(jnp.bfloat16)
-
-
-def down(hidden, weight, spots, rows):
+        for row in range(0, hidden.shape[0], chunk):
+            outs[part][row : row + chunk] = down_product(
+                turned.at[part], held.at[part], row, chunk, 0, cut
+            ).astype(jnp.bfloat16)
+
+
+def down_others(hidden, weight, step, spots, rows):
     parts = len(spots)
     tp_size = lax.axis_size("tp")
     cut = weight.shape[0] // tp_size // parts
-    width = cut
     shape = jax.ShapeDtypeStruct((hidden.shape[0], cut), jnp.bfloat16)
-    outs = kernel_call(
-        functools.partial(down_kernel, spots, tp_size, cut, width, rows),
-        [shape] * (parts * tp_size),
+    return kernel_call(
+        functools.partial(others_kernel, step, spots, tp_size, cut, rows),
+        [shape] * parts,
         [hidden, weight],
-        flops=2 * hidden.size * weight.shape[0],
-        spare=weight.size * 2 + (8 << 20),
+        flops=2 * hidden.size * cut * parts,
+        spare=parts * cut * weight.shape[1] * 2 + (8 << 20),
         in_specs=[WHOLE, pl.BlockSpec(memory_space=pl.ANY)],
         scratch_shapes=[
-            pltpu.VMEM(weight.shape, weight.dtype),
+            pltpu.VMEM((parts, cut, weight.shape[1]), weight.dtype),
             pltpu.VMEM((parts,) + hidden.shape, hidden.dtype),
-            pltpu.SemaphoreType.DMA((parts * tp_size,)),
+            pltpu.SemaphoreType.DMA((parts,)),
         ],
     )
-    return [outs[step * parts : (step + 1) * parts] for step in range(tp_size)]
+
+
+def own_kernel(part, parts, spots, cut, rows, count, hidden, weight, *refs):
+    others, (kept, sent, held, turned, passed, arrived) = refs[:count], refs[count:]
+    start = pl.multiple_of((lax.axis_index("tp") * parts + part) * cut, cut)
+    copies = [pltpu.make_async_copy(weight.at[pl.ds(start, cut)], held, arrived.at[count])]
+    for index, other in enumerate(others):
+        copies.append(pltpu.make_async_copy(other, passed.at[index], arrived.at[index]))
+    for copy in copies:
+        copy.start()
+    turn_rows(hidden, turned, spots, rows)
+    for copy in copies:
+        copy.wait()
+    half = hidden.shape[0] // 2
+    chunk = min(256, hidden.shape[0])
+    width = cut // 2 if cut % 256 == 0 else cut
+    for column in range(0, cut, width):
+        for row in range(0, hidden.shape[0], chunk):
+            total = down_product(turned, held, row, chunk, column, width)
+            for index in range(count):
+                total = total + passed[
+                    index, row : row + chunk, column : column + width
+                ].astype(jnp.float32)
+            total = total.astype(jnp.bfloat16)
+            for first in range(row, row + chunk, min(chunk, half)):
+                out = kept if first < half else sent
+                place = first % half
+                piece = total[first - row : first - row + min(chunk, half)]
+                out[place : place + piece.shape[0], column : column + width] = piece
+
+
+def down_own(hidden, weight, part, parts, spots, rows, others):
+    cut = weight.shape[0] // lax.axis_size("tp") // parts
+    shape = jax.ShapeDtypeStruct((hidden.shape[0] // 2, cut), jnp.bfloat16)
+    anywhere = pl.BlockSpec(memory_space=pl.ANY)
+    return kernel_call(
+        functools.partial(own_kernel, part, parts, spots, cut, rows, len(others)),
+        [shape, shape],
+        [hidden, weight] + others,
+        flops=2 * hidden.size * cut,
+        spare=(cut * weight.shape[1] + hidden.shape[0] * cut * len(others)) * 2 + (8 << 20),
+        in_specs=[WHOLE] + [anywhere] * (1 + len(others)),
+        scratch_shapes=[
+            pltpu.VMEM((cut, weight.shape[1]), weight.dtype),
+            pltpu.VMEM(hidden.shape, hidden.dtype),
+            pltpu.VMEM((len(others), hidden.shape[0], cut), jnp.bfloat16),
+            pltpu.SemaphoreType.DMA((1 + len(others),)),
+        ],
+    )
 
 
 def order_kernel(index, *refs):
@@ -405,11 +456,15 @@
     ).astype(jnp.bfloat16)
 
     down_weight = pltpu.with_memory_space_constraint(expert_down[0], pltpu.HBM)
-    by_step = down(hidden, down_weight, from_first, row_count)
-    sums = [[own] for own in by_step[-1]]
-    for part in range(parts):
-        for step in range(1, tp_size):
-            sums[part].append(pass_tp(by_step[step - 1][part], step))
+    passed = [[] for _ in range(parts)]
+    for step in range(1, tp_size):
+        others = down_others(hidden, down_weight, step, from_first, row_count)
+        for part in range(parts):
+            passed[part].append(pass_tp(others[part], step))
+    sums = [
+        down_own(hidden, down_weight, part, parts, from_first[part], row_count, passed[part])
+        for part in range(parts)
+    ]
 
     def beside_first_sum(sent):
         held["keys"] = cache_in(tie(ordered, sent), block_size, latent)

time: 109 us -> 108 us (level)
  other arithmetic: 11.1 us -> 7.37 us
  Pallas kernels: 11.1 us -> 14.4 us
  waiting for transfers between devices: 41.5 us -> 38.4 us
  starting transfers between devices: 30.4 us -> 32.8 us
    convert_element_type x8 -> x6, other arithmetic: 7.52 us -> 3.14 us  [add_up(): return total.astype(jnp.bfloat16)]
    pallas_call x4 -> x6, Pallas kernels: 11.1 us -> 14.4 us  [kernel_call(): pl.pallas_call(kernel, out_shape=out_shape, in_specs=in_specs or [WHOLE]...]
    ppermute x13, waiting for transfers between devices: 36 us -> 33.3 us  [exchange(): lax.ppermute(value, 'ep', [(index, index ^ bit) for index in range(ep_siz...]
    ppermute x13, starting transfers between devices: 17 us -> 19.5 us  [exchange(): lax.ppermute(value, 'ep', [(index, index ^ bit) for index in range(ep_siz...]
  transfers between devices with their start and end apart: 23 -> 23, of which waited for: 16 -> 16; matrix products, arithmetic and copies ran while one was open for 12% -> 9% of each run, Pallas kernels for 4% -> 9%
where the time goes in v11:
time: 108 us; the launch traced here: 107 us
  waiting for transfers between devices  38.4 us (36%)
  starting transfers between devices  32.8 us (30%)
  Pallas kernels  14.4 us (13%)
  matrix products  7.78 us (7%)
  other arithmetic  7.37 us (7%)
  local copies, waits for them, and re-layouts  5.55 us (5%)
    ppermute x13, waiting for transfers between devices, exchange(): lax.ppermute(value, 'ep', [(index, index ^ bit) for index in range(ep_siz...  33.3 us
    ppermute x13, starting transfers between devices, exchange(): lax.ppermute(value, 'ep', [(index, index ^ bit) for index in range(ep_siz...  19.5 us
    pallas_call x6, Pallas kernels, kernel_call(): pl.pallas_call(kernel, out_shape=out_shape, in_specs=in_specs or [WHOLE]...  14.4 us
    dot_general x1, matrix products, body(): jnp.einsum('sd,dgf->sgf', all_rows, expert_gate_up[0], preferred_element_...  7.78 us
    all_to_all x1, starting transfers between devices, cache_in(): lax.all_to_all(ordered, 'ep', split_axis=0, concat_axis=0, tiled=True)  6.06 us
    all_to_all x1, starting transfers between devices, beside_shared(): lax.all_to_all(pieces, 'ep', split_axis=0, concat_axis=0, tiled=True)  5.54 us
    ppermute x8, waiting for transfers between devices, pass_tp(): lax.ppermute(value, 'tp', [(index, (index + step) % tp_size) for index in...  4.76 us
    unnamed x11, local copies, waits for them, and re-layouts  3.49 us
  transfers between devices with their start and end apart: 23, of which 16 were waited for; matrix products, arithmetic and copies ran while one was open for 9% of the time, Pallas kernels for 9%

profile of v11, /device:TPU:0, one launch (start us, length us, event | category | flops | bytes accessed | tf_op | source)
XLA Modules:
  0.0 107.2 jit_solution(13598755379201147070)
XLA Ops:
  0.6 4.1 %collective-permute-start = (bf16[1,16,3584]{2,1,0:T(8,128)(2,1)}, bf16[1,16,3584]{2,1,0:T(8,128)(2,1)S(1)}, u32[]{:S(2)}, u32[]{:S(2)}) collective-permute-start(bf16[1,16,3584]{2,1,0:T(8,128)(2,1)} %bitcast.51), channel_id=1, source_target_pairs={{0,16},{2,18},{4,20},{6,22},{8,24},{10,26},{12,28},{14,30},{16,0},... | collective-permute-start | bytes 344072 | tf_op jit(solution)/shard_map/ppermute | solution.py:47
  6.6 4.4 %collective-permute-done.1 = bf16[1,16,128]{2,1,0:T(8,128)(2,1)S(1)} collective-permute-done((bf16[1,16,128]{2,1,0:T(8,128)(2,1)S(1)}, bf16[1,16,128]{2,1,0:T(8,128)(2,1)S(1)}, u32[]{:S(2)}, u32[]{:S(2)}) %collective-permute-start.1) | collective-permute-done | bytes 4128 | tf_op jit(solution)/shard_map/ppermute | solution.py:47
  11.9 1.6 %collective-permute-start.2 = (bf16[2,16,3712]{2,1,0:T(8,128)(2,1)S(1)}, bf16[2,16,3712]{2,1,0:T(8,128)(2,1)S(1)}, u32[]{:S(2)}, u32[]{:S(2)}) collective-permute-start(bf16[2,16,3712]{2,1,0:T(8,128)(2,1)S(1)} %maximum_maximum_fusion), channel_id=1, source_target_pairs={{0,8},{2,10},{4,12},{6,14},{8,0},{10,2},{12,4},{14,6},{16,24},{18,... | collective-permute-start | bytes 712712 | tf_op jit(solution)/shard_map/ppermute | solution.py:47
  14.5 5.5 %all-to-all-start = ((bf16[16,24,576]{2,1,0:T(8,128)(2,1)}), bf16[16,24,576]{2,1,0:T(8,128)(2,1)S(1)}, u32[]{:S(2)}, u32[]{:S(2)}) async-start(bf16[16,24,576]{2,1,0:T(8,128)(2,1)} %bitcast.37), calls=%async_computation | async-start | bytes 983040 | tf_op jit(solution)/shard_map/all_to_all | solution.py:422
  20.9 2.0 %collective-permute-start.3 = (bf16[4,16,1792]{2,1,0:T(8,128)(2,1)S(1)}, bf16[4,16,1792]{2,1,0:T(8,128)(2,1)S(1)}, u32[]{:S(2)}, u32[]{:S(2)}) collective-permute-start(bf16[4,16,1792]{2,1,0:T(8,128)(2,1)S(1)} %pad_maximum_fusion.5), channel_id=1, source_target_pairs={{0,4},{2,6},{4,0},{6,2},{8,12},{10,14},{12,8},{14,10},{16,20},{18,... | collective-permute-start | bytes 688136 | tf_op jit(solution)/shard_map/ppermute | solution.py:47
  23.7 1.5 %collective-permute-start.5 = (bf16[4,16,1920]{2,1,0:T(8,128)(2,1)S(1)}, bf16[4,16,1920]{2,1,0:T(8,128)(2,1)S(1)}, u32[]{:S(2)}, u32[]{:S(2)}) collective-permute-start(bf16[4,16,1920]{2,1,0:T(8,128)(2,1)S(1)} %pad_maximum_fusion.2), channel_id=1, source_target_pairs={{0,2},{2,0},{4,6},{6,4},{8,10},{10,8},{12,14},{14,12},{16,18},{18,... | collective-permute-start | bytes 737288 | tf_op jit(solution)/shard_map/ppermute | solution.py:47
  25.2 6.9 %collective-permute-done.3 = bf16[4,16,1792]{2,1,0:T(8,128)(2,1)S(1)} collective-permute-done((bf16[4,16,1792]{2,1,0:T(8,128)(2,1)S(1)}, bf16[4,16,1792]{2,1,0:T(8,128)(2,1)S(1)}, u32[]{:S(2)}, u32[]{:S(2)}) %collective-permute-start.3) | collective-permute-done | bytes 229408 | tf_op jit(solution)/shard_map/ppermute | solution.py:47
  38.7 1.6 %shard_map.113 = bf16[384,576]{1,0:T(8,128)(2,1)} custom-call(s32[384,2]{1,0:T(8,128)S(1)} %fusion.7.index, bf16[384,576]{1,0:T(8,128)(2,1)S(1)} %bitcast.39, bf16[384,576]{1,0:T(8,128)(2,1)S(1)} %bitcast.45), custom_call_target="tpu_custom_call" | custom-call | flops 339738624 | bytes 2217984 | tf_op jit(solution)/shard_map/pallas_call | solution.py:23
  40.2 4.2 %collective-permute-done.4 = bf16[8,16,1792]{2,1,0:T(8,128)(2,1)} collective-permute-done((bf16[8,16,1792]{2,1,0:T(8,128)(2,1)S(1)}, bf16[8,16,1792]{2,1,0:T(8,128)(2,1)}, u32[]{:S(2)}, u32[]{:S(2)}) %collective-permute-start.4) | collective-permute-done | bytes 458784 | tf_op jit(solution)/shard_map/ppermute | solution.py:47
  47.8 1.5 %shard_map.114 = bf16[256,7168]{1,0:T(8,128)(2,1)S(1)} custom-call(bf16[128,1792]{1,0:T(8,128)(2,1)S(1)} %bitcast.40, bf16[128,1792]{1,0:T(8,128)(2,1)} %bitcast.7.refs_1_, bf16[128,1920]{1,0:T(8,128)(2,1)S(1)} %bitcast.38, bf16[128,1920]{1,0:T(8,128)(2,1)S(1)} %bitcast.41, bf16[128,1792]{1,0:T(8,128)(2,1)} %bitcast.10.refs_4_, ...), custom_call_target="tpu_custom_call" | custom-call | bytes 11272192 | tf_op jit(solution)/shard_map/pallas_call | solution.py:23
  49.4 7.8 %fusion = f32[256,2,512]{2,0,1:T(8,128)S(1)} fusion(bf16[7168,2,512]{2,1,0:T(2,128)(2,1)} %bitcast.55, bf16[256,7168]{1,0:T(8,128)(2,1)S(1)} %shard_map.114), kind=kOutput, calls=%fused_computation | convolution fusion | flops 3758096384 | bytes 19398656 | tf_op jit(solution)/shard_map/sd,dgf->sgf/dot_general | solution.py:451
  57.4 3.0 %shard_map.115 = (bf16[256,1792]{1,0:T(8,128)(2,1)S(1)}, bf16[256,1792]{1,0:T(8,128)(2,1)S(1)}) custom-call(bf16[256,512]{1,0:T(8,128)(2,1)S(1)} %fusion.5.hidden, bf16[7168,512]{1,0:T(8,128)(2,1)} %bitcast.48), custom_call_target="tpu_custom_call" | custom-call | flops 939524096 | bytes 9699328 | tf_op jit(solution)/shard_map/pallas_call | solution.py:23
  61.0 2.0 %collective-permute-done.15.refs_0_ = bf16[256,1792]{1,0:T(8,128)(2,1)S(1)} collective-permute-done((bf16[256,1792]{1,0:T(8,128)(2,1)S(1)}, bf16[256,1792]{1,0:T(8,128)(2,1)S(1)}, u32[]{:S(2)}, u32[]{:S(2)}) %collective-permute-start.15) | collective-permute-done | bytes 917536 | tf_op jit(solution)/shard_map/ppermute | solution.py:52
  63.0 3.0 %shard_map.117 = (bf16[128,1792]{1,0:T(8,128)(2,1)S(1)}, bf16[128,1792]{1,0:T(8,128)(2,1)}) custom-call(bf16[256,512]{1,0:T(8,128)(2,1)S(1)} %fusion.5.hidden, bf16[7168,512]{1,0:T(8,128)(2,1)} %bitcast.49, bf16[256,1792]{1,0:T(8,128)(2,1)S(1)} %collective-permute-done.15.refs_0_), custom_call_target="tpu_custom_call" | custom-call | flops 469762048 | bytes 9699328 | tf_op jit(solution)/shard_map/pallas_call | solution.py:23
  66.0 1.3 %collective-permute-start.16 = (bf16[128,1792]{1,0:T(8,128)(2,1)}, bf16[128,1792]{1,0:T(8,128)(2,1)}, u32[]{:S(2)}, u32[]{:S(2)}) collective-permute-start(bf16[128,1792]{1,0:T(8,128)(2,1)} %get-tuple-element.36), channel_id=1, source_target_pairs={{0,4},{2,6},{4,0},{6,2},{8,12},{10,14},{12,8},{14,10},{16,20},{18,... | collective-permute-start | bytes 1376264 | tf_op jit(solution)/shard_map/ppermute | solution.py:47
  68.0 2.3 %shard_map.116 = (bf16[128,1792]{1,0:T(8,128)(2,1)S(1)}, bf16[128,1792]{1,0:T(8,128)(2,1)S(1)}) custom-call(bf16[256,512]{1,0:T(8,128)(2,1)S(1)} %fusion.5.hidden, bf16[7168,512]{1,0:T(8,128)(2,1)} %bitcast.50, bf16[256,1792]{1,0:T(8,128)(2,1)S(1)} %collective-permute-done.12.refs_0_), custom_call_target="tpu_custom_call" | custom-call | flops 469762048 | bytes 9699328 | tf_op jit(solution)/shard_map/pallas_call | solution.py:23
  71.2 6.1 %all-to-all-start.1 = ((bf16[16,24,576]{2,1,0:T(8,128)(2,1)}), bf16[16,24,576]{2,1,0:T(8,128)(2,1)S(1)}, u32[]{:S(2)}, u32[]{:S(2)}) async-start(bf16[16,24,576]{2,1,0:T(8,128)(2,1)} %bitcast.6), calls=%async_computation.1 | async-start | bytes 983040 | tf_op jit(solution)/shard_map/all_to_all | solution.py:321
  77.3 1.7 %collective-permute-done.16 = bf16[128,1792]{1,0:T(8,128)(2,1)} collective-permute-done((bf16[128,1792]{1,0:T(8,128)(2,1)}, bf16[128,1792]{1,0:T(8,128)(2,1)}, u32[]{:S(2)}, u32[]{:S(2)}) %collective-permute-start.16) | collective-permute-done | bytes 458784 | tf_op jit(solution)/shard_map/ppermute | solution.py:47
  81.1 4.0 %collective-permute-done.13 = bf16[128,1792]{1,0:T(8,128)(2,1)} collective-permute-done((bf16[128,1792]{1,0:T(8,128)(2,1)S(1)}, bf16[128,1792]{1,0:T(8,128)(2,1)}, u32[]{:S(2)}, u32[]{:S(2)}) %collective-permute-start.13) | collective-permute-done | bytes 458784 | tf_op jit(solution)/shard_map/ppermute | solution.py:47
  87.1 5.7 %collective-permute-done.17 = bf16[64,1792]{1,0:T(8,128)(2,1)S(1)} collective-permute-done((bf16[64,1792]{1,0:T(8,128)(2,1)S(1)}, bf16[64,1792]{1,0:T(8,128)(2,1)S(1)}, u32[]{:S(2)}, u32[]{:S(2)}) %collective-permute-start.17) | collective-permute-done | bytes 229408 | tf_op jit(solution)/shard_map/ppermute | solution.py:47
  93.0 1.4 %collective-permute-start.18 = (bf16[32,3584]{1,0:T(8,128)(2,1)S(1)}, bf16[32,3584]{1,0:T(8,128)(2,1)S(1)}, u32[]{:S(2)}, u32[]{:S(2)}) collective-permute-start(bf16[32,3584]{1,0:T(8,128)(2,1)S(1)} %pad_maximum_fusion.6), channel_id=1, source_target_pairs={{0,8},{2,10},{4,12},{6,14},{8,0},{10,2},{12,4},{14,6},{16,24},{18,... | collective-permute-start | bytes 688136 | tf_op jit(solution)/shard_map/ppermute | solution.py:47
  95.3 4.2 %collective-permute-done.18 = bf16[32,3584]{1,0:T(8,128)(2,1)S(1)} collective-permute-done((bf16[32,3584]{1,0:T(8,128)(2,1)S(1)}, bf16[32,3584]{1,0:T(8,128)(2,1)S(1)}, u32[]{:S(2)}, u32[]{:S(2)}) %collective-permute-start.18) | collective-permute-done | bytes 229408 | tf_op jit(solution)/shard_map/ppermute | solution.py:47
  99.6 2.3 %collective-permute-start.20 = (bf16[16,3584]{1,0:T(8,128)(2,1)S(1)}, bf16[16,3584]{1,0:T(8,128)(2,1)S(1)}, u32[]{:S(2)}, u32[]{:S(2)}) collective-permute-start(bf16[16,3584]{1,0:T(8,128)(2,1)S(1)} %add_convert_fusion.5), channel_id=1, source_target_pairs={{0,16},{2,18},{4,20},{6,22},{8,24},{10,26},{12,28},{14,30},{16,0},... | collective-permute-start | bytes 344072 | tf_op jit(solution)/shard_map/ppermute | solution.py:47
  102.9 3.0 %shard_map.118 = bf16[512,512]{1,0:T(8,128)(2,1)} custom-call(s32[2,384]{1,0:T(2,128)S(1)} %pad_add_fusion.owner, bf16[512,576]{1,0:T(8,128)(2,1)S(1)} %bitcast.46, bf16[384,576]{1,0:T(8,128)(2,1)S(1)} %bitcast.44, bf16[384,576]{1,0:T(8,128)(2,1)S(1)} %bitcast.47), custom_call_target="tpu_custom_call" | custom-call | flops 905969664 | bytes 3479552 | tf_op jit(solution)/shard_map/pallas_call | solution.py:23
  (77 shorter events, 25.3 us)
Async XLA Ops:
  0.6 12.9 %copy-start = (bf16[48,16,576]{2,1,0:T(8,128)(2,1)S(1)}, bf16[48,16,576]{2,1,0:T(8,128)(2,1)}, u32[]{:S(2)}) copy-start(bf16[48,16,576]{2,1,0:T(8,128)(2,1)} %param.16) | copy-start | bytes 2654212
  0.6 10.3 %collective-permute-start = (bf16[1,16,3584]{2,1,0:T(8,128)(2,1)}, bf16[1,16,3584]{2,1,0:T(8,128)(2,1)S(1)}, u32[]{:S(2)}, u32[]{:S(2)}) collective-permute-start(bf16[1,16,3584]{2,1,0:T(8,128)(2,1)} %bitcast.51), channel_id=1, source_target_pairs={{0,16},{2,18},{4,20},{6,22},{8,24},{10,26},{12,28},{14,30},{16,0},... | collective-permute-start | bytes 344072 | tf_op jit(solution)/shard_map/ppermute | solution.py:47
  6.5 4.5 %collective-permute-start.1 = (bf16[1,16,128]{2,1,0:T(8,128)(2,1)S(1)}, bf16[1,16,128]{2,1,0:T(8,128)(2,1)S(1)}, u32[]{:S(2)}, u32[]{:S(2)}) collective-permute-start(bf16[1,16,128]{2,1,0:T(8,128)(2,1)S(1)} %fusion.18), channel_id=1, source_target_pairs={{0,16},{2,18},{4,20},{6,22},{8,24},{10,26},{12,28},{14,30},{16,0},... | collective-permute-start | bytes 12296 | tf_op jit(solution)/shard_map/ppermute | solution.py:47
  11.9 8.1 %collective-permute-start.2 = (bf16[2,16,3712]{2,1,0:T(8,128)(2,1)S(1)}, bf16[2,16,3712]{2,1,0:T(8,128)(2,1)S(1)}, u32[]{:S(2)}, u32[]{:S(2)}) collective-permute-start(bf16[2,16,3712]{2,1,0:T(8,128)(2,1)S(1)} %maximum_maximum_fusion), channel_id=1, source_target_pairs={{0,8},{2,10},{4,12},{6,14},{8,0},{10,2},{12,4},{14,6},{16,24},{18,... | collective-permute-start | bytes 712712 | tf_op jit(solution)/shard_map/ppermute | solution.py:47
  14.5 19.9 %all-to-all-start = ((bf16[16,24,576]{2,1,0:T(8,128)(2,1)}), bf16[16,24,576]{2,1,0:T(8,128)(2,1)S(1)}, u32[]{:S(2)}, u32[]{:S(2)}) async-start(bf16[16,24,576]{2,1,0:T(8,128)(2,1)} %bitcast.37), calls=%async_computation | async-start | bytes 983040 | tf_op jit(solution)/shard_map/all_to_all | solution.py:422
  20.9 11.3 %collective-permute-start.3 = (bf16[4,16,1792]{2,1,0:T(8,128)(2,1)S(1)}, bf16[4,16,1792]{2,1,0:T(8,128)(2,1)S(1)}, u32[]{:S(2)}, u32[]{:S(2)}) collective-permute-start(bf16[4,16,1792]{2,1,0:T(8,128)(2,1)S(1)} %pad_maximum_fusion.5), channel_id=1, source_target_pairs={{0,4},{2,6},{4,0},{6,2},{8,12},{10,14},{12,8},{14,10},{16,20},{18,... | collective-permute-start | bytes 688136 | tf_op jit(solution)/shard_map/ppermute | solution.py:47
  23.7 10.3 %collective-permute-start.5 = (bf16[4,16,1920]{2,1,0:T(8,128)(2,1)S(1)}, bf16[4,16,1920]{2,1,0:T(8,128)(2,1)S(1)}, u32[]{:S(2)}, u32[]{:S(2)}) collective-permute-start(bf16[4,16,1920]{2,1,0:T(8,128)(2,1)S(1)} %pad_maximum_fusion.2), channel_id=1, source_target_pairs={{0,2},{2,0},{4,6},{6,4},{8,10},{10,8},{12,14},{14,12},{16,18},{18,... | collective-permute-start | bytes 737288 | tf_op jit(solution)/shard_map/ppermute | solution.py:47
  32.2 12.2 %collective-permute-start.4 = (bf16[8,16,1792]{2,1,0:T(8,128)(2,1)S(1)}, bf16[8,16,1792]{2,1,0:T(8,128)(2,1)}, u32[]{:S(2)}, u32[]{:S(2)}) collective-permute-start(bf16[8,16,1792]{2,1,0:T(8,128)(2,1)S(1)} %pad_maximum_fusion.1), channel_id=1, source_target_pairs={{0,2},{2,0},{4,6},{6,4},{8,10},{10,8},{12,14},{14,12},{16,18},{18,... | collective-permute-start | bytes 1376264 | tf_op jit(solution)/shard_map/ppermute | solution.py:47
  34.4 11.6 %collective-permute-start.7 = (bf16[8,16,1920]{2,1,0:T(8,128)(2,1)S(1)}, bf16[8,16,1920]{2,1,0:T(8,128)(2,1)S(1)}, u32[]{:S(2)}, u32[]{:S(2)}) collective-permute-start(bf16[8,16,1920]{2,1,0:T(8,128)(2,1)S(1)} %pad_maximum_fusion), channel_id=1, source_target_pairs={{0,4},{2,6},{4,0},{6,2},{8,12},{10,14},{12,8},{14,10},{16,20},{18,... | collective-permute-start | bytes 1474568 | tf_op jit(solution)/shard_map/ppermute | solution.py:47
  36.7 1.9 %collective-permute-start.6 = (bf16[16,24,576]{2,1,0:T(8,128)(2,1)S(1)}, bf16[16,24,576]{2,1,0:T(8,128)(2,1)S(1)}, u32[]{:S(2)}, u32[]{:S(2)}) collective-permute-start(bf16[16,24,576]{2,1,0:T(8,128)(2,1)S(1)} %all-to-all-done), channel_id=1, source_target_pairs={{0,1},{1,0},{2,3},{3,2},{4,5},{5,4},{6,7},{7,6},{8,9},{9,8},{10,11... | collective-permute-start | bytes 1327112 | tf_op jit(solution)/shard_map/ppermute | solution.py:52
  36.8 9.4 %collective-permute-start.8 = (bf16[8,16,1792]{2,1,0:T(8,128)(2,1)S(1)}, bf16[8,16,1792]{2,1,0:T(8,128)(2,1)}, u32[]{:S(2)}, u32[]{:S(2)}) collective-permute-start(bf16[8,16,1792]{2,1,0:T(8,128)(2,1)S(1)} %pad_maximum_fusion.1), channel_id=1, source_target_pairs={{0,1},{1,0},{2,3},{3,2},{4,5},{5,4},{6,7},{7,6},{8,9},{9,8},{10,11... | collective-permute-start | bytes 1376264 | tf_op jit(solution)/shard_map/ppermute | solution.py:52
  44.4 2.8 %collective-permute-start.9 = (bf16[8,16,1792]{2,1,0:T(8,128)(2,1)}, bf16[8,16,1792]{2,1,0:T(8,128)(2,1)}, u32[]{:S(2)}, u32[]{:S(2)}) collective-permute-start(bf16[8,16,1792]{2,1,0:T(8,128)(2,1)} %collective-permute-done.4), channel_id=1, source_target_pairs={{0,1},{1,0},{2,3},{3,2},{4,5},{5,4},{6,7},{7,6},{8,9},{9,8},{10,11... | collective-permute-start | bytes 1376264 | tf_op jit(solution)/shard_map/ppermute | solution.py:52
  44.4 2.8 %collective-permute-start.10 = (bf16[8,16,1920]{2,1,0:T(8,128)(2,1)S(1)}, bf16[8,16,1920]{2,1,0:T(8,128)(2,1)S(1)}, u32[]{:S(2)}, u32[]{:S(2)}) collective-permute-start(bf16[8,16,1920]{2,1,0:T(8,128)(2,1)S(1)} %pad_maximum_fusion), channel_id=1, source_target_pairs={{0,1},{1,0},{2,3},{3,2},{4,5},{5,4},{6,7},{7,6},{8,9},{9,8},{10,11... | collective-permute-start | bytes 1474568 | tf_op jit(solution)/shard_map/ppermute | solution.py:52
  46.0 1.9 %collective-permute-start.11 = (bf16[8,16,1920]{2,1,0:T(8,128)(2,1)S(1)}, bf16[8,16,1920]{2,1,0:T(8,128)(2,1)S(1)}, u32[]{:S(2)}, u32[]{:S(2)}) collective-permute-start(bf16[8,16,1920]{2,1,0:T(8,128)(2,1)S(1)} %collective-permute-done.7), channel_id=1, source_target_pairs={{0,1},{1,0},{2,3},{3,2},{4,5},{5,4},{6,7},{7,6},{8,9},{9,8},{10,11... | collective-permute-start | bytes 1474568 | tf_op jit(solution)/shard_map/ppermute | solution.py:52
  60.4 2.5 %collective-permute-start.15 = (bf16[256,1792]{1,0:T(8,128)(2,1)S(1)}, bf16[256,1792]{1,0:T(8,128)(2,1)S(1)}, u32[]{:S(2)}, u32[]{:S(2)}) collective-permute-start(bf16[256,1792]{1,0:T(8,128)(2,1)S(1)} %get-tuple-element.34), channel_id=1, source_target_pairs={{0,1},{1,0},{2,3},{3,2},{4,5},{5,4},{6,7},{7,6},{8,9},{9,8},{10,11... | collective-permute-start | bytes 2752520 | tf_op jit(solution)/shard_map/ppermute | solution.py:52
  60.6 7.4 %collective-permute-start.12 = (bf16[256,1792]{1,0:T(8,128)(2,1)S(1)}, bf16[256,1792]{1,0:T(8,128)(2,1)S(1)}, u32[]{:S(2)}, u32[]{:S(2)}) collective-permute-start(bf16[256,1792]{1,0:T(8,128)(2,1)S(1)} %get-tuple-element.31), channel_id=1, source_target_pairs={{0,1},{1,0},{2,3},{3,2},{4,5},{5,4},{6,7},{7,6},{8,9},{9,8},{10,11... | collective-permute-start | bytes 2752520 | tf_op jit(solution)/shard_map/ppermute | solution.py:52
  66.0 12.9 %collective-permute-start.16 = (bf16[128,1792]{1,0:T(8,128)(2,1)}, bf16[128,1792]{1,0:T(8,128)(2,1)}, u32[]{:S(2)}, u32[]{:S(2)}) collective-permute-start(bf16[128,1792]{1,0:T(8,128)(2,1)} %get-tuple-element.36), channel_id=1, source_target_pairs={{0,4},{2,6},{4,0},{6,2},{8,12},{10,14},{12,8},{14,10},{16,20},{18,... | collective-permute-start | bytes 1376264 | tf_op jit(solution)/shard_map/ppermute | solution.py:47
  70.3 14.8 %collective-permute-start.13 = (bf16[128,1792]{1,0:T(8,128)(2,1)S(1)}, bf16[128,1792]{1,0:T(8,128)(2,1)}, u32[]{:S(2)}, u32[]{:S(2)}) collective-permute-start(bf16[128,1792]{1,0:T(8,128)(2,1)S(1)} %get-tuple-element.33), channel_id=1, source_target_pairs={{0,2},{2,0},{4,6},{6,4},{8,10},{10,8},{12,14},{14,12},{16,18},{18,... | collective-permute-start | bytes 1376264 | tf_op jit(solution)/shard_map/ppermute | solution.py:47
  71.2 21.8 %all-to-all-start.1 = ((bf16[16,24,576]{2,1,0:T(8,128)(2,1)}), bf16[16,24,576]{2,1,0:T(8,128)(2,1)S(1)}, u32[]{:S(2)}, u32[]{:S(2)}) async-start(bf16[16,24,576]{2,1,0:T(8,128)(2,1)} %bitcast.6), calls=%async_computation.1 | async-start | bytes 983040 | tf_op jit(solution)/shard_map/all_to_all | solution.py:321
  80.1 12.7 %collective-permute-start.17 = (bf16[64,1792]{1,0:T(8,128)(2,1)S(1)}, bf16[64,1792]{1,0:T(8,128)(2,1)S(1)}, u32[]{:S(2)}, u32[]{:S(2)}) collective-permute-start(bf16[64,1792]{1,0:T(8,128)(2,1)S(1)} %get-tuple-element.52), channel_id=1, source_target_pairs={{0,2},{2,0},{4,6},{6,4},{8,10},{10,8},{12,14},{14,12},{16,18},{18,... | collective-permute-start | bytes 688136 | tf_op jit(solution)/shard_map/ppermute | solution.py:47
  86.3 6.6 %collective-permute-start.14 = (bf16[64,1792]{1,0:T(8,128)(2,1)S(1)}, bf16[64,1792]{1,0:T(8,128)(2,1)S(1)}, u32[]{:S(2)}, u32[]{:S(2)}) collective-permute-start(bf16[64,1792]{1,0:T(8,128)(2,1)S(1)} %get-tuple-element.50), channel_id=1, source_target_pairs={{0,4},{2,6},{4,0},{6,2},{8,12},{10,14},{12,8},{14,10},{16,20},{18,... | collective-permute-start | bytes 688136 | tf_op jit(solution)/shard_map/ppermute | solution.py:47
  93.0 6.5 %collective-permute-start.18 = (bf16[32,3584]{1,0:T(8,128)(2,1)S(1)}, bf16[32,3584]{1,0:T(8,128)(2,1)S(1)}, u32[]{:S(2)}, u32[]{:S(2)}) collective-permute-start(bf16[32,3584]{1,0:T(8,128)(2,1)S(1)} %pad_maximum_fusion.6), channel_id=1, source_target_pairs={{0,8},{2,10},{4,12},{6,14},{8,0},{10,2},{12,4},{14,6},{16,24},{18,... | collective-permute-start | bytes 688136 | tf_op jit(solution)/shard_map/ppermute | solution.py:47
  95.2 4.3 %collective-permute-start.19 = (bf16[16,24,576]{2,1,0:T(8,128)(2,1)S(1)}, bf16[16,24,576]{2,1,0:T(8,128)(2,1)S(1)}, u32[]{:S(2)}, u32[]{:S(2)}) collective-permute-start(bf16[16,24,576]{2,1,0:T(8,128)(2,1)S(1)} %all-to-all-done.1), channel_id=1, source_target_pairs={{0,1},{1,0},{2,3},{3,2},{4,5},{5,4},{6,7},{7,6},{8,9},{9,8},{10,11... | collective-permute-start | bytes 1327112 | tf_op jit(solution)/shard_map/ppermute | solution.py:52
  99.6 7.0 %collective-permute-start.20 = (bf16[16,3584]{1,0:T(8,128)(2,1)S(1)}, bf16[16,3584]{1,0:T(8,128)(2,1)S(1)}, u32[]{:S(2)}, u32[]{:S(2)}) collective-permute-start(bf16[16,3584]{1,0:T(8,128)(2,1)S(1)} %add_convert_fusion.5), channel_id=1, source_target_pairs={{0,16},{2,18},{4,20},{6,22},{8,24},{10,26},{12,28},{14,30},{16,0},... | collective-permute-start | bytes 344072 | tf_op jit(solution)/shard_map/ppermute | solution.py:47
  (3 other events, 21.5 us)

commit v12 on v11

--- a/solution.py
+++ b/solution.py
@@ -126,10 +126,9 @@
     )
 
 
-def scatter_sums(sums, orders, hooks):
+def scatter_sums(kepts, sents, orders, hooks):
     steps = len(orders[0])
-    kepts, sents = zip(*sums)
-    kepts, sents = list(kepts), list(sents)
+    sents = list(sents)
     for step in range(steps):
         if step in hooks:
             sents[-1] = hooks[step](sents[-1])
@@ -179,7 +178,7 @@
     )
 
 
-def others_kernel(step, spots, tp_size, cut, rows, hidden, weight, *refs):
+def group_kernel(step, spots, tp_size, cut, rows, hidden, weight, *refs):
     parts = len(spots)
     outs, (held, turned, arrived) = refs[:parts], refs[parts:]
     target = lax.rem(lax.axis_index("tp") + step, tp_size)
@@ -203,13 +202,13 @@
             ).astype(jnp.bfloat16)
 
 
-def down_others(hidden, weight, step, spots, rows):
+def down_group(hidden, weight, step, spots, rows):
     parts = len(spots)
     tp_size = lax.axis_size("tp")
     cut = weight.shape[0] // tp_size // parts
     shape = jax.ShapeDtypeStruct((hidden.shape[0], cut), jnp.bfloat16)
     return kernel_call(
-        functools.partial(others_kernel, step, spots, tp_size, cut, rows),
+        functools.partial(group_kernel, step, spots, tp_size, cut, rows),
         [shape] * parts,
         [hidden, weight],
         flops=2 * hidden.size * cut * parts,
@@ -223,51 +222,41 @@
     )
 
 
-def own_kernel(part, parts, spots, cut, rows, count, hidden, weight, *refs):
-    others, (kept, sent, held, turned, passed, arrived) = refs[:count], refs[count:]
-    start = pl.multiple_of((lax.axis_index("tp") * parts + part) * cut, cut)
-    copies = [pltpu.make_async_copy(weight.at[pl.ds(start, cut)], held, arrived.at[count])]
-    for index, other in enumerate(others):
-        copies.append(pltpu.make_async_copy(other, passed.at[index], arrived.at[index]))
+def halves_kernel(parts, first, *refs):
+    outs, (held, arrived) = refs[-2 - parts : -2], refs[-2:]
+    terms = refs[: -2 - parts]
+    count = len(terms) // parts
+    half, rows = outs[0].shape[0], 16
+    copies = [
+        pltpu.make_async_copy(term.at[pl.ds(first, half)], held.at[index], arrived.at[index])
+        for index, term in enumerate(terms)
+    ]
     for copy in copies:
         copy.start()
-    turn_rows(hidden, turned, spots, rows)
-    for copy in copies:
-        copy.wait()
-    half = hidden.shape[0] // 2
-    chunk = min(256, hidden.shape[0])
-    width = cut // 2 if cut % 256 == 0 else cut
-    for column in range(0, cut, width):
-        for row in range(0, hidden.shape[0], chunk):
-            total = down_product(turned, held, row, chunk, column, width)
-            for index in range(count):
-                total = total + passed[
-                    index, row : row + chunk, column : column + width
-                ].astype(jnp.float32)
-            total = total.astype(jnp.bfloat16)
-            for first in range(row, row + chunk, min(chunk, half)):
-                out = kept if first < half else sent
-                place = first % half
-                piece = total[first - row : first - row + min(chunk, half)]
-                out[place : place + piece.shape[0], column : column + width] = piece
-
-
-def down_own(hidden, weight, part, parts, spots, rows, others):
-    cut = weight.shape[0] // lax.axis_size("tp") // parts
-    shape = jax.ShapeDtypeStruct((hidden.shape[0] // 2, cut), jnp.bfloat16)
-    anywhere = pl.BlockSpec(memory_space=pl.ANY)
+    for part in range(parts):
+        for index in range(part * count, (part + 1) * count):
+            copies[index].wait()
+        for row in range(0, half, rows):
+            total = held[part * count, row : row + rows].astype(jnp.float32)
+            for index in range(part * count + 1, (part + 1) * count):
+                total = total + held[index, row : row + rows].astype(jnp.float32)
+            outs[part][row : row + rows] = total.astype(jnp.bfloat16)
+
+
+def add_halves(terms, second):
+    parts = len(terms)
+    flat = [term for part in terms for term in part]
+    half, cut = flat[0].shape[0] // 2, flat[0].shape[1]
     return kernel_call(
-        functools.partial(own_kernel, part, parts, spots, cut, rows, len(others)),
-        [shape, shape],
-        [hidden, weight] + others,
-        flops=2 * hidden.size * cut,
-        spare=(cut * weight.shape[1] + hidden.shape[0] * cut * len(others)) * 2 + (8 << 20),
-        in_specs=[WHOLE] + [anywhere] * (1 + len(others)),
+        functools.partial(halves_kernel, parts, half if second else 0),
+        [jax.ShapeDtypeStruct((half, cut), jnp.bfloat16)] * parts,
+        flat,
+        flops=half * cut * len(flat),
+        spare=half * cut * len(flat) * 2 + (2 << 20),
+        in_specs=[pl.BlockSpec(memory_space=pl.ANY)] * len(flat),
         scratch_shapes=[
-            pltpu.VMEM((cut, weight.shape[1]), weight.dtype),
-            pltpu.VMEM(hidden.shape, hidden.dtype),
-            pltpu.VMEM((len(others), hidden.shape[0], cut), jnp.bfloat16),
-            pltpu.SemaphoreType.DMA((1 + len(others),)),
+            pltpu.VMEM((len(flat), half, cut), jnp.bfloat16),
+            pltpu.SemaphoreType.DMA((len(flat),)),
         ],
     )
 
@@ -456,15 +445,14 @@
     ).astype(jnp.bfloat16)
 
     down_weight = pltpu.with_memory_space_constraint(expert_down[0], pltpu.HBM)
-    passed = [[] for _ in range(parts)]
+    terms = [[] for _ in range(parts)]
     for step in range(1, tp_size):
-        others = down_others(hidden, down_weight, step, from_first, row_count)
+        others = down_group(hidden, down_weight, step, from_first, row_count)
         for part in range(parts):
-            passed[part].append(pass_tp(others[part], step))
-    sums = [
-        down_own(hidden, down_weight, part, parts, from_first[part], row_count, passed[part])
-        for part in range(parts)
-    ]
+            terms[part].append(pass_tp(others[part], step))
+    own = down_group(hidden, down_weight, 0, from_first, row_count)
+    terms = [[own[part]] + terms[part] for part in range(parts)]
+    sents, kepts = add_halves(terms, True), add_halves(terms, False)
 
     def beside_first_sum(sent):
         held["keys"] = cache_in(tie(ordered, sent), block_size, latent)
@@ -490,7 +478,7 @@
         len(bits) - 1: beside_last_sum,
         -1: ahead_of_end,
     }
-    return (scatter_sums(sums, orders, hooks), held["attended"])
+    return (scatter_sums(kepts, sents, orders, hooks), held["attended"])
 
 
 def solution(mesh):

time: 108 us -> 108 us (level)
  waiting for transfers between devices: 38.4 us -> 33 us
  local copies, waits for them, and re-layouts: 5.55 us -> 8.28 us
  starting transfers between devices: 32.8 us -> 35.2 us
  Pallas kernels: 14.4 us -> 15.7 us
    ppermute x13, waiting for transfers between devices: 33.3 us -> 29.6 us  [exchange(): lax.ppermute(value, 'ep', [(index, index ^ bit) for index in range(ep_siz...]
    unnamed x11 -> x19, local copies, waits for them, and re-layouts: 3.49 us -> 6.76 us
    ppermute x13, starting transfers between devices: 19.5 us -> 21.9 us  [exchange(): lax.ppermute(value, 'ep', [(index, index ^ bit) for index in range(ep_siz...]
    ppermute x8, waiting for transfers between devices: 4.76 us -> 3.01 us  [pass_tp(): lax.ppermute(value, 'tp', [(index, (index + step) % tp_size) for index in...]
    pallas_call x6 -> x7, Pallas kernels: 14.4 us -> 15.7 us  [kernel_call(): pl.pallas_call(kernel, out_shape=out_shape, in_specs=in_specs or [WHOLE]...]
  transfers between devices with their start and end apart: 23 -> 23, of which waited for: 16 -> 14; matrix products, arithmetic and copies ran while one was open for 9% -> 8% of each run, Pallas kernels for 9% -> 8%
where the time goes in v12:
time: 108 us
  starting transfers between devices  35.2 us (33%)
  waiting for transfers between devices  33 us (31%)
  Pallas kernels  15.7 us (15%)
  local copies, waits for them, and re-layouts  8.28 us (8%)
  matrix products  7.78 us (7%)
  other arithmetic  6.71 us (6%)
    ppermute x13, waiting for transfers between devices, exchange(): lax.ppermute(value, 'ep', [(index, index ^ bit) for index in range(ep_siz...  29.6 us
    ppermute x13, starting transfers between devices, exchange(): lax.ppermute(value, 'ep', [(index, index ^ bit) for index in range(ep_siz...  21.9 us
    pallas_call x7, Pallas kernels, kernel_call(): pl.pallas_call(kernel, out_shape=out_shape, in_specs=in_specs or [WHOLE]...  15.7 us
    dot_general x1, matrix products, body(): jnp.einsum('sd,dgf->sgf', all_rows, expert_gate_up[0], preferred_element_...  7.78 us
    unnamed x19, local copies, waits for them, and re-layouts  6.76 us
    all_to_all x1, starting transfers between devices, cache_in(): lax.all_to_all(ordered, 'ep', split_axis=0, concat_axis=0, tiled=True)  6.06 us
    all_to_all x1, starting transfers between devices, beside_shared(): lax.all_to_all(pieces, 'ep', split_axis=0, concat_axis=0, tiled=True)  5.54 us
    convert_element_type x6, other arithmetic, add_up(): return total.astype(jnp.bfloat16)  3.14 us
  transfers between devices with their start and end apart: 23, of which 14 were waited for; matrix products, arithmetic and copies ran while one was open for 8% of the time, Pallas kernels for 8%

profile of v12, /device:TPU:0, one launch (start us, length us, event | category | flops | bytes accessed | tf_op | source)
XLA Modules:
  0.0 107.6 jit_solution(16113557214939924207)
XLA Ops:
  0.6 4.1 %collective-permute-start = (bf16[1,16,3584]{2,1,0:T(8,128)(2,1)}, bf16[1,16,3584]{2,1,0:T(8,128)(2,1)S(1)}, u32[]{:S(2)}, u32[]{:S(2)}) collective-permute-start(bf16[1,16,3584]{2,1,0:T(8,128)(2,1)} %bitcast.50), channel_id=1, source_target_pairs={{0,16},{2,18},{4,20},{6,22},{8,24},{10,26},{12,28},{14,30},{16,0},... | collective-permute-start | bytes 344072 | tf_op jit(solution)/shard_map/ppermute | solution.py:47
  6.6 4.4 %collective-permute-done.1 = bf16[1,16,128]{2,1,0:T(8,128)(2,1)S(1)} collective-permute-done((bf16[1,16,128]{2,1,0:T(8,128)(2,1)S(1)}, bf16[1,16,128]{2,1,0:T(8,128)(2,1)S(1)}, u32[]{:S(2)}, u32[]{:S(2)}) %collective-permute-start.1) | collective-permute-done | bytes 4128 | tf_op jit(solution)/shard_map/ppermute | solution.py:47
  11.9 1.6 %collective-permute-start.2 = (bf16[2,16,3712]{2,1,0:T(8,128)(2,1)S(1)}, bf16[2,16,3712]{2,1,0:T(8,128)(2,1)S(1)}, u32[]{:S(2)}, u32[]{:S(2)}) collective-permute-start(bf16[2,16,3712]{2,1,0:T(8,128)(2,1)S(1)} %maximum_maximum_fusion), channel_id=1, source_target_pairs={{0,8},{2,10},{4,12},{6,14},{8,0},{10,2},{12,4},{14,6},{16,24},{18,... | collective-permute-start | bytes 712712 | tf_op jit(solution)/shard_map/ppermute | solution.py:47
  14.5 5.5 %all-to-all-start = ((bf16[16,24,576]{2,1,0:T(8,128)(2,1)}), bf16[16,24,576]{2,1,0:T(8,128)(2,1)S(1)}, u32[]{:S(2)}, u32[]{:S(2)}) async-start(bf16[16,24,576]{2,1,0:T(8,128)(2,1)} %bitcast.37), calls=%async_computation | async-start | bytes 983040 | tf_op jit(solution)/shard_map/all_to_all | solution.py:411
  20.9 2.0 %collective-permute-start.3 = (bf16[4,16,1792]{2,1,0:T(8,128)(2,1)S(1)}, bf16[4,16,1792]{2,1,0:T(8,128)(2,1)S(1)}, u32[]{:S(2)}, u32[]{:S(2)}) collective-permute-start(bf16[4,16,1792]{2,1,0:T(8,128)(2,1)S(1)} %pad_maximum_fusion.5), channel_id=1, source_target_pairs={{0,4},{2,6},{4,0},{6,2},{8,12},{10,14},{12,8},{14,10},{16,20},{18,... | collective-permute-start | bytes 688136 | tf_op jit(solution)/shard_map/ppermute | solution.py:47
  23.7 1.5 %collective-permute-start.5 = (bf16[4,16,1920]{2,1,0:T(8,128)(2,1)S(1)}, bf16[4,16,1920]{2,1,0:T(8,128)(2,1)S(1)}, u32[]{:S(2)}, u32[]{:S(2)}) collective-permute-start(bf16[4,16,1920]{2,1,0:T(8,128)(2,1)S(1)} %pad_maximum_fusion.2), channel_id=1, source_target_pairs={{0,2},{2,0},{4,6},{6,4},{8,10},{10,8},{12,14},{14,12},{16,18},{18,... | collective-permute-start | bytes 737288 | tf_op jit(solution)/shard_map/ppermute | solution.py:47
  25.2 6.9 %collective-permute-done.3 = bf16[4,16,1792]{2,1,0:T(8,128)(2,1)S(1)} collective-permute-done((bf16[4,16,1792]{2,1,0:T(8,128)(2,1)S(1)}, bf16[4,16,1792]{2,1,0:T(8,128)(2,1)S(1)}, u32[]{:S(2)}, u32[]{:S(2)}) %collective-permute-start.3) | collective-permute-done | bytes 229408 | tf_op jit(solution)/shard_map/ppermute | solution.py:47
  32.2 1.3 %collective-permute-start.4 = (bf16[8,16,1792]{2,1,0:T(8,128)(2,1)S(1)}, bf16[8,16,1792]{2,1,0:T(8,128)(2,1)}, u32[]{:S(2)}, u32[]{:S(2)}) collective-permute-start(bf16[8,16,1792]{2,1,0:T(8,128)(2,1)S(1)} %pad_maximum_fusion.1), channel_id=1, source_target_pairs={{0,2},{2,0},{4,6},{6,4},{8,10},{10,8},{12,14},{14,12},{16,18},{18,... | collective-permute-start | bytes 1376264 | tf_op jit(solution)/shard_map/ppermute | solution.py:47
  38.7 1.6 %shard_map.113 = bf16[384,576]{1,0:T(8,128)(2,1)} custom-call(s32[384,2]{1,0:T(8,128)S(1)} %fusion.7.index, bf16[384,576]{1,0:T(8,128)(2,1)S(1)} %bitcast.39, bf16[384,576]{1,0:T(8,128)(2,1)S(1)} %bitcast.45), custom_call_target="tpu_custom_call" | custom-call | flops 339738624 | bytes 2217984 | tf_op jit(solution)/shard_map/pallas_call | solution.py:23
  40.2 4.2 %collective-permute-done.4 = bf16[8,16,1792]{2,1,0:T(8,128)(2,1)} collective-permute-done((bf16[8,16,1792]{2,1,0:T(8,128)(2,1)S(1)}, bf16[8,16,1792]{2,1,0:T(8,128)(2,1)}, u32[]{:S(2)}, u32[]{:S(2)}) %collective-permute-start.4) | collective-permute-done | bytes 458784 | tf_op jit(solution)/shard_map/ppermute | solution.py:47
  47.8 1.5 %shard_map.114 = bf16[256,7168]{1,0:T(8,128)(2,1)S(1)} custom-call(bf16[128,1792]{1,0:T(8,128)(2,1)S(1)} %bitcast.40, bf16[128,1792]{1,0:T(8,128)(2,1)} %bitcast.7.refs_1_, bf16[128,1920]{1,0:T(8,128)(2,1)S(1)} %bitcast.38, bf16[128,1920]{1,0:T(8,128)(2,1)S(1)} %bitcast.41, bf16[128,1792]{1,0:T(8,128)(2,1)} %bitcast.10.refs_4_, ...), custom_call_target="tpu_custom_call" | custom-call | bytes 11272192 | tf_op jit(solution)/shard_map/pallas_call | solution.py:23
  49.4 7.8 %fusion = f32[256,2,512]{2,0,1:T(8,128)S(1)} fusion(bf16[7168,2,512]{2,1,0:T(2,128)(2,1)} %bitcast.54, bf16[256,7168]{1,0:T(8,128)(2,1)S(1)} %shard_map.114), kind=kOutput, calls=%fused_computation | convolution fusion | flops 3758096384 | bytes 19398656 | tf_op jit(solution)/shard_map/sd,dgf->sgf/dot_general | solution.py:440
  57.4 3.0 %shard_map.116 = (bf16[256,1792]{1,0:T(8,128)(2,1)S(1)}, bf16[256,1792]{1,0:T(8,128)(2,1)S(1)}) custom-call(bf16[256,512]{1,0:T(8,128)(2,1)S(1)} %fusion.5.hidden, bf16[7168,512]{1,0:T(8,128)(2,1)} %bitcast.48), custom_call_target="tpu_custom_call" | custom-call | flops 939524096 | bytes 9699328 | tf_op jit(solution)/shard_map/pallas_call | solution.py:23
  61.0 3.0 %shard_map.115 = (bf16[256,1792]{1,0:T(8,128)(2,1)S(1)}, bf16[256,1792]{1,0:T(8,128)(2,1)S(1)}) custom-call(bf16[256,512]{1,0:T(8,128)(2,1)S(1)} %fusion.5.hidden, bf16[7168,512]{1,0:T(8,128)(2,1)} %bitcast.49), custom_call_target="tpu_custom_call" | custom-call | flops 939524096 | bytes 9699328 | tf_op jit(solution)/shard_map/pallas_call | solution.py:23
  64.3 2.2 %shard_map.118 = (bf16[128,1792]{1,0:T(8,128)(2,1)}, bf16[128,1792]{1,0:T(8,128)(2,1)}) custom-call(bf16[256,1792]{1,0:T(8,128)(2,1)S(1)} %get-tuple-element.33.refs_0_, bf16[256,1792]{1,0:T(8,128)(2,1)S(1)} %collective-permute-done.12.refs_1_, bf16[256,1792]{1,0:T(8,128)(2,1)S(1)} %get-tuple-element.35.refs_2_, ...), custom_call_target="tpu_custom_call" | custom-call | flops 917504 | bytes 4587520 | tf_op jit(solution)/shard_map/pallas_call | solution.py:23
  67.4 1.3 %collective-permute-start.16 = (bf16[128,1792]{1,0:T(8,128)(2,1)}, bf16[128,1792]{1,0:T(8,128)(2,1)}, u32[]{:S(2)}, u32[]{:S(2)}) collective-permute-start(bf16[128,1792]{1,0:T(8,128)(2,1)} %get-tuple-element.40), channel_id=1, source_target_pairs={{0,4},{2,6},{4,0},{6,2},{8,12},{10,14},{12,8},{14,10},{16,20},{18,... | collective-permute-start | bytes 1376264 | tf_op jit(solution)/shard_map/ppermute | solution.py:47
  69.7 6.1 %all-to-all-start.1 = ((bf16[16,24,576]{2,1,0:T(8,128)(2,1)}), bf16[16,24,576]{2,1,0:T(8,128)(2,1)S(1)}, u32[]{:S(2)}, u32[]{:S(2)}) async-start(bf16[16,24,576]{2,1,0:T(8,128)(2,1)} %bitcast.6), calls=%async_computation.1 | async-start | bytes 983040 | tf_op jit(solution)/shard_map/all_to_all | solution.py:310
  78.1 1.3 %shard_map.117 = (bf16[128,1792]{1,0:T(8,128)(2,1)S(1)}, bf16[128,1792]{1,0:T(8,128)(2,1)S(1)}) custom-call(bf16[256,1792]{1,0:T(8,128)(2,1)S(1)} %copy-done.2, bf16[256,1792]{1,0:T(8,128)(2,1)S(1)} %collective-permute-done.12.refs_1_, bf16[256,1792]{1,0:T(8,128)(2,1)S(1)} %copy-done.4, bf16[256,1792]{1,0:T(8,128)(2,1)S(1)} %collective-permute-done.13.refs_3_), custom_call_target="tpu_custom_call" | custom-call | flops 917504 | bytes 4587520 | tf_op jit(solution)/shard_map/pallas_call | solution.py:23
  79.4 3.1 %collective-permute-done.16 = bf16[128,1792]{1,0:T(8,128)(2,1)} collective-permute-done((bf16[128,1792]{1,0:T(8,128)(2,1)}, bf16[128,1792]{1,0:T(8,128)(2,1)}, u32[]{:S(2)}, u32[]{:S(2)}) %collective-permute-start.16) | collective-permute-done | bytes 458784 | tf_op jit(solution)/shard_map/ppermute | solution.py:47
  85.4 1.8 %collective-permute-start.15 = (bf16[64,1792]{1,0:T(8,128)(2,1)S(1)}, bf16[64,1792]{1,0:T(8,128)(2,1)S(1)}, u32[]{:S(2)}, u32[]{:S(2)}) collective-permute-start(bf16[64,1792]{1,0:T(8,128)(2,1)S(1)} %get-tuple-element.54), channel_id=1, source_target_pairs={{0,4},{2,6},{4,0},{6,2},{8,12},{10,14},{12,8},{14,10},{16,20},{18,... | collective-permute-start | bytes 688136 | tf_op jit(solution)/shard_map/ppermute | solution.py:47
  87.2 4.3 %collective-permute-done.17 = bf16[64,1792]{1,0:T(8,128)(2,1)S(1)} collective-permute-done((bf16[64,1792]{1,0:T(8,128)(2,1)S(1)}, bf16[64,1792]{1,0:T(8,128)(2,1)S(1)}, u32[]{:S(2)}, u32[]{:S(2)}) %collective-permute-start.17) | collective-permute-done | bytes 229408 | tf_op jit(solution)/shard_map/ppermute | solution.py:47
  93.6 4.6 %collective-permute-done.18 = bf16[32,3584]{1,0:T(8,128)(2,1)S(1)} collective-permute-done((bf16[32,3584]{1,0:T(8,128)(2,1)S(1)}, bf16[32,3584]{1,0:T(8,128)(2,1)S(1)}, u32[]{:S(2)}, u32[]{:S(2)}) %collective-permute-start.18) | collective-permute-done | bytes 229408 | tf_op jit(solution)/shard_map/ppermute | solution.py:47
  98.2 4.6 %collective-permute-start.20 = (bf16[16,3584]{1,0:T(8,128)(2,1)S(1)}, bf16[16,3584]{1,0:T(8,128)(2,1)S(1)}, u32[]{:S(2)}, u32[]{:S(2)}) collective-permute-start(bf16[16,3584]{1,0:T(8,128)(2,1)S(1)} %add_convert_fusion.5), channel_id=1, source_target_pairs={{0,16},{2,18},{4,20},{6,22},{8,24},{10,26},{12,28},{14,30},{16,0},... | collective-permute-start | bytes 344072 | tf_op jit(solution)/shard_map/ppermute | solution.py:47
  103.9 3.0 %shard_map.119 = bf16[512,512]{1,0:T(8,128)(2,1)} custom-call(s32[2,384]{1,0:T(2,128)S(1)} %pad_add_fusion.owner, bf16[512,576]{1,0:T(8,128)(2,1)S(1)} %bitcast.46, bf16[384,576]{1,0:T(8,128)(2,1)S(1)} %bitcast.44, bf16[384,576]{1,0:T(8,128)(2,1)S(1)} %bitcast.47), custom_call_target="tpu_custom_call" | custom-call | flops 905969664 | bytes 3479552 | tf_op jit(solution)/shard_map/pallas_call | solution.py:23
  (86 shorter events, 25.9 us)
Async XLA Ops:
  0.6 12.9 %copy-start = (bf16[48,16,576]{2,1,0:T(8,128)(2,1)S(1)}, bf16[48,16,576]{2,1,0:T(8,128)(2,1)}, u32[]{:S(2)}) copy-start(bf16[48,16,576]{2,1,0:T(8,128)(2,1)} %param.16) | copy-start | bytes 2654212
  0.6 10.3 %collective-permute-start = (bf16[1,16,3584]{2,1,0:T(8,128)(2,1)}, bf16[1,16,3584]{2,1,0:T(8,128)(2,1)S(1)}, u32[]{:S(2)}, u32[]{:S(2)}) collective-permute-start(bf16[1,16,3584]{2,1,0:T(8,128)(2,1)} %bitcast.50), channel_id=1, source_target_pairs={{0,16},{2,18},{4,20},{6,22},{8,24},{10,26},{12,28},{14,30},{16,0},... | collective-permute-start | bytes 344072 | tf_op jit(solution)/shard_map/ppermute | solution.py:47
  6.5 4.5 %collective-permute-start.1 = (bf16[1,16,128]{2,1,0:T(8,128)(2,1)S(1)}, bf16[1,16,128]{2,1,0:T(8,128)(2,1)S(1)}, u32[]{:S(2)}, u32[]{:S(2)}) collective-permute-start(bf16[1,16,128]{2,1,0:T(8,128)(2,1)S(1)} %fusion.18), channel_id=1, source_target_pairs={{0,16},{2,18},{4,20},{6,22},{8,24},{10,26},{12,28},{14,30},{16,0},... | collective-permute-start | bytes 12296 | tf_op jit(solution)/shard_map/ppermute | solution.py:47
  11.9 8.1 %collective-permute-start.2 = (bf16[2,16,3712]{2,1,0:T(8,128)(2,1)S(1)}, bf16[2,16,3712]{2,1,0:T(8,128)(2,1)S(1)}, u32[]{:S(2)}, u32[]{:S(2)}) collective-permute-start(bf16[2,16,3712]{2,1,0:T(8,128)(2,1)S(1)} %maximum_maximum_fusion), channel_id=1, source_target_pairs={{0,8},{2,10},{4,12},{6,14},{8,0},{10,2},{12,4},{14,6},{16,24},{18,... | collective-permute-start | bytes 712712 | tf_op jit(solution)/shard_map/ppermute | solution.py:47
  14.5 19.9 %all-to-all-start = ((bf16[16,24,576]{2,1,0:T(8,128)(2,1)}), bf16[16,24,576]{2,1,0:T(8,128)(2,1)S(1)}, u32[]{:S(2)}, u32[]{:S(2)}) async-start(bf16[16,24,576]{2,1,0:T(8,128)(2,1)} %bitcast.37), calls=%async_computation | async-start | bytes 983040 | tf_op jit(solution)/shard_map/all_to_all | solution.py:411
  20.9 11.3 %collective-permute-start.3 = (bf16[4,16,1792]{2,1,0:T(8,128)(2,1)S(1)}, bf16[4,16,1792]{2,1,0:T(8,128)(2,1)S(1)}, u32[]{:S(2)}, u32[]{:S(2)}) collective-permute-start(bf16[4,16,1792]{2,1,0:T(8,128)(2,1)S(1)} %pad_maximum_fusion.5), channel_id=1, source_target_pairs={{0,4},{2,6},{4,0},{6,2},{8,12},{10,14},{12,8},{14,10},{16,20},{18,... | collective-permute-start | bytes 688136 | tf_op jit(solution)/shard_map/ppermute | solution.py:47
  23.7 10.3 %collective-permute-start.5 = (bf16[4,16,1920]{2,1,0:T(8,128)(2,1)S(1)}, bf16[4,16,1920]{2,1,0:T(8,128)(2,1)S(1)}, u32[]{:S(2)}, u32[]{:S(2)}) collective-permute-start(bf16[4,16,1920]{2,1,0:T(8,128)(2,1)S(1)} %pad_maximum_fusion.2), channel_id=1, source_target_pairs={{0,2},{2,0},{4,6},{6,4},{8,10},{10,8},{12,14},{14,12},{16,18},{18,... | collective-permute-start | bytes 737288 | tf_op jit(solution)/shard_map/ppermute | solution.py:47
  32.2 12.2 %collective-permute-start.4 = (bf16[8,16,1792]{2,1,0:T(8,128)(2,1)S(1)}, bf16[8,16,1792]{2,1,0:T(8,128)(2,1)}, u32[]{:S(2)}, u32[]{:S(2)}) collective-permute-start(bf16[8,16,1792]{2,1,0:T(8,128)(2,1)S(1)} %pad_maximum_fusion.1), channel_id=1, source_target_pairs={{0,2},{2,0},{4,6},{6,4},{8,10},{10,8},{12,14},{14,12},{16,18},{18,... | collective-permute-start | bytes 1376264 | tf_op jit(solution)/shard_map/ppermute | solution.py:47
  34.4 11.6 %collective-permute-start.7 = (bf16[8,16,1920]{2,1,0:T(8,128)(2,1)S(1)}, bf16[8,16,1920]{2,1,0:T(8,128)(2,1)S(1)}, u32[]{:S(2)}, u32[]{:S(2)}) collective-permute-start(bf16[8,16,1920]{2,1,0:T(8,128)(2,1)S(1)} %pad_maximum_fusion), channel_id=1, source_target_pairs={{0,4},{2,6},{4,0},{6,2},{8,12},{10,14},{12,8},{14,10},{16,20},{18,... | collective-permute-start | bytes 1474568 | tf_op jit(solution)/shard_map/ppermute | solution.py:47
  36.7 1.9 %collective-permute-start.6 = (bf16[16,24,576]{2,1,0:T(8,128)(2,1)S(1)}, bf16[16,24,576]{2,1,0:T(8,128)(2,1)S(1)}, u32[]{:S(2)}, u32[]{:S(2)}) collective-permute-start(bf16[16,24,576]{2,1,0:T(8,128)(2,1)S(1)} %all-to-all-done), channel_id=1, source_target_pairs={{0,1},{1,0},{2,3},{3,2},{4,5},{5,4},{6,7},{7,6},{8,9},{9,8},{10,11... | collective-permute-start | bytes 1327112 | tf_op jit(solution)/shard_map/ppermute | solution.py:52
  36.8 9.4 %collective-permute-start.8 = (bf16[8,16,1792]{2,1,0:T(8,128)(2,1)S(1)}, bf16[8,16,1792]{2,1,0:T(8,128)(2,1)}, u32[]{:S(2)}, u32[]{:S(2)}) collective-permute-start(bf16[8,16,1792]{2,1,0:T(8,128)(2,1)S(1)} %pad_maximum_fusion.1), channel_id=1, source_target_pairs={{0,1},{1,0},{2,3},{3,2},{4,5},{5,4},{6,7},{7,6},{8,9},{9,8},{10,11... | collective-permute-start | bytes 1376264 | tf_op jit(solution)/shard_map/ppermute | solution.py:52
  44.4 2.8 %collective-permute-start.9 = (bf16[8,16,1792]{2,1,0:T(8,128)(2,1)}, bf16[8,16,1792]{2,1,0:T(8,128)(2,1)}, u32[]{:S(2)}, u32[]{:S(2)}) collective-permute-start(bf16[8,16,1792]{2,1,0:T(8,128)(2,1)} %collective-permute-done.4), channel_id=1, source_target_pairs={{0,1},{1,0},{2,3},{3,2},{4,5},{5,4},{6,7},{7,6},{8,9},{9,8},{10,11... | collective-permute-start | bytes 1376264 | tf_op jit(solution)/shard_map/ppermute | solution.py:52
  44.4 2.8 %collective-permute-start.10 = (bf16[8,16,1920]{2,1,0:T(8,128)(2,1)S(1)}, bf16[8,16,1920]{2,1,0:T(8,128)(2,1)S(1)}, u32[]{:S(2)}, u32[]{:S(2)}) collective-permute-start(bf16[8,16,1920]{2,1,0:T(8,128)(2,1)S(1)} %pad_maximum_fusion), channel_id=1, source_target_pairs={{0,1},{1,0},{2,3},{3,2},{4,5},{5,4},{6,7},{7,6},{8,9},{9,8},{10,11... | collective-permute-start | bytes 1474568 | tf_op jit(solution)/shard_map/ppermute | solution.py:52
  46.0 1.9 %collective-permute-start.11 = (bf16[8,16,1920]{2,1,0:T(8,128)(2,1)S(1)}, bf16[8,16,1920]{2,1,0:T(8,128)(2,1)S(1)}, u32[]{:S(2)}, u32[]{:S(2)}) collective-permute-start(bf16[8,16,1920]{2,1,0:T(8,128)(2,1)S(1)} %collective-permute-done.7), channel_id=1, source_target_pairs={{0,1},{1,0},{2,3},{3,2},{4,5},{5,4},{6,7},{7,6},{8,9},{9,8},{10,11... | collective-permute-start | bytes 1474568 | tf_op jit(solution)/shard_map/ppermute | solution.py:52
  60.4 3.6 %collective-permute-start.12 = (bf16[256,1792]{1,0:T(8,128)(2,1)S(1)}, bf16[256,1792]{1,0:T(8,128)(2,1)S(1)}, u32[]{:S(2)}, u32[]{:S(2)}) collective-permute-start(bf16[256,1792]{1,0:T(8,128)(2,1)S(1)} %get-tuple-element.34), channel_id=1, source_target_pairs={{0,1},{1,0},{2,3},{3,2},{4,5},{5,4},{6,7},{7,6},{8,9},{9,8},{10,11... | collective-permute-start | bytes 2752520 | tf_op jit(solution)/shard_map/ppermute | solution.py:52
  60.6 3.7 %collective-permute-start.13 = (bf16[256,1792]{1,0:T(8,128)(2,1)S(1)}, bf16[256,1792]{1,0:T(8,128)(2,1)S(1)}, u32[]{:S(2)}, u32[]{:S(2)}) collective-permute-start(bf16[256,1792]{1,0:T(8,128)(2,1)S(1)} %get-tuple-element.36), channel_id=1, source_target_pairs={{0,1},{1,0},{2,3},{3,2},{4,5},{5,4},{6,7},{7,6},{8,9},{9,8},{10,11... | collective-permute-start | bytes 2752520 | tf_op jit(solution)/shard_map/ppermute | solution.py:52
  67.4 15.2 %collective-permute-start.16 = (bf16[128,1792]{1,0:T(8,128)(2,1)}, bf16[128,1792]{1,0:T(8,128)(2,1)}, u32[]{:S(2)}, u32[]{:S(2)}) collective-permute-start(bf16[128,1792]{1,0:T(8,128)(2,1)} %get-tuple-element.40), channel_id=1, source_target_pairs={{0,4},{2,6},{4,0},{6,2},{8,12},{10,14},{12,8},{14,10},{16,20},{18,... | collective-permute-start | bytes 1376264 | tf_op jit(solution)/shard_map/ppermute | solution.py:47
  68.7 15.5 %collective-permute-start.14 = (bf16[128,1792]{1,0:T(8,128)(2,1)}, bf16[128,1792]{1,0:T(8,128)(2,1)}, u32[]{:S(2)}, u32[]{:S(2)}) collective-permute-start(bf16[128,1792]{1,0:T(8,128)(2,1)} %get-tuple-element.38), channel_id=1, source_target_pairs={{0,2},{2,0},{4,6},{6,4},{8,10},{10,8},{12,14},{14,12},{16,18},{18,... | collective-permute-start | bytes 1376264 | tf_op jit(solution)/shard_map/ppermute | solution.py:47
  69.7 22.4 %all-to-all-start.1 = ((bf16[16,24,576]{2,1,0:T(8,128)(2,1)}), bf16[16,24,576]{2,1,0:T(8,128)(2,1)S(1)}, u32[]{:S(2)}, u32[]{:S(2)}) async-start(bf16[16,24,576]{2,1,0:T(8,128)(2,1)} %bitcast.6), calls=%async_computation.1 | async-start | bytes 983040 | tf_op jit(solution)/shard_map/all_to_all | solution.py:310
  83.7 7.7 %collective-permute-start.17 = (bf16[64,1792]{1,0:T(8,128)(2,1)S(1)}, bf16[64,1792]{1,0:T(8,128)(2,1)S(1)}, u32[]{:S(2)}, u32[]{:S(2)}) collective-permute-start(bf16[64,1792]{1,0:T(8,128)(2,1)S(1)} %get-tuple-element.56), channel_id=1, source_target_pairs={{0,2},{2,0},{4,6},{6,4},{8,10},{10,8},{12,14},{14,12},{16,18},{18,... | collective-permute-start | bytes 688136 | tf_op jit(solution)/shard_map/ppermute | solution.py:47
  85.4 6.6 %collective-permute-start.15 = (bf16[64,1792]{1,0:T(8,128)(2,1)S(1)}, bf16[64,1792]{1,0:T(8,128)(2,1)S(1)}, u32[]{:S(2)}, u32[]{:S(2)}) collective-permute-start(bf16[64,1792]{1,0:T(8,128)(2,1)S(1)} %get-tuple-element.54), channel_id=1, source_target_pairs={{0,4},{2,6},{4,0},{6,2},{8,12},{10,14},{12,8},{14,10},{16,20},{18,... | collective-permute-start | bytes 688136 | tf_op jit(solution)/shard_map/ppermute | solution.py:47
  92.1 6.1 %collective-permute-start.18 = (bf16[32,3584]{1,0:T(8,128)(2,1)S(1)}, bf16[32,3584]{1,0:T(8,128)(2,1)S(1)}, u32[]{:S(2)}, u32[]{:S(2)}) collective-permute-start(bf16[32,3584]{1,0:T(8,128)(2,1)S(1)} %pad_maximum_fusion.6), channel_id=1, source_target_pairs={{0,8},{2,10},{4,12},{6,14},{8,0},{10,2},{12,4},{14,6},{16,24},{18,... | collective-permute-start | bytes 688136 | tf_op jit(solution)/shard_map/ppermute | solution.py:47
  93.5 4.7 %collective-permute-start.19 = (bf16[16,24,576]{2,1,0:T(8,128)(2,1)S(1)}, bf16[16,24,576]{2,1,0:T(8,128)(2,1)S(1)}, u32[]{:S(2)}, u32[]{:S(2)}) collective-permute-start(bf16[16,24,576]{2,1,0:T(8,128)(2,1)S(1)} %all-to-all-done.1), channel_id=1, source_target_pairs={{0,1},{1,0},{2,3},{3,2},{4,5},{5,4},{6,7},{7,6},{8,9},{9,8},{10,11... | collective-permute-start | bytes 1327112 | tf_op jit(solution)/shard_map/ppermute | solution.py:52
  98.2 8.7 %collective-permute-start.20 = (bf16[16,3584]{1,0:T(8,128)(2,1)S(1)}, bf16[16,3584]{1,0:T(8,128)(2,1)S(1)}, u32[]{:S(2)}, u32[]{:S(2)}) collective-permute-start(bf16[16,3584]{1,0:T(8,128)(2,1)S(1)} %add_convert_fusion.5), channel_id=1, source_target_pairs={{0,16},{2,18},{4,20},{6,22},{8,24},{10,26},{12,28},{14,30},{16,0},... | collective-permute-start | bytes 344072 | tf_op jit(solution)/shard_map/ppermute | solution.py:47
  (7 other events, 29.8 us)

commit v13 on v11

--- a/solution.py
+++ b/solution.py
@@ -126,10 +126,9 @@
     )
 
 
-def scatter_sums(sums, orders, hooks):
+def scatter_sums(kepts, sents, orders, hooks):
     steps = len(orders[0])
-    kepts, sents = zip(*sums)
-    kepts, sents = list(kepts), list(sents)
+    sents = list(sents)
     for step in range(steps):
         if step in hooks:
             sents[-1] = hooks[step](sents[-1])
@@ -179,46 +178,45 @@
     )
 
 
-def others_kernel(step, spots, tp_size, cut, rows, hidden, weight, *refs):
-    parts = len(spots)
-    outs, (held, turned, arrived) = refs[:parts], refs[parts:]
+def group_kernel(step, chosen, spots, tp_size, cut, rows, hidden, weight, *refs):
+    outs, (held, turned, arrived) = refs[: len(chosen)], refs[len(chosen) :]
     target = lax.rem(lax.axis_index("tp") + step, tp_size)
     copies = []
-    for part in range(parts):
-        start = pl.multiple_of((target * parts + part) * cut, cut)
+    for index, part in enumerate(chosen):
+        start = pl.multiple_of((target * len(spots) + part) * cut, cut)
         copies.append(
             pltpu.make_async_copy(
-                weight.at[pl.ds(start, cut)], held.at[part], arrived.at[part]
+                weight.at[pl.ds(start, cut)], held.at[index], arrived.at[index]
             )
         )
     for copy in copies:
         copy.start()
     chunk = min(256, hidden.shape[0])
-    for part, copy in enumerate(copies):
-        turn_rows(hidden, turned.at[part], spots[part], rows)
-        copy.wait()
+    for index, part in enumerate(chosen):
+        turn_rows(hidden, turned.at[index], spots[part], rows)
+        copies[index].wait()
         for row in range(0, hidden.shape[0], chunk):
-            outs[part][row : row + chunk] = down_product(
-                turned.at[part], held.at[part], row, chunk, 0, cut
+            outs[index][row : row + chunk] = down_product(
+                turned.at[index], held.at[index], row, chunk, 0, cut
             ).astype(jnp.bfloat16)
 
 
-def down_others(hidden, weight, step, spots, rows):
-    parts = len(spots)
+def down_group(hidden, weight, step, chosen, spots, rows):
+    count = len(chosen)
     tp_size = lax.axis_size("tp")
-    cut = weight.shape[0] // tp_size // parts
+    cut = weight.shape[0] // tp_size // len(spots)
     shape = jax.ShapeDtypeStruct((hidden.shape[0], cut), jnp.bfloat16)
     return kernel_call(
-        functools.partial(others_kernel, step, spots, tp_size, cut, rows),
-        [shape] * parts,
+        functools.partial(group_kernel, step, chosen, spots, tp_size, cut, rows),
+        [shape] * count,
         [hidden, weight],
-        flops=2 * hidden.size * cut * parts,
-        spare=parts * cut * weight.shape[1] * 2 + (8 << 20),
+        flops=2 * hidden.size * cut * count,
+        spare=count * cut * weight.shape[1] * 2 + (8 << 20),
         in_specs=[WHOLE, pl.BlockSpec(memory_space=pl.ANY)],
         scratch_shapes=[
-            pltpu.VMEM((parts, cut, weight.shape[1]), weight.dtype),
-            pltpu.VMEM((parts,) + hidden.shape, hidden.dtype),
-            pltpu.SemaphoreType.DMA((parts,)),
+            pltpu.VMEM((count, cut, weight.shape[1]), weight.dtype),
+            pltpu.VMEM((count,) + hidden.shape, hidden.dtype),
+            pltpu.SemaphoreType.DMA((count,)),
         ],
     )
 
@@ -268,6 +266,45 @@
             pltpu.VMEM(hidden.shape, hidden.dtype),
             pltpu.VMEM((len(others), hidden.shape[0], cut), jnp.bfloat16),
             pltpu.SemaphoreType.DMA((1 + len(others),)),
+        ],
+    )
+
+
+def halves_kernel(parts, first, *refs):
+    outs, (held, arrived) = refs[-2 - parts : -2], refs[-2:]
+    terms = refs[: -2 - parts]
+    count = len(terms) // parts
+    half, rows = outs[0].shape[0], 16
+    copies = [
+        pltpu.make_async_copy(term.at[pl.ds(first, half)], held.at[index], arrived.at[index])
+        for index, term in enumerate(terms)
+    ]
+    for copy in copies:
+        copy.start()
+    for part in range(parts):
+        for index in range(part * count, (part + 1) * count):
+            copies[index].wait()
+        for row in range(0, half, rows):
+            total = held[part * count, row : row + rows].astype(jnp.float32)
+            for index in range(part * count + 1, (part + 1) * count):
+                total = total + held[index, row : row + rows].astype(jnp.float32)
+            outs[part][row : row + rows] = total.astype(jnp.bfloat16)
+
+
+def add_halves(terms, second):
+    parts = len(terms)
+    flat = [term for part in terms for term in part]
+    half, cut = flat[0].shape[0] // 2, flat[0].shape[1]
+    return kernel_call(
+        functools.partial(halves_kernel, parts, half if second else 0),
+        [jax.ShapeDtypeStruct((half, cut), jnp.bfloat16)] * parts,
+        flat,
+        flops=half * cut * len(flat),
+        spare=half * cut * len(flat) * 2 + (2 << 20),
+        in_specs=[pl.BlockSpec(memory_space=pl.ANY)] * len(flat),
+        scratch_shapes=[
+            pltpu.VMEM((len(flat), half, cut), jnp.bfloat16),
+            pltpu.SemaphoreType.DMA((len(flat),)),
         ],
     )
 
@@ -358,10 +395,9 @@
         out[start : start + chunk] = attended.astype(out.dtype)
 
 
-def attend(queries, keys, block_request, block_used):
+def token_owners(block_request, block_used, block_size):
     tp_size = lax.axis_size("tp")
-    row_count, heads, latent = queries.shape
-    block_size, share = keys[0].shape[:2]
+    share = block_request.shape[0] // tp_size
     within = jnp.arange(block_size, dtype=jnp.int32)[:, None]
     owners = []
     for step in range(tp_size):
@@ -369,14 +405,19 @@
         owner = lax.dynamic_slice_in_dim(block_request, first, share)[None, :]
         limit = lax.dynamic_slice_in_dim(block_used, first, share)[None, :]
         owners.append(jnp.where(within < limit, owner, -1).reshape(1, -1))
+    return jnp.concatenate(owners, axis=0)
+
+
+def attend(queries, keys, owners):
+    row_count, heads, latent = queries.shape
     keys = [part.reshape(-1, latent) for part in keys]
     rows = queries.reshape(-1, latent)
     shape = jax.ShapeDtypeStruct((rows.shape[0], KV), jnp.bfloat16)
     result = kernel_call(
         functools.partial(attention_kernel, heads, min(256, rows.shape[0])),
         shape,
-        [jnp.concatenate(owners, axis=0), rows] + keys,
-        flops=4 * rows.size * keys[0].shape[0] * tp_size,
+        [owners, rows] + keys,
+        flops=4 * rows.size * keys[0].shape[0] * len(keys),
         spare=8 << 20,
     )
     return result.reshape(row_count, heads, KV)
@@ -428,7 +469,8 @@
     halves = gather_rows(tokens, gates, orders, ends, beside_shared, ahead_of_last)
     last_sent = halves[-1][0]
     ordered = cache_turn(held["spread"], tie(block_source, last_sent), slot_total)
-    first_late, ordered = lax.optimization_barrier((halves[0][1], ordered))
+    owners = token_owners(block_request, block_used, block_size)
+    first_late, ordered, owners = lax.optimization_barrier((halves[0][1], ordered, owners))
     halves[0] = (halves[0][0], first_late)
     places = [places_of(order) for order in orders]
     to_first = [[places[0].index(place) for place in own] for own in places]
@@ -458,13 +500,14 @@
     down_weight = pltpu.with_memory_space_constraint(expert_down[0], pltpu.HBM)
     passed = [[] for _ in range(parts)]
     for step in range(1, tp_size):
-        others = down_others(hidden, down_weight, step, from_first, row_count)
+        others = down_group(hidden, down_weight, step, range(parts), from_first, row_count)
         for part in range(parts):
             passed[part].append(pass_tp(others[part], step))
-    sums = [
-        down_own(hidden, down_weight, part, parts, from_first[part], row_count, passed[part])
-        for part in range(parts)
-    ]
+    later = down_group(hidden, down_weight, 0, range(1, parts), from_first, row_count)
+    later = [[own] + others for own, others in zip(later, passed[1:])]
+    kept, sent = down_own(hidden, down_weight, 0, parts, from_first[0], row_count, passed[0])
+    sents = [sent, *add_halves(later, True)]
+    kepts = [kept, *add_halves(later, False)]
 
     def beside_first_sum(sent):
         held["keys"] = cache_in(tie(ordered, sent), block_size, latent)
@@ -477,7 +520,7 @@
 
     def beside_last_sum(sent):
         sent, keys = lax.optimization_barrier((sent, held["keys"]))
-        held["attended"] = attend(queries, keys, block_request, block_used)
+        held["attended"] = attend(queries, keys, owners)
         return sent
 
     def ahead_of_end(arrived):
@@ -490,7 +533,7 @@
         len(bits) - 1: beside_last_sum,
         -1: ahead_of_end,
     }
-    return (scatter_sums(sums, orders, hooks), held["attended"])
+    return (scatter_sums(kepts, sents, orders, hooks), held["attended"])
 
 
 def solution(mesh):

time: 108 us -> 108 us (level)
  waiting for transfers between devices: 38.4 us -> 34.5 us
  Pallas kernels: 14.4 us -> 16.5 us
  starting transfers between devices: 32.8 us -> 33.9 us
    ppermute x13, waiting for transfers between devices: 33.3 us -> 31.1 us  [exchange(): lax.ppermute(value, 'ep', [(index, index ^ bit) for index in range(ep_siz...]
    pallas_call x6 -> x8, Pallas kernels: 14.4 us -> 16.5 us  [kernel_call(): pl.pallas_call(kernel, out_shape=out_shape, in_specs=in_specs or [WHOLE]...]
    ppermute x8, waiting for transfers between devices: 4.76 us -> 2.96 us  [pass_tp(): lax.ppermute(value, 'tp', [(index, (index + step) % tp_size) for index in...]
    unnamed x11 -> x9, local copies, waits for them, and re-layouts: 3.49 us -> 4.32 us
  transfers between devices with their start and end apart: 23 -> 23, of which waited for: 16 -> 13; matrix products, arithmetic and copies ran while one was open for 9% -> 8% of each run, Pallas kernels for 9% -> 11%
where the time goes in v13:
time: 108 us; the launch traced here: 107 us
  waiting for transfers between devices  34.5 us (32%)
  starting transfers between devices  33.9 us (31%)
  Pallas kernels  16.5 us (15%)
  matrix products  7.58 us (7%)
  other arithmetic  6.99 us (6%)
  local copies, waits for them, and re-layouts  6.58 us (6%)
    ppermute x13, waiting for transfers between devices, exchange(): lax.ppermute(value, 'ep', [(index, index ^ bit) for index in range(ep_siz...  31.1 us
    ppermute x13, starting transfers between devices, exchange(): lax.ppermute(value, 'ep', [(index, index ^ bit) for index in range(ep_siz...  20.1 us
    pallas_call x8, Pallas kernels, kernel_call(): pl.pallas_call(kernel, out_shape=out_shape, in_specs=in_specs or [WHOLE]...  16.5 us
    dot_general x1, matrix products, body(): jnp.einsum('sd,dgf->sgf', all_rows, expert_gate_up[0], preferred_element_...  7.58 us
    all_to_all x1, starting transfers between devices, cache_in(): lax.all_to_all(ordered, 'ep', split_axis=0, concat_axis=0, tiled=True)  6.92 us
    all_to_all x1, starting transfers between devices, beside_shared(): lax.all_to_all(pieces, 'ep', split_axis=0, concat_axis=0, tiled=True)  5.28 us
    unnamed x9, local copies, waits for them, and re-layouts  4.32 us
    convert_element_type x6, other arithmetic, add_up(): return total.astype(jnp.bfloat16)  3.42 us
  transfers between devices with their start and end apart: 23, of which 13 were waited for; matrix products, arithmetic and copies ran while one was open for 8% of the time, Pallas kernels for 11%

profile of v13, /device:TPU:0, one launch (start us, length us, event | category | flops | bytes accessed | tf_op | source)
XLA Modules:
  0.0 107.1 jit_solution(5748544724613744892)
XLA Ops:
  2.5 4.0 %collective-permute-start.1 = (bf16[1,16,128]{2,1,0:T(8,128)(2,1)S(1)}, bf16[1,16,128]{2,1,0:T(8,128)(2,1)S(1)}, u32[]{:S(2)}, u32[]{:S(2)}) collective-permute-start(bf16[1,16,128]{2,1,0:T(8,128)(2,1)S(1)} %fusion.18), channel_id=1, source_target_pairs={{0,16},{2,18},{4,20},{6,22},{8,24},{10,26},{12,28},{14,30},{16,0},... | collective-permute-start | bytes 12296 | tf_op jit(solution)/shard_map/ppermute | solution.py:47
  8.4 6.2 %collective-permute-done = bf16[1,16,3584]{2,1,0:T(8,128)(2,1)S(1)} collective-permute-done((bf16[1,16,3584]{2,1,0:T(8,128)(2,1)}, bf16[1,16,3584]{2,1,0:T(8,128)(2,1)S(1)}, u32[]{:S(2)}, u32[]{:S(2)}) %collective-permute-start) | collective-permute-done | bytes 114720 | tf_op jit(solution)/shard_map/ppermute | solution.py:47
  15.8 5.3 %all-to-all-start = ((bf16[16,24,576]{2,1,0:T(8,128)(2,1)}), bf16[16,24,576]{2,1,0:T(8,128)(2,1)S(1)}, u32[]{:S(2)}, u32[]{:S(2)}) async-start(bf16[16,24,576]{2,1,0:T(8,128)(2,1)} %bitcast.37), calls=%async_computation | async-start | bytes 983040 | tf_op jit(solution)/shard_map/all_to_all | solution.py:463
  23.1 1.6 %collective-permute-start.3 = (bf16[4,16,1792]{2,1,0:T(8,128)(2,1)S(1)}, bf16[4,16,1792]{2,1,0:T(8,128)(2,1)S(1)}, u32[]{:S(2)}, u32[]{:S(2)}) collective-permute-start(bf16[4,16,1792]{2,1,0:T(8,128)(2,1)S(1)} %pad_maximum_fusion.5), channel_id=1, source_target_pairs={{0,4},{2,6},{4,0},{6,2},{8,12},{10,14},{12,8},{14,10},{16,20},{18,... | collective-permute-start | bytes 688136 | tf_op jit(solution)/shard_map/ppermute | solution.py:47
  25.6 1.6 %collective-permute-start.5 = (bf16[4,16,1920]{2,1,0:T(8,128)(2,1)S(1)}, bf16[4,16,1920]{2,1,0:T(8,128)(2,1)S(1)}, u32[]{:S(2)}, u32[]{:S(2)}) collective-permute-start(bf16[4,16,1920]{2,1,0:T(8,128)(2,1)S(1)} %pad_maximum_fusion.2), channel_id=1, source_target_pairs={{0,2},{2,0},{4,6},{6,4},{8,10},{10,8},{12,14},{14,12},{16,18},{18,... | collective-permute-start | bytes 737288 | tf_op jit(solution)/shard_map/ppermute | solution.py:47
  27.1 6.0 %collective-permute-done.3 = bf16[4,16,1792]{2,1,0:T(8,128)(2,1)S(1)} collective-permute-done((bf16[4,16,1792]{2,1,0:T(8,128)(2,1)S(1)}, bf16[4,16,1792]{2,1,0:T(8,128)(2,1)S(1)}, u32[]{:S(2)}, u32[]{:S(2)}) %collective-permute-start.3) | collective-permute-done | bytes 229408 | tf_op jit(solution)/shard_map/ppermute | solution.py:47
  39.6 1.6 %shard_map.113 = bf16[384,576]{1,0:T(8,128)(2,1)} custom-call(s32[384,2]{1,0:T(8,128)S(1)} %fusion.7.index, bf16[384,576]{1,0:T(8,128)(2,1)S(1)} %bitcast.39, bf16[384,576]{1,0:T(8,128)(2,1)S(1)} %bitcast.45), custom_call_target="tpu_custom_call" | custom-call | flops 339738624 | bytes 2217984 | tf_op jit(solution)/shard_map/pallas_call | solution.py:23
  41.2 4.0 %collective-permute-done.4 = bf16[8,16,1792]{2,1,0:T(8,128)(2,1)} collective-permute-done((bf16[8,16,1792]{2,1,0:T(8,128)(2,1)S(1)}, bf16[8,16,1792]{2,1,0:T(8,128)(2,1)}, u32[]{:S(2)}, u32[]{:S(2)}) %collective-permute-start.4) | collective-permute-done | bytes 458784 | tf_op jit(solution)/shard_map/ppermute | solution.py:47
  48.4 1.5 %shard_map.114 = bf16[256,7168]{1,0:T(8,128)(2,1)S(1)} custom-call(bf16[128,1792]{1,0:T(8,128)(2,1)S(1)} %bitcast.40, bf16[128,1792]{1,0:T(8,128)(2,1)} %bitcast.7.refs_1_, bf16[128,1920]{1,0:T(8,128)(2,1)S(1)} %bitcast.38, bf16[128,1920]{1,0:T(8,128)(2,1)S(1)} %bitcast.41, bf16[128,1792]{1,0:T(8,128)(2,1)} %bitcast.10.refs_4_, ...), custom_call_target="tpu_custom_call" | custom-call | bytes 11272192 | tf_op jit(solution)/shard_map/pallas_call | solution.py:23
  50.0 7.6 %fusion = f32[256,2,512]{2,0,1:T(8,128)S(1)} fusion(bf16[7168,2,512]{2,1,0:T(2,128)(2,1)} %bitcast.55, bf16[256,7168]{1,0:T(8,128)(2,1)S(1)} %shard_map.114), kind=kOutput, calls=%fused_computation | convolution fusion | flops 3758096384 | bytes 19398656 | tf_op jit(solution)/shard_map/sd,dgf->sgf/dot_general | solution.py:493
  57.7 3.0 %shard_map.115 = (bf16[256,1792]{1,0:T(8,128)(2,1)S(1)}, bf16[256,1792]{1,0:T(8,128)(2,1)S(1)}) custom-call(bf16[256,512]{1,0:T(8,128)(2,1)S(1)} %fusion.5.hidden, bf16[7168,512]{1,0:T(8,128)(2,1)} %bitcast.48), custom_call_target="tpu_custom_call" | custom-call | flops 939524096 | bytes 9699328 | tf_op jit(solution)/shard_map/pallas_call | solution.py:23
  61.4 2.2 %shard_map.117.refs_0_ = bf16[256,1792]{1,0:T(8,128)(2,1)S(1)} custom-call(bf16[256,512]{1,0:T(8,128)(2,1)S(1)} %fusion.5.hidden, bf16[7168,512]{1,0:T(8,128)(2,1)} %bitcast.49), custom_call_target="tpu_custom_call" | custom-call | flops 469762048 | bytes 8781824 | tf_op jit(solution)/shard_map/pallas_call | solution.py:23
  63.6 1.4 %shard_map.119 = bf16[128,1792]{1,0:T(8,128)(2,1)} custom-call(bf16[256,1792]{1,0:T(8,128)(2,1)S(1)} %shard_map.117.refs_0_, bf16[256,1792]{1,0:T(8,128)(2,1)S(1)} %collective-permute-done.15.refs_1_), custom_call_target="tpu_custom_call" | custom-call | flops 458752 | bytes 2293760 | tf_op jit(solution)/shard_map/pallas_call | solution.py:23
  65.8 3.1 %shard_map.116 = (bf16[128,1792]{1,0:T(8,128)(2,1)S(1)}, bf16[128,1792]{1,0:T(8,128)(2,1)}) custom-call(bf16[256,512]{1,0:T(8,128)(2,1)S(1)} %fusion.5.hidden, bf16[7168,512]{1,0:T(8,128)(2,1)} %bitcast.50, bf16[256,1792]{1,0:T(8,128)(2,1)S(1)} %collective-permute-done.12.refs_0_), custom_call_target="tpu_custom_call" | custom-call | flops 469762048 | bytes 9699328 | tf_op jit(solution)/shard_map/pallas_call | solution.py:23
  70.6 6.9 %all-to-all-start.1 = ((bf16[16,24,576]{2,1,0:T(8,128)(2,1)}), bf16[16,24,576]{2,1,0:T(8,128)(2,1)S(1)}, u32[]{:S(2)}, u32[]{:S(2)}) async-start(bf16[16,24,576]{2,1,0:T(8,128)(2,1)} %bitcast.6), calls=%async_computation.1 | async-start | bytes 983040 | tf_op jit(solution)/shard_map/all_to_all | solution.py:358
  79.4 2.0 %collective-permute-start.17 = (bf16[64,1792]{1,0:T(8,128)(2,1)S(1)}, bf16[64,1792]{1,0:T(8,128)(2,1)S(1)}, u32[]{:S(2)}, u32[]{:S(2)}) collective-permute-start(bf16[64,1792]{1,0:T(8,128)(2,1)S(1)} %get-tuple-element.50), channel_id=1, source_target_pairs={{0,2},{2,0},{4,6},{6,4},{8,10},{10,8},{12,14},{14,12},{16,18},{18,... | collective-permute-start | bytes 688136 | tf_op jit(solution)/shard_map/ppermute | solution.py:47
  81.4 2.8 %collective-permute-done.13 = bf16[128,1792]{1,0:T(8,128)(2,1)} collective-permute-done((bf16[128,1792]{1,0:T(8,128)(2,1)}, bf16[128,1792]{1,0:T(8,128)(2,1)}, u32[]{:S(2)}, u32[]{:S(2)}) %collective-permute-start.13) | collective-permute-done | bytes 458784 | tf_op jit(solution)/shard_map/ppermute | solution.py:47
  84.2 1.4 %add_convert_fusion.3 = (bf16[64,1792]{1,0:T(8,128)(2,1)S(1)}, bf16[64,1792]{1,0:T(8,128)(2,1)S(1)}) fusion(bf16[128,1792]{1,0:T(8,128)(2,1)} %collective-permute-done.13, bf16[128,1792]{1,0:T(8,128)(2,1)} %copy-done.1), kind=kLoop, calls=%fused_computation.14 | loop fusion | flops 917504 | bytes 1376256 | tf_op jit(solution)/shard_map/convert_element_type | solution.py:155
  85.6 1.8 %collective-permute-start.14 = (bf16[64,1792]{1,0:T(8,128)(2,1)S(1)}, bf16[64,1792]{1,0:T(8,128)(2,1)S(1)}, u32[]{:S(2)}, u32[]{:S(2)}) collective-permute-start(bf16[64,1792]{1,0:T(8,128)(2,1)S(1)} %get-tuple-element.48), channel_id=1, source_target_pairs={{0,4},{2,6},{4,0},{6,2},{8,12},{10,14},{12,8},{14,10},{16,20},{18,... | collective-permute-start | bytes 688136 | tf_op jit(solution)/shard_map/ppermute | solution.py:47
  87.4 4.9 %collective-permute-done.17 = bf16[64,1792]{1,0:T(8,128)(2,1)S(1)} collective-permute-done((bf16[64,1792]{1,0:T(8,128)(2,1)S(1)}, bf16[64,1792]{1,0:T(8,128)(2,1)S(1)}, u32[]{:S(2)}, u32[]{:S(2)}) %collective-permute-start.17) | collective-permute-done | bytes 229408 | tf_op jit(solution)/shard_map/ppermute | solution.py:47
  92.5 2.7 %collective-permute-start.18 = (bf16[32,3584]{1,0:T(8,128)(2,1)S(1)}, bf16[32,3584]{1,0:T(8,128)(2,1)S(1)}, u32[]{:S(2)}, u32[]{:S(2)}) collective-permute-start(bf16[32,3584]{1,0:T(8,128)(2,1)S(1)} %pad_maximum_fusion.6), channel_id=1, source_target_pairs={{0,8},{2,10},{4,12},{6,14},{8,0},{10,2},{12,4},{14,6},{16,24},{18,... | collective-permute-start | bytes 688136 | tf_op jit(solution)/shard_map/ppermute | solution.py:47
  95.1 4.7 %collective-permute-done.18 = bf16[32,3584]{1,0:T(8,128)(2,1)S(1)} collective-permute-done((bf16[32,3584]{1,0:T(8,128)(2,1)S(1)}, bf16[32,3584]{1,0:T(8,128)(2,1)S(1)}, u32[]{:S(2)}, u32[]{:S(2)}) %collective-permute-start.18) | collective-permute-done | bytes 229408 | tf_op jit(solution)/shard_map/ppermute | solution.py:47
  99.9 2.4 %collective-permute-start.20 = (bf16[16,3584]{1,0:T(8,128)(2,1)S(1)}, bf16[16,3584]{1,0:T(8,128)(2,1)S(1)}, u32[]{:S(2)}, u32[]{:S(2)}) collective-permute-start(bf16[16,3584]{1,0:T(8,128)(2,1)S(1)} %add_convert_fusion.5), channel_id=1, source_target_pairs={{0,16},{2,18},{4,20},{6,22},{8,24},{10,26},{12,28},{14,30},{16,0},... | collective-permute-start | bytes 344072 | tf_op jit(solution)/shard_map/ppermute | solution.py:47
  103.4 3.0 %shard_map.120 = bf16[512,512]{1,0:T(8,128)(2,1)} custom-call(s32[2,384]{1,0:T(2,128)S(1)} %pad_add_fusion.owner, bf16[512,576]{1,0:T(8,128)(2,1)S(1)} %bitcast.46, bf16[384,576]{1,0:T(8,128)(2,1)S(1)} %bitcast.44, bf16[384,576]{1,0:T(8,128)(2,1)S(1)} %bitcast.47), custom_call_target="tpu_custom_call" | custom-call | flops 905969664 | bytes 3479552 | tf_op jit(solution)/shard_map/pallas_call | solution.py:23
  (77 shorter events, 24.4 us)
Async XLA Ops:
  0.6 6.8 %copy-start = (bf16[48,16,576]{2,1,0:T(8,128)(2,1)S(1)}, bf16[48,16,576]{2,1,0:T(8,128)(2,1)}, u32[]{:S(2)}) copy-start(bf16[48,16,576]{2,1,0:T(8,128)(2,1)} %param.16) | copy-start | bytes 2654212
  2.5 6.0 %collective-permute-start.1 = (bf16[1,16,128]{2,1,0:T(8,128)(2,1)S(1)}, bf16[1,16,128]{2,1,0:T(8,128)(2,1)S(1)}, u32[]{:S(2)}, u32[]{:S(2)}) collective-permute-start(bf16[1,16,128]{2,1,0:T(8,128)(2,1)S(1)} %fusion.18), channel_id=1, source_target_pairs={{0,16},{2,18},{4,20},{6,22},{8,24},{10,26},{12,28},{14,30},{16,0},... | collective-permute-start | bytes 12296 | tf_op jit(solution)/shard_map/ppermute | solution.py:47
  6.5 8.2 %collective-permute-start = (bf16[1,16,3584]{2,1,0:T(8,128)(2,1)}, bf16[1,16,3584]{2,1,0:T(8,128)(2,1)S(1)}, u32[]{:S(2)}, u32[]{:S(2)}) collective-permute-start(bf16[1,16,3584]{2,1,0:T(8,128)(2,1)} %bitcast.51), channel_id=1, source_target_pairs={{0,16},{2,18},{4,20},{6,22},{8,24},{10,26},{12,28},{14,30},{16,0},... | collective-permute-start | bytes 344072 | tf_op jit(solution)/shard_map/ppermute | solution.py:47
  15.6 6.7 %collective-permute-start.2 = (bf16[2,16,3712]{2,1,0:T(8,128)(2,1)S(1)}, bf16[2,16,3712]{2,1,0:T(8,128)(2,1)S(1)}, u32[]{:S(2)}, u32[]{:S(2)}) collective-permute-start(bf16[2,16,3712]{2,1,0:T(8,128)(2,1)S(1)} %maximum_maximum_fusion), channel_id=1, source_target_pairs={{0,8},{2,10},{4,12},{6,14},{8,0},{10,2},{12,4},{14,6},{16,24},{18,... | collective-permute-start | bytes 712712 | tf_op jit(solution)/shard_map/ppermute | solution.py:47
  15.8 19.7 %all-to-all-start = ((bf16[16,24,576]{2,1,0:T(8,128)(2,1)}), bf16[16,24,576]{2,1,0:T(8,128)(2,1)S(1)}, u32[]{:S(2)}, u32[]{:S(2)}) async-start(bf16[16,24,576]{2,1,0:T(8,128)(2,1)} %bitcast.37), calls=%async_computation | async-start | bytes 983040 | tf_op jit(solution)/shard_map/all_to_all | solution.py:463
  23.1 10.0 %collective-permute-start.3 = (bf16[4,16,1792]{2,1,0:T(8,128)(2,1)S(1)}, bf16[4,16,1792]{2,1,0:T(8,128)(2,1)S(1)}, u32[]{:S(2)}, u32[]{:S(2)}) collective-permute-start(bf16[4,16,1792]{2,1,0:T(8,128)(2,1)S(1)} %pad_maximum_fusion.5), channel_id=1, source_target_pairs={{0,4},{2,6},{4,0},{6,2},{8,12},{10,14},{12,8},{14,10},{16,20},{18,... | collective-permute-start | bytes 688136 | tf_op jit(solution)/shard_map/ppermute | solution.py:47
  25.6 9.3 %collective-permute-start.5 = (bf16[4,16,1920]{2,1,0:T(8,128)(2,1)S(1)}, bf16[4,16,1920]{2,1,0:T(8,128)(2,1)S(1)}, u32[]{:S(2)}, u32[]{:S(2)}) collective-permute-start(bf16[4,16,1920]{2,1,0:T(8,128)(2,1)S(1)} %pad_maximum_fusion.2), channel_id=1, source_target_pairs={{0,2},{2,0},{4,6},{6,4},{8,10},{10,8},{12,14},{14,12},{16,18},{18,... | collective-permute-start | bytes 737288 | tf_op jit(solution)/shard_map/ppermute | solution.py:47
  33.1 12.1 %collective-permute-start.4 = (bf16[8,16,1792]{2,1,0:T(8,128)(2,1)S(1)}, bf16[8,16,1792]{2,1,0:T(8,128)(2,1)}, u32[]{:S(2)}, u32[]{:S(2)}) collective-permute-start(bf16[8,16,1792]{2,1,0:T(8,128)(2,1)S(1)} %pad_maximum_fusion.1), channel_id=1, source_target_pairs={{0,2},{2,0},{4,6},{6,4},{8,10},{10,8},{12,14},{14,12},{16,18},{18,... | collective-permute-start | bytes 1376264 | tf_op jit(solution)/shard_map/ppermute | solution.py:47
  35.4 11.0 %collective-permute-start.7 = (bf16[8,16,1920]{2,1,0:T(8,128)(2,1)S(1)}, bf16[8,16,1920]{2,1,0:T(8,128)(2,1)S(1)}, u32[]{:S(2)}, u32[]{:S(2)}) collective-permute-start(bf16[8,16,1920]{2,1,0:T(8,128)(2,1)S(1)} %pad_maximum_fusion), channel_id=1, source_target_pairs={{0,4},{2,6},{4,0},{6,2},{8,12},{10,14},{12,8},{14,10},{16,20},{18,... | collective-permute-start | bytes 1474568 | tf_op jit(solution)/shard_map/ppermute | solution.py:47
  37.7 1.9 %collective-permute-start.6 = (bf16[16,24,576]{2,1,0:T(8,128)(2,1)S(1)}, bf16[16,24,576]{2,1,0:T(8,128)(2,1)S(1)}, u32[]{:S(2)}, u32[]{:S(2)}) collective-permute-start(bf16[16,24,576]{2,1,0:T(8,128)(2,1)S(1)} %all-to-all-done), channel_id=1, source_target_pairs={{0,1},{1,0},{2,3},{3,2},{4,5},{5,4},{6,7},{7,6},{8,9},{9,8},{10,11... | collective-permute-start | bytes 1327112 | tf_op jit(solution)/shard_map/ppermute | solution.py:52
  37.7 8.9 %collective-permute-start.8 = (bf16[8,16,1792]{2,1,0:T(8,128)(2,1)S(1)}, bf16[8,16,1792]{2,1,0:T(8,128)(2,1)}, u32[]{:S(2)}, u32[]{:S(2)}) collective-permute-start(bf16[8,16,1792]{2,1,0:T(8,128)(2,1)S(1)} %pad_maximum_fusion.1), channel_id=1, source_target_pairs={{0,1},{1,0},{2,3},{3,2},{4,5},{5,4},{6,7},{7,6},{8,9},{9,8},{10,11... | collective-permute-start | bytes 1376264 | tf_op jit(solution)/shard_map/ppermute | solution.py:52
  45.2 2.8 %collective-permute-start.9 = (bf16[8,16,1792]{2,1,0:T(8,128)(2,1)}, bf16[8,16,1792]{2,1,0:T(8,128)(2,1)}, u32[]{:S(2)}, u32[]{:S(2)}) collective-permute-start(bf16[8,16,1792]{2,1,0:T(8,128)(2,1)} %collective-permute-done.4), channel_id=1, source_target_pairs={{0,1},{1,0},{2,3},{3,2},{4,5},{5,4},{6,7},{7,6},{8,9},{9,8},{10,11... | collective-permute-start | bytes 1376264 | tf_op jit(solution)/shard_map/ppermute | solution.py:52
  45.2 2.8 %collective-permute-start.10 = (bf16[8,16,1920]{2,1,0:T(8,128)(2,1)S(1)}, bf16[8,16,1920]{2,1,0:T(8,128)(2,1)S(1)}, u32[]{:S(2)}, u32[]{:S(2)}) collective-permute-start(bf16[8,16,1920]{2,1,0:T(8,128)(2,1)S(1)} %pad_maximum_fusion), channel_id=1, source_target_pairs={{0,1},{1,0},{2,3},{3,2},{4,5},{5,4},{6,7},{7,6},{8,9},{9,8},{10,11... | collective-permute-start | bytes 1474568 | tf_op jit(solution)/shard_map/ppermute | solution.py:52
  46.4 2.0 %collective-permute-start.11 = (bf16[8,16,1920]{2,1,0:T(8,128)(2,1)S(1)}, bf16[8,16,1920]{2,1,0:T(8,128)(2,1)S(1)}, u32[]{:S(2)}, u32[]{:S(2)}) collective-permute-start(bf16[8,16,1920]{2,1,0:T(8,128)(2,1)S(1)} %collective-permute-done.7), channel_id=1, source_target_pairs={{0,1},{1,0},{2,3},{3,2},{4,5},{5,4},{6,7},{7,6},{8,9},{9,8},{10,11... | collective-permute-start | bytes 1474568 | tf_op jit(solution)/shard_map/ppermute | solution.py:52
  60.8 2.8 %collective-permute-start.15 = (bf16[256,1792]{1,0:T(8,128)(2,1)S(1)}, bf16[256,1792]{1,0:T(8,128)(2,1)S(1)}, u32[]{:S(2)}, u32[]{:S(2)}) collective-permute-start(bf16[256,1792]{1,0:T(8,128)(2,1)S(1)} %get-tuple-element.33), channel_id=1, source_target_pairs={{0,1},{1,0},{2,3},{3,2},{4,5},{5,4},{6,7},{7,6},{8,9},{9,8},{10,11... | collective-permute-start | bytes 2752520 | tf_op jit(solution)/shard_map/ppermute | solution.py:52
  61.0 4.8 %collective-permute-start.12 = (bf16[256,1792]{1,0:T(8,128)(2,1)S(1)}, bf16[256,1792]{1,0:T(8,128)(2,1)S(1)}, u32[]{:S(2)}, u32[]{:S(2)}) collective-permute-start(bf16[256,1792]{1,0:T(8,128)(2,1)S(1)} %get-tuple-element.30), channel_id=1, source_target_pairs={{0,1},{1,0},{2,3},{3,2},{4,5},{5,4},{6,7},{7,6},{8,9},{9,8},{10,11... | collective-permute-start | bytes 2752520 | tf_op jit(solution)/shard_map/ppermute | solution.py:52
  65.0 13.2 %collective-permute-start.16 = (bf16[128,1792]{1,0:T(8,128)(2,1)}, bf16[128,1792]{1,0:T(8,128)(2,1)}, u32[]{:S(2)}, u32[]{:S(2)}) collective-permute-start(bf16[128,1792]{1,0:T(8,128)(2,1)} %shard_map.119), channel_id=1, source_target_pairs={{0,4},{2,6},{4,0},{6,2},{8,12},{10,14},{12,8},{14,10},{16,20},{18,... | collective-permute-start | bytes 1376264 | tf_op jit(solution)/shard_map/ppermute | solution.py:47
  69.6 14.5 %collective-permute-start.13 = (bf16[128,1792]{1,0:T(8,128)(2,1)}, bf16[128,1792]{1,0:T(8,128)(2,1)}, u32[]{:S(2)}, u32[]{:S(2)}) collective-permute-start(bf16[128,1792]{1,0:T(8,128)(2,1)} %get-tuple-element.32), channel_id=1, source_target_pairs={{0,2},{2,0},{4,6},{6,4},{8,10},{10,8},{12,14},{14,12},{16,18},{18,... | collective-permute-start | bytes 1376264 | tf_op jit(solution)/shard_map/ppermute | solution.py:47
  70.6 21.9 %all-to-all-start.1 = ((bf16[16,24,576]{2,1,0:T(8,128)(2,1)}), bf16[16,24,576]{2,1,0:T(8,128)(2,1)S(1)}, u32[]{:S(2)}, u32[]{:S(2)}) async-start(bf16[16,24,576]{2,1,0:T(8,128)(2,1)} %bitcast.6), calls=%async_computation.1 | async-start | bytes 983040 | tf_op jit(solution)/shard_map/all_to_all | solution.py:358
  79.4 12.9 %collective-permute-start.17 = (bf16[64,1792]{1,0:T(8,128)(2,1)S(1)}, bf16[64,1792]{1,0:T(8,128)(2,1)S(1)}, u32[]{:S(2)}, u32[]{:S(2)}) collective-permute-start(bf16[64,1792]{1,0:T(8,128)(2,1)S(1)} %get-tuple-element.50), channel_id=1, source_target_pairs={{0,2},{2,0},{4,6},{6,4},{8,10},{10,8},{12,14},{14,12},{16,18},{18,... | collective-permute-start | bytes 688136 | tf_op jit(solution)/shard_map/ppermute | solution.py:47
  85.6 6.8 %collective-permute-start.14 = (bf16[64,1792]{1,0:T(8,128)(2,1)S(1)}, bf16[64,1792]{1,0:T(8,128)(2,1)S(1)}, u32[]{:S(2)}, u32[]{:S(2)}) collective-permute-start(bf16[64,1792]{1,0:T(8,128)(2,1)S(1)} %get-tuple-element.48), channel_id=1, source_target_pairs={{0,4},{2,6},{4,0},{6,2},{8,12},{10,14},{12,8},{14,10},{16,20},{18,... | collective-permute-start | bytes 688136 | tf_op jit(solution)/shard_map/ppermute | solution.py:47
  92.5 7.4 %collective-permute-start.18 = (bf16[32,3584]{1,0:T(8,128)(2,1)S(1)}, bf16[32,3584]{1,0:T(8,128)(2,1)S(1)}, u32[]{:S(2)}, u32[]{:S(2)}) collective-permute-start(bf16[32,3584]{1,0:T(8,128)(2,1)S(1)} %pad_maximum_fusion.6), channel_id=1, source_target_pairs={{0,8},{2,10},{4,12},{6,14},{8,0},{10,2},{12,4},{14,6},{16,24},{18,... | collective-permute-start | bytes 688136 | tf_op jit(solution)/shard_map/ppermute | solution.py:47
  95.1 4.8 %collective-permute-start.19 = (bf16[16,24,576]{2,1,0:T(8,128)(2,1)S(1)}, bf16[16,24,576]{2,1,0:T(8,128)(2,1)S(1)}, u32[]{:S(2)}, u32[]{:S(2)}) collective-permute-start(bf16[16,24,576]{2,1,0:T(8,128)(2,1)S(1)} %all-to-all-done.1), channel_id=1, source_target_pairs={{0,1},{1,0},{2,3},{3,2},{4,5},{5,4},{6,7},{7,6},{8,9},{9,8},{10,11... | collective-permute-start | bytes 1327112 | tf_op jit(solution)/shard_map/ppermute | solution.py:52
  99.9 6.4 %collective-permute-start.20 = (bf16[16,3584]{1,0:T(8,128)(2,1)S(1)}, bf16[16,3584]{1,0:T(8,128)(2,1)S(1)}, u32[]{:S(2)}, u32[]{:S(2)}) collective-permute-start(bf16[16,3584]{1,0:T(8,128)(2,1)S(1)} %add_convert_fusion.5), channel_id=1, source_target_pairs={{0,16},{2,18},{4,20},{6,22},{8,24},{10,26},{12,28},{14,30},{16,0},... | collective-permute-start | bytes 344072 | tf_op jit(solution)/shard_map/ppermute | solution.py:47
  (2 other events, 1.9 us)

commit v14 on v13

--- a/solution.py
+++ b/solution.py
@@ -15,7 +15,9 @@
 WHOLE = pl.BlockSpec(memory_space=pltpu.VMEM)
 
 
-def kernel_call(kernel, out_shape, arguments, flops, spare, in_specs=None, scratch_shapes=()):
+def kernel_call(
+    kernel, out_shape, arguments, flops, spare, in_specs=None, scratch_shapes=(), counted=True
+):
     held = sum(array.size * array.dtype.itemsize for array in jax.tree.leaves(out_shape))
     for array, spec in zip(arguments, in_specs or [WHOLE] * len(arguments)):
         held += array.size * array.dtype.itemsize if spec is WHOLE else 0
@@ -28,7 +30,7 @@
         scratch_shapes=scratch_shapes,
         compiler_params=pltpu.CompilerParams(vmem_limit_bytes=held + spare),
         cost_estimate=pl.CostEstimate(
-            flops=flops, bytes_accessed=moved + held, transcendentals=0
+            flops=flops, bytes_accessed=(moved + held) * counted, transcendentals=0
         ),
     )(*arguments)
 
@@ -123,6 +125,7 @@
         arrays,
         flops=0,
         spare=4 << 20,
+        counted=False,
     )
 
 
@@ -145,7 +148,7 @@
             sents = [jnp.concatenate(sents, axis=1)]
             kepts = [jnp.concatenate(kepts, axis=1)]
     kept, arrived = terms[0]
-    return add_up([kept, hooks[-1](arrived)])
+    return add_up([kept, arrived])
 
 
 def add_up(terms):
@@ -469,6 +472,7 @@
     halves = gather_rows(tokens, gates, orders, ends, beside_shared, ahead_of_last)
     last_sent = halves[-1][0]
     ordered = cache_turn(held["spread"], tie(block_source, last_sent), slot_total)
+    keys = cache_in(ordered, block_size, latent)
     owners = token_owners(block_request, block_used, block_size)
     first_late, ordered, owners = lax.optimization_barrier((halves[0][1], ordered, owners))
     halves[0] = (halves[0][0], first_late)
@@ -497,6 +501,7 @@
         jax.nn.silu(gate_and_up[:, 0]) * gate_and_up[:, 1] * my_gate[:, None]
     ).astype(jnp.bfloat16)
 
+    hidden, keys = lax.optimization_barrier((hidden, keys))
     down_weight = pltpu.with_memory_space_constraint(expert_down[0], pltpu.HBM)
     passed = [[] for _ in range(parts)]
     for step in range(1, tp_size):
@@ -510,29 +515,15 @@
     kepts = [kept, *add_halves(later, False)]
 
     def beside_first_sum(sent):
-        held["keys"] = cache_in(tie(ordered, sent), block_size, latent)
+        near = tie(keys, sent)
+        held["attended"] = attend(queries, [near] + swap_tp(near), owners)
         return sent
 
-    def beside_third_sum(sent):
-        sent, near = lax.optimization_barrier((sent, held["keys"]))
-        held["keys"] = [near] + swap_tp(near)
+    def beside_second_sum(sent):
+        sent, held["attended"] = lax.optimization_barrier((sent, held["attended"]))
         return sent
 
-    def beside_last_sum(sent):
-        sent, keys = lax.optimization_barrier((sent, held["keys"]))
-        held["attended"] = attend(queries, keys, owners)
-        return sent
-
-    def ahead_of_end(arrived):
-        arrived, held["attended"] = lax.optimization_barrier((arrived, held["attended"]))
-        return arrived
-
-    hooks = {
-        0: beside_first_sum,
-        2: beside_third_sum,
-        len(bits) - 1: beside_last_sum,
-        -1: ahead_of_end,
-    }
+    hooks = {0: beside_first_sum, 1: beside_second_sum}
     return (scatter_sums(kepts, sents, orders, hooks), held["attended"])
 
 

time: 108 us -> 111 us (1.028)
  waiting for transfers between devices: 34.5 us -> 48.2 us
  starting transfers between devices: 33.9 us -> 27.7 us
  other arithmetic: 6.99 us -> 4.62 us
  local copies, waits for them, and re-layouts: 6.58 us -> 4.73 us
    ppermute x13, waiting for transfers between devices: 31.1 us -> 41.4 us  [exchange(): lax.ppermute(value, 'ep', [(index, index ^ bit) for index in range(ep_siz...]
    ppermute x13, starting transfers between devices: 20.1 us -> 14.5 us  [exchange(): lax.ppermute(value, 'ep', [(index, index ^ bit) for index in range(ep_siz...]
    all_to_all x1, waiting for transfers between devices: 0.01 us -> 5.18 us  [cache_in(): lax.all_to_all(ordered, 'ep', split_axis=0, concat_axis=0, tiled=True)]
    convert_element_type x6, other arithmetic: 3.42 us -> 1.04 us  [add_up(): return total.astype(jnp.bfloat16)]
    unnamed x9 -> x7, local copies, waits for them, and re-layouts: 4.32 us -> 2.48 us
    ppermute x8, waiting for transfers between devices: 2.96 us -> 1.18 us  [pass_tp(): lax.ppermute(value, 'tp', [(index, (index + step) % tp_size) for index in...]
  transfers between devices with their start and end apart: 23 -> 23, of which waited for: 13 -> 15; matrix products, arithmetic and copies ran while one was open for 8% -> 12% of each run, Pallas kernels for 11% -> 12%
where the time goes in v14:
time: 111 us; the launch traced here: 110 us
  waiting for transfers between devices  48.2 us (43%)
  starting transfers between devices  27.7 us (25%)
  Pallas kernels  16 us (14%)
  matrix products  7.79 us (7%)
  local copies, waits for them, and re-layouts  4.73 us (4%)
  other arithmetic  4.62 us (4%)
    ppermute x13, waiting for transfers between devices, exchange(): lax.ppermute(value, 'ep', [(index, index ^ bit) for index in range(ep_siz...  41.4 us
    pallas_call x8, Pallas kernels, kernel_call(): pl.pallas_call(kernel, out_shape=out_shape, in_specs=in_specs or [WHOLE]...  16 us
    ppermute x13, starting transfers between devices, exchange(): lax.ppermute(value, 'ep', [(index, index ^ bit) for index in range(ep_siz...  14.5 us
    dot_general x1, matrix products, body(): jnp.einsum('sd,dgf->sgf', all_rows, expert_gate_up[0], preferred_element_...  7.79 us
    all_to_all x1, starting transfers between devices, cache_in(): lax.all_to_all(ordered, 'ep', split_axis=0, concat_axis=0, tiled=True)  6.13 us
    all_to_all x1, starting transfers between devices, beside_shared(): lax.all_to_all(pieces, 'ep', split_axis=0, concat_axis=0, tiled=True)  5.28 us
    all_to_all x1, waiting for transfers between devices, cache_in(): lax.all_to_all(ordered, 'ep', split_axis=0, concat_axis=0, tiled=True)  5.18 us
    unnamed x7, local copies, waits for them, and re-layouts  2.48 us
  transfers between devices with their start and end apart: 23, of which 15 were waited for; matrix products, arithmetic and copies ran while one was open for 12% of the time, Pallas kernels for 12%

profile of v14, /device:TPU:0, one launch (start us, length us, event | category | flops | bytes accessed | tf_op | source)
XLA Modules:
  0.0 110.0 jit_solution(6195609984106993257)
XLA Ops:
  2.5 4.0 %collective-permute-start.1 = (bf16[1,16,128]{2,1,0:T(8,128)(2,1)S(1)}, bf16[1,16,128]{2,1,0:T(8,128)(2,1)S(1)}, u32[]{:S(2)}, u32[]{:S(2)}) collective-permute-start(bf16[1,16,128]{2,1,0:T(8,128)(2,1)S(1)} %fusion.18), channel_id=1, source_target_pairs={{0,16},{2,18},{4,20},{6,22},{8,24},{10,26},{12,28},{14,30},{16,0},... | collective-permute-start | bytes 12296 | tf_op jit(solution)/shard_map/ppermute | solution.py:49
  8.4 6.2 %collective-permute-done = bf16[1,16,3584]{2,1,0:T(8,128)(2,1)S(1)} collective-permute-done((bf16[1,16,3584]{2,1,0:T(8,128)(2,1)}, bf16[1,16,3584]{2,1,0:T(8,128)(2,1)S(1)}, u32[]{:S(2)}, u32[]{:S(2)}) %collective-permute-start) | collective-permute-done | bytes 114720 | tf_op jit(solution)/shard_map/ppermute | solution.py:49
  15.8 5.3 %all-to-all-start = ((bf16[16,24,576]{2,1,0:T(8,128)(2,1)}), bf16[16,24,576]{2,1,0:T(8,128)(2,1)S(1)}, u32[]{:S(2)}, u32[]{:S(2)}) async-start(bf16[16,24,576]{2,1,0:T(8,128)(2,1)} %bitcast.37), calls=%async_computation | async-start | bytes 983040 | tf_op jit(solution)/shard_map/all_to_all | solution.py:466
  23.1 1.6 %collective-permute-start.3 = (bf16[4,16,1792]{2,1,0:T(8,128)(2,1)S(1)}, bf16[4,16,1792]{2,1,0:T(8,128)(2,1)S(1)}, u32[]{:S(2)}, u32[]{:S(2)}) collective-permute-start(bf16[4,16,1792]{2,1,0:T(8,128)(2,1)S(1)} %pad_maximum_fusion.5), channel_id=1, source_target_pairs={{0,4},{2,6},{4,0},{6,2},{8,12},{10,14},{12,8},{14,10},{16,20},{18,... | collective-permute-start | bytes 688136 | tf_op jit(solution)/shard_map/ppermute | solution.py:49
  25.6 1.6 %collective-permute-start.5 = (bf16[4,16,1920]{2,1,0:T(8,128)(2,1)S(1)}, bf16[4,16,1920]{2,1,0:T(8,128)(2,1)S(1)}, u32[]{:S(2)}, u32[]{:S(2)}) collective-permute-start(bf16[4,16,1920]{2,1,0:T(8,128)(2,1)S(1)} %pad_maximum_fusion.2), channel_id=1, source_target_pairs={{0,2},{2,0},{4,6},{6,4},{8,10},{10,8},{12,14},{14,12},{16,18},{18,... | collective-permute-start | bytes 737288 | tf_op jit(solution)/shard_map/ppermute | solution.py:49
  27.1 6.0 %collective-permute-done.3 = bf16[4,16,1792]{2,1,0:T(8,128)(2,1)S(1)} collective-permute-done((bf16[4,16,1792]{2,1,0:T(8,128)(2,1)S(1)}, bf16[4,16,1792]{2,1,0:T(8,128)(2,1)S(1)}, u32[]{:S(2)}, u32[]{:S(2)}) %collective-permute-start.3) | collective-permute-done | bytes 229408 | tf_op jit(solution)/shard_map/ppermute | solution.py:49
  33.1 1.3 %collective-permute-start.4 = (bf16[8,16,1792]{2,1,0:T(8,128)(2,1)S(1)}, bf16[8,16,1792]{2,1,0:T(8,128)(2,1)}, u32[]{:S(2)}, u32[]{:S(2)}) collective-permute-start(bf16[8,16,1792]{2,1,0:T(8,128)(2,1)S(1)} %pad_maximum_fusion.1), channel_id=1, source_target_pairs={{0,2},{2,0},{4,6},{6,4},{8,10},{10,8},{12,14},{14,12},{16,18},{18,... | collective-permute-start | bytes 1376264 | tf_op jit(solution)/shard_map/ppermute | solution.py:49
  39.6 1.6 %shard_map.113 = bf16[384,576]{1,0:T(8,128)(2,1)} custom-call(s32[384,2]{1,0:T(8,128)S(1)} %fusion.7.index, bf16[384,576]{1,0:T(8,128)(2,1)S(1)} %bitcast.39, bf16[384,576]{1,0:T(8,128)(2,1)S(1)} %bitcast.44), custom_call_target="tpu_custom_call" | custom-call | flops 339738624 | bytes 2217984 | tf_op jit(solution)/shard_map/pallas_call | solution.py:25
  41.2 4.0 %collective-permute-done.4 = bf16[8,16,1792]{2,1,0:T(8,128)(2,1)} collective-permute-done((bf16[8,16,1792]{2,1,0:T(8,128)(2,1)S(1)}, bf16[8,16,1792]{2,1,0:T(8,128)(2,1)}, u32[]{:S(2)}, u32[]{:S(2)}) %collective-permute-start.4) | collective-permute-done | bytes 458784 | tf_op jit(solution)/shard_map/ppermute | solution.py:49
  46.4 6.1 %all-to-all-start.1 = ((bf16[16,24,576]{2,1,0:T(8,128)(2,1)}), bf16[16,24,576]{2,1,0:T(8,128)(2,1)}, u32[]{:S(2)}, u32[]{:S(2)}) async-start(bf16[16,24,576]{2,1,0:T(8,128)(2,1)} %bitcast.6), calls=%async_computation.1 | async-start | bytes 983040 | tf_op jit(solution)/shard_map/all_to_all | solution.py:361
  52.8 1.5 %shard_map.114 = bf16[256,7168]{1,0:T(8,128)(2,1)S(1)} custom-call(bf16[128,1792]{1,0:T(8,128)(2,1)S(1)} %bitcast.40, bf16[128,1792]{1,0:T(8,128)(2,1)} %bitcast.7.refs_1_, bf16[128,1920]{1,0:T(8,128)(2,1)S(1)} %bitcast.38, bf16[128,1920]{1,0:T(8,128)(2,1)S(1)} %bitcast.41, bf16[128,1792]{1,0:T(8,128)(2,1)} %bitcast.10.refs_4_, ...), custom_call_target="tpu_custom_call" | custom-call | tf_op jit(solution)/shard_map/pallas_call | solution.py:25
  54.4 7.8 %fusion = f32[256,2,512]{2,0,1:T(8,128)S(1)} fusion(bf16[7168,2,512]{2,1,0:T(2,128)(2,1)} %bitcast.54, bf16[256,7168]{1,0:T(8,128)(2,1)S(1)} %shard_map.114), kind=kOutput, calls=%fused_computation | convolution fusion | flops 3758096384 | bytes 19398656 | tf_op jit(solution)/shard_map/sd,dgf->sgf/dot_general | solution.py:497
  62.3 5.2 %all-to-all-done.1 = bf16[16,24,576]{2,1,0:T(8,128)(2,1)} async-done(((bf16[16,24,576]{2,1,0:T(8,128)(2,1)}), bf16[16,24,576]{2,1,0:T(8,128)(2,1)}, u32[]{:S(2)}, u32[]{:S(2)}) %all-to-all-start.1) | async-done | bytes 442400 | tf_op jit(solution)/shard_map/all_to_all | solution.py:361
  67.5 3.1 %shard_map.115 = (bf16[256,1792]{1,0:T(8,128)(2,1)S(1)}, bf16[256,1792]{1,0:T(8,128)(2,1)S(1)}) custom-call(bf16[256,512]{1,0:T(8,128)(2,1)S(1)} %fusion.5.hidden, bf16[7168,512]{1,0:T(8,128)(2,1)} %bitcast.47), custom_call_target="tpu_custom_call" | custom-call | flops 939524096 | bytes 9699328 | tf_op jit(solution)/shard_map/pallas_call | solution.py:25
  71.2 2.2 %shard_map.117.refs_0_ = bf16[256,1792]{1,0:T(8,128)(2,1)S(1)} custom-call(bf16[256,512]{1,0:T(8,128)(2,1)S(1)} %fusion.5.hidden, bf16[7168,512]{1,0:T(8,128)(2,1)} %bitcast.48), custom_call_target="tpu_custom_call" | custom-call | flops 469762048 | bytes 8781824 | tf_op jit(solution)/shard_map/pallas_call | solution.py:25
  75.4 2.3 %shard_map.116 = (bf16[128,1792]{1,0:T(8,128)(2,1)S(1)}, bf16[128,1792]{1,0:T(8,128)(2,1)S(1)}) custom-call(bf16[256,512]{1,0:T(8,128)(2,1)S(1)} %fusion.5.hidden, bf16[7168,512]{1,0:T(8,128)(2,1)} %bitcast.49, bf16[256,1792]{1,0:T(8,128)(2,1)S(1)} %collective-permute-done.12.refs_0_), custom_call_target="tpu_custom_call" | custom-call | flops 469762048 | bytes 9699328 | tf_op jit(solution)/shard_map/pallas_call | solution.py:25
  79.0 4.0 %shard_map.120 = bf16[512,512]{1,0:T(8,128)(2,1)} custom-call(s32[2,384]{1,0:T(2,128)S(1)} %pad_add_fusion.owner, bf16[512,576]{1,0:T(8,128)(2,1)S(1)} %bitcast.45, bf16[384,576]{1,0:T(8,128)(2,1)} %bitcast.20.refs_0_, bf16[384,576]{1,0:T(8,128)(2,1)S(1)} %bitcast.46), custom_call_target="tpu_custom_call" | custom-call | flops 905969664 | bytes 3479552 | tf_op jit(solution)/shard_map/pallas_call | solution.py:25
  82.9 4.2 %collective-permute-done.16 = bf16[128,1792]{1,0:T(8,128)(2,1)S(1)} collective-permute-done((bf16[128,1792]{1,0:T(8,128)(2,1)S(1)}, bf16[128,1792]{1,0:T(8,128)(2,1)S(1)}, u32[]{:S(2)}, u32[]{:S(2)}) %collective-permute-start.16) | collective-permute-done | bytes 458784 | tf_op jit(solution)/shard_map/ppermute | solution.py:49
  87.8 3.3 %collective-permute-done.13 = bf16[128,1792]{1,0:T(8,128)(2,1)S(1)} collective-permute-done((bf16[128,1792]{1,0:T(8,128)(2,1)S(1)}, bf16[128,1792]{1,0:T(8,128)(2,1)S(1)}, u32[]{:S(2)}, u32[]{:S(2)}) %collective-permute-start.13) | collective-permute-done | bytes 458784 | tf_op jit(solution)/shard_map/ppermute | solution.py:49
  91.8 3.5 %collective-permute-done.18 = bf16[64,1792]{1,0:T(8,128)(2,1)S(1)} collective-permute-done((bf16[64,1792]{1,0:T(8,128)(2,1)S(1)}, bf16[64,1792]{1,0:T(8,128)(2,1)S(1)}, u32[]{:S(2)}, u32[]{:S(2)}) %collective-permute-start.18) | collective-permute-done | bytes 229408 | tf_op jit(solution)/shard_map/ppermute | solution.py:49
  95.3 2.0 %collective-permute-done.14 = bf16[64,1792]{1,0:T(8,128)(2,1)S(1)} collective-permute-done((bf16[64,1792]{1,0:T(8,128)(2,1)S(1)}, bf16[64,1792]{1,0:T(8,128)(2,1)S(1)}, u32[]{:S(2)}, u32[]{:S(2)}) %collective-permute-start.14) | collective-permute-done | bytes 229408 | tf_op jit(solution)/shard_map/ppermute | solution.py:49
  97.4 1.3 %collective-permute-start.19 = (bf16[32,3584]{1,0:T(8,128)(2,1)S(1)}, bf16[32,3584]{1,0:T(8,128)(2,1)S(1)}, u32[]{:S(2)}, u32[]{:S(2)}) collective-permute-start(bf16[32,3584]{1,0:T(8,128)(2,1)S(1)} %pad_maximum_fusion.6), channel_id=1, source_target_pairs={{0,8},{2,10},{4,12},{6,14},{8,0},{10,2},{12,4},{14,6},{16,24},{18,... | collective-permute-start | bytes 688136 | tf_op jit(solution)/shard_map/ppermute | solution.py:49
  98.7 4.8 %collective-permute-done.19 = bf16[32,3584]{1,0:T(8,128)(2,1)S(1)} collective-permute-done((bf16[32,3584]{1,0:T(8,128)(2,1)S(1)}, bf16[32,3584]{1,0:T(8,128)(2,1)S(1)}, u32[]{:S(2)}, u32[]{:S(2)}) %collective-permute-start.19) | collective-permute-done | bytes 229408 | tf_op jit(solution)/shard_map/ppermute | solution.py:49
  104.3 5.0 %collective-permute-done.20 = bf16[16,3584]{1,0:T(8,128)(2,1)S(1)} collective-permute-done((bf16[16,3584]{1,0:T(8,128)(2,1)S(1)}, bf16[16,3584]{1,0:T(8,128)(2,1)S(1)}, u32[]{:S(2)}, u32[]{:S(2)}) %collective-permute-start.20) | collective-permute-done | bytes 114720 | tf_op jit(solution)/shard_map/ppermute | solution.py:49
  (75 shorter events, 21.3 us)
Async XLA Ops:
  2.5 6.0 %collective-permute-start.1 = (bf16[1,16,128]{2,1,0:T(8,128)(2,1)S(1)}, bf16[1,16,128]{2,1,0:T(8,128)(2,1)S(1)}, u32[]{:S(2)}, u32[]{:S(2)}) collective-permute-start(bf16[1,16,128]{2,1,0:T(8,128)(2,1)S(1)} %fusion.18), channel_id=1, source_target_pairs={{0,16},{2,18},{4,20},{6,22},{8,24},{10,26},{12,28},{14,30},{16,0},... | collective-permute-start | bytes 12296 | tf_op jit(solution)/shard_map/ppermute | solution.py:49
  6.5 8.2 %collective-permute-start = (bf16[1,16,3584]{2,1,0:T(8,128)(2,1)}, bf16[1,16,3584]{2,1,0:T(8,128)(2,1)S(1)}, u32[]{:S(2)}, u32[]{:S(2)}) collective-permute-start(bf16[1,16,3584]{2,1,0:T(8,128)(2,1)} %bitcast.50), channel_id=1, source_target_pairs={{0,16},{2,18},{4,20},{6,22},{8,24},{10,26},{12,28},{14,30},{16,0},... | collective-permute-start | bytes 344072 | tf_op jit(solution)/shard_map/ppermute | solution.py:49
  15.6 6.7 %collective-permute-start.2 = (bf16[2,16,3712]{2,1,0:T(8,128)(2,1)S(1)}, bf16[2,16,3712]{2,1,0:T(8,128)(2,1)S(1)}, u32[]{:S(2)}, u32[]{:S(2)}) collective-permute-start(bf16[2,16,3712]{2,1,0:T(8,128)(2,1)S(1)} %maximum_maximum_fusion), channel_id=1, source_target_pairs={{0,8},{2,10},{4,12},{6,14},{8,0},{10,2},{12,4},{14,6},{16,24},{18,... | collective-permute-start | bytes 712712 | tf_op jit(solution)/shard_map/ppermute | solution.py:49
  15.8 19.7 %all-to-all-start = ((bf16[16,24,576]{2,1,0:T(8,128)(2,1)}), bf16[16,24,576]{2,1,0:T(8,128)(2,1)S(1)}, u32[]{:S(2)}, u32[]{:S(2)}) async-start(bf16[16,24,576]{2,1,0:T(8,128)(2,1)} %bitcast.37), calls=%async_computation | async-start | bytes 983040 | tf_op jit(solution)/shard_map/all_to_all | solution.py:466
  23.1 10.0 %collective-permute-start.3 = (bf16[4,16,1792]{2,1,0:T(8,128)(2,1)S(1)}, bf16[4,16,1792]{2,1,0:T(8,128)(2,1)S(1)}, u32[]{:S(2)}, u32[]{:S(2)}) collective-permute-start(bf16[4,16,1792]{2,1,0:T(8,128)(2,1)S(1)} %pad_maximum_fusion.5), channel_id=1, source_target_pairs={{0,4},{2,6},{4,0},{6,2},{8,12},{10,14},{12,8},{14,10},{16,20},{18,... | collective-permute-start | bytes 688136 | tf_op jit(solution)/shard_map/ppermute | solution.py:49
  25.6 9.3 %collective-permute-start.5 = (bf16[4,16,1920]{2,1,0:T(8,128)(2,1)S(1)}, bf16[4,16,1920]{2,1,0:T(8,128)(2,1)S(1)}, u32[]{:S(2)}, u32[]{:S(2)}) collective-permute-start(bf16[4,16,1920]{2,1,0:T(8,128)(2,1)S(1)} %pad_maximum_fusion.2), channel_id=1, source_target_pairs={{0,2},{2,0},{4,6},{6,4},{8,10},{10,8},{12,14},{14,12},{16,18},{18,... | collective-permute-start | bytes 737288 | tf_op jit(solution)/shard_map/ppermute | solution.py:49
  33.1 12.1 %collective-permute-start.4 = (bf16[8,16,1792]{2,1,0:T(8,128)(2,1)S(1)}, bf16[8,16,1792]{2,1,0:T(8,128)(2,1)}, u32[]{:S(2)}, u32[]{:S(2)}) collective-permute-start(bf16[8,16,1792]{2,1,0:T(8,128)(2,1)S(1)} %pad_maximum_fusion.1), channel_id=1, source_target_pairs={{0,2},{2,0},{4,6},{6,4},{8,10},{10,8},{12,14},{14,12},{16,18},{18,... | collective-permute-start | bytes 1376264 | tf_op jit(solution)/shard_map/ppermute | solution.py:49
  35.4 11.0 %collective-permute-start.7 = (bf16[8,16,1920]{2,1,0:T(8,128)(2,1)S(1)}, bf16[8,16,1920]{2,1,0:T(8,128)(2,1)S(1)}, u32[]{:S(2)}, u32[]{:S(2)}) collective-permute-start(bf16[8,16,1920]{2,1,0:T(8,128)(2,1)S(1)} %pad_maximum_fusion), channel_id=1, source_target_pairs={{0,4},{2,6},{4,0},{6,2},{8,12},{10,14},{12,8},{14,10},{16,20},{18,... | collective-permute-start | bytes 1474568 | tf_op jit(solution)/shard_map/ppermute | solution.py:49
  37.7 1.9 %collective-permute-start.6 = (bf16[16,24,576]{2,1,0:T(8,128)(2,1)S(1)}, bf16[16,24,576]{2,1,0:T(8,128)(2,1)S(1)}, u32[]{:S(2)}, u32[]{:S(2)}) collective-permute-start(bf16[16,24,576]{2,1,0:T(8,128)(2,1)S(1)} %all-to-all-done), channel_id=1, source_target_pairs={{0,1},{1,0},{2,3},{3,2},{4,5},{5,4},{6,7},{7,6},{8,9},{9,8},{10,11... | collective-permute-start | bytes 1327112 | tf_op jit(solution)/shard_map/ppermute | solution.py:54
  37.7 15.0 %collective-permute-start.8 = (bf16[8,16,1792]{2,1,0:T(8,128)(2,1)S(1)}, bf16[8,16,1792]{2,1,0:T(8,128)(2,1)}, u32[]{:S(2)}, u32[]{:S(2)}) collective-permute-start(bf16[8,16,1792]{2,1,0:T(8,128)(2,1)S(1)} %pad_maximum_fusion.1), channel_id=1, source_target_pairs={{0,1},{1,0},{2,3},{3,2},{4,5},{5,4},{6,7},{7,6},{8,9},{9,8},{10,11... | collective-permute-start | bytes 1376264 | tf_op jit(solution)/shard_map/ppermute | solution.py:54
  45.2 7.6 %collective-permute-start.9 = (bf16[8,16,1792]{2,1,0:T(8,128)(2,1)}, bf16[8,16,1792]{2,1,0:T(8,128)(2,1)}, u32[]{:S(2)}, u32[]{:S(2)}) collective-permute-start(bf16[8,16,1792]{2,1,0:T(8,128)(2,1)} %collective-permute-done.4), channel_id=1, source_target_pairs={{0,1},{1,0},{2,3},{3,2},{4,5},{5,4},{6,7},{7,6},{8,9},{9,8},{10,11... | collective-permute-start | bytes 1376264 | tf_op jit(solution)/shard_map/ppermute | solution.py:54
  45.2 7.6 %collective-permute-start.10 = (bf16[8,16,1920]{2,1,0:T(8,128)(2,1)S(1)}, bf16[8,16,1920]{2,1,0:T(8,128)(2,1)S(1)}, u32[]{:S(2)}, u32[]{:S(2)}) collective-permute-start(bf16[8,16,1920]{2,1,0:T(8,128)(2,1)S(1)} %pad_maximum_fusion), channel_id=1, source_target_pairs={{0,1},{1,0},{2,3},{3,2},{4,5},{5,4},{6,7},{7,6},{8,9},{9,8},{10,11... | collective-permute-start | bytes 1474568 | tf_op jit(solution)/shard_map/ppermute | solution.py:54
  46.4 6.4 %collective-permute-start.11 = (bf16[8,16,1920]{2,1,0:T(8,128)(2,1)S(1)}, bf16[8,16,1920]{2,1,0:T(8,128)(2,1)S(1)}, u32[]{:S(2)}, u32[]{:S(2)}) collective-permute-start(bf16[8,16,1920]{2,1,0:T(8,128)(2,1)S(1)} %collective-permute-done.7), channel_id=1, source_target_pairs={{0,1},{1,0},{2,3},{3,2},{4,5},{5,4},{6,7},{7,6},{8,9},{9,8},{10,11... | collective-permute-start | bytes 1474568 | tf_op jit(solution)/shard_map/ppermute | solution.py:54
  46.4 21.1 %all-to-all-start.1 = ((bf16[16,24,576]{2,1,0:T(8,128)(2,1)}), bf16[16,24,576]{2,1,0:T(8,128)(2,1)}, u32[]{:S(2)}, u32[]{:S(2)}) async-start(bf16[16,24,576]{2,1,0:T(8,128)(2,1)} %bitcast.6), calls=%async_computation.1 | async-start | bytes 983040 | tf_op jit(solution)/shard_map/all_to_all | solution.py:361
  67.5 11.5 %copy-start.1 = (bf16[16,32,576]{2,1,0:T(8,128)(2,1)S(1)}, bf16[16,32,576]{2,1,0:T(8,128)(2,1)}, u32[]{:S(2)}) copy-start(bf16[16,32,576]{2,1,0:T(8,128)(2,1)} %param.15) | copy-start | bytes 1769476
  70.6 2.8 %collective-permute-start.15 = (bf16[256,1792]{1,0:T(8,128)(2,1)S(1)}, bf16[256,1792]{1,0:T(8,128)(2,1)S(1)}, u32[]{:S(2)}, u32[]{:S(2)}) collective-permute-start(bf16[256,1792]{1,0:T(8,128)(2,1)S(1)} %get-tuple-element.30), channel_id=1, source_target_pairs={{0,1},{1,0},{2,3},{3,2},{4,5},{5,4},{6,7},{7,6},{8,9},{9,8},{10,11... | collective-permute-start | bytes 2752520 | tf_op jit(solution)/shard_map/ppermute | solution.py:54
  70.7 4.7 %collective-permute-start.12 = (bf16[256,1792]{1,0:T(8,128)(2,1)S(1)}, bf16[256,1792]{1,0:T(8,128)(2,1)S(1)}, u32[]{:S(2)}, u32[]{:S(2)}) collective-permute-start(bf16[256,1792]{1,0:T(8,128)(2,1)S(1)} %get-tuple-element.27), channel_id=1, source_target_pairs={{0,1},{1,0},{2,3},{3,2},{4,5},{5,4},{6,7},{7,6},{8,9},{9,8},{10,11... | collective-permute-start | bytes 2752520 | tf_op jit(solution)/shard_map/ppermute | solution.py:54
  74.1 4.9 %collective-permute-start.17 = (bf16[16,24,576]{2,1,0:T(8,128)(2,1)}, bf16[16,24,576]{2,1,0:T(8,128)(2,1)S(1)}, u32[]{:S(2)}, u32[]{:S(2)}) collective-permute-start(bf16[16,24,576]{2,1,0:T(8,128)(2,1)} %all-to-all-done.1), channel_id=1, source_target_pairs={{0,1},{1,0},{2,3},{3,2},{4,5},{5,4},{6,7},{7,6},{8,9},{9,8},{10,11... | collective-permute-start | bytes 1327112 | tf_op jit(solution)/shard_map/ppermute | solution.py:54
  74.2 12.9 %collective-permute-start.16 = (bf16[128,1792]{1,0:T(8,128)(2,1)S(1)}, bf16[128,1792]{1,0:T(8,128)(2,1)S(1)}, u32[]{:S(2)}, u32[]{:S(2)}) collective-permute-start(bf16[128,1792]{1,0:T(8,128)(2,1)S(1)} %shard_map.119), channel_id=1, source_target_pairs={{0,4},{2,6},{4,0},{6,2},{8,12},{10,14},{12,8},{14,10},{16,20},{18,... | collective-permute-start | bytes 1376264 | tf_op jit(solution)/shard_map/ppermute | solution.py:49
  77.7 13.4 %collective-permute-start.13 = (bf16[128,1792]{1,0:T(8,128)(2,1)S(1)}, bf16[128,1792]{1,0:T(8,128)(2,1)S(1)}, u32[]{:S(2)}, u32[]{:S(2)}) collective-permute-start(bf16[128,1792]{1,0:T(8,128)(2,1)S(1)} %get-tuple-element.29), channel_id=1, source_target_pairs={{0,2},{2,0},{4,6},{6,4},{8,10},{10,8},{12,14},{14,12},{16,18},{18,... | collective-permute-start | bytes 1376264 | tf_op jit(solution)/shard_map/ppermute | solution.py:49
  87.2 8.0 %collective-permute-start.18 = (bf16[64,1792]{1,0:T(8,128)(2,1)S(1)}, bf16[64,1792]{1,0:T(8,128)(2,1)S(1)}, u32[]{:S(2)}, u32[]{:S(2)}) collective-permute-start(bf16[64,1792]{1,0:T(8,128)(2,1)S(1)} %get-tuple-element.34), channel_id=1, source_target_pairs={{0,2},{2,0},{4,6},{6,4},{8,10},{10,8},{12,14},{14,12},{16,18},{18,... | collective-permute-start | bytes 688136 | tf_op jit(solution)/shard_map/ppermute | solution.py:49
  91.2 6.1 %collective-permute-start.14 = (bf16[64,1792]{1,0:T(8,128)(2,1)S(1)}, bf16[64,1792]{1,0:T(8,128)(2,1)S(1)}, u32[]{:S(2)}, u32[]{:S(2)}) collective-permute-start(bf16[64,1792]{1,0:T(8,128)(2,1)S(1)} %get-tuple-element.40), channel_id=1, source_target_pairs={{0,4},{2,6},{4,0},{6,2},{8,12},{10,14},{12,8},{14,10},{16,20},{18,... | collective-permute-start | bytes 688136 | tf_op jit(solution)/shard_map/ppermute | solution.py:49
  97.4 6.1 %collective-permute-start.19 = (bf16[32,3584]{1,0:T(8,128)(2,1)S(1)}, bf16[32,3584]{1,0:T(8,128)(2,1)S(1)}, u32[]{:S(2)}, u32[]{:S(2)}) collective-permute-start(bf16[32,3584]{1,0:T(8,128)(2,1)S(1)} %pad_maximum_fusion.6), channel_id=1, source_target_pairs={{0,8},{2,10},{4,12},{6,14},{8,0},{10,2},{12,4},{14,6},{16,24},{18,... | collective-permute-start | bytes 688136 | tf_op jit(solution)/shard_map/ppermute | solution.py:49
  103.6 5.8 %collective-permute-start.20 = (bf16[16,3584]{1,0:T(8,128)(2,1)S(1)}, bf16[16,3584]{1,0:T(8,128)(2,1)S(1)}, u32[]{:S(2)}, u32[]{:S(2)}) collective-permute-start(bf16[16,3584]{1,0:T(8,128)(2,1)S(1)} %add_convert_fusion.5), channel_id=1, source_target_pairs={{0,16},{2,18},{4,20},{6,22},{8,24},{10,26},{12,28},{14,30},{16,0},... | collective-permute-start | bytes 344072 | tf_op jit(solution)/shard_map/ppermute | solution.py:49
  (1 other events, 6.8 us)

commit v15 on v14

--- a/solution.py
+++ b/solution.py
@@ -213,7 +213,8 @@
         functools.partial(group_kernel, step, chosen, spots, tp_size, cut, rows),
         [shape] * count,
         [hidden, weight],
-        flops=2 * hidden.size * cut * count,
+        flops=0,
+        counted=False,
         spare=count * cut * weight.shape[1] * 2 + (8 << 20),
         in_specs=[WHOLE, pl.BlockSpec(memory_space=pl.ANY)],
         scratch_shapes=[
@@ -501,11 +502,11 @@
         jax.nn.silu(gate_and_up[:, 0]) * gate_and_up[:, 1] * my_gate[:, None]
     ).astype(jnp.bfloat16)
 
-    hidden, keys = lax.optimization_barrier((hidden, keys))
     down_weight = pltpu.with_memory_space_constraint(expert_down[0], pltpu.HBM)
     passed = [[] for _ in range(parts)]
     for step in range(1, tp_size):
         others = down_group(hidden, down_weight, step, range(parts), from_first, row_count)
+        others, keys = lax.optimization_barrier((others, keys))
         for part in range(parts):
             passed[part].append(pass_tp(others[part], step))
     later = down_group(hidden, down_weight, 0, range(1, parts), from_first, row_count)

time: 111 us -> 108 us (0.973)
  waiting for transfers between devices: 48.2 us -> 44.9 us
    all_to_all x1, waiting for transfers between devices: 5.18 us -> 2.12 us  [cache_in(): lax.all_to_all(ordered, 'ep', split_axis=0, concat_axis=0, tiled=True)]
  transfers between devices with their start and end apart: 23 -> 23, of which waited for: 15 -> 15; matrix products, arithmetic and copies ran while one was open for 12% -> 13% of each run, Pallas kernels for 12% -> 15%
where the time goes in v15:
time: 108 us; the launch traced here: 107 us
  waiting for transfers between devices  44.9 us (42%)
  starting transfers between devices  28 us (26%)
  Pallas kernels  15.9 us (15%)
  matrix products  7.79 us (7%)
  local copies, waits for them, and re-layouts  4.73 us (4%)
  other arithmetic  4.62 us (4%)
    ppermute x13, waiting for transfers between devices, exchange(): lax.ppermute(value, 'ep', [(index, index ^ bit) for index in range(ep_siz...  41.1 us
    pallas_call x8, Pallas kernels, kernel_call(): pl.pallas_call(kernel, out_shape=out_shape, in_specs=in_specs or [WHOLE]...  15.9 us
    ppermute x13, starting transfers between devices, exchange(): lax.ppermute(value, 'ep', [(index, index ^ bit) for index in range(ep_siz...  14.9 us
    dot_general x1, matrix products, body(): jnp.einsum('sd,dgf->sgf', all_rows, expert_gate_up[0], preferred_element_...  7.79 us
    all_to_all x1, starting transfers between devices, cache_in(): lax.all_to_all(ordered, 'ep', split_axis=0, concat_axis=0, tiled=True)  6.13 us
    all_to_all x1, starting transfers between devices, beside_shared(): lax.all_to_all(pieces, 'ep', split_axis=0, concat_axis=0, tiled=True)  5.28 us
    unnamed x7, local copies, waits for them, and re-layouts  2.48 us
  transfers between devices with their start and end apart: 23, of which 15 were waited for; matrix products, arithmetic and copies ran while one was open for 13% of the time, Pallas kernels for 15%

profile of v15, /device:TPU:0, one launch (start us, length us, event | category | flops | bytes accessed | tf_op | source)
XLA Modules:
  0.0 106.8 jit_solution(14929854940304607750)
XLA Ops:
  2.5 4.0 %collective-permute-start.1 = (bf16[1,16,128]{2,1,0:T(8,128)(2,1)S(1)}, bf16[1,16,128]{2,1,0:T(8,128)(2,1)S(1)}, u32[]{:S(2)}, u32[]{:S(2)}) collective-permute-start(bf16[1,16,128]{2,1,0:T(8,128)(2,1)S(1)} %fusion.18), channel_id=1, source_target_pairs={{0,16},{2,18},{4,20},{6,22},{8,24},{10,26},{12,28},{14,30},{16,0},... | collective-permute-start | bytes 12296 | tf_op jit(solution)/shard_map/ppermute | solution.py:49
  8.4 6.2 %collective-permute-done = bf16[1,16,3584]{2,1,0:T(8,128)(2,1)S(1)} collective-permute-done((bf16[1,16,3584]{2,1,0:T(8,128)(2,1)}, bf16[1,16,3584]{2,1,0:T(8,128)(2,1)S(1)}, u32[]{:S(2)}, u32[]{:S(2)}) %collective-permute-start) | collective-permute-done | bytes 114720 | tf_op jit(solution)/shard_map/ppermute | solution.py:49
  15.8 5.3 %all-to-all-start = ((bf16[16,24,576]{2,1,0:T(8,128)(2,1)}), bf16[16,24,576]{2,1,0:T(8,128)(2,1)S(1)}, u32[]{:S(2)}, u32[]{:S(2)}) async-start(bf16[16,24,576]{2,1,0:T(8,128)(2,1)} %bitcast.37), calls=%async_computation | async-start | bytes 983040 | tf_op jit(solution)/shard_map/all_to_all | solution.py:467
  23.1 1.6 %collective-permute-start.3 = (bf16[4,16,1792]{2,1,0:T(8,128)(2,1)S(1)}, bf16[4,16,1792]{2,1,0:T(8,128)(2,1)S(1)}, u32[]{:S(2)}, u32[]{:S(2)}) collective-permute-start(bf16[4,16,1792]{2,1,0:T(8,128)(2,1)S(1)} %pad_maximum_fusion.5), channel_id=1, source_target_pairs={{0,4},{2,6},{4,0},{6,2},{8,12},{10,14},{12,8},{14,10},{16,20},{18,... | collective-permute-start | bytes 688136 | tf_op jit(solution)/shard_map/ppermute | solution.py:49
  25.6 1.6 %collective-permute-start.5 = (bf16[4,16,1920]{2,1,0:T(8,128)(2,1)S(1)}, bf16[4,16,1920]{2,1,0:T(8,128)(2,1)S(1)}, u32[]{:S(2)}, u32[]{:S(2)}) collective-permute-start(bf16[4,16,1920]{2,1,0:T(8,128)(2,1)S(1)} %pad_maximum_fusion.2), channel_id=1, source_target_pairs={{0,2},{2,0},{4,6},{6,4},{8,10},{10,8},{12,14},{14,12},{16,18},{18,... | collective-permute-start | bytes 737288 | tf_op jit(solution)/shard_map/ppermute | solution.py:49
  27.1 6.0 %collective-permute-done.3 = bf16[4,16,1792]{2,1,0:T(8,128)(2,1)S(1)} collective-permute-done((bf16[4,16,1792]{2,1,0:T(8,128)(2,1)S(1)}, bf16[4,16,1792]{2,1,0:T(8,128)(2,1)S(1)}, u32[]{:S(2)}, u32[]{:S(2)}) %collective-permute-start.3) | collective-permute-done | bytes 229408 | tf_op jit(solution)/shard_map/ppermute | solution.py:49
  33.1 1.3 %collective-permute-start.4 = (bf16[8,16,1792]{2,1,0:T(8,128)(2,1)S(1)}, bf16[8,16,1792]{2,1,0:T(8,128)(2,1)}, u32[]{:S(2)}, u32[]{:S(2)}) collective-permute-start(bf16[8,16,1792]{2,1,0:T(8,128)(2,1)S(1)} %pad_maximum_fusion.1), channel_id=1, source_target_pairs={{0,2},{2,0},{4,6},{6,4},{8,10},{10,8},{12,14},{14,12},{16,18},{18,... | collective-permute-start | bytes 1376264 | tf_op jit(solution)/shard_map/ppermute | solution.py:49
  39.6 1.6 %shard_map.113 = bf16[384,576]{1,0:T(8,128)(2,1)} custom-call(s32[384,2]{1,0:T(8,128)S(1)} %fusion.7.index, bf16[384,576]{1,0:T(8,128)(2,1)S(1)} %bitcast.39, bf16[384,576]{1,0:T(8,128)(2,1)S(1)} %bitcast.44), custom_call_target="tpu_custom_call" | custom-call | flops 339738624 | bytes 2217984 | tf_op jit(solution)/shard_map/pallas_call | solution.py:25
  41.2 4.0 %collective-permute-done.4 = bf16[8,16,1792]{2,1,0:T(8,128)(2,1)} collective-permute-done((bf16[8,16,1792]{2,1,0:T(8,128)(2,1)S(1)}, bf16[8,16,1792]{2,1,0:T(8,128)(2,1)}, u32[]{:S(2)}, u32[]{:S(2)}) %collective-permute-start.4) | collective-permute-done | bytes 458784 | tf_op jit(solution)/shard_map/ppermute | solution.py:49
  46.4 6.1 %all-to-all-start.1 = ((bf16[16,24,576]{2,1,0:T(8,128)(2,1)}), bf16[16,24,576]{2,1,0:T(8,128)(2,1)}, u32[]{:S(2)}, u32[]{:S(2)}) async-start(bf16[16,24,576]{2,1,0:T(8,128)(2,1)} %bitcast.6), calls=%async_computation.1 | async-start | bytes 983040 | tf_op jit(solution)/shard_map/all_to_all | solution.py:362
  52.8 1.5 %shard_map.114 = bf16[256,7168]{1,0:T(8,128)(2,1)S(1)} custom-call(bf16[128,1792]{1,0:T(8,128)(2,1)S(1)} %bitcast.40, bf16[128,1792]{1,0:T(8,128)(2,1)} %bitcast.7.refs_1_, bf16[128,1920]{1,0:T(8,128)(2,1)S(1)} %bitcast.38, bf16[128,1920]{1,0:T(8,128)(2,1)S(1)} %bitcast.41, bf16[128,1792]{1,0:T(8,128)(2,1)} %bitcast.10.refs_4_, ...), custom_call_target="tpu_custom_call" | custom-call | tf_op jit(solution)/shard_map/pallas_call | solution.py:25
  54.4 7.8 %fusion = f32[256,2,512]{2,0,1:T(8,128)S(1)} fusion(bf16[7168,2,512]{2,1,0:T(2,128)(2,1)} %bitcast.54, bf16[256,7168]{1,0:T(8,128)(2,1)S(1)} %shard_map.114), kind=kOutput, calls=%fused_computation | convolution fusion | flops 3758096384 | bytes 19398656 | tf_op jit(solution)/shard_map/sd,dgf->sgf/dot_general | solution.py:498
  62.3 3.0 %shard_map.115 = (bf16[256,1792]{1,0:T(8,128)(2,1)S(1)}, bf16[256,1792]{1,0:T(8,128)(2,1)S(1)}) custom-call(bf16[256,512]{1,0:T(8,128)(2,1)S(1)} %fusion.5.hidden, bf16[7168,512]{1,0:T(8,128)(2,1)} %bitcast.47), custom_call_target="tpu_custom_call" | custom-call | tf_op jit(solution)/shard_map/pallas_call | solution.py:25
  65.4 2.1 %all-to-all-done.1 = bf16[16,24,576]{2,1,0:T(8,128)(2,1)} async-done(((bf16[16,24,576]{2,1,0:T(8,128)(2,1)}), bf16[16,24,576]{2,1,0:T(8,128)(2,1)}, u32[]{:S(2)}, u32[]{:S(2)}) %all-to-all-start.1) | async-done | bytes 442400 | tf_op jit(solution)/shard_map/all_to_all | solution.py:362
  68.0 2.2 %shard_map.117.refs_0_ = bf16[256,1792]{1,0:T(8,128)(2,1)S(1)} custom-call(bf16[256,512]{1,0:T(8,128)(2,1)S(1)} %fusion.5.hidden, bf16[7168,512]{1,0:T(8,128)(2,1)} %bitcast.48), custom_call_target="tpu_custom_call" | custom-call | tf_op jit(solution)/shard_map/pallas_call | solution.py:25
  72.2 2.3 %shard_map.116 = (bf16[128,1792]{1,0:T(8,128)(2,1)S(1)}, bf16[128,1792]{1,0:T(8,128)(2,1)S(1)}) custom-call(bf16[256,512]{1,0:T(8,128)(2,1)S(1)} %fusion.5.hidden, bf16[7168,512]{1,0:T(8,128)(2,1)} %bitcast.49, bf16[256,1792]{1,0:T(8,128)(2,1)S(1)} %collective-permute-done.12.refs_0_), custom_call_target="tpu_custom_call" | custom-call | flops 469762048 | bytes 9699328 | tf_op jit(solution)/shard_map/pallas_call | solution.py:25
  75.8 4.0 %shard_map.120 = bf16[512,512]{1,0:T(8,128)(2,1)} custom-call(s32[2,384]{1,0:T(2,128)S(1)} %pad_add_fusion.owner, bf16[512,576]{1,0:T(8,128)(2,1)S(1)} %bitcast.45, bf16[384,576]{1,0:T(8,128)(2,1)} %bitcast.20.refs_0_, bf16[384,576]{1,0:T(8,128)(2,1)S(1)} %bitcast.46), custom_call_target="tpu_custom_call" | custom-call | flops 905969664 | bytes 3479552 | tf_op jit(solution)/shard_map/pallas_call | solution.py:25
  79.8 4.2 %collective-permute-done.16 = bf16[128,1792]{1,0:T(8,128)(2,1)S(1)} collective-permute-done((bf16[128,1792]{1,0:T(8,128)(2,1)S(1)}, bf16[128,1792]{1,0:T(8,128)(2,1)S(1)}, u32[]{:S(2)}, u32[]{:S(2)}) %collective-permute-start.16) | collective-permute-done | bytes 458784 | tf_op jit(solution)/shard_map/ppermute | solution.py:49
  84.7 3.3 %collective-permute-done.13 = bf16[128,1792]{1,0:T(8,128)(2,1)S(1)} collective-permute-done((bf16[128,1792]{1,0:T(8,128)(2,1)S(1)}, bf16[128,1792]{1,0:T(8,128)(2,1)S(1)}, u32[]{:S(2)}, u32[]{:S(2)}) %collective-permute-start.13) | collective-permute-done | bytes 458784 | tf_op jit(solution)/shard_map/ppermute | solution.py:49
  88.6 3.5 %collective-permute-done.18 = bf16[64,1792]{1,0:T(8,128)(2,1)S(1)} collective-permute-done((bf16[64,1792]{1,0:T(8,128)(2,1)S(1)}, bf16[64,1792]{1,0:T(8,128)(2,1)S(1)}, u32[]{:S(2)}, u32[]{:S(2)}) %collective-permute-start.18) | collective-permute-done | bytes 229408 | tf_op jit(solution)/shard_map/ppermute | solution.py:49
  92.2 2.0 %collective-permute-done.14 = bf16[64,1792]{1,0:T(8,128)(2,1)S(1)} collective-permute-done((bf16[64,1792]{1,0:T(8,128)(2,1)S(1)}, bf16[64,1792]{1,0:T(8,128)(2,1)S(1)}, u32[]{:S(2)}, u32[]{:S(2)}) %collective-permute-start.14) | collective-permute-done | bytes 229408 | tf_op jit(solution)/shard_map/ppermute | solution.py:49
  94.3 1.3 %collective-permute-start.19 = (bf16[32,3584]{1,0:T(8,128)(2,1)S(1)}, bf16[32,3584]{1,0:T(8,128)(2,1)S(1)}, u32[]{:S(2)}, u32[]{:S(2)}) collective-permute-start(bf16[32,3584]{1,0:T(8,128)(2,1)S(1)} %pad_maximum_fusion.6), channel_id=1, source_target_pairs={{0,8},{2,10},{4,12},{6,14},{8,0},{10,2},{12,4},{14,6},{16,24},{18,... | collective-permute-start | bytes 688136 | tf_op jit(solution)/shard_map/ppermute | solution.py:49
  95.6 4.8 %collective-permute-done.19 = bf16[32,3584]{1,0:T(8,128)(2,1)S(1)} collective-permute-done((bf16[32,3584]{1,0:T(8,128)(2,1)S(1)}, bf16[32,3584]{1,0:T(8,128)(2,1)S(1)}, u32[]{:S(2)}, u32[]{:S(2)}) %collective-permute-start.19) | collective-permute-done | bytes 229408 | tf_op jit(solution)/shard_map/ppermute | solution.py:49
  101.5 4.7 %collective-permute-done.20 = bf16[16,3584]{1,0:T(8,128)(2,1)S(1)} collective-permute-done((bf16[16,3584]{1,0:T(8,128)(2,1)S(1)}, bf16[16,3584]{1,0:T(8,128)(2,1)S(1)}, u32[]{:S(2)}, u32[]{:S(2)}) %collective-permute-start.20) | collective-permute-done | bytes 114720 | tf_op jit(solution)/shard_map/ppermute | solution.py:49
  (75 shorter events, 21.5 us)
Async XLA Ops:
  2.5 6.0 %collective-permute-start.1 = (bf16[1,16,128]{2,1,0:T(8,128)(2,1)S(1)}, bf16[1,16,128]{2,1,0:T(8,128)(2,1)S(1)}, u32[]{:S(2)}, u32[]{:S(2)}) collective-permute-start(bf16[1,16,128]{2,1,0:T(8,128)(2,1)S(1)} %fusion.18), channel_id=1, source_target_pairs={{0,16},{2,18},{4,20},{6,22},{8,24},{10,26},{12,28},{14,30},{16,0},... | collective-permute-start | bytes 12296 | tf_op jit(solution)/shard_map/ppermute | solution.py:49
  6.5 8.2 %collective-permute-start = (bf16[1,16,3584]{2,1,0:T(8,128)(2,1)}, bf16[1,16,3584]{2,1,0:T(8,128)(2,1)S(1)}, u32[]{:S(2)}, u32[]{:S(2)}) collective-permute-start(bf16[1,16,3584]{2,1,0:T(8,128)(2,1)} %bitcast.50), channel_id=1, source_target_pairs={{0,16},{2,18},{4,20},{6,22},{8,24},{10,26},{12,28},{14,30},{16,0},... | collective-permute-start | bytes 344072 | tf_op jit(solution)/shard_map/ppermute | solution.py:49
  15.6 6.7 %collective-permute-start.2 = (bf16[2,16,3712]{2,1,0:T(8,128)(2,1)S(1)}, bf16[2,16,3712]{2,1,0:T(8,128)(2,1)S(1)}, u32[]{:S(2)}, u32[]{:S(2)}) collective-permute-start(bf16[2,16,3712]{2,1,0:T(8,128)(2,1)S(1)} %maximum_maximum_fusion), channel_id=1, source_target_pairs={{0,8},{2,10},{4,12},{6,14},{8,0},{10,2},{12,4},{14,6},{16,24},{18,... | collective-permute-start | bytes 712712 | tf_op jit(solution)/shard_map/ppermute | solution.py:49
  15.8 19.7 %all-to-all-start = ((bf16[16,24,576]{2,1,0:T(8,128)(2,1)}), bf16[16,24,576]{2,1,0:T(8,128)(2,1)S(1)}, u32[]{:S(2)}, u32[]{:S(2)}) async-start(bf16[16,24,576]{2,1,0:T(8,128)(2,1)} %bitcast.37), calls=%async_computation | async-start | bytes 983040 | tf_op jit(solution)/shard_map/all_to_all | solution.py:467
  23.1 10.0 %collective-permute-start.3 = (bf16[4,16,1792]{2,1,0:T(8,128)(2,1)S(1)}, bf16[4,16,1792]{2,1,0:T(8,128)(2,1)S(1)}, u32[]{:S(2)}, u32[]{:S(2)}) collective-permute-start(bf16[4,16,1792]{2,1,0:T(8,128)(2,1)S(1)} %pad_maximum_fusion.5), channel_id=1, source_target_pairs={{0,4},{2,6},{4,0},{6,2},{8,12},{10,14},{12,8},{14,10},{16,20},{18,... | collective-permute-start | bytes 688136 | tf_op jit(solution)/shard_map/ppermute | solution.py:49
  25.6 9.3 %collective-permute-start.5 = (bf16[4,16,1920]{2,1,0:T(8,128)(2,1)S(1)}, bf16[4,16,1920]{2,1,0:T(8,128)(2,1)S(1)}, u32[]{:S(2)}, u32[]{:S(2)}) collective-permute-start(bf16[4,16,1920]{2,1,0:T(8,128)(2,1)S(1)} %pad_maximum_fusion.2), channel_id=1, source_target_pairs={{0,2},{2,0},{4,6},{6,4},{8,10},{10,8},{12,14},{14,12},{16,18},{18,... | collective-permute-start | bytes 737288 | tf_op jit(solution)/shard_map/ppermute | solution.py:49
  33.1 12.1 %collective-permute-start.4 = (bf16[8,16,1792]{2,1,0:T(8,128)(2,1)S(1)}, bf16[8,16,1792]{2,1,0:T(8,128)(2,1)}, u32[]{:S(2)}, u32[]{:S(2)}) collective-permute-start(bf16[8,16,1792]{2,1,0:T(8,128)(2,1)S(1)} %pad_maximum_fusion.1), channel_id=1, source_target_pairs={{0,2},{2,0},{4,6},{6,4},{8,10},{10,8},{12,14},{14,12},{16,18},{18,... | collective-permute-start | bytes 1376264 | tf_op jit(solution)/shard_map/ppermute | solution.py:49
  35.4 11.0 %collective-permute-start.7 = (bf16[8,16,1920]{2,1,0:T(8,128)(2,1)S(1)}, bf16[8,16,1920]{2,1,0:T(8,128)(2,1)S(1)}, u32[]{:S(2)}, u32[]{:S(2)}) collective-permute-start(bf16[8,16,1920]{2,1,0:T(8,128)(2,1)S(1)} %pad_maximum_fusion), channel_id=1, source_target_pairs={{0,4},{2,6},{4,0},{6,2},{8,12},{10,14},{12,8},{14,10},{16,20},{18,... | collective-permute-start | bytes 1474568 | tf_op jit(solution)/shard_map/ppermute | solution.py:49
  37.7 1.9 %collective-permute-start.6 = (bf16[16,24,576]{2,1,0:T(8,128)(2,1)S(1)}, bf16[16,24,576]{2,1,0:T(8,128)(2,1)S(1)}, u32[]{:S(2)}, u32[]{:S(2)}) collective-permute-start(bf16[16,24,576]{2,1,0:T(8,128)(2,1)S(1)} %all-to-all-done), channel_id=1, source_target_pairs={{0,1},{1,0},{2,3},{3,2},{4,5},{5,4},{6,7},{7,6},{8,9},{9,8},{10,11... | collective-permute-start | bytes 1327112 | tf_op jit(solution)/shard_map/ppermute | solution.py:54
  37.7 15.0 %collective-permute-start.8 = (bf16[8,16,1792]{2,1,0:T(8,128)(2,1)S(1)}, bf16[8,16,1792]{2,1,0:T(8,128)(2,1)}, u32[]{:S(2)}, u32[]{:S(2)}) collective-permute-start(bf16[8,16,1792]{2,1,0:T(8,128)(2,1)S(1)} %pad_maximum_fusion.1), channel_id=1, source_target_pairs={{0,1},{1,0},{2,3},{3,2},{4,5},{5,4},{6,7},{7,6},{8,9},{9,8},{10,11... | collective-permute-start | bytes 1376264 | tf_op jit(solution)/shard_map/ppermute | solution.py:54
  45.2 7.6 %collective-permute-start.9 = (bf16[8,16,1792]{2,1,0:T(8,128)(2,1)}, bf16[8,16,1792]{2,1,0:T(8,128)(2,1)}, u32[]{:S(2)}, u32[]{:S(2)}) collective-permute-start(bf16[8,16,1792]{2,1,0:T(8,128)(2,1)} %collective-permute-done.4), channel_id=1, source_target_pairs={{0,1},{1,0},{2,3},{3,2},{4,5},{5,4},{6,7},{7,6},{8,9},{9,8},{10,11... | collective-permute-start | bytes 1376264 | tf_op jit(solution)/shard_map/ppermute | solution.py:54
  45.2 7.6 %collective-permute-start.10 = (bf16[8,16,1920]{2,1,0:T(8,128)(2,1)S(1)}, bf16[8,16,1920]{2,1,0:T(8,128)(2,1)S(1)}, u32[]{:S(2)}, u32[]{:S(2)}) collective-permute-start(bf16[8,16,1920]{2,1,0:T(8,128)(2,1)S(1)} %pad_maximum_fusion), channel_id=1, source_target_pairs={{0,1},{1,0},{2,3},{3,2},{4,5},{5,4},{6,7},{7,6},{8,9},{9,8},{10,11... | collective-permute-start | bytes 1474568 | tf_op jit(solution)/shard_map/ppermute | solution.py:54
  46.4 6.4 %collective-permute-start.11 = (bf16[8,16,1920]{2,1,0:T(8,128)(2,1)S(1)}, bf16[8,16,1920]{2,1,0:T(8,128)(2,1)S(1)}, u32[]{:S(2)}, u32[]{:S(2)}) collective-permute-start(bf16[8,16,1920]{2,1,0:T(8,128)(2,1)S(1)} %collective-permute-done.7), channel_id=1, source_target_pairs={{0,1},{1,0},{2,3},{3,2},{4,5},{5,4},{6,7},{7,6},{8,9},{9,8},{10,11... | collective-permute-start | bytes 1474568 | tf_op jit(solution)/shard_map/ppermute | solution.py:54
  46.4 21.1 %all-to-all-start.1 = ((bf16[16,24,576]{2,1,0:T(8,128)(2,1)}), bf16[16,24,576]{2,1,0:T(8,128)(2,1)}, u32[]{:S(2)}, u32[]{:S(2)}) async-start(bf16[16,24,576]{2,1,0:T(8,128)(2,1)} %bitcast.6), calls=%async_computation.1 | async-start | bytes 983040 | tf_op jit(solution)/shard_map/all_to_all | solution.py:362
  67.5 8.3 %copy-start.1 = (bf16[16,32,576]{2,1,0:T(8,128)(2,1)S(1)}, bf16[16,32,576]{2,1,0:T(8,128)(2,1)}, u32[]{:S(2)}) copy-start(bf16[16,32,576]{2,1,0:T(8,128)(2,1)} %param.15) | copy-start | bytes 1769476
  67.5 2.7 %collective-permute-start.15 = (bf16[256,1792]{1,0:T(8,128)(2,1)S(1)}, bf16[256,1792]{1,0:T(8,128)(2,1)S(1)}, u32[]{:S(2)}, u32[]{:S(2)}) collective-permute-start(bf16[256,1792]{1,0:T(8,128)(2,1)S(1)} %get-tuple-element.32), channel_id=1, source_target_pairs={{0,1},{1,0},{2,3},{3,2},{4,5},{5,4},{6,7},{7,6},{8,9},{9,8},{10,11... | collective-permute-start | bytes 2752520 | tf_op jit(solution)/shard_map/ppermute | solution.py:54
  67.5 4.7 %collective-permute-start.12 = (bf16[256,1792]{1,0:T(8,128)(2,1)S(1)}, bf16[256,1792]{1,0:T(8,128)(2,1)S(1)}, u32[]{:S(2)}, u32[]{:S(2)}) collective-permute-start(bf16[256,1792]{1,0:T(8,128)(2,1)S(1)} %get-tuple-element.29), channel_id=1, source_target_pairs={{0,1},{1,0},{2,3},{3,2},{4,5},{5,4},{6,7},{7,6},{8,9},{9,8},{10,11... | collective-permute-start | bytes 2752520 | tf_op jit(solution)/shard_map/ppermute | solution.py:54
  70.9 4.9 %collective-permute-start.17 = (bf16[16,24,576]{2,1,0:T(8,128)(2,1)}, bf16[16,24,576]{2,1,0:T(8,128)(2,1)S(1)}, u32[]{:S(2)}, u32[]{:S(2)}) collective-permute-start(bf16[16,24,576]{2,1,0:T(8,128)(2,1)} %all-to-all-done.1), channel_id=1, source_target_pairs={{0,1},{1,0},{2,3},{3,2},{4,5},{5,4},{6,7},{7,6},{8,9},{9,8},{10,11... | collective-permute-start | bytes 1327112 | tf_op jit(solution)/shard_map/ppermute | solution.py:54
  71.0 12.9 %collective-permute-start.16 = (bf16[128,1792]{1,0:T(8,128)(2,1)S(1)}, bf16[128,1792]{1,0:T(8,128)(2,1)S(1)}, u32[]{:S(2)}, u32[]{:S(2)}) collective-permute-start(bf16[128,1792]{1,0:T(8,128)(2,1)S(1)} %shard_map.119), channel_id=1, source_target_pairs={{0,4},{2,6},{4,0},{6,2},{8,12},{10,14},{12,8},{14,10},{16,20},{18,... | collective-permute-start | bytes 1376264 | tf_op jit(solution)/shard_map/ppermute | solution.py:49
  74.5 13.4 %collective-permute-start.13 = (bf16[128,1792]{1,0:T(8,128)(2,1)S(1)}, bf16[128,1792]{1,0:T(8,128)(2,1)S(1)}, u32[]{:S(2)}, u32[]{:S(2)}) collective-permute-start(bf16[128,1792]{1,0:T(8,128)(2,1)S(1)} %get-tuple-element.31), channel_id=1, source_target_pairs={{0,2},{2,0},{4,6},{6,4},{8,10},{10,8},{12,14},{14,12},{16,18},{18,... | collective-permute-start | bytes 1376264 | tf_op jit(solution)/shard_map/ppermute | solution.py:49
  84.0 8.1 %collective-permute-start.18 = (bf16[64,1792]{1,0:T(8,128)(2,1)S(1)}, bf16[64,1792]{1,0:T(8,128)(2,1)S(1)}, u32[]{:S(2)}, u32[]{:S(2)}) collective-permute-start(bf16[64,1792]{1,0:T(8,128)(2,1)S(1)} %get-tuple-element.36), channel_id=1, source_target_pairs={{0,2},{2,0},{4,6},{6,4},{8,10},{10,8},{12,14},{14,12},{16,18},{18,... | collective-permute-start | bytes 688136 | tf_op jit(solution)/shard_map/ppermute | solution.py:49
  88.1 6.1 %collective-permute-start.14 = (bf16[64,1792]{1,0:T(8,128)(2,1)S(1)}, bf16[64,1792]{1,0:T(8,128)(2,1)S(1)}, u32[]{:S(2)}, u32[]{:S(2)}) collective-permute-start(bf16[64,1792]{1,0:T(8,128)(2,1)S(1)} %get-tuple-element.42), channel_id=1, source_target_pairs={{0,4},{2,6},{4,0},{6,2},{8,12},{10,14},{12,8},{14,10},{16,20},{18,... | collective-permute-start | bytes 688136 | tf_op jit(solution)/shard_map/ppermute | solution.py:49
  94.3 6.1 %collective-permute-start.19 = (bf16[32,3584]{1,0:T(8,128)(2,1)S(1)}, bf16[32,3584]{1,0:T(8,128)(2,1)S(1)}, u32[]{:S(2)}, u32[]{:S(2)}) collective-permute-start(bf16[32,3584]{1,0:T(8,128)(2,1)S(1)} %pad_maximum_fusion.6), channel_id=1, source_target_pairs={{0,8},{2,10},{4,12},{6,14},{8,0},{10,2},{12,4},{14,6},{16,24},{18,... | collective-permute-start | bytes 688136 | tf_op jit(solution)/shard_map/ppermute | solution.py:49
  100.4 5.8 %collective-permute-start.20 = (bf16[16,3584]{1,0:T(8,128)(2,1)S(1)}, bf16[16,3584]{1,0:T(8,128)(2,1)S(1)}, u32[]{:S(2)}, u32[]{:S(2)}) collective-permute-start(bf16[16,3584]{1,0:T(8,128)(2,1)S(1)} %add_convert_fusion.5), channel_id=1, source_target_pairs={{0,16},{2,18},{4,20},{6,22},{8,24},{10,26},{12,28},{14,30},{16,0},... | collective-permute-start | bytes 344072 | tf_op jit(solution)/shard_map/ppermute | solution.py:49
  (1 other events, 6.8 us)

commit v16 on v15

--- a/solution.py
+++ b/solution.py
@@ -184,24 +184,31 @@
 def group_kernel(step, chosen, spots, tp_size, cut, rows, hidden, weight, *refs):
     outs, (held, turned, arrived) = refs[: len(chosen)], refs[len(chosen) :]
     target = lax.rem(lax.axis_index("tp") + step, tp_size)
+    pieces = 2 if cut % 256 == 0 else 1
+    width = cut // pieces
     copies = []
     for index, part in enumerate(chosen):
-        start = pl.multiple_of((target * len(spots) + part) * cut, cut)
-        copies.append(
-            pltpu.make_async_copy(
-                weight.at[pl.ds(start, cut)], held.at[index], arrived.at[index]
+        for piece in range(pieces):
+            start = pl.multiple_of((target * len(spots) + part) * cut + piece * width, width)
+            copies.append(
+                pltpu.make_async_copy(
+                    weight.at[pl.ds(start, width)],
+                    held.at[index, pl.ds(piece * width, width)],
+                    arrived.at[index * pieces + piece],
+                )
             )
-        )
     for copy in copies:
         copy.start()
     chunk = min(256, hidden.shape[0])
     for index, part in enumerate(chosen):
         turn_rows(hidden, turned.at[index], spots[part], rows)
-        copies[index].wait()
-        for row in range(0, hidden.shape[0], chunk):
-            outs[index][row : row + chunk] = down_product(
-                turned.at[index], held.at[index], row, chunk, 0, cut
-            ).astype(jnp.bfloat16)
+        for piece in range(pieces):
+            copies[index * pieces + piece].wait()
+            column = piece * width
+            for row in range(0, hidden.shape[0], chunk):
+                outs[index][row : row + chunk, column : column + width] = down_product(
+                    turned.at[index], held.at[index], row, chunk, column, width
+                ).astype(jnp.bfloat16)
 
 
 def down_group(hidden, weight, step, chosen, spots, rows):
@@ -220,7 +227,7 @@
         scratch_shapes=[
             pltpu.VMEM((count, cut, weight.shape[1]), weight.dtype),
             pltpu.VMEM((count,) + hidden.shape, hidden.dtype),
-            pltpu.SemaphoreType.DMA((count,)),
+            pltpu.SemaphoreType.DMA((2 * count,)),
         ],
     )
 

time: 108 us -> 107 us (level)
  no operation moved by 1% of the time
where the time goes in v16:
time: 107 us
  waiting for transfers between devices  44.5 us (42%)
  starting transfers between devices  28.2 us (26%)
  Pallas kernels  15.9 us (15%)
  matrix products  7.79 us (7%)
  local copies, waits for them, and re-layouts  4.73 us (4%)
  other arithmetic  4.62 us (4%)
    ppermute x13, waiting for transfers between devices, exchange(): lax.ppermute(value, 'ep', [(index, index ^ bit) for index in range(ep_siz...  40.8 us
    pallas_call x8, Pallas kernels, kernel_call(): pl.pallas_call(kernel, out_shape=out_shape, in_specs=in_specs or [WHOLE]...  15.9 us
    ppermute x13, starting transfers between devices, exchange(): lax.ppermute(value, 'ep', [(index, index ^ bit) for index in range(ep_siz...  15.1 us
    dot_general x1, matrix products, body(): jnp.einsum('sd,dgf->sgf', all_rows, expert_gate_up[0], preferred_element_...  7.79 us
    all_to_all x1, starting transfers between devices, cache_in(): lax.all_to_all(ordered, 'ep', split_axis=0, concat_axis=0, tiled=True)  6.13 us
    all_to_all x1, starting transfers between devices, beside_shared(): lax.all_to_all(pieces, 'ep', split_axis=0, concat_axis=0, tiled=True)  5.28 us
    unnamed x7, local copies, waits for them, and re-layouts  2.48 us
  transfers between devices with their start and end apart: 23, of which 15 were waited for; matrix products, arithmetic and copies ran while one was open for 13% of the time, Pallas kernels for 15%

profile of v16, /device:TPU:0, one launch (start us, length us, event | category | flops | bytes accessed | tf_op | source)
XLA Modules:
  0.0 106.8 jit_solution(1224626032645022889)
XLA Ops:
  2.5 4.0 %collective-permute-start.1 = (bf16[1,16,128]{2,1,0:T(8,128)(2,1)S(1)}, bf16[1,16,128]{2,1,0:T(8,128)(2,1)S(1)}, u32[]{:S(2)}, u32[]{:S(2)}) collective-permute-start(bf16[1,16,128]{2,1,0:T(8,128)(2,1)S(1)} %fusion.18), channel_id=1, source_target_pairs={{0,16},{2,18},{4,20},{6,22},{8,24},{10,26},{12,28},{14,30},{16,0},... | collective-permute-start | bytes 12296 | tf_op jit(solution)/shard_map/ppermute | solution.py:49
  8.4 6.2 %collective-permute-done = bf16[1,16,3584]{2,1,0:T(8,128)(2,1)S(1)} collective-permute-done((bf16[1,16,3584]{2,1,0:T(8,128)(2,1)}, bf16[1,16,3584]{2,1,0:T(8,128)(2,1)S(1)}, u32[]{:S(2)}, u32[]{:S(2)}) %collective-permute-start) | collective-permute-done | bytes 114720 | tf_op jit(solution)/shard_map/ppermute | solution.py:49
  15.8 5.3 %all-to-all-start = ((bf16[16,24,576]{2,1,0:T(8,128)(2,1)}), bf16[16,24,576]{2,1,0:T(8,128)(2,1)S(1)}, u32[]{:S(2)}, u32[]{:S(2)}) async-start(bf16[16,24,576]{2,1,0:T(8,128)(2,1)} %bitcast.37), calls=%async_computation | async-start | bytes 983040 | tf_op jit(solution)/shard_map/all_to_all | solution.py:474
  23.1 1.6 %collective-permute-start.3 = (bf16[4,16,1792]{2,1,0:T(8,128)(2,1)S(1)}, bf16[4,16,1792]{2,1,0:T(8,128)(2,1)S(1)}, u32[]{:S(2)}, u32[]{:S(2)}) collective-permute-start(bf16[4,16,1792]{2,1,0:T(8,128)(2,1)S(1)} %pad_maximum_fusion.5), channel_id=1, source_target_pairs={{0,4},{2,6},{4,0},{6,2},{8,12},{10,14},{12,8},{14,10},{16,20},{18,... | collective-permute-start | bytes 688136 | tf_op jit(solution)/shard_map/ppermute | solution.py:49
  25.6 1.6 %collective-permute-start.5 = (bf16[4,16,1920]{2,1,0:T(8,128)(2,1)S(1)}, bf16[4,16,1920]{2,1,0:T(8,128)(2,1)S(1)}, u32[]{:S(2)}, u32[]{:S(2)}) collective-permute-start(bf16[4,16,1920]{2,1,0:T(8,128)(2,1)S(1)} %pad_maximum_fusion.2), channel_id=1, source_target_pairs={{0,2},{2,0},{4,6},{6,4},{8,10},{10,8},{12,14},{14,12},{16,18},{18,... | collective-permute-start | bytes 737288 | tf_op jit(solution)/shard_map/ppermute | solution.py:49
  27.1 6.0 %collective-permute-done.3 = bf16[4,16,1792]{2,1,0:T(8,128)(2,1)S(1)} collective-permute-done((bf16[4,16,1792]{2,1,0:T(8,128)(2,1)S(1)}, bf16[4,16,1792]{2,1,0:T(8,128)(2,1)S(1)}, u32[]{:S(2)}, u32[]{:S(2)}) %collective-permute-start.3) | collective-permute-done | bytes 229408 | tf_op jit(solution)/shard_map/ppermute | solution.py:49
  33.1 1.3 %collective-permute-start.4 = (bf16[8,16,1792]{2,1,0:T(8,128)(2,1)S(1)}, bf16[8,16,1792]{2,1,0:T(8,128)(2,1)}, u32[]{:S(2)}, u32[]{:S(2)}) collective-permute-start(bf16[8,16,1792]{2,1,0:T(8,128)(2,1)S(1)} %pad_maximum_fusion.1), channel_id=1, source_target_pairs={{0,2},{2,0},{4,6},{6,4},{8,10},{10,8},{12,14},{14,12},{16,18},{18,... | collective-permute-start | bytes 1376264 | tf_op jit(solution)/shard_map/ppermute | solution.py:49
  39.6 1.6 %shard_map.113 = bf16[384,576]{1,0:T(8,128)(2,1)} custom-call(s32[384,2]{1,0:T(8,128)S(1)} %fusion.7.index, bf16[384,576]{1,0:T(8,128)(2,1)S(1)} %bitcast.39, bf16[384,576]{1,0:T(8,128)(2,1)S(1)} %bitcast.44), custom_call_target="tpu_custom_call" | custom-call | flops 339738624 | bytes 2217984 | tf_op jit(solution)/shard_map/pallas_call | solution.py:25
  41.2 4.0 %collective-permute-done.4 = bf16[8,16,1792]{2,1,0:T(8,128)(2,1)} collective-permute-done((bf16[8,16,1792]{2,1,0:T(8,128)(2,1)S(1)}, bf16[8,16,1792]{2,1,0:T(8,128)(2,1)}, u32[]{:S(2)}, u32[]{:S(2)}) %collective-permute-start.4) | collective-permute-done | bytes 458784 | tf_op jit(solution)/shard_map/ppermute | solution.py:49
  46.4 6.1 %all-to-all-start.1 = ((bf16[16,24,576]{2,1,0:T(8,128)(2,1)}), bf16[16,24,576]{2,1,0:T(8,128)(2,1)}, u32[]{:S(2)}, u32[]{:S(2)}) async-start(bf16[16,24,576]{2,1,0:T(8,128)(2,1)} %bitcast.6), calls=%async_computation.1 | async-start | bytes 983040 | tf_op jit(solution)/shard_map/all_to_all | solution.py:369
  52.8 1.5 %shard_map.114 = bf16[256,7168]{1,0:T(8,128)(2,1)S(1)} custom-call(bf16[128,1792]{1,0:T(8,128)(2,1)S(1)} %bitcast.40, bf16[128,1792]{1,0:T(8,128)(2,1)} %bitcast.7.refs_1_, bf16[128,1920]{1,0:T(8,128)(2,1)S(1)} %bitcast.38, bf16[128,1920]{1,0:T(8,128)(2,1)S(1)} %bitcast.41, bf16[128,1792]{1,0:T(8,128)(2,1)} %bitcast.10.refs_4_, ...), custom_call_target="tpu_custom_call" | custom-call | tf_op jit(solution)/shard_map/pallas_call | solution.py:25
  54.4 7.8 %fusion = f32[256,2,512]{2,0,1:T(8,128)S(1)} fusion(bf16[7168,2,512]{2,1,0:T(2,128)(2,1)} %bitcast.54, bf16[256,7168]{1,0:T(8,128)(2,1)S(1)} %shard_map.114), kind=kOutput, calls=%fused_computation | convolution fusion | flops 3758096384 | bytes 19398656 | tf_op jit(solution)/shard_map/sd,dgf->sgf/dot_general | solution.py:505
  62.3 3.1 %shard_map.115 = (bf16[256,1792]{1,0:T(8,128)(2,1)S(1)}, bf16[256,1792]{1,0:T(8,128)(2,1)S(1)}) custom-call(bf16[256,512]{1,0:T(8,128)(2,1)S(1)} %fusion.5.hidden, bf16[7168,512]{1,0:T(8,128)(2,1)} %bitcast.47), custom_call_target="tpu_custom_call" | custom-call | tf_op jit(solution)/shard_map/pallas_call | solution.py:25
  65.5 2.0 %all-to-all-done.1 = bf16[16,24,576]{2,1,0:T(8,128)(2,1)} async-done(((bf16[16,24,576]{2,1,0:T(8,128)(2,1)}), bf16[16,24,576]{2,1,0:T(8,128)(2,1)}, u32[]{:S(2)}, u32[]{:S(2)}) %all-to-all-start.1) | async-done | bytes 442400 | tf_op jit(solution)/shard_map/all_to_all | solution.py:369
  68.0 2.2 %shard_map.117.refs_0_ = bf16[256,1792]{1,0:T(8,128)(2,1)S(1)} custom-call(bf16[256,512]{1,0:T(8,128)(2,1)S(1)} %fusion.5.hidden, bf16[7168,512]{1,0:T(8,128)(2,1)} %bitcast.48), custom_call_target="tpu_custom_call" | custom-call | tf_op jit(solution)/shard_map/pallas_call | solution.py:25
  72.2 2.3 %shard_map.116 = (bf16[128,1792]{1,0:T(8,128)(2,1)S(1)}, bf16[128,1792]{1,0:T(8,128)(2,1)S(1)}) custom-call(bf16[256,512]{1,0:T(8,128)(2,1)S(1)} %fusion.5.hidden, bf16[7168,512]{1,0:T(8,128)(2,1)} %bitcast.49, bf16[256,1792]{1,0:T(8,128)(2,1)S(1)} %collective-permute-done.12.refs_0_), custom_call_target="tpu_custom_call" | custom-call | flops 469762048 | bytes 9699328 | tf_op jit(solution)/shard_map/pallas_call | solution.py:25
  75.8 4.0 %shard_map.120 = bf16[512,512]{1,0:T(8,128)(2,1)} custom-call(s32[2,384]{1,0:T(2,128)S(1)} %pad_add_fusion.owner, bf16[512,576]{1,0:T(8,128)(2,1)S(1)} %bitcast.45, bf16[384,576]{1,0:T(8,128)(2,1)} %bitcast.20.refs_0_, bf16[384,576]{1,0:T(8,128)(2,1)S(1)} %bitcast.46), custom_call_target="tpu_custom_call" | custom-call | flops 905969664 | bytes 3479552 | tf_op jit(solution)/shard_map/pallas_call | solution.py:25
  79.7 4.2 %collective-permute-done.16 = bf16[128,1792]{1,0:T(8,128)(2,1)S(1)} collective-permute-done((bf16[128,1792]{1,0:T(8,128)(2,1)S(1)}, bf16[128,1792]{1,0:T(8,128)(2,1)S(1)}, u32[]{:S(2)}, u32[]{:S(2)}) %collective-permute-start.16) | collective-permute-done | bytes 458784 | tf_op jit(solution)/shard_map/ppermute | solution.py:49
  84.6 3.3 %collective-permute-done.13 = bf16[128,1792]{1,0:T(8,128)(2,1)S(1)} collective-permute-done((bf16[128,1792]{1,0:T(8,128)(2,1)S(1)}, bf16[128,1792]{1,0:T(8,128)(2,1)S(1)}, u32[]{:S(2)}, u32[]{:S(2)}) %collective-permute-start.13) | collective-permute-done | bytes 458784 | tf_op jit(solution)/shard_map/ppermute | solution.py:49
  88.6 3.4 %collective-permute-done.18 = bf16[64,1792]{1,0:T(8,128)(2,1)S(1)} collective-permute-done((bf16[64,1792]{1,0:T(8,128)(2,1)S(1)}, bf16[64,1792]{1,0:T(8,128)(2,1)S(1)}, u32[]{:S(2)}, u32[]{:S(2)}) %collective-permute-start.18) | collective-permute-done | bytes 229408 | tf_op jit(solution)/shard_map/ppermute | solution.py:49
  92.1 2.0 %collective-permute-done.14 = bf16[64,1792]{1,0:T(8,128)(2,1)S(1)} collective-permute-done((bf16[64,1792]{1,0:T(8,128)(2,1)S(1)}, bf16[64,1792]{1,0:T(8,128)(2,1)S(1)}, u32[]{:S(2)}, u32[]{:S(2)}) %collective-permute-start.14) | collective-permute-done | bytes 229408 | tf_op jit(solution)/shard_map/ppermute | solution.py:49
  94.2 1.3 %collective-permute-start.19 = (bf16[32,3584]{1,0:T(8,128)(2,1)S(1)}, bf16[32,3584]{1,0:T(8,128)(2,1)S(1)}, u32[]{:S(2)}, u32[]{:S(2)}) collective-permute-start(bf16[32,3584]{1,0:T(8,128)(2,1)S(1)} %pad_maximum_fusion.6), channel_id=1, source_target_pairs={{0,8},{2,10},{4,12},{6,14},{8,0},{10,2},{12,4},{14,6},{16,24},{18,... | collective-permute-start | bytes 688136 | tf_op jit(solution)/shard_map/ppermute | solution.py:49
  95.5 4.8 %collective-permute-done.19 = bf16[32,3584]{1,0:T(8,128)(2,1)S(1)} collective-permute-done((bf16[32,3584]{1,0:T(8,128)(2,1)S(1)}, bf16[32,3584]{1,0:T(8,128)(2,1)S(1)}, u32[]{:S(2)}, u32[]{:S(2)}) %collective-permute-start.19) | collective-permute-done | bytes 229408 | tf_op jit(solution)/shard_map/ppermute | solution.py:49
  101.5 4.5 %collective-permute-done.20 = bf16[16,3584]{1,0:T(8,128)(2,1)S(1)} collective-permute-done((bf16[16,3584]{1,0:T(8,128)(2,1)S(1)}, bf16[16,3584]{1,0:T(8,128)(2,1)S(1)}, u32[]{:S(2)}, u32[]{:S(2)}) %collective-permute-start.20) | collective-permute-done | bytes 114720 | tf_op jit(solution)/shard_map/ppermute | solution.py:49
  (75 shorter events, 21.7 us)
Async XLA Ops:
  2.5 6.0 %collective-permute-start.1 = (bf16[1,16,128]{2,1,0:T(8,128)(2,1)S(1)}, bf16[1,16,128]{2,1,0:T(8,128)(2,1)S(1)}, u32[]{:S(2)}, u32[]{:S(2)}) collective-permute-start(bf16[1,16,128]{2,1,0:T(8,128)(2,1)S(1)} %fusion.18), channel_id=1, source_target_pairs={{0,16},{2,18},{4,20},{6,22},{8,24},{10,26},{12,28},{14,30},{16,0},... | collective-permute-start | bytes 12296 | tf_op jit(solution)/shard_map/ppermute | solution.py:49
  6.5 8.2 %collective-permute-start = (bf16[1,16,3584]{2,1,0:T(8,128)(2,1)}, bf16[1,16,3584]{2,1,0:T(8,128)(2,1)S(1)}, u32[]{:S(2)}, u32[]{:S(2)}) collective-permute-start(bf16[1,16,3584]{2,1,0:T(8,128)(2,1)} %bitcast.50), channel_id=1, source_target_pairs={{0,16},{2,18},{4,20},{6,22},{8,24},{10,26},{12,28},{14,30},{16,0},... | collective-permute-start | bytes 344072 | tf_op jit(solution)/shard_map/ppermute | solution.py:49
  15.6 6.7 %collective-permute-start.2 = (bf16[2,16,3712]{2,1,0:T(8,128)(2,1)S(1)}, bf16[2,16,3712]{2,1,0:T(8,128)(2,1)S(1)}, u32[]{:S(2)}, u32[]{:S(2)}) collective-permute-start(bf16[2,16,3712]{2,1,0:T(8,128)(2,1)S(1)} %maximum_maximum_fusion), channel_id=1, source_target_pairs={{0,8},{2,10},{4,12},{6,14},{8,0},{10,2},{12,4},{14,6},{16,24},{18,... | collective-permute-start | bytes 712712 | tf_op jit(solution)/shard_map/ppermute | solution.py:49
  15.8 19.7 %all-to-all-start = ((bf16[16,24,576]{2,1,0:T(8,128)(2,1)}), bf16[16,24,576]{2,1,0:T(8,128)(2,1)S(1)}, u32[]{:S(2)}, u32[]{:S(2)}) async-start(bf16[16,24,576]{2,1,0:T(8,128)(2,1)} %bitcast.37), calls=%async_computation | async-start | bytes 983040 | tf_op jit(solution)/shard_map/all_to_all | solution.py:474
  23.1 10.0 %collective-permute-start.3 = (bf16[4,16,1792]{2,1,0:T(8,128)(2,1)S(1)}, bf16[4,16,1792]{2,1,0:T(8,128)(2,1)S(1)}, u32[]{:S(2)}, u32[]{:S(2)}) collective-permute-start(bf16[4,16,1792]{2,1,0:T(8,128)(2,1)S(1)} %pad_maximum_fusion.5), channel_id=1, source_target_pairs={{0,4},{2,6},{4,0},{6,2},{8,12},{10,14},{12,8},{14,10},{16,20},{18,... | collective-permute-start | bytes 688136 | tf_op jit(solution)/shard_map/ppermute | solution.py:49
  25.6 9.3 %collective-permute-start.5 = (bf16[4,16,1920]{2,1,0:T(8,128)(2,1)S(1)}, bf16[4,16,1920]{2,1,0:T(8,128)(2,1)S(1)}, u32[]{:S(2)}, u32[]{:S(2)}) collective-permute-start(bf16[4,16,1920]{2,1,0:T(8,128)(2,1)S(1)} %pad_maximum_fusion.2), channel_id=1, source_target_pairs={{0,2},{2,0},{4,6},{6,4},{8,10},{10,8},{12,14},{14,12},{16,18},{18,... | collective-permute-start | bytes 737288 | tf_op jit(solution)/shard_map/ppermute | solution.py:49
  33.1 12.1 %collective-permute-start.4 = (bf16[8,16,1792]{2,1,0:T(8,128)(2,1)S(1)}, bf16[8,16,1792]{2,1,0:T(8,128)(2,1)}, u32[]{:S(2)}, u32[]{:S(2)}) collective-permute-start(bf16[8,16,1792]{2,1,0:T(8,128)(2,1)S(1)} %pad_maximum_fusion.1), channel_id=1, source_target_pairs={{0,2},{2,0},{4,6},{6,4},{8,10},{10,8},{12,14},{14,12},{16,18},{18,... | collective-permute-start | bytes 1376264 | tf_op jit(solution)/shard_map/ppermute | solution.py:49
  35.4 11.0 %collective-permute-start.7 = (bf16[8,16,1920]{2,1,0:T(8,128)(2,1)S(1)}, bf16[8,16,1920]{2,1,0:T(8,128)(2,1)S(1)}, u32[]{:S(2)}, u32[]{:S(2)}) collective-permute-start(bf16[8,16,1920]{2,1,0:T(8,128)(2,1)S(1)} %pad_maximum_fusion), channel_id=1, source_target_pairs={{0,4},{2,6},{4,0},{6,2},{8,12},{10,14},{12,8},{14,10},{16,20},{18,... | collective-permute-start | bytes 1474568 | tf_op jit(solution)/shard_map/ppermute | solution.py:49
  37.7 1.9 %collective-permute-start.6 = (bf16[16,24,576]{2,1,0:T(8,128)(2,1)S(1)}, bf16[16,24,576]{2,1,0:T(8,128)(2,1)S(1)}, u32[]{:S(2)}, u32[]{:S(2)}) collective-permute-start(bf16[16,24,576]{2,1,0:T(8,128)(2,1)S(1)} %all-to-all-done), channel_id=1, source_target_pairs={{0,1},{1,0},{2,3},{3,2},{4,5},{5,4},{6,7},{7,6},{8,9},{9,8},{10,11... | collective-permute-start | bytes 1327112 | tf_op jit(solution)/shard_map/ppermute | solution.py:54
  37.7 15.0 %collective-permute-start.8 = (bf16[8,16,1792]{2,1,0:T(8,128)(2,1)S(1)}, bf16[8,16,1792]{2,1,0:T(8,128)(2,1)}, u32[]{:S(2)}, u32[]{:S(2)}) collective-permute-start(bf16[8,16,1792]{2,1,0:T(8,128)(2,1)S(1)} %pad_maximum_fusion.1), channel_id=1, source_target_pairs={{0,1},{1,0},{2,3},{3,2},{4,5},{5,4},{6,7},{7,6},{8,9},{9,8},{10,11... | collective-permute-start | bytes 1376264 | tf_op jit(solution)/shard_map/ppermute | solution.py:54
  45.2 7.6 %collective-permute-start.9 = (bf16[8,16,1792]{2,1,0:T(8,128)(2,1)}, bf16[8,16,1792]{2,1,0:T(8,128)(2,1)}, u32[]{:S(2)}, u32[]{:S(2)}) collective-permute-start(bf16[8,16,1792]{2,1,0:T(8,128)(2,1)} %collective-permute-done.4), channel_id=1, source_target_pairs={{0,1},{1,0},{2,3},{3,2},{4,5},{5,4},{6,7},{7,6},{8,9},{9,8},{10,11... | collective-permute-start | bytes 1376264 | tf_op jit(solution)/shard_map/ppermute | solution.py:54
  45.2 7.6 %collective-permute-start.10 = (bf16[8,16,1920]{2,1,0:T(8,128)(2,1)S(1)}, bf16[8,16,1920]{2,1,0:T(8,128)(2,1)S(1)}, u32[]{:S(2)}, u32[]{:S(2)}) collective-permute-start(bf16[8,16,1920]{2,1,0:T(8,128)(2,1)S(1)} %pad_maximum_fusion), channel_id=1, source_target_pairs={{0,1},{1,0},{2,3},{3,2},{4,5},{5,4},{6,7},{7,6},{8,9},{9,8},{10,11... | collective-permute-start | bytes 1474568 | tf_op jit(solution)/shard_map/ppermute | solution.py:54
  46.4 6.4 %collective-permute-start.11 = (bf16[8,16,1920]{2,1,0:T(8,128)(2,1)S(1)}, bf16[8,16,1920]{2,1,0:T(8,128)(2,1)S(1)}, u32[]{:S(2)}, u32[]{:S(2)}) collective-permute-start(bf16[8,16,1920]{2,1,0:T(8,128)(2,1)S(1)} %collective-permute-done.7), channel_id=1, source_target_pairs={{0,1},{1,0},{2,3},{3,2},{4,5},{5,4},{6,7},{7,6},{8,9},{9,8},{10,11... | collective-permute-start | bytes 1474568 | tf_op jit(solution)/shard_map/ppermute | solution.py:54
  46.4 21.1 %all-to-all-start.1 = ((bf16[16,24,576]{2,1,0:T(8,128)(2,1)}), bf16[16,24,576]{2,1,0:T(8,128)(2,1)}, u32[]{:S(2)}, u32[]{:S(2)}) async-start(bf16[16,24,576]{2,1,0:T(8,128)(2,1)} %bitcast.6), calls=%async_computation.1 | async-start | bytes 983040 | tf_op jit(solution)/shard_map/all_to_all | solution.py:369
  67.5 8.3 %copy-start.1 = (bf16[16,32,576]{2,1,0:T(8,128)(2,1)S(1)}, bf16[16,32,576]{2,1,0:T(8,128)(2,1)}, u32[]{:S(2)}) copy-start(bf16[16,32,576]{2,1,0:T(8,128)(2,1)} %param.15) | copy-start | bytes 1769476
  67.5 2.7 %collective-permute-start.15 = (bf16[256,1792]{1,0:T(8,128)(2,1)S(1)}, bf16[256,1792]{1,0:T(8,128)(2,1)S(1)}, u32[]{:S(2)}, u32[]{:S(2)}) collective-permute-start(bf16[256,1792]{1,0:T(8,128)(2,1)S(1)} %get-tuple-element.32), channel_id=1, source_target_pairs={{0,1},{1,0},{2,3},{3,2},{4,5},{5,4},{6,7},{7,6},{8,9},{9,8},{10,11... | collective-permute-start | bytes 2752520 | tf_op jit(solution)/shard_map/ppermute | solution.py:54
  67.5 4.7 %collective-permute-start.12 = (bf16[256,1792]{1,0:T(8,128)(2,1)S(1)}, bf16[256,1792]{1,0:T(8,128)(2,1)S(1)}, u32[]{:S(2)}, u32[]{:S(2)}) collective-permute-start(bf16[256,1792]{1,0:T(8,128)(2,1)S(1)} %get-tuple-element.29), channel_id=1, source_target_pairs={{0,1},{1,0},{2,3},{3,2},{4,5},{5,4},{6,7},{7,6},{8,9},{9,8},{10,11... | collective-permute-start | bytes 2752520 | tf_op jit(solution)/shard_map/ppermute | solution.py:54
  70.9 4.9 %collective-permute-start.17 = (bf16[16,24,576]{2,1,0:T(8,128)(2,1)}, bf16[16,24,576]{2,1,0:T(8,128)(2,1)S(1)}, u32[]{:S(2)}, u32[]{:S(2)}) collective-permute-start(bf16[16,24,576]{2,1,0:T(8,128)(2,1)} %all-to-all-done.1), channel_id=1, source_target_pairs={{0,1},{1,0},{2,3},{3,2},{4,5},{5,4},{6,7},{7,6},{8,9},{9,8},{10,11... | collective-permute-start | bytes 1327112 | tf_op jit(solution)/shard_map/ppermute | solution.py:54
  70.9 12.9 %collective-permute-start.16 = (bf16[128,1792]{1,0:T(8,128)(2,1)S(1)}, bf16[128,1792]{1,0:T(8,128)(2,1)S(1)}, u32[]{:S(2)}, u32[]{:S(2)}) collective-permute-start(bf16[128,1792]{1,0:T(8,128)(2,1)S(1)} %shard_map.119), channel_id=1, source_target_pairs={{0,4},{2,6},{4,0},{6,2},{8,12},{10,14},{12,8},{14,10},{16,20},{18,... | collective-permute-start | bytes 1376264 | tf_op jit(solution)/shard_map/ppermute | solution.py:49
  74.4 13.4 %collective-permute-start.13 = (bf16[128,1792]{1,0:T(8,128)(2,1)S(1)}, bf16[128,1792]{1,0:T(8,128)(2,1)S(1)}, u32[]{:S(2)}, u32[]{:S(2)}) collective-permute-start(bf16[128,1792]{1,0:T(8,128)(2,1)S(1)} %get-tuple-element.31), channel_id=1, source_target_pairs={{0,2},{2,0},{4,6},{6,4},{8,10},{10,8},{12,14},{14,12},{16,18},{18,... | collective-permute-start | bytes 1376264 | tf_op jit(solution)/shard_map/ppermute | solution.py:49
  84.0 8.0 %collective-permute-start.18 = (bf16[64,1792]{1,0:T(8,128)(2,1)S(1)}, bf16[64,1792]{1,0:T(8,128)(2,1)S(1)}, u32[]{:S(2)}, u32[]{:S(2)}) collective-permute-start(bf16[64,1792]{1,0:T(8,128)(2,1)S(1)} %get-tuple-element.36), channel_id=1, source_target_pairs={{0,2},{2,0},{4,6},{6,4},{8,10},{10,8},{12,14},{14,12},{16,18},{18,... | collective-permute-start | bytes 688136 | tf_op jit(solution)/shard_map/ppermute | solution.py:49
  88.0 6.1 %collective-permute-start.14 = (bf16[64,1792]{1,0:T(8,128)(2,1)S(1)}, bf16[64,1792]{1,0:T(8,128)(2,1)S(1)}, u32[]{:S(2)}, u32[]{:S(2)}) collective-permute-start(bf16[64,1792]{1,0:T(8,128)(2,1)S(1)} %get-tuple-element.42), channel_id=1, source_target_pairs={{0,4},{2,6},{4,0},{6,2},{8,12},{10,14},{12,8},{14,10},{16,20},{18,... | collective-permute-start | bytes 688136 | tf_op jit(solution)/shard_map/ppermute | solution.py:49
  94.2 6.1 %collective-permute-start.19 = (bf16[32,3584]{1,0:T(8,128)(2,1)S(1)}, bf16[32,3584]{1,0:T(8,128)(2,1)S(1)}, u32[]{:S(2)}, u32[]{:S(2)}) collective-permute-start(bf16[32,3584]{1,0:T(8,128)(2,1)S(1)} %pad_maximum_fusion.6), channel_id=1, source_target_pairs={{0,8},{2,10},{4,12},{6,14},{8,0},{10,2},{12,4},{14,6},{16,24},{18,... | collective-permute-start | bytes 688136 | tf_op jit(solution)/shard_map/ppermute | solution.py:49
  100.3 5.8 %collective-permute-start.20 = (bf16[16,3584]{1,0:T(8,128)(2,1)S(1)}, bf16[16,3584]{1,0:T(8,128)(2,1)S(1)}, u32[]{:S(2)}, u32[]{:S(2)}) collective-permute-start(bf16[16,3584]{1,0:T(8,128)(2,1)S(1)} %add_convert_fusion.5), channel_id=1, source_target_pairs={{0,16},{2,18},{4,20},{6,22},{8,24},{10,26},{12,28},{14,30},{16,0},... | collective-permute-start | bytes 344072 | tf_op jit(solution)/shard_map/ppermute | solution.py:49
  (1 other events, 6.8 us)
